TPU v7x, 32 devices: a whole 2x2x4 slice. The times are simulated.
32 devices in a mesh: dp: 4 (over x, core), seq: 8 (over z, y).
Axes of the slice: x: 2, y: 2, z: 4, core: 2. Of those that a mesh axis runs over, the one named last changes fastest.
Arguments:
- tokens: bfloat16 [8, 2048, 2048], P('dp', 'seq'), may hold values from -6 to 6
- cotangent: bfloat16 [8, 2048, 2048], P('dp', 'seq'), may hold values from -6 to 6
- segments: int32 [8, 2048], P('dp'), may hold values from 0 to 3, as said below
- joint_projection_matrix: bfloat16 [2048, 2560], P(('dp', 'seq')), may hold values from -0.125 to 0.125
- output_weight_rows: bfloat16 [2048, 2048], P(('dp', 'seq')), may hold values from -1 to 1
- gate_up_weight: bfloat16 [2048, 11264], P(('dp', 'seq')), may hold values from -0.125 to 0.125
- down_weight_rows: bfloat16 [2048, 5632], P(('dp', 'seq')), may hold values from -0.078125 to 0.078125
- attn_gain: bfloat16 [2048], replicated, may hold values from 0.099609375 to 1.8984375
- ffn_gain: bfloat16 [2048], replicated, may hold values from 0.099609375 to 1.8984375
Outputs:
- output: bfloat16 [8, 2048, 2048], P('dp', 'seq')
- d_tokens: float32 [8, 2048, 2048], P('dp', 'seq')
- d_w_qkv: float32 [2048, 2560], P(('dp', 'seq'))
- d_w_out_t: float32 [2048, 2048], P(('dp', 'seq'))
- d_w_gate_up: float32 [2048, 11264], P(('dp', 'seq'))
- d_w_down_t: float32 [2048, 5632], P(('dp', 'seq'))
- d_attn_gain: float32 [2048], replicated
- d_ffn_gain: float32 [2048], replicated
Inputs may be any that keep to these rules, and one draw needn't show every extreme that they name: `segments`: segment numbers start at 0 and never fall along a sequence. A sequence holds one document or 4; of the 2 sequences of each index of dp, one chosen at random is a single document.
All inputs are finite; a program needn't handle non-finite values.
Results may differ from a plain program's by a relative error of at most 0.015.
Values may be sent and summed in bfloat16 or wider, within the bound.
No kernel may reach another device: no remote copies, remote signals or barrier semaphores. Data moves between devices by JAX's collectives and lax.ppermute only.
A program may use at most 640 MiB of HBM per device.

v0:
```python
import jax
import jax.numpy as jnp
from jax import lax
from jax.sharding import PartitionSpec as P

H = 32
HD = 64
KV = 4
FF = 5632


EPSILON = 1e-05
MASKED = -1e30
ROTARY_BASE = 10000.0


def doc_positions(segments):
    length = segments.shape[-1]
    column = jnp.arange(length, dtype=jnp.int32)
    starts_here = jnp.concatenate(
        [jnp.ones(segments.shape[:-1] + (1,), dtype=bool), segments[..., 1:] != segments[..., :-1]],
        axis=-1,
    )
    doc_start = lax.cummax(jnp.where(starts_here, column, 0), axis=segments.ndim - 1)
    return column - doc_start


def rotary_tables(position, head_size):
    half_size = head_size // 2
    frequency = ROTARY_BASE ** (-(jnp.arange(half_size, dtype=jnp.float32) * 2.0) / head_size)
    angles = position.astype(jnp.float32)[..., None] * frequency
    return (jnp.cos(angles), jnp.sin(angles))


def rotate(values, cosine, sine_part):
    half_size = values.shape[-1] // 2
    first_half = values[..., :half_size]
    second_half = values[..., half_size:]
    return jnp.concatenate(
        [
            first_half * cosine - second_half * sine_part,
            second_half * cosine + first_half * sine_part,
        ],
        axis=-1,
    )


def rms_scale(hidden):
    return lax.rsqrt(jnp.mean(hidden * hidden, axis=-1, keepdims=True) + EPSILON)


def rms_back(grad_scaled, rescaled_tokens, inverse):
    return inverse * (
        grad_scaled
        - rescaled_tokens * jnp.mean(grad_scaled * rescaled_tokens, axis=-1, keepdims=True)
    )


def column_adder(operand, piece):
    return jnp.dot(operand, piece, preferred_element_type=jnp.float32)


def row_projector(operand, piece):
    return lax.dot_general(
        operand, piece, (((1,), (1,)), ((), ())), preferred_element_type=jnp.float32
    )


def outer_rows(left_part, right_part):
    return lax.dot_general(
        left_part, right_part, (((0,), (0,)), ((), ())), preferred_element_type=jnp.float32
    )


def local(
    tokens,
    cotangent,
    segments,
    joint_projection_matrix,
    output_weight_rows,
    gate_up_weight,
    down_weight_rows,
    attn_gain,
    ffn_gain,
):
    sequence_shard_count = lax.axis_size("seq")
    seq_index = lax.axis_index("seq")
    local_seqs, local_len, width = tokens.shape
    full_len = segments.shape[1]
    tok_rows = local_seqs * local_len
    heads_dev = H // sequence_shard_count
    head_width = heads_dev * HD
    q_width = H * HD
    kv_width = KV * HD
    proj_cols = joint_projection_matrix.shape[1]
    copies = sequence_shard_count // KV
    score_scale = HD ** (-0.5)
    query_block = min(512, full_len)
    block_count = full_len // query_block
    key_index = jnp.arange(full_len, dtype=jnp.int32)
    gain_one = attn_gain.astype(jnp.float32)
    gain_two = ffn_gain.astype(jnp.float32)
    position = doc_positions(segments)
    cos_full, sin_full = rotary_tables(position, HD)
    cos_local = lax.dynamic_slice_in_dim(cos_full, seq_index * local_len, local_len, 1).reshape(
        tok_rows, 1, HD // 2
    )
    sine_table_shard = lax.dynamic_slice_in_dim(
        sin_full, seq_index * local_len, local_len, 1
    ).reshape(tok_rows, 1, HD // 2)
    hidden_in = tokens.reshape(tok_rows, width).astype(jnp.float32)
    inverse_one = rms_scale(hidden_in)
    scaled_one = hidden_in * inverse_one
    prenorm_activations = (scaled_one * gain_one).astype(jnp.bfloat16)
    piece_qkv = lax.all_gather(joint_projection_matrix, ("dp", "seq"), axis=0, tiled=True)
    piece_out = lax.all_gather(output_weight_rows, ("dp", "seq"), axis=0, tiled=True)
    columns = prenorm_activations
    running = jnp.dot(columns, piece_qkv, preferred_element_type=jnp.float32)
    out_weight = piece_out
    mapped_token_vectors, out_weight = (running, out_weight)
    query = mapped_token_vectors[:, :q_width].reshape(tok_rows, H, HD)
    key_part = mapped_token_vectors[:, q_width : q_width + kv_width].reshape(tok_rows, KV, HD)
    value_part = mapped_token_vectors[:, q_width + kv_width :].reshape(tok_rows, KV, HD)
    query = rotate(query, cos_local, sine_table_shard).astype(jnp.bfloat16)
    key_part = rotate(key_part, cos_local, sine_table_shard).astype(jnp.bfloat16)
    value_part = value_part.astype(jnp.bfloat16)
    kv_slots = jnp.repeat(jnp.concatenate([key_part, value_part], axis=-1), copies, axis=1)
    query_send = query.reshape(local_seqs, local_len, sequence_shard_count, head_width)
    kv_send = kv_slots.reshape(local_seqs, local_len, sequence_shard_count, 2 * HD)
    query_heads, keyval_heads = (
        lax.all_to_all(query_send, "seq", split_axis=2, concat_axis=1, tiled=True),
        lax.all_to_all(kv_send, "seq", split_axis=2, concat_axis=1, tiled=True),
    )
    query_heads = query_heads.reshape(local_seqs, full_len, heads_dev, HD)
    keyval_heads = keyval_heads.reshape(local_seqs, full_len, 2 * HD)

    def block_mask(seg_ids, block_start):
        query_pos = block_start + jnp.arange(query_block, dtype=jnp.int32)
        query_ids = lax.dynamic_slice_in_dim(seg_ids, block_start, query_block, 0)
        return (query_ids[:, None] == seg_ids[None, :]) & (key_index[None, :] <= query_pos[:, None])

    def block_scores(query_blk, key_seq, seg_ids, block_start):
        scores = (
            jnp.einsum("qhd,kd->hqk", query_blk, key_seq, preferred_element_type=jnp.float32)
            * score_scale
        )
        return jnp.where(block_mask(seg_ids, block_start)[None], scores, MASKED)

    def attend_seq(operands):
        query_seq, keyval_seq, seg_ids = operands
        key_seq = keyval_seq[:, :HD]
        value_seq = keyval_seq[:, HD:]

        def attend_block(block_idx):
            block_start = block_idx * query_block
            query_blk = lax.dynamic_slice_in_dim(query_seq, block_start, query_block, 0)
            scores = block_scores(query_blk, key_seq, seg_ids, block_start)
            log_total = jax.nn.logsumexp(scores, axis=-1)
            probs_low = jnp.exp(scores - log_total[..., None]).astype(jnp.bfloat16)
            result = jnp.einsum(
                "hqk,kd->qhd", probs_low, value_seq, preferred_element_type=jnp.float32
            )
            return (result.astype(jnp.bfloat16), log_total)

        return lax.map(attend_block, jnp.arange(block_count, dtype=jnp.int32))

    attended_rows, log_totals = lax.map(attend_seq, (query_heads, keyval_heads, segments))
    attended_send = attended_rows.reshape(local_seqs, full_len, 1, head_width)
    attended_tok = lax.all_to_all(
        attended_send, "seq", split_axis=1, concat_axis=2, tiled=True
    ).reshape(tok_rows, q_width)
    attention_output = lax.dot_general(
        attended_tok, out_weight, (((1,), (1,)), ((), ())), preferred_element_type=jnp.float32
    )
    middle_hidden = hidden_in + attention_output
    inverse_two = rms_scale(middle_hidden)
    scaled_two = middle_hidden * inverse_two
    second_normed = (scaled_two * gain_two).astype(jnp.bfloat16)
    gate_and_up = column_adder(
        second_normed, lax.all_gather(gate_up_weight, ("dp", "seq"), axis=0, tiled=True)
    )
    gate = gate_and_up[:, :FF]
    up_part = gate_and_up[:, FF:]
    sigmoid_gate = jax.nn.sigmoid(gate)
    silu_gate = gate * sigmoid_gate
    active_branch = (silu_gate * up_part).astype(jnp.bfloat16)
    ffn_out = row_projector(
        active_branch, lax.all_gather(down_weight_rows, ("dp", "seq"), axis=0, tiled=True)
    )
    result = (middle_hidden + ffn_out).astype(jnp.bfloat16).reshape(tokens.shape)
    grad_out = cotangent.reshape(tok_rows, width)
    grad_active = column_adder(
        grad_out, lax.all_gather(down_weight_rows, ("dp", "seq"), axis=0, tiled=True)
    )
    grad_gate = grad_active * up_part * sigmoid_gate * (1.0 + gate * (1.0 - sigmoid_gate))
    grad_up = grad_active * silu_gate
    grad_both = jnp.concatenate([grad_gate, grad_up], axis=1).astype(jnp.bfloat16)
    grad_normed_two = row_projector(
        grad_both, lax.all_gather(gate_up_weight, ("dp", "seq"), axis=0, tiled=True)
    )
    ffn_gain_grad = jnp.sum(grad_normed_two * scaled_two, axis=0)
    grad_middle = grad_out.astype(jnp.float32) + rms_back(
        grad_normed_two * gain_two, scaled_two, inverse_two
    )
    grad_branch = grad_middle.astype(jnp.bfloat16)
    piece_qkv = lax.all_gather(joint_projection_matrix, ("dp", "seq"), axis=0, tiled=True)
    piece_out = lax.all_gather(output_weight_rows, ("dp", "seq"), axis=0, tiled=True)
    columns = grad_branch
    running = jnp.dot(columns, piece_out, preferred_element_type=jnp.float32)
    qkv_weight = piece_qkv
    grad_attended, qkv_weight = (running, qkv_weight)
    grad_send = grad_attended.astype(jnp.bfloat16).reshape(
        local_seqs, local_len, sequence_shard_count, head_width
    )
    grad_heads = lax.all_to_all(grad_send, "seq", split_axis=2, concat_axis=1, tiled=True).reshape(
        local_seqs, full_len, heads_dev, HD
    )

    def attend_back(operands):
        query_seq, keyval_seq, seg_ids, grad_seq, log_seq = operands
        key_seq = keyval_seq[:, :HD]
        value_seq = keyval_seq[:, HD:]

        def back_block(sums, block_idx):
            key_sum, value_sum = sums
            block_start = block_idx * query_block
            query_blk = lax.dynamic_slice_in_dim(query_seq, block_start, query_block, 0)
            grad_blk = lax.dynamic_slice_in_dim(grad_seq, block_start, query_block, 0)
            log_blk = lax.dynamic_index_in_dim(log_seq, block_idx, 0, keepdims=False)
            scores = block_scores(query_blk, key_seq, seg_ids, block_start)
            probs = jnp.exp(scores - log_blk[..., None])
            probs_low = probs.astype(jnp.bfloat16)
            grad_probs = jnp.einsum(
                "qhd,kd->hqk", grad_blk, value_seq, preferred_element_type=jnp.float32
            )
            inner = jnp.sum(probs * grad_probs, axis=-1, keepdims=True)
            grad_scores = (probs * (grad_probs - inner)).astype(jnp.bfloat16)
            grad_query = (
                jnp.einsum("hqk,kd->qhd", grad_scores, key_seq, preferred_element_type=jnp.float32)
                * score_scale
            )
            key_sum = (
                key_sum
                + jnp.einsum(
                    "hqk,qhd->kd", grad_scores, query_blk, preferred_element_type=jnp.float32
                )
                * score_scale
            )
            value_sum = value_sum + jnp.einsum(
                "hqk,qhd->kd", probs_low, grad_blk, preferred_element_type=jnp.float32
            )
            return ((key_sum, value_sum), grad_query.astype(jnp.bfloat16))

        empty = jnp.zeros((full_len, HD), jnp.float32)
        (key_sum, value_sum), grad_query = lax.scan(
            back_block, (empty, empty), jnp.arange(block_count, dtype=jnp.int32)
        )
        return (grad_query, jnp.concatenate([key_sum, value_sum], axis=-1).astype(jnp.bfloat16))

    grad_query_heads, grad_kv_heads = lax.map(
        attend_back, (query_heads, keyval_heads, segments, grad_heads, log_totals)
    )
    grad_query_send = grad_query_heads.reshape(local_seqs, full_len, 1, head_width)
    grad_kv_send = grad_kv_heads.reshape(local_seqs, full_len, 1, 2 * HD)
    grad_query_tok, grad_kv_tok = (
        lax.all_to_all(grad_query_send, "seq", split_axis=1, concat_axis=2, tiled=True),
        lax.all_to_all(grad_kv_send, "seq", split_axis=1, concat_axis=2, tiled=True),
    )
    grad_query_full = grad_query_tok.reshape(tok_rows, H, HD).astype(jnp.float32)
    grad_slots = jnp.sum(
        grad_kv_tok.reshape(tok_rows, KV, copies, 2 * HD).astype(jnp.float32), axis=2
    )
    grad_query_rot = (
        rotate(grad_query_full, cos_local, -sine_table_shard)
        .astype(jnp.bfloat16)
        .reshape(tok_rows, q_width)
    )
    grad_key_rot = (
        rotate(grad_slots[..., :HD], cos_local, -sine_table_shard)
        .astype(jnp.bfloat16)
        .reshape(tok_rows, kv_width)
    )
    grad_value = grad_slots[..., HD:].astype(jnp.bfloat16).reshape(tok_rows, kv_width)
    grad_proj = jnp.concatenate([grad_query_rot, grad_key_rot, grad_value], axis=1)
    grad_normed_one = lax.dot_general(
        grad_proj, qkv_weight, (((1,), (1,)), ((), ())), preferred_element_type=jnp.float32
    )
    attn_gain_grad = jnp.sum(grad_normed_one * scaled_one, axis=0)
    grad_input = grad_middle + rms_back(grad_normed_one * gain_one, scaled_one, inverse_one)
    summed = lax.psum_scatter(
        jnp.concatenate(
            [
                jnp.concatenate(
                    [
                        outer_rows(prenorm_activations, grad_proj),
                        outer_rows(grad_branch, attended_tok),
                    ],
                    axis=1,
                ),
                jnp.concatenate(
                    [outer_rows(second_normed, grad_both), outer_rows(grad_out, active_branch)],
                    axis=1,
                ),
            ],
            axis=1,
        ),
        ("dp", "seq"),
        scatter_dimension=0,
        tiled=True,
    )
    attn_gain_grad, ffn_gain_grad = lax.psum((attn_gain_grad, ffn_gain_grad), ("dp", "seq"))
    second_end = proj_cols + q_width
    third_end = second_end + 2 * FF
    return (
        result,
        grad_input.reshape(tokens.shape),
        summed[:, :proj_cols],
        summed[:, proj_cols:second_end],
        summed[:, second_end:third_end],
        summed[:, third_end:],
        attn_gain_grad,
        ffn_gain_grad,
    )


def solution(mesh):
    return jax.shard_map(
        local,
        mesh=mesh,
        in_specs=(
            P("dp", "seq", None),
            P("dp", "seq", None),
            P("dp", None),
            P(("dp", "seq"), None),
            P(("dp", "seq"), None),
            P(("dp", "seq"), None),
            P(("dp", "seq"), None),
            P(),
            P(),
        ),
        out_specs=(
            P("dp", "seq", None),
            P("dp", "seq", None),
            P(("dp", "seq"), None),
            P(("dp", "seq"), None),
            P(("dp", "seq"), None),
            P(("dp", "seq"), None),
            P(),
            P(),
        ),
        check_vma=False,
    )
```

profile of v0, /device:TPU:0, one launch (start us, length us, event | category | flops | bytes accessed | tf_op | source)
XLA Modules:
  0.0 2860.7 jit_solution(3535612049045171270)
XLA Ops:
  17.8 82.7 %all-gather.5.cloned.1.call-done = bf16[2048,2560]{1,0:T(8,128)(2,1)} async-done(((bf16[64,2560]{1,0:T(8,128)(2,1)}), bf16[2048,2560]{1,0:T(8,128)(2,1)}) %all-gather.5.cloned.1.call-update) | async-done | bytes 10485776 | tf_op jit(solution)/shard_map/all_gather | solution.py:115
  100.5 8.9 fusion.93
  136.5 22.3 all-to-all-done.1
  166.8 64.2 %all-to-all-done = bf16[2,256,8,256]{1,0,3,2:T(2,128)(2,1)S(1)} async-done(((bf16[2,256,8,256]{1,0,3,2:T(2,128)(2,1)}), bf16[2,256,8,256]{1,0,3,2:T(2,128)(2,1)S(1)}, u32[]{:S(2)}, u32[]{:S(2)}) %all-to-all-start) | async-done | bytes 2097184 | tf_op jit(solution)/shard_map/all_to_all | solution.py:131
  238.1 137.8 %while.56 = (s32[]{:T(128)}, bf16[2,4,512,4,64]{2,4,3,1,0:T(8,128)(2,1)}, f32[2,4,4,512]{3,2,1,0:T(4,128)S(1)}, bf16[2,2048,4,64]{1,3,2,0:T(8,128)(2,1)S(1)}, bf...) while((s32[]{:T(128)}, ...), condition=%wide.region_8.9_spmd.clone, body=%wide.region_3.8_spmd.clone.sunk | while | flops 1123172864 | bytes 62081504 | solution.py:167
  240.0 64.7 %while.59 = (s32[]{:T(128)}, bf16[4,512,4,64]{1,3,2,0:T(8,128)(2,1)}, f32[4,4,512]{2,1,0:T(4,128)S(1)}, s32[4]{0:T(128)S(1)}, s32[2048]{0:T(1024)S(1)}, /*index=...) while((s32[]{:T(128)}, ...), condition=%wide.region_7.7_spmd, body=%wide.region_4.6_spmd.sunk | while | flops 1123172864 | bytes 55699664 | solution.py:165
  308.9 64.7 %while.59 = (s32[]{:T(128)}, bf16[4,512,4,64]{1,3,2,0:T(8,128)(2,1)}, f32[4,4,512]{2,1,0:T(4,128)S(1)}, s32[4]{0:T(128)S(1)}, s32[2048]{0:T(1024)S(1)}, /*index=...) while((s32[]{:T(128)}, ...), condition=%wide.region_7.7_spmd, body=%wide.region_4.6_spmd.sunk | while | flops 1123172864 | bytes 55699664 | solution.py:165
  375.9 7.2 copy.118
  383.1 8.2 reshape.386
  395.4 107.7 %all-to-all-done.2 = bf16[2,2048,1,256]{3,0,2,1:T(2,128)(2,1)S(1)} async-done(((bf16[2,2048,1,256]{3,0,2,1:T(2,128)(2,1)}), bf16[2,2048,1,256]{3,0,2,1:T(2,128)(2,1)S(1)}, u32[]{:S(2)}, u32[]{:S(2)}) %all-to-all-start.2) | async-done | bytes 2097184 | tf_op jit(solution)/shard_map/all_to_all | solution.py:169
  506.6 11.4 multiply_reduce_fusion.2
  521.8 33.2 %fusion.89 = f32[512,11264]{1,0:T(8,128)} fusion(bf16[2048,11264]{1,0:T(8,128)(2,1)} %all-gather.9.cloned.1.call-done, f32[512,2048]{1,0:T(8,128)} %get-tuple-element.442, f32[2048]{0:T(1024)S(1)} %convert_element_type.130, f32[512]{0:T(512)S(1)} %add_rsqrt_fusion), kind=kOutput, calls=%fused_computation.155 | convolution fusion | flops 23625465856 | bytes 73410560 | tf_op jit(solution)/shard_map/dot_general | solution.py:60
  555.1 113.2 %all-gather.11.cloned.1.call-done = bf16[2048,5632]{1,0:T(8,128)(2,1)} async-done(((bf16[64,5632]{1,0:T(8,128)(2,1)}), bf16[2048,5632]{1,0:T(8,128)(2,1)}) %all-gather.11.cloned.1.call-update) | async-done | bytes 23068688 | tf_op jit(solution)/shard_map/all_gather | solution.py:188
  668.2 28.2 multiply_convert_fusion.1
  696.4 34.7 %multiply_reduce_fusion = (f32[2048]{0:T(1024)}, f32[512]{0:T(512)S(1)}, f32[512,2048]{1,0:T(8,128)}) fusion(f32[512,2048]{1,0:T(8,128)} %get-tuple-element.442, f32[512]{0:T(512)S(1)} %add_rsqrt_fusion, f32[2048]{0:T(1024)S(1)} %convert_element_type.130, bf16[2048,11264]{1,0:T(8,128)(2,1)} %all-gather.9.cloned.1.call-done, ...), kind=kOutput, calls=%fused_computation.106 | convolution fusion | flops 23651678208 | bytes 66080768 | tf_op jit(solution)/shard_map/dot_general | solution.py:64
  748.7 48.0 %all-to-all-done.3 = bf16[2,256,8,256]{3,1,0,2:T(8,128)(2,1)S(1)} async-done(((bf16[2,256,8,256]{3,1,0,2:T(8,128)(2,1)}), bf16[2,256,8,256]{3,1,0,2:T(8,128)(2,1)S(1)}, u32[]{:S(2)}, u32[]{:S(2)}) %all-to-all-start.3) | async-done | bytes 2097184 | tf_op jit(solution)/shard_map/all_to_all | solution.py:215
  804.4 337.8 %while.58 = (s32[]{:T(128)}, bf16[2,4,512,4,64]{2,4,3,1,0:T(8,128)(2,1)}, bf16[2,2048,128]{1,2,0:T(8,128)(2,1)}, bf16[2,2048,4,64]{1,3,2,0:T(8,128)(2,1)}, bf16[...) while((s32[]{:T(128)}, ...), condition=%wide.region_15.16_spmd.clone, body=%wide.region_11.15_spmd.clone.sunk | while | flops 2752641536 | bytes 167816112 | solution.py:260
  811.0 156.9 %while.60 = (s32[]{:T(128)}, f32[2048,64]{0,1:T(8,128)}, f32[2048,64]{0,1:T(8,128)}, bf16[4,512,4,64]{1,3,2,0:T(8,128)(2,1)}, s32[4]{0:T(128)S(1)}, /*index=5*/s...) while((s32[]{:T(128)}, f32[2048,64]{0,1:T(8,128)}, ...), condition=%wide.region_14.14_spmd.clone, body=%wide.region_12.13_spmd.clone.sunk | while | flops 2751330816 | bytes 139938352 | solution.py:255
  825.1 10.5 fusion.145
  835.6 8.4 fusion.146
  864.4 10.5 fusion.145
  874.8 8.4 fusion.146
  903.6 10.5 fusion.145
  914.1 8.4 fusion.146
  936.3 6.7 fusion.148
  942.9 10.5 fusion.145
  953.4 8.4 fusion.146
  979.6 156.9 %while.60 = (s32[]{:T(128)}, f32[2048,64]{0,1:T(8,128)}, f32[2048,64]{0,1:T(8,128)}, bf16[4,512,4,64]{1,3,2,0:T(8,128)(2,1)}, s32[4]{0:T(128)S(1)}, /*index=5*/s...) while((s32[]{:T(128)}, f32[2048,64]{0,1:T(8,128)}, ...), condition=%wide.region_14.14_spmd.clone, body=%wide.region_12.13_spmd.clone.sunk | while | flops 2751330816 | bytes 139938352 | solution.py:255
  993.7 10.5 fusion.145
  1004.2 8.4 fusion.146
  1033.0 10.5 fusion.145
  1043.5 8.4 fusion.146
  1072.3 10.5 fusion.145
  1082.7 8.4 fusion.146
  1111.6 10.5 fusion.145
  1122.0 8.4 fusion.146
  1149.5 40.3 %fusion.65 = f32[2048,11264]{1,0:T(8,128)} fusion(bf16[512,5632]{1,0:T(8,128)(2,1)} %get-tuple-element.427, bf16[512,5632]{1,0:T(8,128)(2,1)} %get-tuple-element.426, f32[512,2048]{1,0:T(8,128)} %get-tuple-element.442, f32[2048]{0:T(1024)S(1)} %copy-done.30, f32[512]{0:T(512)S(1)} %copy-done.33), kind=kOutput, calls=%fused_computation.89 | convolution fusion | flops 23648534528 | bytes 108013568 | tf_op jit(solution)/shard_map/dot_general | solution.py:70
  1194.5 8.2 reshape.387
  1209.7 13.2 fusion.80
  1222.9 24.0 convolution_bitcast_fusion.1
  1260.3 7.3 copy.107
  1278.7 10.9 fusion.78
  1289.5 114.9 %pad_maximum_fusion = f32[2048,21504]{1,0:T(8,128)} fusion(f32[2048,5632]{1,0:T(8,128)} %convolution_bitcast_fusion.1, f32[2048,11264]{1,0:T(8,128)} %fusion.65, f32[2048,2048]{1,0:T(8,128)} %fusion.80, f32[2048,2560]{1,0:T(8,128)} %fusion.78), kind=kLoop, calls=%fused_computation.81 | loop fusion | flops 132120576 | bytes 352321536 | tf_op jit(solution)/shard_map/concatenate | solution.py:291
  1404.5 21.4 add_convert_fusion
  1426.0 14.2 fusion.76
  1440.2 37.5 %all-reduce.1 = (f32[2048]{0:T(1024)}, f32[2048]{0:T(1024)}) all-reduce(f32[2048]{0:T(1024)S(1)} %get-tuple-element.342, f32[2048]{0:T(1024)S(1)} %copy-done.46), channel_id=1, replica_groups=mesh['dp'=4,'seq'=8] {'dp','seq'}, use_global_device_ids=true, to_apply=%region_20.21 | all-reduce | flops 4096 | bytes 32768 | tf_op jit(solution)/shard_map/psum | solution.py:311
  1477.7 8.2 fusion.75
  1485.9 1357.9 %reduce-scatter.2.cloned.1.call-done = f32[64,21504]{1,0:T(8,128)} async-done(((f32[2048,21504]{1,0:T(8,128)}), f32[64,21504]{1,0:T(8,128)}) %reduce-scatter.2.cloned.1.call-update) | async-done | bytes 5505040 | tf_op jit(solution)/shard_map/reduce_scatter | solution.py:290
  (526 shorter events, 433.5 us)
Async XLA Ops:
  7.2 8.7 copy-start.7
  7.2 93.3 %all-gather.5.cloned.1.call-start = ((), (), s32[]{:S(2)}) async-start(), calls=%async_computation.7 | async-start | bytes 10813440 | tf_op jit(solution)/shard_map/all_gather | solution.py:115
  7.9 498.7 %all-gather.7.cloned.1.call-start = ((), (), s32[]{:S(2)}) async-start(), calls=%async_computation.8 | async-start | bytes 8650752 | tf_op jit(solution)/shard_map/all_gather | solution.py:116
  8.7 513.2 %all-gather.9.cloned.1.call-start = ((), (), s32[]{:S(2)}) async-start(), calls=%async_computation.9 | async-start | bytes 47579136 | tf_op jit(solution)/shard_map/all_gather | solution.py:180
  11.5 97.9 %copy-start.44 = (f32[1,2,2,128]{3,1,2,0:T(2,128)}, f32[1,2,2,128]{3,1,2,0:T(2,128)S(1)}, u32[]{:S(2)}) copy-start(f32[1,2,2,128]{3,1,2,0:T(2,128)S(1)} %copy.124) | copy-start | bytes 6148
  12.2 97.2 %copy-start.42 = (f32[2048]{0:T(1024)}, f32[2048]{0:T(1024)S(1)}, u32[]{:S(2)}) copy-start(f32[2048]{0:T(1024)S(1)} %convert_element_type.125) | copy-start | bytes 24580
  15.9 105.2 %copy-start.17 = (f32[2,256,32]{2,1,0:T(8,128)}, f32[2,256,32]{2,1,0:T(8,128)S(1)}, u32[]{:S(2)}) copy-start(f32[2,256,32]{2,1,0:T(8,128)S(1)} %get-tuple-element.435) | copy-start | bytes 196612
  15.9 105.3 %copy-start.19 = (f32[2,256,32]{2,1,0:T(8,128)}, f32[2,256,32]{2,1,0:T(8,128)S(1)}, u32[]{:S(2)}) copy-start(f32[2,256,32]{2,1,0:T(8,128)S(1)} %get-tuple-element.436) | copy-start | bytes 196612
  116.8 41.9 %all-to-all-start.1 = ((bf16[2,256,8,128]{3,1,0,2:T(8,128)(2,1)}), bf16[2,256,8,128]{3,1,0,2:T(8,128)(2,1)}, u32[]{:S(2)}, u32[]{:S(2)}) async-start(bf16[2,256,8,128]{3,1,0,2:T(8,128)(2,1)} %bitcast.16), calls=%async_computation.1 | async-start | bytes 2097152 | tf_op jit(solution)/shard_map/all_to_all | solution.py:132
  121.2 10.2 copy-start.34
  158.7 72.3 %all-to-all-start = ((bf16[2,256,8,256]{1,0,3,2:T(2,128)(2,1)}), bf16[2,256,8,256]{1,0,3,2:T(2,128)(2,1)S(1)}, u32[]{:S(2)}, u32[]{:S(2)}) async-start(bf16[2,256,8,256]{1,0,3,2:T(2,128)(2,1)} %convert_element_type.128), calls=%async_computation | async-start | bytes 4194304 | tf_op jit(solution)/shard_map/all_to_all | solution.py:131
  162.4 505.8 %all-gather.11.cloned.1.call-start = ((), (), s32[]{:S(2)}) async-start(), calls=%async_computation.10 | async-start | bytes 23789568 | tf_op jit(solution)/shard_map/all_gather | solution.py:188
  375.9 15.4 copy-start.3
  375.9 15.4 copy-start.4
  375.9 15.4 copy-start.36
  383.1 12.3 copy-start.47
  391.3 111.8 %all-to-all-start.2 = ((bf16[2,2048,1,256]{3,0,2,1:T(2,128)(2,1)}), bf16[2,2048,1,256]{3,0,2,1:T(2,128)(2,1)S(1)}, u32[]{:S(2)}, u32[]{:S(2)}) async-start(bf16[2,2048,1,256]{3,0,2,1:T(2,128)(2,1)} %reshape.386), calls=%async_computation.2 | async-start | bytes 4194304 | tf_op jit(solution)/shard_map/all_to_all | solution.py:169
  395.4 335.7 %copy-start.29 = (f32[2048]{0:T(1024)}, f32[2048]{0:T(1024)S(1)}, u32[]{:S(2)}) copy-start(f32[2048]{0:T(1024)S(1)} %convert_element_type.130) | copy-start | bytes 24580
  518.1 213.1 %copy-start.32 = (f32[512]{0:T(512)}, f32[512]{0:T(512)S(1)}, u32[]{:S(2)}) copy-start(f32[512]{0:T(512)S(1)} %add_rsqrt_fusion) | copy-start | bytes 6148
  521.8 146.4 %copy-start.28 = (bf16[2,256,2048]{2,1,0:T(8,128)(2,1)S(1)}, bf16[2,256,2048]{2,1,0:T(8,128)(2,1)}, u32[]{:S(2)}) copy-start(bf16[2,256,2048]{2,1,0:T(8,128)(2,1)} %param.18) | copy-start | bytes 6291460
  744.3 52.5 %all-to-all-start.3 = ((bf16[2,256,8,256]{3,1,0,2:T(8,128)(2,1)}), bf16[2,256,8,256]{3,1,0,2:T(8,128)(2,1)S(1)}, u32[]{:S(2)}, u32[]{:S(2)}) async-start(bf16[2,256,8,256]{3,1,0,2:T(8,128)(2,1)} %copy.101), calls=%async_computation.3 | async-start | bytes 4194304 | tf_op jit(solution)/shard_map/all_to_all | solution.py:215
  748.0 54.7 %copy-start.25 = (f32[512,32]{1,0:T(8,128)}, f32[512,32]{1,0:T(8,128)S(1)}, u32[]{:S(2)}) copy-start(f32[512,32]{1,0:T(8,128)S(1)} %bitcast_negate_fusion) | copy-start | bytes 196612
  804.7 6.3 copy-start.5
  835.6 8.4 copy-start.1
  874.8 8.4 copy-start.1
  914.1 8.4 copy-start.1
  953.4 8.4 copy-start.1
  1004.2 8.4 copy-start.1
  1043.5 8.4 copy-start.1
  1082.7 8.4 copy-start.1
  1122.0 8.4 copy-start.1
  1142.1 7.3 copy-start.30
  1142.1 7.3 copy-start.33
  1145.8 56.9 %all-to-all-start.5 = ((bf16[2,2048,1,128]{3,0,2,1:T(2,128)(2,1)}), bf16[2,2048,1,128]{3,0,2,1:T(2,128)(2,1)S(1)}, u32[]{:S(2)}, u32[]{:S(2)}) async-start(bf16[2,2048,1,128]{3,0,2,1:T(2,128)(2,1)} %bitcast.29), calls=%async_computation.5 | async-start | bytes 2097152 | tf_op jit(solution)/shard_map/all_to_all | solution.py:267
  1149.5 40.3 %copy-start.13 = (bf16[2,4,512,4,64]{2,4,3,1,0:T(8,128)(2,1)S(1)}, bf16[2,4,512,4,64]{2,4,3,1,0:T(8,128)(2,1)}, u32[]{:S(2)}) copy-start(bf16[2,4,512,4,64]{2,4,3,1,0:T(8,128)(2,1)} %get-tuple-element.208) | copy-start | bytes 6291460
  1203.7 53.9 %all-to-all-start.4 = ((bf16[2,2048,1,256]{3,0,2,1:T(2,128)(2,1)}), bf16[2,2048,1,256]{3,0,2,1:T(2,128)(2,1)S(1)}, u32[]{:S(2)}, u32[]{:S(2)}) async-start(bf16[2,2048,1,256]{3,0,2,1:T(2,128)(2,1)} %reshape.387), calls=%async_computation.4 | async-start | bytes 4194304 | tf_op jit(solution)/shard_map/all_to_all | solution.py:266
  1209.7 1634.1 %reduce-scatter.2.cloned.1.call-start = ((), (), s32[]{:S(2)}) async-start(), calls=%async_computation.11 | async-start | bytes 181665792 | tf_op jit(solution)/shard_map/reduce_scatter | solution.py:290
  1222.9 24.0 copy-start.22
  1247.2 6.2 copy-start.18
  1255.4 22.0 copy-start.40
  1267.6 6.5 copy-start.35
  1267.6 6.5 copy-start.37
  1404.5 21.5 copy-start.9
  1404.5 21.5 copy-start.39
  1404.5 21.5 copy-start.41
  1404.5 21.5 copy-start.43
  1404.5 21.5 copy-start.45
  1426.0 14.2 copy-start.46
  (77 other events, 264.1 us)
Sparse Core Ops, SparseCore 0:
  10.9 89.5 all-gather.4
  103.5 105.3 all-gather.6
  211.8 310.0 all-gather.8
  524.6 143.5 all-gather.10
  1404.6 1439.1 reduce-scatter.1
where the time goes:
time: 2870 us; the launch traced here: 2860 us
  waiting for transfers between devices  1800 us (63%)
  matrix products  533 us (19%)
  other arithmetic  272 us (9%)
  local copies, waits for them, and re-layouts  146 us (5%)
  blocking collectives  37.5 us (1%)
    reduce_scatter x1, waiting for transfers between devices, local(): lax.psum_scatter(jnp.concatenate([jnp.concatenate([outer_rows(prenorm_act...  1360 us
    concatenate x1, other arithmetic, local(): jnp.concatenate([jnp.concatenate([outer_rows(prenorm_activations, grad_pr...  115 us
    all_gather x1, waiting for transfers between devices, local(): lax.all_gather(down_weight_rows, ('dp', 'seq'), axis=0, tiled=True)  113 us
    all_to_all x1, waiting for transfers between devices, local(): lax.all_to_all(attended_send, 'seq', split_axis=1, concat_axis=2, tiled=T...  108 us
    dot_general x4, matrix products, outer_rows(): lax.dot_general(left_part, right_part, (((0,), (0,)), ((), ())), preferre...  88.3 us
    dot_general x8, matrix products, back_block(): jnp.einsum('qhd,kd->hqk', grad_blk, value_seq, preferred_element_type=jnp...  83.7 us
    all_gather x1, waiting for transfers between devices, local(): lax.all_gather(joint_projection_matrix, ('dp', 'seq'), axis=0, tiled=True)  82.7 us
    convert_element_type x8, other arithmetic, back_block(): grad_scores = (probs * (grad_probs - inner)).astype(jnp.bfloat16)  66.8 us
  transfers between devices with their start and end apart: 11, of which 9 were waited for; matrix products, arithmetic and copies ran while one was open for 14% of the time, Pallas kernels for 0%

commit v1 on v0

v1 whole, which is shorter than its diff:
```python
import functools
import math

import jax
import jax.numpy as jnp
from jax import lax
from jax.experimental import pallas as pl
from jax.experimental.pallas import tpu as pltpu
from jax.sharding import Mesh
from jax.sharding import PartitionSpec as P

H = 32
HD = 64
KV = 4
FF = 5632

EPSILON = 1e-05
NEG = -1e30
ROTARY_BASE = 10000.0
LOG2E = math.log2(math.e)
LANES = 128

bf16 = jnp.bfloat16
f32 = jnp.float32


def dot(a, b, dims=((1,), (0,))):
    return lax.dot_general(a, b, (dims, ((), ())), preferred_element_type=f32)


def bits_of(size):
    return max(size - 1, 0).bit_length()


def axis_bits(axis):
    return [(axis, b) for b in reversed(range(bits_of(lax.axis_size(axis))))]


def canonical():
    return axis_bits("x") + axis_bits("core") + axis_bits("z") + axis_bits("y")


def my_bit(key):
    axis, b = key
    return (lax.axis_index(axis) >> b) & 1


def swap(values, key):
    axis, b = key
    return lax.ppermute(values, axis, [(i, i ^ (1 << b)) for i in range(lax.axis_size(axis))])


def place_of(key, have):
    order = canonical()
    return sum(order.index(k) < order.index(key) for k in have)


def gather_bits(piece, have, keys):
    have = list(have)
    for key in keys:
        other = swap(piece, key)
        low = my_bit(key) == 0
        piece = jnp.stack(
            [jnp.where(low, piece, other), jnp.where(low, other, piece)], axis=place_of(key, have)
        )
        have.append(key)
    return piece


def scatter_bits(terms, have, keys):
    have = list(have)
    for key in keys:
        at = place_of(key, [k for k in have if k != key])
        bit = my_bit(key)
        arrived = swap(lax.dynamic_index_in_dim(terms, 1 - bit, at, keepdims=False), key)
        kept = lax.dynamic_index_in_dim(terms, bit, at, keepdims=False)
        have.remove(key)
        terms = kept.astype(f32) + arrived.astype(f32)
        if have:
            terms = terms.astype(bf16)
    return terms


def sum_all(values):
    for key in canonical():
        values = values + swap(values, key)
    return values


def stack_heads(x, heads):
    return jnp.concatenate([x[:, h * HD : (h + 1) * HD] for h in range(heads)], axis=0)


def unstack_heads(x, heads):
    rows = x.shape[0] // heads
    return jnp.concatenate([x[h * rows : (h + 1) * rows] for h in range(heads)], axis=1)


def block_allowed(i, j, rows, start):
    key_pos = j * rows + lax.broadcasted_iota(jnp.int32, (rows, rows), 0)
    query_pos = i * rows + lax.broadcasted_iota(jnp.int32, (rows, rows), 1)
    return (key_pos <= query_pos) & (key_pos >= start)


def attend_kernel(
    heads, me_ref, lo_ref, hi_ref, start_ref, qkv_ref, out_ref, raw_ref, lse_ref, m_s, l_s, acc_s
):
    rows = qkv_ref.shape[1]
    qw = heads * HD
    scale = LOG2E * HD**-0.5
    me = me_ref[0]
    i = pl.program_id(0)
    q = stack_heads(qkv_ref[i ^ me, :, :qw], heads)
    m_s[...] = jnp.full_like(m_s, NEG)
    l_s[...] = jnp.zeros_like(l_s)
    acc_s[...] = jnp.zeros_like(acc_s)

    def block(j, masked):
        k = qkv_ref[j ^ me, :, qw : qw + HD]
        v = qkv_ref[j ^ me, :, qw + HD : qw + 2 * HD]
        s = dot(k, q, ((1,), (1,)))
        if masked:
            ok = block_allowed(i, j, rows, start_ref[0])
            s = jnp.where(jnp.concatenate([ok] * heads, axis=1), s, NEG)
        m_old = m_s[...]
        m_new = jnp.maximum(m_old, jnp.max(s, axis=0, keepdims=True) * scale)
        p = jnp.exp2(s * scale - m_new)
        keep = jnp.exp2(m_old - m_new)
        l_s[...] = l_s[...] * keep + jnp.sum(p, axis=0, keepdims=True)
        acc_s[...] = acc_s[...] * keep + dot(v, p.astype(bf16), ((0,), (0,)))
        m_s[...] = m_new

    def masked_step(j, carry):
        block(j, True)
        return carry

    def plain_step(j, carry):
        block(j, False)
        return carry

    block(i, True)
    lax.fori_loop(lo_ref[i], hi_ref[i], masked_step, 0)
    lax.fori_loop(hi_ref[i], i, plain_step, 0)
    total = l_s[...]
    result = unstack_heads(jnp.transpose(acc_s[...] / total), heads)
    raw_ref[0] = result
    out_ref[0] = result.astype(bf16)
    lse_ref[0] = jnp.broadcast_to(m_s[...] + jnp.log2(total), (8, heads * rows))


def attend(me, lo, hi, start, qkv, heads):
    n, rows, w = qkv.shape
    qw = heads * HD
    smem = pl.BlockSpec(memory_space=pltpu.SMEM)
    pairs = heads * (n * rows) ** 2 // 2
    per_block = lambda shape: pl.BlockSpec((1,) + shape, lambda i: (i, 0, 0))
    return pl.pallas_call(
        functools.partial(attend_kernel, heads),
        grid=(n,),
        out_shape=(
            jax.ShapeDtypeStruct((n, rows, qw), bf16),
            jax.ShapeDtypeStruct((n, rows, qw), f32),
            jax.ShapeDtypeStruct((n, 8, heads * rows), f32),
        ),
        in_specs=[
            smem,
            smem,
            smem,
            per_block((1, rows)),
            pl.BlockSpec((n, rows, w), lambda i: (0, 0, 0)),
        ],
        out_specs=(per_block((rows, qw)), per_block((rows, qw)), per_block((8, heads * rows))),
        scratch_shapes=[
            pltpu.VMEM((1, heads * rows), f32),
            pltpu.VMEM((1, heads * rows), f32),
            pltpu.VMEM((HD, heads * rows), f32),
        ],
        compiler_params=pltpu.CompilerParams(vmem_limit_bytes=48 << 20),
        cost_estimate=pl.CostEstimate(
            flops=16 * HD * pairs, bytes_accessed=8 << 20, transcendentals=pairs
        ),
        name="attend",
    )(me, lo, hi, start, qkv)


def attend_back_kernel(
    heads,
    me_ref,
    lo_ref,
    hi_ref,
    start_ref,
    qkv_ref,
    g_ref,
    raw_ref,
    lse_ref,
    dq_ref,
    dkv_ref,
    dkv_s,
    dq_s,
):
    n, rows, _ = qkv_ref.shape
    qw = heads * HD
    scale = LOG2E * HD**-0.5
    me = me_ref[0]
    i = pl.program_id(0)

    @pl.when(i == 0)
    def _():
        dkv_s[...] = jnp.zeros_like(dkv_s)

    dq_s[...] = jnp.zeros_like(dq_s)
    q = stack_heads(qkv_ref[i ^ me, :, :qw], heads)
    g_flat = g_ref[i ^ me]
    g = stack_heads(g_flat, heads)
    product = g_flat.astype(f32) * raw_ref[0]
    inner = jnp.concatenate(
        [
            jnp.sum(product[:, h * HD : (h + 1) * HD], axis=1, keepdims=True)
            for h in range(heads)
        ],
        axis=0,
    )
    inner = jnp.transpose(jnp.broadcast_to(inner, (heads * rows, LANES)))[:1]
    lse = lse_ref[0, :1]

    def block(j, masked):
        k = qkv_ref[j ^ me, :, qw : qw + HD]
        v = qkv_ref[j ^ me, :, qw + HD : qw + 2 * HD]
        s = dot(k, q, ((1,), (1,)))
        grad_probs = dot(v, g, ((1,), (1,)))
        p = jnp.exp2(s * scale - lse)
        if masked:
            ok = block_allowed(i, j, rows, start_ref[0])
            p = jnp.where(jnp.concatenate([ok] * heads, axis=1), p, 0.0)
        grad_scores = (p * (grad_probs - inner)).astype(bf16)
        dkv_s[j, :, :HD] += dot(grad_scores, q)
        dkv_s[j, :, HD:] += dot(p.astype(bf16), g)
        dq_s[...] += dot(k, grad_scores, ((0,), (0,)))

    def masked_step(j, carry):
        block(j, True)
        return carry

    def plain_step(j, carry):
        block(j, False)
        return carry

    lax.fori_loop(lo_ref[i], hi_ref[i], masked_step, 0)
    lax.fori_loop(hi_ref[i], i, plain_step, 0)
    block(i, True)
    dq = unstack_heads(jnp.transpose(dq_s[...] * HD**-0.5), heads)
    dq_ref[0] = dq.astype(bf16)

    @pl.when(i == n - 1)
    def _():
        for r in range(n):
            done = dkv_s[r]
            dkv_ref[r] = jnp.concatenate([done[:, :HD] * HD**-0.5, done[:, HD:]], axis=1).astype(
                bf16
            )


def attend_back(me, lo, hi, start, qkv, grad, raw, lse, heads):
    n, rows, w = qkv.shape
    qw = heads * HD
    smem = pl.BlockSpec(memory_space=pltpu.SMEM)
    pairs = heads * (n * rows) ** 2 // 2
    per_block = lambda shape: pl.BlockSpec((1,) + shape, lambda i: (i, 0, 0))
    whole = lambda shape: pl.BlockSpec(shape, lambda i: (0, 0, 0))
    return pl.pallas_call(
        functools.partial(attend_back_kernel, heads),
        grid=(n,),
        out_shape=(
            jax.ShapeDtypeStruct((n, rows, qw), bf16),
            jax.ShapeDtypeStruct((n, rows, 2 * HD), bf16),
        ),
        in_specs=[
            smem,
            smem,
            smem,
            per_block((1, rows)),
            whole((n, rows, w)),
            whole((n, rows, qw)),
            per_block((rows, qw)),
            per_block((8, heads * rows)),
        ],
        out_specs=(per_block((rows, qw)), whole((n, rows, 2 * HD))),
        scratch_shapes=[
            pltpu.VMEM((n, rows, 2 * HD), f32),
            pltpu.VMEM((HD, heads * rows), f32),
        ],
        compiler_params=pltpu.CompilerParams(vmem_limit_bytes=48 << 20),
        cost_estimate=pl.CostEstimate(
            flops=28 * HD * pairs, bytes_accessed=8 << 20, transcendentals=pairs
        ),
        name="attend_back",
    )(me, lo, hi, start, qkv, grad, raw, lse)


def rotate_lanes(v, cosine, signed_sine):
    parts = []
    for c in range(v.shape[1] // LANES):
        part = v[:, c * LANES : (c + 1) * LANES]
        lane = lax.broadcasted_iota(jnp.int32, part.shape, 1)
        other = jnp.where(
            lane % HD < HD // 2,
            pltpu.roll(part, LANES - HD // 2, 1),
            pltpu.roll(part, HD // 2, 1),
        )
        parts.append(part * cosine + other * signed_sine)
    return jnp.concatenate(parts, axis=1) if len(parts) > 1 else parts[0]


def pack_kernel(copies, q_ref, k_ref, v_ref, cos_ref, sin_ref, out_ref):
    qw = q_ref.shape[1]
    head = pl.program_id(1) // copies
    cosine = cos_ref[...]
    sine = sin_ref[...]
    out_ref[0, 0, :, :qw] = rotate_lanes(q_ref[...], cosine, sine).astype(bf16)
    k = rotate_lanes(k_ref[...], cosine, sine)
    v = v_ref[...]
    first = head % 2 == 0
    lane = lax.broadcasted_iota(jnp.int32, k.shape, 1)
    k = jnp.where(first, k, pltpu.roll(k, HD, 1))
    v = jnp.where(first, pltpu.roll(v, HD, 1), v)
    out_ref[0, 0, :, qw:] = jnp.where(lane < HD, k, v).astype(bf16)


def pack_heads(projected, cosine, sine, seqs, n):
    rows = projected.shape[0] // seqs
    qw = H * HD // n
    copies = n // KV
    k_at = H * HD // LANES
    v_at = k_at + KV * HD // LANES
    return pl.pallas_call(
        functools.partial(pack_kernel, copies),
        grid=(seqs, n),
        out_shape=jax.ShapeDtypeStruct((seqs, n, rows, qw + 2 * HD), bf16),
        in_specs=[
            pl.BlockSpec((rows, qw), lambda b, d: (b, d)),
            pl.BlockSpec((rows, LANES), lambda b, d: (b, k_at + d // copies // 2)),
            pl.BlockSpec((rows, LANES), lambda b, d: (b, v_at + d // copies // 2)),
            pl.BlockSpec((rows, LANES), lambda b, d: (b, 0)),
            pl.BlockSpec((rows, LANES), lambda b, d: (b, 0)),
        ],
        out_specs=pl.BlockSpec((1, 1, rows, qw + 2 * HD), lambda b, d: (b, d, 0, 0)),
        cost_estimate=pl.CostEstimate(flops=0, bytes_accessed=10 << 20, transcendentals=0),
        name="pack_heads",
    )(projected, projected, projected, cosine, sine)


def unpack_kernel(n, me_ref, in_ref, cos_ref, sin_ref, out_ref):
    qw = in_ref.shape[3] - 2 * HD
    copies = n // KV
    me = me_ref[0]
    cosine = cos_ref[...]
    sine = -sin_ref[...]
    for d in range(n):
        part = in_ref[0, d ^ me, :, :qw].astype(f32)
        out_ref[:, d * qw : (d + 1) * qw] = rotate_lanes(part, cosine, sine).astype(bf16)
    lane = lax.broadcasted_iota(jnp.int32, cosine.shape, 1)
    for pair in range(KV // 2):
        sums = []
        for head in (2 * pair, 2 * pair + 1):
            total = in_ref[0, (head * copies) ^ me, :, qw:].astype(f32)
            for c in range(1, copies):
                total = total + in_ref[0, (head * copies + c) ^ me, :, qw:].astype(f32)
            sums.append(total)
        k = jnp.where(lane < HD, sums[0], pltpu.roll(sums[1], HD, 1))
        v = jnp.where(lane < HD, pltpu.roll(sums[0], HD, 1), sums[1])
        k_at = H * HD + pair * LANES
        v_at = k_at + KV * HD
        out_ref[:, k_at : k_at + LANES] = rotate_lanes(k, cosine, sine).astype(bf16)
        out_ref[:, v_at : v_at + LANES] = v.astype(bf16)


def unpack_heads(me, pieces, cosine, sine):
    seqs, n, rows, w = pieces.shape
    cols = H * HD + 2 * KV * HD
    return pl.pallas_call(
        functools.partial(unpack_kernel, n),
        grid=(seqs,),
        out_shape=jax.ShapeDtypeStruct((seqs * rows, cols), bf16),
        in_specs=[
            pl.BlockSpec(memory_space=pltpu.SMEM),
            pl.BlockSpec((1, n, rows, w), lambda b: (b, 0, 0, 0)),
            pl.BlockSpec((rows, LANES), lambda b: (b, 0)),
            pl.BlockSpec((rows, LANES), lambda b: (b, 0)),
        ],
        out_specs=pl.BlockSpec((rows, cols), lambda b: (b, 0)),
        cost_estimate=pl.CostEstimate(flops=0, bytes_accessed=6 << 20, transcendentals=0),
        name="unpack_heads",
    )(me, pieces, cosine, sine)


def rms_scale(hidden):
    return lax.rsqrt(jnp.mean(hidden * hidden, axis=-1, keepdims=True) + EPSILON)


def rms_back(grad_scaled, scaled, inverse):
    return inverse * (grad_scaled - scaled * jnp.mean(grad_scaled * scaled, axis=-1, keepdims=True))


def to_owners(pieces, me, n):
    parts = [lax.dynamic_index_in_dim(pieces, me, 0, keepdims=False)]
    for r in range(1, n):
        piece = lax.dynamic_index_in_dim(pieces, me ^ r, 0, keepdims=False)
        parts.append(lax.ppermute(piece, ("z", "y"), [(i, i ^ r) for i in range(n)]))
    return jnp.stack(parts)


def local(
    tokens,
    cotangent,
    segments,
    joint_projection_matrix,
    output_weight_rows,
    gate_up_weight,
    down_weight_rows,
    attn_gain,
    ffn_gain,
):
    n = lax.axis_size("z") * lax.axis_size("y")
    me = lax.axis_index("z") * lax.axis_size("y") + lax.axis_index("y")
    me_arg = me.astype(jnp.int32).reshape(1)
    core = lax.axis_index("core")
    core_key = ("core", 0)
    seqs, rows, width = tokens.shape
    full_len = segments.shape[1]
    tok_rows = seqs * rows
    heads = H // n
    qw = heads * HD
    q_width = H * HD
    half = FF // 2
    xs, zs, ys = axis_bits("x"), axis_bits("z"), axis_bits("y")
    gain_one = attn_gain.astype(f32)
    gain_two = ffn_gain.astype(f32)

    column = jnp.arange(full_len, dtype=jnp.int32)
    starts_here = jnp.concatenate(
        [jnp.ones((seqs, 1), dtype=bool), segments[:, 1:] != segments[:, :-1]], axis=1
    )
    doc_start = lax.cummax(jnp.where(starts_here, column, 0), axis=1)
    position = lax.dynamic_slice_in_dim(column - doc_start, me * rows, rows, 1).reshape(tok_rows, 1)
    doc_start = doc_start.reshape(seqs, n, rows)
    first_block = doc_start[:, :, 0] // rows
    plain_from = jnp.minimum((doc_start[:, :, -1] + rows - 1) // rows, jnp.arange(n))
    plain_from = jnp.maximum(plain_from, first_block)
    doc_start = doc_start[:, :, None, :]
    frequency = ROTARY_BASE ** (-(jnp.arange(HD // 2, dtype=f32) * 2.0) / HD)
    angles = position.astype(f32) * frequency
    cosine = jnp.concatenate([jnp.cos(angles)] * 4, axis=1)
    sine = jnp.concatenate([-jnp.sin(angles), jnp.sin(angles)] * 2, axis=1)

    w_qkv = gather_bits(joint_projection_matrix, [], zs + ys + xs + [core_key])
    w_qkv = w_qkv.reshape(width, -1)
    w_out = gather_bits(output_weight_rows, [], zs + xs + ys + [core_key]).reshape(width, -1)

    def half_columns(weight, owner):
        blocks = weight.reshape(weight.shape[0], -1, 2, half)
        picked = lax.dynamic_index_in_dim(blocks, owner, 2, keepdims=False)
        return picked.reshape(weight.shape[0], -1)

    def gather_half(weight, keys):
        mine = half_columns(weight, core)
        other = swap(half_columns(weight, 1 - core), core_key)
        low = core == 0
        pair = jnp.stack([jnp.where(low, mine, other), jnp.where(low, other, mine)])
        return gather_bits(pair, [core_key], keys).reshape(width, -1)

    w_gate_up = gather_half(gate_up_weight, zs + ys + xs)
    w_down = gather_half(down_weight_rows, zs + xs + ys)

    def with_sibling(values):
        return jnp.concatenate([values, swap(values, core_key)], axis=0)

    def summed_with_sibling(partial):
        arrived = swap(partial[tok_rows:].astype(bf16), core_key)
        return partial[:tok_rows] + arrived.astype(f32)

    hidden = tokens.reshape(tok_rows, width).astype(f32)
    inverse_one = rms_scale(hidden)
    scaled_one = hidden * inverse_one
    normed_one = (scaled_one * gain_one).astype(bf16)
    packed = pack_heads(dot(normed_one, w_qkv), cosine, sine, seqs, n)
    qkv, raw, lse, returned = [], [], [], []
    for b in range(seqs):
        qkv.append(to_owners(packed[b], me, n))
        out_b, raw_b, lse_b = attend(
            me_arg, first_block[b], plain_from[b], doc_start[b], qkv[b], heads
        )
        raw.append(raw_b)
        lse.append(lse_b)
        back = to_owners(out_b, me, n)
        returned.append(
            jnp.concatenate(
                [lax.dynamic_index_in_dim(back, s ^ me, 0, keepdims=False) for s in range(n)],
                axis=1,
            )
        )
    attended = jnp.concatenate(returned, axis=0)
    middle = hidden + dot(attended, w_out, ((1,), (1,)))

    inverse_two = rms_scale(middle)
    scaled_two = middle * inverse_two
    normed_two = (scaled_two * gain_two).astype(bf16)
    normed_pair = with_sibling(normed_two)
    both = dot(normed_pair, w_gate_up)
    gate = both[:, :half]
    up = both[:, half:]
    sigmoid_gate = jax.nn.sigmoid(gate)
    silu_gate = gate * sigmoid_gate
    active = (silu_gate * up).astype(bf16)
    result = middle + summed_with_sibling(dot(active, w_down, ((1,), (1,))))
    result = result.astype(bf16).reshape(tokens.shape)

    grad_out = cotangent.reshape(tok_rows, width)
    grad_pair = with_sibling(grad_out)
    grad_active = dot(grad_pair, w_down)
    grad_gate = grad_active * up * sigmoid_gate * (1.0 + gate * (1.0 - sigmoid_gate))
    grad_up = grad_active * silu_gate
    grad_both = jnp.concatenate([grad_gate, grad_up], axis=1).astype(bf16)
    grad_normed_two = summed_with_sibling(dot(grad_both, w_gate_up, ((1,), (1,))))
    ffn_gain_grad = jnp.sum(grad_normed_two * scaled_two, axis=0)
    grad_middle = grad_out.astype(f32) + rms_back(
        grad_normed_two * gain_two, scaled_two, inverse_two
    )
    grad_branch = grad_middle.astype(bf16)

    def bit_shape(terms, keys):
        return terms.astype(bf16).reshape((2,) * len(keys) + (-1, terms.shape[1]))

    outer = lambda a, b: dot(a, b, ((0,), (0,)))

    def scatter_columns(terms, keys):
        have = canonical()
        pair = scatter_bits_open(bit_shape(terms, have), have, keys)
        mine = lax.dynamic_index_in_dim(pair, core, 0, keepdims=False)
        other = swap(lax.dynamic_index_in_dim(pair, 1 - core, 0, keepdims=False), core_key)
        low = core == 0
        blocks = pair.shape[-1] // half
        mine = mine.reshape(-1, blocks, 1, half)
        other = other.reshape(-1, blocks, 1, half)
        joined = jnp.concatenate(
            [jnp.where(low, mine, other), jnp.where(low, other, mine)], axis=2
        )
        return joined.reshape(mine.shape[0], -1)

    def scatter_bits_open(terms, have, keys):
        have = list(have)
        for step, key in enumerate(keys):
            at = place_of(key, [k for k in have if k != key])
            bit = my_bit(key)
            arrived = swap(lax.dynamic_index_in_dim(terms, 1 - bit, at, keepdims=False), key)
            kept = lax.dynamic_index_in_dim(terms, bit, at, keepdims=False)
            have.remove(key)
            terms = kept.astype(f32) + arrived.astype(f32)
            if step < len(keys) - 1:
                terms = terms.astype(bf16)
        return terms

    d_gate_up = scatter_columns(outer(normed_pair, grad_both), xs + ys + zs[::-1])
    d_down = scatter_columns(outer(grad_pair, active), ys + xs + zs[::-1])

    grad_attended = dot(grad_branch, w_out).astype(bf16)
    grad_heads = jnp.moveaxis(grad_attended.reshape(seqs, rows, n, qw), 2, 1)
    back = []
    for b in range(seqs):
        grad_b = to_owners(grad_heads[b], me, n)
        dq, dkv = attend_back(
            me_arg, first_block[b], plain_from[b], doc_start[b], qkv[b], grad_b, raw[b], lse[b], heads
        )
        back.append(to_owners(jnp.concatenate([dq, dkv], axis=2), me, n))
    grad_proj = unpack_heads(me_arg, jnp.stack(back), cosine, sine)
    grad_normed_one = dot(grad_proj, w_qkv, ((1,), (1,)))
    attn_gain_grad = jnp.sum(grad_normed_one * scaled_one, axis=0)
    grad_input = grad_middle + rms_back(grad_normed_one * gain_one, scaled_one, inverse_one)

    def scatter_rows(terms, keys):
        return scatter_bits(bit_shape(terms, canonical()), canonical(), keys)

    d_out = scatter_rows(outer(grad_branch, attended), [core_key] + xs + ys + zs[::-1])
    d_qkv = scatter_rows(outer(normed_one, grad_proj), [core_key] + ys + xs + zs[::-1])
    return (
        result,
        grad_input.reshape(tokens.shape),
        d_qkv,
        d_out,
        d_gate_up,
        d_down,
        sum_all(attn_gain_grad),
        sum_all(ffn_gain_grad),
    )


def solution(mesh):
    dp, seq = mesh.devices.shape
    fine = Mesh(mesh.devices.reshape(dp // 2, 2, seq // 2, 2), ("x", "core", "z", "y"))
    by_token = P(("x", "core"), ("z", "y"), None)
    by_row = P(("x", "core", "z", "y"), None)
    return jax.shard_map(
        local,
        mesh=fine,
        in_specs=(
            by_token,
            by_token,
            P(("x", "core"), None),
            by_row,
            by_row,
            by_row,
            by_row,
            P(),
            P(),
        ),
        out_specs=(by_token, by_token, by_row, by_row, by_row, by_row, P(), P()),
        check_vma=False,
    )
```

time: 2870 us -> 1920 us (0.67)
  waiting for transfers between devices: 1800 us -> 1070 us
  matrix products: 533 us -> 211 us
  starting transfers between devices: 25.7 us -> 202 us
  Pallas kernels: 0 us -> 134 us
  other arithmetic: 272 us -> 171 us
  blocking collectives: 37.5 us -> 0 us
    reduce_scatter x1 -> x0, waiting for transfers between devices: 1360 us -> none  [local(): lax.psum_scatter(jnp.concatenate([jnp.concatenate([outer_rows(prenorm_act...]
    ppermute x0 -> x110, waiting for transfers between devices: none -> 1070 us  [the longest x54 807 us: swap(): lax.ppermute(values, axis, [(i, i ^ 1 << b) for i in range(lax.axis_size(...]
    dot_general x68 -> x12, matrix products: 533 us -> 211 us  [dot(): return lax.dot_general(a, b, (dims, ((), ())), preferred_element_type=f32)]
    all_to_all x6 -> x0, waiting for transfers between devices: 244 us -> none  [the longest x1 108 us: local(): lax.all_to_all(attended_send, 'seq', split_axis=1, concat_axis=2, tiled=T...]
    ppermute x0 -> x110, starting transfers between devices: none -> 202 us  [the longest x56 143 us: to_owners(): lax.ppermute(piece, ('z', 'y'), [(i, i ^ r) for i in range(n)])]
    all_gather x4 -> x0, waiting for transfers between devices: 200 us -> none  [the longest x1 113 us: local(): lax.all_gather(down_weight_rows, ('dp', 'seq'), axis=0, tiled=True)]
    pallas_call x0 -> x6, Pallas kernels: none -> 134 us  [the longest x2 67 us: attend_back(): pl.pallas_call(functools.partial(attend_back_kernel, heads), grid=(n,), o...]
    concatenate x9 -> x3, other arithmetic: 120 us -> 3.96 us  [the longest x2 2.69 us: scatter_columns(): jnp.concatenate([jnp.where(low, mine, other), jnp.where(low, other, mine)...]
  transfers between devices with their start and end apart: 11 -> 110, of which waited for: 9 -> 57; matrix products, arithmetic and copies ran while one was open for 14% -> 22% of each run, Pallas kernels for 0% -> 7%
where the time goes in v1:
time: 1920 us; the launch traced here: 1910 us
  waiting for transfers between devices  1070 us (56%)
  matrix products  211 us (11%)
  starting transfers between devices  202 us (11%)
  other arithmetic  171 us (9%)
  Pallas kernels  134 us (7%)
  local copies, waits for them, and re-layouts  121 us (6%)
    ppermute x54, waiting for transfers between devices, swap(): lax.ppermute(values, axis, [(i, i ^ 1 << b) for i in range(lax.axis_size(...  807 us
    ppermute x56, waiting for transfers between devices, to_owners(): lax.ppermute(piece, ('z', 'y'), [(i, i ^ r) for i in range(n)])  262 us
    dot_general x12, matrix products, dot(): return lax.dot_general(a, b, (dims, ((), ())), preferred_element_type=f32)  211 us
    ppermute x56, starting transfers between devices, to_owners(): lax.ppermute(piece, ('z', 'y'), [(i, i ^ r) for i in range(n)])  143 us
    another operation x36, other arithmetic, gather_bits(): jnp.stack([jnp.where(low, piece, other), jnp.where(low, other, piece)], a...  94.6 us
    pallas_call x2, Pallas kernels, attend_back(): pl.pallas_call(functools.partial(attend_back_kernel, heads), grid=(n,), o...  67 us
    ppermute x54, starting transfers between devices, swap(): lax.ppermute(values, axis, [(i, i ^ 1 << b) for i in range(lax.axis_size(...  58.8 us
    pallas_call x2, Pallas kernels, attend(): pl.pallas_call(functools.partial(attend_kernel, heads), grid=(n,), out_sh...  48.4 us
  transfers between devices with their start and end apart: 110, of which 57 were waited for; matrix products, arithmetic and copies ran while one was open for 22% of the time, Pallas kernels for 7%

profile of v1, /device:TPU:0, one launch (start us, length us, event | category | flops | bytes accessed | tf_op | source)
XLA Modules:
  0.0 1910.2 jit_solution(2587637860684542711)
XLA Ops:
  14.1 10.2 dynamic-slice_reduce_fusion.1
  47.5 28.5 %collective-permute-done.34 = bf16[2,64,2048]{2,1,0:T(8,128)(2,1)S(1)} collective-permute-done((bf16[2,64,2048]{2,1,0:T(8,128)(2,1)S(1)}, bf16[2,64,2048]{2,1,0:T(8,128)(2,1)S(1)}, u32[]{:S(2)}, u32[]{:S(2)}) %collective-permute-start.34) | collective-permute-done | bytes 524320 | tf_op jit(solution)/shard_map/ppermute | solution.py:50
  78.0 11.3 collective-permute-done.1
  91.5 8.4 collective-permute-done.35
  101.8 37.4 %collective-permute-done.40 = bf16[2,64,5632]{2,1,0:T(8,128)(2,1)S(1)} collective-permute-done((bf16[2,64,5632]{2,1,0:T(8,128)(2,1)S(1)}, bf16[2,64,5632]{2,1,0:T(8,128)(2,1)S(1)}, u32[]{:S(2)}, u32[]{:S(2)}) %collective-permute-start.40) | collective-permute-done | bytes 1441824 | tf_op jit(solution)/shard_map/ppermute | solution.py:50
  151.9 12.7 collective-permute-done.36
  167.3 32.6 %collective-permute-done.3 = bf16[2,2,2,64,2560]{4,3,2,1,0:T(8,128)(2,1)} collective-permute-done((bf16[2,2,2,64,2560]{4,3,2,1,0:T(8,128)(2,1)S(1)}, bf16[2,2,2,64,2560]{4,3,2,1,0:T(8,128)(2,1)}, u32[]{:S(2)}, u32[]{:S(2)}) %collective-permute-start.3) | collective-permute-done | bytes 2621472 | tf_op jit(solution)/shard_map/ppermute | solution.py:50
  216.5 42.9 %collective-permute-done.47 = bf16[2,2,2,64,2816]{4,3,0,1,2:T(8,128)(2,1)} collective-permute-done((bf16[2,2,2,64,2816]{4,3,0,1,2:T(8,128)(2,1)S(1)}, bf16[2,2,2,64,2816]{4,3,0,1,2:T(8,128)(2,1)}, u32[]{:S(2)}, u32[]{:S(2)}) %collective-permute-start.47) | collective-permute-done | bytes 2883616 | tf_op jit(solution)/shard_map/ppermute | solution.py:50
  271.3 7.5 pad_maximum_fusion.5
  278.8 8.1 select_bitcast_fusion.7
  286.9 8.9 pad_maximum_fusion.4
  295.9 10.5 fusion.56.q_ref.k_ref.v_ref
  306.3 13.1 pack_heads.1
  323.5 144.6 %collective-permute-done.5 = bf16[256,384]{1,0:T(8,128)(2,1)S(1)} collective-permute-done((bf16[256,384]{1,0:T(8,128)(2,1)S(1)}, bf16[256,384]{1,0:T(8,128)(2,1)S(1)}, u32[]{:S(2)}, u32[]{:S(2)}) %collective-permute-start.5) | collective-permute-done | bytes 196640 | tf_op jit(solution)/shard_map/ppermute | solution.py:408
  512.4 19.9 %attend.2 = (bf16[8,256,256]{2,1,0:T(8,128)(2,1)S(1)}, f32[8,256,256]{2,1,0:T(8,128)S(1)}, f32[8,8,1024]{2,1,0:T(8,128)S(1)}) custom-call(s32[1]{0:T(128)} %bitcast.1.me_ref, s32[8]{0:T(128)S(1)} %get-tuple-element.175.lo_ref, s32[8]{0:T(128)S(1)} %get-tuple-element.167.hi_ref, s32[8,1,256]{2,1,0:T(1,128)S(1)} %bitcast.592, ...), custom_call_target="tpu_custom_call" | custom-call | flops 8589934592 | bytes 8388608 | tf_op jit(solution)/shard_map/attend/pallas_call | solution.py:157
  548.8 8.2 collective-permute-done.23
  572.4 28.5 %attend.3 = (bf16[8,256,256]{2,1,0:T(8,128)(2,1)S(1)}, f32[8,256,256]{2,1,0:T(8,128)S(1)}, f32[8,8,1024]{2,1,0:T(8,128)S(1)}) custom-call(s32[1]{0:T(128)} %bitcast.1.me_ref, s32[8]{0:T(128)S(1)} %get-tuple-element.174.lo_ref, s32[8]{0:T(128)S(1)} %get-tuple-element.168.hi_ref, s32[8,1,256]{2,1,0:T(1,128)S(1)} %bitcast.590, ...), custom_call_target="tpu_custom_call" | custom-call | flops 8589934592 | bytes 8388608 | tf_op jit(solution)/shard_map/attend/pallas_call | solution.py:157
  610.7 8.1 collective-permute-start.17
  657.7 7.5 multiply_reduce_fusion.2
  680.3 110.1 %collective-permute-done.43 = bf16[2,2,2,2,64,5632]{5,4,0,1,2,3:T(8,128)(2,1)} collective-permute-done((bf16[2,2,2,2,64,5632]{5,4,0,1,2,3:T(8,128)(2,1)}, bf16[2,2,2,2,64,5632]{5,4,0,1,2,3:T(8,128)(2,1)}, u32[]{:S(2)}, u32[]{:S(2)}) %collective-permute-start.43) | collective-permute-done | bytes 11534368 | tf_op jit(solution)/shard_map/ppermute | solution.py:50
  790.4 13.5 select_bitcast_fusion.1
  803.9 11.1 pad_maximum_fusion
  815.0 8.2 copy.71
  824.5 34.2 %fusion.28 = f32[1024,5632]{1,0:T(8,128)} fusion(bf16[2048,5632]{1,0:T(8,128)(2,1)} %bitcast.598, bf16[512,2048]{1,0:T(8,128)(2,1)} %copy-done.56, bf16[512,2048]{1,0:T(8,128)(2,1)} %copy-done.34), kind=kOutput, calls=%fused_computation.102 | convolution fusion | flops 23630708736 | bytes 50331648 | tf_op jit(solution)/shard_map/dot_general | solution.py:28
  858.7 26.2 %multiply_convert_fusion.1 = (bf16[1024,2816]{1,0:T(8,128)(2,1)}, bf16[1024,2816]{1,0:T(8,128)(2,1)}, bf16[1024,2816]{1,0:T(8,128)(2,1)}) fusion(f32[1024,5632]{1,0:T(8,128)} %fusion.28, bf16[2048,2816]{1,0:T(8,128)(2,1)} %bitcast.604, bf16[512,2048]{1,0:T(8,128)(2,1)} %collective-permute-done.50, bf16[512,2048]{1,0:T(8,128)(2,1)S(1)} %bitcast.620), kind=kOutput, calls=%fused_computation.13 | convolution fusion | flops 11862802432 | bytes 56098816 | tf_op jit(solution)/shard_map/dot_general | solution.py:28
  884.9 32.0 %fusion.6 = f32[1024,2048]{1,0:T(8,128)} fusion(bf16[2048,5632]{1,0:T(8,128)(2,1)} %bitcast.599, bf16[1024,2816]{1,0:T(8,128)(2,1)} %get-tuple-element.37, bf16[1024,2816]{1,0:T(8,128)(2,1)} %get-tuple-element.36), kind=kOutput, calls=%fused_computation.28 | convolution fusion | flops 23645388800 | bytes 42991616 | tf_op jit(solution)/shard_map/dot_general | solution.py:28
  925.6 16.6 fusion.57
  946.4 15.7 convolution_convert_fusion.1
  968.7 32.4 %convolution_convert_fusion = bf16[2048,5632]{1,0:T(8,128)(2,1)} fusion(bf16[1024,2816]{1,0:T(8,128)(2,1)} %get-tuple-element.37, bf16[1024,2816]{1,0:T(8,128)(2,1)} %get-tuple-element.36, bf16[512,2048]{1,0:T(8,128)(2,1)} %copy-done.56, bf16[512,2048]{1,0:T(8,128)(2,1)} %copy-done.34), kind=kOutput, calls=%fused_computation.3 | convolution fusion | flops 23665311744 | bytes 38797312 | tf_op jit(solution)/shard_map/dot_general | solution.py:28
  1001.2 11.8 dynamic-slice_bitcast_fusion
  1020.6 9.6 convolution_convert_fusion.4
  1042.1 221.3 %collective-permute-done.105 = f32[2048]{0:T(1024)S(1)} collective-permute-done((f32[2048]{0:T(1024)S(1)}, f32[2048]{0:T(1024)S(1)}, u32[]{:S(2)}, u32[]{:S(2)}) %collective-permute-start.105) | collective-permute-done | bytes 8224 | tf_op jit(solution)/shard_map/ppermute | solution.py:50
  1282.5 7.7 collective-permute-done.55
  1299.5 28.8 %attend_back.2 = (bf16[8,256,256]{2,1,0:T(8,128)(2,1)S(1)}, bf16[8,256,128]{2,1,0:T(8,128)(2,1)S(1)}) custom-call(s32[1]{0:T(128)} %bitcast.1.me_ref, s32[8]{0:T(128)S(1)} %get-tuple-element.175.lo_ref, s32[8]{0:T(128)S(1)} %get-tuple-element.167.hi_ref, s32[8,1,256]{2,1,0:T(1,128)S(1)} %bitcast.593, bf16[8,256,384]{2,1,0:T(8,128)(2,1)S(1)} %copy-done.3, ...), custom_call_target="tpu_custom_call" | custom-call | flops 15032385536 | bytes 8388608 | tf_op jit(solution)/shard_map/attend_back/pallas_call | solution.py:270
  1335.7 10.7 collective-permute-start.72
  1355.5 38.2 %attend_back.3 = (bf16[8,256,256]{2,1,0:T(8,128)(2,1)S(1)}, bf16[8,256,128]{2,1,0:T(8,128)(2,1)S(1)}) custom-call(s32[1]{0:T(128)} %bitcast.1.me_ref, s32[8]{0:T(128)S(1)} %get-tuple-element.174.lo_ref, s32[8]{0:T(128)S(1)} %get-tuple-element.168.hi_ref, s32[8,1,256]{2,1,0:T(1,128)S(1)} %bitcast.591, bf16[8,256,384]{2,1,0:T(8,128)(2,1)S(1)} %copy-done.1, ...), custom_call_target="tpu_custom_call" | custom-call | flops 15032385536 | bytes 8388608 | tf_op jit(solution)/shard_map/attend_back/pallas_call | solution.py:270
  1443.8 8.9 collective-permute-done.76
  1462.6 8.4 collective-permute-done.79
  1478.1 11.0 fusion.22
  1499.3 8.7 convolution_convert_fusion.2
  1510.6 9.0 constant_dynamic-slice_fusion.4
  1548.9 9.6 fusion
  1566.1 82.2 %collective-permute-done.86 = bf16[2,2,2,64,2048]{4,3,0,1,2:T(8,128)(2,1)} collective-permute-done((bf16[2,2,2,64,2048]{4,3,0,1,2:T(8,128)(2,1)}, bf16[2,2,2,64,2048]{4,3,0,1,2:T(8,128)(2,1)}, u32[]{:S(2)}, u32[]{:S(2)}) %collective-permute-start.86) | collective-permute-done | bytes 2097184 | tf_op jit(solution)/shard_map/ppermute | solution.py:50
  1657.4 54.5 %collective-permute-done.87 = bf16[2,2,64,2048]{3,2,0,1:T(8,128)(2,1)S(1)} collective-permute-done((bf16[2,2,64,2048]{3,2,0,1:T(8,128)(2,1)S(1)}, bf16[2,2,64,2048]{3,2,0,1:T(8,128)(2,1)S(1)}, u32[]{:S(2)}, u32[]{:S(2)}) %collective-permute-start.87) | collective-permute-done | bytes 1048608 | tf_op jit(solution)/shard_map/ppermute | solution.py:50
  1738.1 39.9 %collective-permute-done.81 = bf16[2,2,2,64,2560]{4,3,1,2,0:T(8,128)(2,1)} collective-permute-done((bf16[2,2,2,64,2560]{4,3,1,2,0:T(8,128)(2,1)}, bf16[2,2,2,64,2560]{4,3,1,2,0:T(8,128)(2,1)}, u32[]{:S(2)}, u32[]{:S(2)}) %collective-permute-start.81) | collective-permute-done | bytes 2621472 | tf_op jit(solution)/shard_map/ppermute | solution.py:50
  1782.2 25.7 %collective-permute-done.98 = bf16[2,64,2816]{2,1,0:T(8,128)(2,1)S(1)} collective-permute-done((bf16[2,64,2816]{2,1,0:T(8,128)(2,1)S(1)}, bf16[2,64,2816]{2,1,0:T(8,128)(2,1)S(1)}, u32[]{:S(2)}, u32[]{:S(2)}) %collective-permute-start.98) | collective-permute-done | bytes 720928 | tf_op jit(solution)/shard_map/ppermute | solution.py:50
  1816.6 59.6 %collective-permute-done.93 = bf16[2,64,5632]{2,1,0:T(8,128)(2,1)S(1)} collective-permute-done((bf16[2,64,5632]{2,1,0:T(8,128)(2,1)S(1)}, bf16[2,64,5632]{2,1,0:T(8,128)(2,1)S(1)}, u32[]{:S(2)}, u32[]{:S(2)}) %collective-permute-start.93) | collective-permute-done | bytes 1441824 | tf_op jit(solution)/shard_map/ppermute | solution.py:50
  1880.8 15.4 collective-permute-done.84
  (551 shorter events, 497.3 us)
Async XLA Ops:
  5.9 36.0 %collective-permute-start.44 = (bf16[64,2816]{1,0:T(8,128)(2,1)}, bf16[64,2816]{1,0:T(8,128)(2,1)}, u32[]{:S(2)}, u32[]{:S(2)}) collective-permute-start(bf16[64,2816]{1,0:T(8,128)(2,1)} %bitcast.586), channel_id=1, source_target_pairs={{0,8},{8,0},{1,9},{9,1},{2,10},{10,2},{3,11},{11,3},{4,12},{12,4},... | collective-permute-start | bytes 1081352 | tf_op jit(solution)/shard_map/ppermute | solution.py:50
  6.4 34.1 %collective-permute-start = (bf16[64,2560]{1,0:T(8,128)(2,1)}, bf16[64,2560]{1,0:T(8,128)(2,1)}, u32[]{:S(2)}, u32[]{:S(2)}) collective-permute-start(bf16[64,2560]{1,0:T(8,128)(2,1)} %param.12), channel_id=1, source_target_pairs={{0,4},{2,6},{4,0},{6,2},{1,5},{3,7},{5,1},{7,3},{8,12},{10,14},{12... | collective-permute-start | bytes 983048 | tf_op jit(solution)/shard_map/ppermute | solution.py:50
  24.7 834.0 %collective-permute-start.50 = (bf16[512,2048]{1,0:T(8,128)(2,1)}, bf16[512,2048]{1,0:T(8,128)(2,1)}, u32[]{:S(2)}, u32[]{:S(2)}) collective-permute-start(bf16[512,2048]{1,0:T(8,128)(2,1)} %bitcast.619), channel_id=1, source_target_pairs={{0,8},{8,0},{1,9},{9,1},{2,10},{10,2},{3,11},{11,3},{4,12},{12,4},... | collective-permute-start | bytes 6291464 | tf_op jit(solution)/shard_map/ppermute | solution.py:50
  38.5 37.4 %collective-permute-start.34 = (bf16[2,64,2048]{2,1,0:T(8,128)(2,1)S(1)}, bf16[2,64,2048]{2,1,0:T(8,128)(2,1)S(1)}, u32[]{:S(2)}, u32[]{:S(2)}) collective-permute-start(bf16[2,64,2048]{2,1,0:T(8,128)(2,1)S(1)} %pad_maximum_fusion.34), channel_id=1, source_target_pairs={{0,2},{2,0},{4,6},{6,4},{1,3},{3,1},{5,7},{7,5},{8,10},{10,8},{12,... | collective-permute-start | bytes 1572872 | tf_op jit(solution)/shard_map/ppermute | solution.py:50
  41.7 47.6 %collective-permute-start.1 = (bf16[2,64,2560]{2,1,0:T(8,128)(2,1)S(1)}, bf16[2,64,2560]{2,1,0:T(8,128)(2,1)S(1)}, u32[]{:S(2)}, u32[]{:S(2)}) collective-permute-start(bf16[2,64,2560]{2,1,0:T(8,128)(2,1)S(1)} %pad_maximum_fusion.33), channel_id=1, source_target_pairs={{0,2},{2,0},{4,6},{6,4},{1,3},{3,1},{5,7},{7,5},{8,10},{10,8},{12,... | collective-permute-start | bytes 1966088 | tf_op jit(solution)/shard_map/ppermute | solution.py:50
  43.0 48.2 %collective-permute-start.45 = (bf16[2,64,2816]{2,1,0:T(8,128)(2,1)S(1)}, bf16[2,64,2816]{2,1,0:T(8,128)(2,1)S(1)}, u32[]{:S(2)}, u32[]{:S(2)}) collective-permute-start(bf16[2,64,2816]{2,1,0:T(8,128)(2,1)S(1)} %pad_maximum_fusion.32), channel_id=1, source_target_pairs={{0,4},{2,6},{4,0},{6,2},{1,5},{3,7},{5,1},{7,3},{8,12},{10,14},{12... | collective-permute-start | bytes 2162696 | tf_op jit(solution)/shard_map/ppermute | solution.py:50
  47.4 91.9 %collective-permute-start.40 = (bf16[2,64,5632]{2,1,0:T(8,128)(2,1)S(1)}, bf16[2,64,5632]{2,1,0:T(8,128)(2,1)S(1)}, u32[]{:S(2)}, u32[]{:S(2)}) collective-permute-start(bf16[2,64,5632]{2,1,0:T(8,128)(2,1)S(1)} %pad_maximum_fusion.25), channel_id=1, source_target_pairs={{0,4},{2,6},{4,0},{6,2},{1,5},{3,7},{5,1},{7,3},{8,12},{10,14},{12... | collective-permute-start | bytes 4325384 | tf_op jit(solution)/shard_map/ppermute | solution.py:50
  89.5 49.9 %collective-permute-start.2 = (bf16[2,2,64,2560]{3,2,1,0:T(8,128)(2,1)S(1)}, bf16[2,2,64,2560]{3,2,1,0:T(8,128)(2,1)S(1)}, u32[]{:S(2)}, u32[]{:S(2)}) collective-permute-start(bf16[2,2,64,2560]{3,2,1,0:T(8,128)(2,1)S(1)} %pad_maximum_fusion.30), channel_id=1, source_target_pairs={{0,1},{1,0},{2,3},{3,2},{4,5},{5,4},{6,7},{7,6},{8,9},{9,8},{10,11... | collective-permute-start | bytes 3932168 | tf_op jit(solution)/shard_map/ppermute | solution.py:50
  91.4 58.4 %collective-permute-start.46 = (bf16[2,2,64,2816]{3,2,0,1:T(8,128)(2,1)S(1)}, bf16[2,2,64,2816]{3,2,0,1:T(8,128)(2,1)S(1)}, u32[]{:S(2)}, u32[]{:S(2)}) collective-permute-start(bf16[2,2,64,2816]{3,2,0,1:T(8,128)(2,1)S(1)} %pad_maximum_fusion.26), channel_id=1, source_target_pairs={{0,2},{2,0},{4,6},{6,4},{1,3},{3,1},{5,7},{7,5},{8,10},{10,8},{12,... | collective-permute-start | bytes 4325384 | tf_op jit(solution)/shard_map/ppermute | solution.py:50
  100.3 64.3 %collective-permute-start.36 = (bf16[2,2,2,64,2048]{4,3,2,1,0:T(8,128)(2,1)S(1)}, bf16[2,2,2,64,2048]{4,3,2,1,0:T(8,128)(2,1)S(1)}, u32[]{:S(2)}, u32[]{:S(2)}) collective-permute-start(bf16[2,2,2,64,2048]{4,3,2,1,0:T(8,128)(2,1)S(1)} %pad_maximum_fusion.24), channel_id=1, source_target_pairs={{0,1},{1,0},{2,3},{3,2},{4,5},{5,4},{6,7},{7,6},{8,9},{9,8},{10,11... | collective-permute-start | bytes 6291464 | tf_op jit(solution)/shard_map/ppermute | solution.py:50
  139.9 60.0 %collective-permute-start.3 = (bf16[2,2,2,64,2560]{4,3,2,1,0:T(8,128)(2,1)S(1)}, bf16[2,2,2,64,2560]{4,3,2,1,0:T(8,128)(2,1)}, u32[]{:S(2)}, u32[]{:S(2)}) collective-permute-start(bf16[2,2,2,64,2560]{4,3,2,1,0:T(8,128)(2,1)S(1)} %pad_maximum_fusion.22), channel_id=1, source_target_pairs={{0,16},{16,0},{1,17},{17,1},{2,18},{18,2},{3,19},{19,3},{4,20},{20... | collective-permute-start | bytes 7864328 | tf_op jit(solution)/shard_map/ppermute | solution.py:50
  141.7 67.9 %collective-permute-start.41 = (bf16[2,2,64,5632]{3,2,0,1:T(8,128)(2,1)S(1)}, bf16[2,2,64,5632]{3,2,0,1:T(8,128)(2,1)}, u32[]{:S(2)}, u32[]{:S(2)}) collective-permute-start(bf16[2,2,64,5632]{3,2,0,1:T(8,128)(2,1)S(1)} %pad_maximum_fusion.15), channel_id=1, source_target_pairs={{0,2},{2,0},{4,6},{6,4},{1,3},{3,1},{5,7},{7,5},{8,10},{10,8},{12,... | collective-permute-start | bytes 8650760 | tf_op jit(solution)/shard_map/ppermute | solution.py:50
  150.3 109.2 %collective-permute-start.47 = (bf16[2,2,2,64,2816]{4,3,0,1,2:T(8,128)(2,1)S(1)}, bf16[2,2,2,64,2816]{4,3,0,1,2:T(8,128)(2,1)}, u32[]{:S(2)}, u32[]{:S(2)}) collective-permute-start(bf16[2,2,2,64,2816]{4,3,0,1,2:T(8,128)(2,1)S(1)} %pad_maximum_fusion.16), channel_id=1, source_target_pairs={{0,16},{16,0},{1,17},{17,1},{2,18},{18,2},{3,19},{19,3},{4,20},{20... | collective-permute-start | bytes 8650760 | tf_op jit(solution)/shard_map/ppermute | solution.py:50
  167.3 98.8 %collective-permute-start.37 = (bf16[2,2,2,2,64,2048]{5,4,3,2,1,0:T(8,128)(2,1)}, bf16[2,2,2,2,64,2048]{5,4,3,2,1,0:T(8,128)(2,1)}, u32[]{:S(2)}, u32[]{:S(2)}) collective-permute-start(bf16[2,2,2,2,64,2048]{5,4,3,2,1,0:T(8,128)(2,1)} %pad_maximum_fusion.11), channel_id=1, source_target_pairs={{0,8},{8,0},{1,9},{9,1},{2,10},{10,2},{3,11},{11,3},{4,12},{12,4},... | collective-permute-start | bytes 12582920 | tf_op jit(solution)/shard_map/ppermute | solution.py:50
  205.0 73.8 %collective-permute-start.4 = (bf16[2,2,2,2,64,2560]{5,4,3,2,1,0:T(8,128)(2,1)}, bf16[2,2,2,2,64,2560]{5,4,3,2,1,0:T(8,128)(2,1)}, u32[]{:S(2)}, u32[]{:S(2)}) collective-permute-start(bf16[2,2,2,2,64,2560]{5,4,3,2,1,0:T(8,128)(2,1)} %pad_maximum_fusion.10), channel_id=1, source_target_pairs={{0,8},{8,0},{1,9},{9,1},{2,10},{10,2},{3,11},{11,3},{4,12},{12,4},... | collective-permute-start | bytes 15728648 | tf_op jit(solution)/shard_map/ppermute | solution.py:50
  215.9 316.4 %collective-permute-start.42 = (bf16[2,2,2,64,5632]{4,3,0,1,2:T(8,128)(2,1)}, bf16[2,2,2,64,5632]{4,3,0,1,2:T(8,128)(2,1)}, u32[]{:S(2)}, u32[]{:S(2)}) collective-permute-start(bf16[2,2,2,64,5632]{4,3,0,1,2:T(8,128)(2,1)} %pad_maximum_fusion.8), channel_id=1, source_target_pairs={{0,1},{1,0},{2,3},{3,2},{4,5},{5,4},{6,7},{7,6},{8,9},{9,8},{10,11... | collective-permute-start | bytes 17301512 | tf_op jit(solution)/shard_map/ppermute | solution.py:50
  264.8 402.5 %collective-permute-start.48 = (bf16[2,2,2,2,64,2816]{5,4,1,2,3,0:T(8,128)(2,1)}, bf16[2,2,2,2,64,2816]{5,4,1,2,3,0:T(8,128)(2,1)}, u32[]{:S(2)}, u32[]{:S(2)}) collective-permute-start(bf16[2,2,2,2,64,2816]{5,4,1,2,3,0:T(8,128)(2,1)} %pad_maximum_fusion.9), channel_id=1, source_target_pairs={{0,1},{1,0},{2,3},{3,2},{4,5},{5,4},{6,7},{7,6},{8,9},{9,8},{10,11... | collective-permute-start | bytes 17301512 | tf_op jit(solution)/shard_map/ppermute | solution.py:50
  321.9 146.2 %collective-permute-start.5 = (bf16[256,384]{1,0:T(8,128)(2,1)S(1)}, bf16[256,384]{1,0:T(8,128)(2,1)S(1)}, u32[]{:S(2)}, u32[]{:S(2)}) collective-permute-start(bf16[256,384]{1,0:T(8,128)(2,1)S(1)} %get-tuple-element.104), channel_id=1, source_target_pairs={{0,1},{1,0},{2,3},{3,2},{4,5},{5,4},{6,7},{7,6},{8,9},{9,8},{10,11... | collective-permute-start | bytes 589832 | tf_op jit(solution)/shard_map/ppermute | solution.py:408
  322.7 145.6 %collective-permute-start.6 = (bf16[256,384]{1,0:T(8,128)(2,1)S(1)}, bf16[256,384]{1,0:T(8,128)(2,1)S(1)}, u32[]{:S(2)}, u32[]{:S(2)}) collective-permute-start(bf16[256,384]{1,0:T(8,128)(2,1)S(1)} %get-tuple-element.103), channel_id=1, source_target_pairs={{0,2},{1,3},{2,0},{3,1},{4,6},{5,7},{6,4},{7,5},{8,10},{9,11},{10,... | collective-permute-start | bytes 589832 | tf_op jit(solution)/shard_map/ppermute | solution.py:408
  505.6 39.6 %collective-permute-start.21 = (bf16[256,384]{1,0:T(8,128)(2,1)S(1)}, bf16[256,384]{1,0:T(8,128)(2,1)S(1)}, u32[]{:S(2)}, u32[]{:S(2)}) collective-permute-start(bf16[256,384]{1,0:T(8,128)(2,1)S(1)} %get-tuple-element.109), channel_id=1, source_target_pairs={{0,3},{1,2},{2,1},{3,0},{4,7},{5,6},{6,5},{7,4},{8,11},{9,10},{10,... | collective-permute-start | bytes 589832 | tf_op jit(solution)/shard_map/ppermute | solution.py:408
  509.7 37.2 %collective-permute-start.22 = (bf16[256,384]{1,0:T(8,128)(2,1)S(1)}, bf16[256,384]{1,0:T(8,128)(2,1)S(1)}, u32[]{:S(2)}, u32[]{:S(2)}) collective-permute-start(bf16[256,384]{1,0:T(8,128)(2,1)S(1)} %get-tuple-element.108), channel_id=1, source_target_pairs={{0,4},{1,5},{2,6},{3,7},{4,0},{5,1},{6,2},{7,3},{8,12},{9,13},{10,... | collective-permute-start | bytes 589832 | tf_op jit(solution)/shard_map/ppermute | solution.py:408
  544.4 246.0 %collective-permute-start.43 = (bf16[2,2,2,2,64,5632]{5,4,0,1,2,3:T(8,128)(2,1)}, bf16[2,2,2,2,64,5632]{5,4,0,1,2,3:T(8,128)(2,1)}, u32[]{:S(2)}, u32[]{:S(2)}) collective-permute-start(bf16[2,2,2,2,64,5632]{5,4,0,1,2,3:T(8,128)(2,1)} %pad_maximum_fusion.1), channel_id=1, source_target_pairs={{0,16},{16,0},{1,17},{17,1},{2,18},{18,2},{3,19},{19,3},{4,20},{20... | collective-permute-start | bytes 34603016 | tf_op jit(solution)/shard_map/ppermute | solution.py:50
  559.3 41.8 %collective-permute-start.12 = (bf16[256,256]{1,0:T(8,128)(2,1)}, bf16[256,256]{1,0:T(8,128)(2,1)S(1)}, u32[]{:S(2)}, u32[]{:S(2)}) collective-permute-start(bf16[256,256]{1,0:T(8,128)(2,1)} %get-tuple-element.140), channel_id=1, source_target_pairs={{0,1},{1,0},{2,3},{3,2},{4,5},{5,4},{6,7},{7,6},{8,9},{9,8},{10,11... | collective-permute-start | bytes 393224 | tf_op jit(solution)/shard_map/ppermute | solution.py:408
  565.3 37.6 %collective-permute-start.13 = (bf16[256,256]{1,0:T(8,128)(2,1)}, bf16[256,256]{1,0:T(8,128)(2,1)S(1)}, u32[]{:S(2)}, u32[]{:S(2)}) collective-permute-start(bf16[256,256]{1,0:T(8,128)(2,1)} %get-tuple-element.139), channel_id=1, source_target_pairs={{0,2},{1,3},{2,0},{3,1},{4,6},{5,7},{6,4},{7,5},{8,10},{9,11},{10,... | collective-permute-start | bytes 393224 | tf_op jit(solution)/shard_map/ppermute | solution.py:408
  667.3 155.9 %collective-permute-start.38 = (bf16[512,2048]{1,0:T(8,128)(2,1)S(1)}, bf16[512,2048]{1,0:T(8,128)(2,1)S(1)}, u32[]{:S(2)}, u32[]{:S(2)}) collective-permute-start(bf16[512,2048]{1,0:T(8,128)(2,1)S(1)} %multiply_convert_fusion.3), channel_id=1, source_target_pairs={{0,8},{8,0},{1,9},{9,1},{2,10},{10,2},{3,11},{11,3},{4,12},{12,4},... | collective-permute-start | bytes 6291464 | tf_op jit(solution)/shard_map/ppermute | solution.py:50
  920.7 92.3 %collective-permute-start.51 = (bf16[512,2048]{1,0:T(8,128)(2,1)}, bf16[512,2048]{1,0:T(8,128)(2,1)S(1)}, u32[]{:S(2)}, u32[]{:S(2)}) collective-permute-start(bf16[512,2048]{1,0:T(8,128)(2,1)} %slice.143), channel_id=1, source_target_pairs={{0,8},{8,0},{1,9},{9,1},{2,10},{10,2},{3,11},{11,3},{4,12},{12,4},... | collective-permute-start | bytes 6291464 | tf_op jit(solution)/shard_map/ppermute | solution.py:50
  946.4 68.1 %collective-permute-start.49 = (bf16[512,2048]{1,0:T(8,128)(2,1)}, bf16[512,2048]{1,0:T(8,128)(2,1)}, u32[]{:S(2)}, u32[]{:S(2)}) collective-permute-start(bf16[512,2048]{1,0:T(8,128)(2,1)} %slice.144), channel_id=1, source_target_pairs={{0,8},{8,0},{1,9},{9,1},{2,10},{10,2},{3,11},{11,3},{4,12},{12,4},... | collective-permute-start | bytes 6291464 | tf_op jit(solution)/shard_map/ppermute | solution.py:50
  968.1 565.3 %collective-permute-start.95 = (bf16[2,2,2,2,64,2816]{5,4,3,2,1,0:T(8,128)(2,1)}, bf16[2,2,2,2,64,2816]{5,4,3,2,1,0:T(8,128)(2,1)}, u32[]{:S(2)}, u32[]{:S(2)}) collective-permute-start(bf16[2,2,2,2,64,2816]{5,4,3,2,1,0:T(8,128)(2,1)} %dynamic-slice_bitcast_fusion.1), channel_id=1, source_target_pairs={{0,1},{1,0},{2,3},{3,2},{4,5},{5,4},{6,7},{7,6},{8,9},{9,8},{10,11... | collective-permute-start | bytes 17301512 | tf_op jit(solution)/shard_map/ppermute | solution.py:50
  1013.0 535.9 %collective-permute-start.90 = (bf16[2,2,2,2,64,5632]{5,4,3,2,1,0:T(8,128)(2,1)}, bf16[2,2,2,2,64,5632]{5,4,3,2,1,0:T(8,128)(2,1)}, u32[]{:S(2)}, u32[]{:S(2)}) collective-permute-start(bf16[2,2,2,2,64,5632]{5,4,3,2,1,0:T(8,128)(2,1)} %dynamic-slice_bitcast_fusion), channel_id=1, source_target_pairs={{0,16},{16,0},{1,17},{17,1},{2,18},{18,2},{3,19},{19,3},{4,20},{20... | collective-permute-start | bytes 34603016 | tf_op jit(solution)/shard_map/ppermute | solution.py:50
  1037.3 226.1 %collective-permute-start.105 = (f32[2048]{0:T(1024)S(1)}, f32[2048]{0:T(1024)S(1)}, u32[]{:S(2)}, u32[]{:S(2)}) collective-permute-start(f32[2048]{0:T(1024)S(1)} %get-tuple-element.28), channel_id=1, source_target_pairs={{0,16},{16,0},{1,17},{17,1},{2,18},{18,2},{3,19},{19,3},{4,20},{20... | collective-permute-start | bytes 24584 | tf_op jit(solution)/shard_map/ppermute | solution.py:50
  1040.7 233.6 %collective-permute-start.52 = (bf16[256,256]{1,0:T(8,128)(2,1)S(1)}, bf16[256,256]{1,0:T(8,128)(2,1)S(1)}, u32[]{:S(2)}, u32[]{:S(2)}) collective-permute-start(bf16[256,256]{1,0:T(8,128)(2,1)S(1)} %get-tuple-element.126), channel_id=1, source_target_pairs={{0,1},{1,0},{2,3},{3,2},{4,5},{5,4},{6,7},{7,6},{8,9},{9,8},{10,11... | collective-permute-start | bytes 393224 | tf_op jit(solution)/shard_map/ppermute | solution.py:408
  1293.6 34.8 %collective-permute-start.66 = (bf16[256,256]{1,0:T(8,128)(2,1)S(1)}, bf16[256,256]{1,0:T(8,128)(2,1)S(1)}, u32[]{:S(2)}, u32[]{:S(2)}) collective-permute-start(bf16[256,256]{1,0:T(8,128)(2,1)S(1)} %get-tuple-element.133), channel_id=1, source_target_pairs={{0,1},{1,0},{2,3},{3,2},{4,5},{5,4},{6,7},{7,6},{8,9},{9,8},{10,11... | collective-permute-start | bytes 393224 | tf_op jit(solution)/shard_map/ppermute | solution.py:408
  1294.5 35.9 %collective-permute-start.67 = (bf16[256,256]{1,0:T(8,128)(2,1)S(1)}, bf16[256,256]{1,0:T(8,128)(2,1)S(1)}, u32[]{:S(2)}, u32[]{:S(2)}) collective-permute-start(bf16[256,256]{1,0:T(8,128)(2,1)S(1)} %get-tuple-element.132), channel_id=1, source_target_pairs={{0,2},{1,3},{2,0},{3,1},{4,6},{5,7},{6,4},{7,5},{8,10},{9,11},{10,... | collective-permute-start | bytes 393224 | tf_op jit(solution)/shard_map/ppermute | solution.py:408
  1346.7 151.5 %collective-permute-start.109 = (f32[2048]{0:T(1024)S(1)}, f32[2048]{0:T(1024)S(1)}, u32[]{:S(2)}, u32[]{:S(2)}) collective-permute-start(f32[2048]{0:T(1024)S(1)} %add.391), channel_id=1, source_target_pairs={{0,1},{1,0},{2,3},{3,2},{4,5},{5,4},{6,7},{7,6},{8,9},{9,8},{10,11... | collective-permute-start | bytes 24584 | tf_op jit(solution)/shard_map/ppermute | solution.py:50
  1347.1 47.0 %collective-permute-start.59 = (bf16[256,384]{1,0:T(8,128)(2,1)S(1)}, bf16[256,384]{1,0:T(8,128)(2,1)S(1)}, u32[]{:S(2)}, u32[]{:S(2)}) collective-permute-start(bf16[256,384]{1,0:T(8,128)(2,1)S(1)} %get-tuple-element.88), channel_id=1, source_target_pairs={{0,1},{1,0},{2,3},{3,2},{4,5},{5,4},{6,7},{7,6},{8,9},{9,8},{10,11... | collective-permute-start | bytes 589832 | tf_op jit(solution)/shard_map/ppermute | solution.py:408
  1350.0 44.2 %collective-permute-start.60 = (bf16[256,384]{1,0:T(8,128)(2,1)S(1)}, bf16[256,384]{1,0:T(8,128)(2,1)S(1)}, u32[]{:S(2)}, u32[]{:S(2)}) collective-permute-start(bf16[256,384]{1,0:T(8,128)(2,1)S(1)} %get-tuple-element.87), channel_id=1, source_target_pairs={{0,2},{1,3},{2,0},{3,1},{4,6},{5,7},{6,4},{7,5},{8,10},{9,11},{10,... | collective-permute-start | bytes 589832 | tf_op jit(solution)/shard_map/ppermute | solution.py:408
  1498.2 43.5 %collective-permute-start.85 = (bf16[2,2,2,2,64,2048]{5,4,1,2,3,0:T(8,128)(2,1)}, bf16[2,2,2,2,64,2048]{5,4,1,2,3,0:T(8,128)(2,1)}, u32[]{:S(2)}, u32[]{:S(2)}) collective-permute-start(bf16[2,2,2,2,64,2048]{5,4,1,2,3,0:T(8,128)(2,1)} %bitcast.584), channel_id=1, source_target_pairs={{0,8},{8,0},{1,9},{9,1},{2,10},{10,2},{3,11},{11,3},{4,12},{12,4},... | collective-permute-start | bytes 12582920 | tf_op jit(solution)/shard_map/ppermute | solution.py:50
  1525.4 188.4 %collective-permute-start.80 = (bf16[2,2,2,2,64,2560]{5,4,1,2,0,3:T(8,128)(2,1)}, bf16[2,2,2,2,64,2560]{5,4,1,2,0,3:T(8,128)(2,1)}, u32[]{:S(2)}, u32[]{:S(2)}) collective-permute-start(bf16[2,2,2,2,64,2560]{5,4,1,2,0,3:T(8,128)(2,1)} %bitcast.583), channel_id=1, source_target_pairs={{0,8},{8,0},{1,9},{9,1},{2,10},{10,2},{3,11},{11,3},{4,12},{12,4},... | collective-permute-start | bytes 15728648 | tf_op jit(solution)/shard_map/ppermute | solution.py:50
  1539.6 113.6 %collective-permute-start.96 = (bf16[2,2,2,64,2816]{4,3,2,1,0:T(8,128)(2,1)S(1)}, bf16[2,2,2,64,2816]{4,3,2,1,0:T(8,128)(2,1)}, u32[]{:S(2)}, u32[]{:S(2)}) collective-permute-start(bf16[2,2,2,64,2816]{4,3,2,1,0:T(8,128)(2,1)S(1)} %dynamic-slice_bitcast_fusion.3), channel_id=1, source_target_pairs={{0,16},{16,0},{1,17},{17,1},{2,18},{18,2},{3,19},{19,3},{4,20},{20... | collective-permute-start | bytes 8650760 | tf_op jit(solution)/shard_map/ppermute | solution.py:50
  1547.0 101.3 %collective-permute-start.86 = (bf16[2,2,2,64,2048]{4,3,0,1,2:T(8,128)(2,1)}, bf16[2,2,2,64,2048]{4,3,0,1,2:T(8,128)(2,1)}, u32[]{:S(2)}, u32[]{:S(2)}) collective-permute-start(bf16[2,2,2,64,2048]{4,3,0,1,2:T(8,128)(2,1)} %dynamic-slice_bitcast_fusion.6), channel_id=1, source_target_pairs={{0,16},{16,0},{1,17},{17,1},{2,18},{18,2},{3,19},{19,3},{4,20},{20... | collective-permute-start | bytes 6291464 | tf_op jit(solution)/shard_map/ppermute | solution.py:50
  1564.5 161.8 %collective-permute-start.91 = (bf16[2,2,2,64,5632]{4,3,2,1,0:T(8,128)(2,1)}, bf16[2,2,2,64,5632]{4,3,2,1,0:T(8,128)(2,1)}, u32[]{:S(2)}, u32[]{:S(2)}) collective-permute-start(bf16[2,2,2,64,5632]{4,3,2,1,0:T(8,128)(2,1)} %dynamic-slice_bitcast_fusion.2), channel_id=1, source_target_pairs={{0,1},{1,0},{2,3},{3,2},{4,5},{5,4},{6,7},{7,6},{8,9},{9,8},{10,11... | collective-permute-start | bytes 17301512 | tf_op jit(solution)/shard_map/ppermute | solution.py:50
  1651.4 60.6 %collective-permute-start.87 = (bf16[2,2,64,2048]{3,2,0,1:T(8,128)(2,1)S(1)}, bf16[2,2,64,2048]{3,2,0,1:T(8,128)(2,1)S(1)}, u32[]{:S(2)}, u32[]{:S(2)}) collective-permute-start(bf16[2,2,64,2048]{3,2,0,1:T(8,128)(2,1)S(1)} %dynamic-slice_bitcast_fusion.11), channel_id=1, source_target_pairs={{0,1},{1,0},{2,3},{3,2},{4,5},{5,4},{6,7},{7,6},{8,9},{9,8},{10,11... | collective-permute-start | bytes 3145736 | tf_op jit(solution)/shard_map/ppermute | solution.py:50
  1656.0 68.7 %collective-permute-start.97 = (bf16[2,2,64,2816]{3,2,1,0:T(8,128)(2,1)S(1)}, bf16[2,2,64,2816]{3,2,1,0:T(8,128)(2,1)S(1)}, u32[]{:S(2)}, u32[]{:S(2)}) collective-permute-start(bf16[2,2,64,2816]{3,2,1,0:T(8,128)(2,1)S(1)} %dynamic-slice_bitcast_fusion.7), channel_id=1, source_target_pairs={{0,2},{2,0},{4,6},{6,4},{1,3},{3,1},{5,7},{7,5},{8,10},{10,8},{12,... | collective-permute-start | bytes 4325384 | tf_op jit(solution)/shard_map/ppermute | solution.py:50
  1721.5 56.6 %collective-permute-start.81 = (bf16[2,2,2,64,2560]{4,3,1,2,0:T(8,128)(2,1)}, bf16[2,2,2,64,2560]{4,3,1,2,0:T(8,128)(2,1)}, u32[]{:S(2)}, u32[]{:S(2)}) collective-permute-start(bf16[2,2,2,64,2560]{4,3,1,2,0:T(8,128)(2,1)} %dynamic-slice_bitcast_fusion.5), channel_id=1, source_target_pairs={{0,1},{1,0},{2,3},{3,2},{4,5},{5,4},{6,7},{7,6},{8,9},{9,8},{10,11... | collective-permute-start | bytes 7864328 | tf_op jit(solution)/shard_map/ppermute | solution.py:50
  1732.4 78.9 %collective-permute-start.92 = (bf16[2,2,64,5632]{3,2,1,0:T(8,128)(2,1)S(1)}, bf16[2,2,64,5632]{3,2,1,0:T(8,128)(2,1)S(1)}, u32[]{:S(2)}, u32[]{:S(2)}) collective-permute-start(bf16[2,2,64,5632]{3,2,1,0:T(8,128)(2,1)S(1)} %dynamic-slice_bitcast_fusion.4), channel_id=1, source_target_pairs={{0,2},{2,0},{4,6},{6,4},{1,3},{3,1},{5,7},{7,5},{8,10},{10,8},{12,... | collective-permute-start | bytes 8650760 | tf_op jit(solution)/shard_map/ppermute | solution.py:50
  1734.2 73.7 %collective-permute-start.98 = (bf16[2,64,2816]{2,1,0:T(8,128)(2,1)S(1)}, bf16[2,64,2816]{2,1,0:T(8,128)(2,1)S(1)}, u32[]{:S(2)}, u32[]{:S(2)}) collective-permute-start(bf16[2,64,2816]{2,1,0:T(8,128)(2,1)S(1)} %dynamic-slice_bitcast_fusion.13), channel_id=1, source_target_pairs={{0,4},{2,6},{4,0},{6,2},{1,5},{3,7},{5,1},{7,3},{8,12},{10,14},{12... | collective-permute-start | bytes 2162696 | tf_op jit(solution)/shard_map/ppermute | solution.py:50
  1812.1 64.1 %collective-permute-start.93 = (bf16[2,64,5632]{2,1,0:T(8,128)(2,1)S(1)}, bf16[2,64,5632]{2,1,0:T(8,128)(2,1)S(1)}, u32[]{:S(2)}, u32[]{:S(2)}) collective-permute-start(bf16[2,64,5632]{2,1,0:T(8,128)(2,1)S(1)} %dynamic-slice_bitcast_fusion.9), channel_id=1, source_target_pairs={{0,4},{2,6},{4,0},{6,2},{1,5},{3,7},{5,1},{7,3},{8,12},{10,14},{12... | collective-permute-start | bytes 4325384 | tf_op jit(solution)/shard_map/ppermute | solution.py:50
  1814.1 63.8 %collective-permute-start.83 = (bf16[2,64,2560]{2,1,0:T(8,128)(2,1)S(1)}, bf16[2,64,2560]{2,1,0:T(8,128)(2,1)S(1)}, u32[]{:S(2)}, u32[]{:S(2)}) collective-permute-start(bf16[2,64,2560]{2,1,0:T(8,128)(2,1)S(1)} %dynamic-slice_bitcast_fusion.14), channel_id=1, source_target_pairs={{0,2},{2,0},{4,6},{6,4},{1,3},{3,1},{5,7},{7,5},{8,10},{10,8},{12,... | collective-permute-start | bytes 1966088 | tf_op jit(solution)/shard_map/ppermute | solution.py:50
  (123 other events, 2438.4 us)

commit v2 on v1

v2 whole, which is shorter than its diff:
```python
import functools
import math

import jax
import jax.numpy as jnp
from jax import lax
from jax.experimental import pallas as pl
from jax.experimental.pallas import tpu as pltpu
from jax.sharding import Mesh
from jax.sharding import PartitionSpec as P

H = 32
HD = 64
KV = 4
FF = 5632

EPSILON = 1e-05
NEG = -1e30
ROTARY_BASE = 10000.0
LOG2E = math.log2(math.e)
LANES = 128

bf16 = jnp.bfloat16
f32 = jnp.float32


def dot(a, b, dims=((1,), (0,))):
    return lax.dot_general(a, b, (dims, ((), ())), preferred_element_type=f32)


CORE = ("core", 0)
NEAR = ("z", 0)


def axis_bits(axis):
    return [(axis, b) for b in reversed(range((lax.axis_size(axis) - 1).bit_length()))]


def my_bit(key):
    axis, b = key
    return (lax.axis_index(axis) >> b) & 1


def swap(values, key):
    axis, b = key
    return lax.ppermute(values, axis, [(i, i ^ (1 << b)) for i in range(lax.axis_size(axis))])


class Flow:
    def __init__(self):
        self.token = jnp.zeros((), f32)

    def open(self, *values):
        opened = lax.optimization_barrier(values + (self.token,))[:-1]
        return opened if len(values) > 1 else opened[0]

    def close(self, *values):
        *values, self.token = lax.optimization_barrier(values + (self.token,))
        return values if len(values) > 1 else values[0]


def pair_rows(values, key):
    other = swap(values, key)
    low = my_bit(key) == 0
    return jnp.concatenate([jnp.where(low, values, other), jnp.where(low, other, values)], axis=0)


def choose(values, key, axis):
    bit = my_bit(key)
    return (
        lax.dynamic_index_in_dim(values, bit, axis, keepdims=False),
        lax.dynamic_index_in_dim(values, 1 - bit, axis, keepdims=False),
    )


def by_bit(mine, other, key, axis):
    low = my_bit(key) == 0
    return jnp.stack([jnp.where(low, mine, other), jnp.where(low, other, mine)], axis=axis)


def chunk_keys():
    return axis_bits("x") + axis_bits("y") + axis_bits("z")[:-1]


def mask_of(key):
    keys = chunk_keys()
    return 1 << (len(keys) - 1 - keys.index(key))


def gather_step(chunks, have, key):
    at = sum(mask_of(k) > mask_of(key) for k in have)
    return jnp.stack([chunks, swap(chunks, key)], axis=at), have + [key]


def gather_steps(chunks, have, keys):
    for key in keys:
        chunks, have = gather_step(chunks, have, key)
    return chunks, have


def scatter_step(terms, have, key):
    at = sum(mask_of(k) > mask_of(key) for k in have)
    mine = lax.index_in_dim(terms, 0, at, keepdims=False)
    arrived = swap(lax.index_in_dim(terms, 1, at, keepdims=False), key)
    have = [k for k in have if k != key]
    total = mine.astype(f32) + arrived.astype(f32)
    return (total.astype(bf16) if have else total), have


def scatter_steps(terms, have, keys):
    for key in keys:
        terms, have = scatter_step(terms, have, key)
    return terms, have


def sum_all(values):
    for axis in ("core", "x", "y", "z"):
        for key in axis_bits(axis):
            values = values + swap(values, key)
    return values


def stack_heads(x, heads):
    return jnp.concatenate([x[:, h * HD : (h + 1) * HD] for h in range(heads)], axis=0)


def unstack_heads(x, heads):
    rows = x.shape[0] // heads
    return jnp.concatenate([x[h * rows : (h + 1) * rows] for h in range(heads)], axis=1)


def block_allowed(i, j, rows, start):
    key_pos = j * rows + lax.broadcasted_iota(jnp.int32, (rows, rows), 0)
    query_pos = i * rows + lax.broadcasted_iota(jnp.int32, (rows, rows), 1)
    return (key_pos <= query_pos) & (key_pos >= start)


def attend_kernel(
    heads, lo_ref, hi_ref, start_ref, qkv_ref, out_ref, raw_ref, lse_ref, m_s, l_s, acc_s
):
    rows = qkv_ref.shape[1]
    qw = heads * HD
    scale = LOG2E * HD**-0.5
    i = pl.program_id(0)
    q = stack_heads(qkv_ref[i, :, :qw], heads)
    m_s[...] = jnp.full_like(m_s, NEG)
    l_s[...] = jnp.zeros_like(l_s)
    acc_s[...] = jnp.zeros_like(acc_s)

    def block(j, masked):
        k = qkv_ref[j, :, qw : qw + HD]
        v = qkv_ref[j, :, qw + HD : qw + 2 * HD]
        s = dot(k, q, ((1,), (1,)))
        if masked:
            ok = block_allowed(i, j, rows, start_ref[0])
            s = jnp.where(jnp.concatenate([ok] * heads, axis=1), s, NEG)
        m_old = m_s[...]
        m_new = jnp.maximum(m_old, jnp.max(s, axis=0, keepdims=True) * scale)
        p = jnp.exp2(s * scale - m_new)
        keep = jnp.exp2(m_old - m_new)
        l_s[...] = l_s[...] * keep + jnp.sum(p, axis=0, keepdims=True)
        acc_s[...] = acc_s[...] * keep + dot(v, p.astype(bf16), ((0,), (0,)))
        m_s[...] = m_new

    def masked_step(j, carry):
        block(j, True)
        return carry

    def plain_step(j, carry):
        block(j, False)
        return carry

    block(i, True)
    lax.fori_loop(lo_ref[i], hi_ref[i], masked_step, 0)
    lax.fori_loop(hi_ref[i], i, plain_step, 0)
    total = l_s[...]
    result = unstack_heads(jnp.transpose(acc_s[...] / total), heads)
    raw_ref[0] = result
    out_ref[0] = result.astype(bf16)
    lse_ref[0] = jnp.broadcast_to(m_s[...] + jnp.log2(total), (8, heads * rows))


def attend(lo, hi, start, qkv, heads):
    n, rows, w = qkv.shape
    qw = heads * HD
    smem = pl.BlockSpec(memory_space=pltpu.SMEM)
    pairs = heads * (n * rows) ** 2 // 2
    per_block = lambda shape: pl.BlockSpec((1,) + shape, lambda i: (i, 0, 0))
    return pl.pallas_call(
        functools.partial(attend_kernel, heads),
        grid=(n,),
        out_shape=(
            jax.ShapeDtypeStruct((n, rows, qw), bf16),
            jax.ShapeDtypeStruct((n, rows, qw), f32),
            jax.ShapeDtypeStruct((n, 8, heads * rows), f32),
        ),
        in_specs=[
            smem,
            smem,
            per_block((1, rows)),
            pl.BlockSpec((n, rows, w), lambda i: (0, 0, 0)),
        ],
        out_specs=(per_block((rows, qw)), per_block((rows, qw)), per_block((8, heads * rows))),
        scratch_shapes=[
            pltpu.VMEM((1, heads * rows), f32),
            pltpu.VMEM((1, heads * rows), f32),
            pltpu.VMEM((HD, heads * rows), f32),
        ],
        compiler_params=pltpu.CompilerParams(vmem_limit_bytes=48 << 20),
        cost_estimate=pl.CostEstimate(
            flops=16 * HD * pairs, bytes_accessed=8 << 20, transcendentals=pairs
        ),
        name="attend",
    )(lo, hi, start, qkv)


def attend_back_kernel(
    heads,
    lo_ref,
    hi_ref,
    start_ref,
    qkv_ref,
    g_ref,
    raw_ref,
    lse_ref,
    dq_ref,
    dkv_ref,
    dkv_s,
    dq_s,
):
    n, rows, _ = qkv_ref.shape
    qw = heads * HD
    scale = LOG2E * HD**-0.5
    i = pl.program_id(0)

    @pl.when(i == 0)
    def _():
        dkv_s[...] = jnp.zeros_like(dkv_s)

    dq_s[...] = jnp.zeros_like(dq_s)
    q = stack_heads(qkv_ref[i, :, :qw], heads)
    g_flat = g_ref[i]
    g = stack_heads(g_flat, heads)
    product = g_flat.astype(f32) * raw_ref[0]
    inner = jnp.concatenate(
        [
            jnp.sum(product[:, h * HD : (h + 1) * HD], axis=1, keepdims=True)
            for h in range(heads)
        ],
        axis=0,
    )
    inner = jnp.transpose(jnp.broadcast_to(inner, (heads * rows, LANES)))[:1]
    lse = lse_ref[0, :1]

    def block(j, masked):
        k = qkv_ref[j, :, qw : qw + HD]
        v = qkv_ref[j, :, qw + HD : qw + 2 * HD]
        s = dot(k, q, ((1,), (1,)))
        grad_probs = dot(v, g, ((1,), (1,)))
        p = jnp.exp2(s * scale - lse)
        if masked:
            ok = block_allowed(i, j, rows, start_ref[0])
            p = jnp.where(jnp.concatenate([ok] * heads, axis=1), p, 0.0)
        grad_scores = (p * (grad_probs - inner)).astype(bf16)
        dkv_s[j, :, :HD] += dot(grad_scores, q)
        dkv_s[j, :, HD:] += dot(p.astype(bf16), g)
        dq_s[...] += dot(k, grad_scores, ((0,), (0,)))

    def masked_step(j, carry):
        block(j, True)
        return carry

    def plain_step(j, carry):
        block(j, False)
        return carry

    lax.fori_loop(lo_ref[i], hi_ref[i], masked_step, 0)
    lax.fori_loop(hi_ref[i], i, plain_step, 0)
    block(i, True)
    dq = unstack_heads(jnp.transpose(dq_s[...] * HD**-0.5), heads)
    dq_ref[0] = dq.astype(bf16)

    @pl.when(i == n - 1)
    def _():
        for r in range(n):
            done = dkv_s[r]
            dkv_ref[r] = jnp.concatenate([done[:, :HD] * HD**-0.5, done[:, HD:]], axis=1).astype(
                bf16
            )


def attend_back(lo, hi, start, qkv, grad, raw, lse, heads):
    n, rows, w = qkv.shape
    qw = heads * HD
    smem = pl.BlockSpec(memory_space=pltpu.SMEM)
    pairs = heads * (n * rows) ** 2 // 2
    per_block = lambda shape: pl.BlockSpec((1,) + shape, lambda i: (i, 0, 0))
    whole = lambda shape: pl.BlockSpec(shape, lambda i: (0, 0, 0))
    return pl.pallas_call(
        functools.partial(attend_back_kernel, heads),
        grid=(n,),
        out_shape=(
            jax.ShapeDtypeStruct((n, rows, qw), bf16),
            jax.ShapeDtypeStruct((n, rows, 2 * HD), bf16),
        ),
        in_specs=[
            smem,
            smem,
            per_block((1, rows)),
            whole((n, rows, w)),
            whole((n, rows, qw)),
            per_block((rows, qw)),
            per_block((8, heads * rows)),
        ],
        out_specs=(per_block((rows, qw)), whole((n, rows, 2 * HD))),
        scratch_shapes=[
            pltpu.VMEM((n, rows, 2 * HD), f32),
            pltpu.VMEM((HD, heads * rows), f32),
        ],
        compiler_params=pltpu.CompilerParams(vmem_limit_bytes=48 << 20),
        cost_estimate=pl.CostEstimate(
            flops=28 * HD * pairs, bytes_accessed=8 << 20, transcendentals=pairs
        ),
        name="attend_back",
    )(lo, hi, start, qkv, grad, raw, lse)


def rotate_lanes(v, cosine, signed_sine):
    parts = []
    for c in range(v.shape[1] // LANES):
        part = v[:, c * LANES : (c + 1) * LANES]
        lane = lax.broadcasted_iota(jnp.int32, part.shape, 1)
        other = jnp.where(
            lane % HD < HD // 2,
            pltpu.roll(part, LANES - HD // 2, 1),
            pltpu.roll(part, HD // 2, 1),
        )
        parts.append(part * cosine + other * signed_sine)
    return jnp.concatenate(parts, axis=1) if len(parts) > 1 else parts[0]


def pack_kernel(copies, core_ref, q_own, q_other, k_own, k_other, v_own, v_other, cos_ref, sin_ref, out_ref):
    qw = q_own.shape[1]
    n = pl.num_programs(1)
    d = pl.program_id(1)
    here = d // (n // 2) == core_ref[0]
    cosine = cos_ref[...]
    sine = sin_ref[...]
    q = jnp.where(here, q_own[...], q_other[...])
    out_ref[0, 0, :, :qw] = rotate_lanes(q, cosine, sine).astype(bf16)
    k = rotate_lanes(jnp.where(here, k_own[...], k_other[...]), cosine, sine)
    v = jnp.where(here, v_own[...], v_other[...])
    first = (d // copies) % 2 == 0
    lane = lax.broadcasted_iota(jnp.int32, k.shape, 1)
    k = jnp.where(first, k, pltpu.roll(k, HD, 1))
    v = jnp.where(first, pltpu.roll(v, HD, 1), v)
    out_ref[0, 0, :, qw:] = jnp.where(lane < HD, k, v).astype(bf16)


def pack_heads(core, projected, cosine, sine, seqs, n):
    own, other = projected
    rows = own.shape[0] // seqs
    qw = H * HD // n
    kv_at = H * HD // 2 // LANES
    q_spec = pl.BlockSpec((rows, qw), lambda b, d: (b, d % (n // 2)))
    k_spec = pl.BlockSpec((rows, LANES), lambda b, d: (b, kv_at))
    v_spec = pl.BlockSpec((rows, LANES), lambda b, d: (b, kv_at + 1))
    table = pl.BlockSpec((rows, LANES), lambda b, d: (b, 0))
    return [
        pl.pallas_call(
            functools.partial(pack_kernel, n // KV),
            grid=(1, n),
            in_specs=[pl.BlockSpec(memory_space=pltpu.SMEM)]
            + [
                pl.BlockSpec(spec.block_shape, lambda _, d, spec=spec, seq=seq: spec.index_map(seq, d))
                for spec in (q_spec, q_spec, k_spec, k_spec, v_spec, v_spec, table, table)
            ],
            out_specs=pl.BlockSpec((1, 1, rows, qw + 2 * HD), lambda b, d: (b, d, 0, 0)),
            out_shape=jax.ShapeDtypeStruct((1, n, rows, qw + 2 * HD), bf16),
            cost_estimate=pl.CostEstimate(flops=0, bytes_accessed=6 << 20, transcendentals=0),
            name="pack_heads",
        )(core, own, other, own, other, own, other, cosine, sine)[0]
        for seq in range(seqs)
    ]


def unpack_kernel(n, core_ref, in_ref, cos_ref, sin_ref, out_ref):
    qw = in_ref.shape[2] - 2 * HD
    copies = n // KV
    own = core_ref[0] * (n // 2)
    cosine = cos_ref[...]
    sine = -sin_ref[...]
    lane = lax.broadcasted_iota(jnp.int32, cosine.shape, 1)
    half_cols = out_ref.shape[1] // 2
    for half in range(2):
        at = half * half_cols
        first = half * (n // 2)
        for d in range(n // 2):
            part = in_ref[(first + d) ^ own, :, :qw].astype(f32)
            rotated = rotate_lanes(part, cosine, sine).astype(bf16)
            out_ref[:, at + d * qw : at + (d + 1) * qw] = rotated
        sums = []
        for head in range(2):
            total = None
            for c in range(copies):
                slot = in_ref[(first + head * copies + c) ^ own, :, qw:].astype(f32)
                total = slot if total is None else total + slot
            sums.append(total)
        k = jnp.where(lane < HD, sums[0], pltpu.roll(sums[1], HD, 1))
        v = jnp.where(lane < HD, pltpu.roll(sums[0], HD, 1), sums[1])
        k_at = at + H * HD // 2
        out_ref[:, k_at : k_at + LANES] = rotate_lanes(k, cosine, sine).astype(bf16)
        out_ref[:, k_at + LANES : k_at + 2 * LANES] = v.astype(bf16)


def unpack_heads(core, pieces, cosine, sine):
    n, rows, w = pieces.shape
    cols = H * HD + 2 * KV * HD
    return pl.pallas_call(
        functools.partial(unpack_kernel, n),
        out_shape=jax.ShapeDtypeStruct((rows, cols), bf16),
        in_specs=[pl.BlockSpec(memory_space=pltpu.SMEM)]
        + [pl.BlockSpec(memory_space=pltpu.VMEM)] * 3,
        out_specs=pl.BlockSpec(memory_space=pltpu.VMEM),
        compiler_params=pltpu.CompilerParams(vmem_limit_bytes=32 << 20),
        cost_estimate=pl.CostEstimate(flops=0, bytes_accessed=4 << 20, transcendentals=0),
        name="unpack_heads",
    )(core, pieces, cosine, sine)


def rms_scale(hidden):
    return lax.rsqrt(jnp.mean(hidden * hidden, axis=-1, keepdims=True) + EPSILON)


def rms_back(grad_scaled, scaled, inverse):
    return inverse * (grad_scaled - scaled * jnp.mean(grad_scaled * scaled, axis=-1, keepdims=True))


def exchange(pieces):
    return lax.all_to_all(pieces, ("z", "y"), split_axis=0, concat_axis=0, tiled=True)


def pick(values, index):
    return lax.dynamic_index_in_dim(values, index, 0, keepdims=False)


def feature_order(width, sub):
    place = jnp.arange(width, dtype=jnp.int32)
    group = place // sub
    chunk = group // 4
    at = {"core": group % 2, "x": 0, "y": 0, "z": (group // 2) % 2}
    for key in chunk_keys():
        bit = ((chunk // mask_of(key)) % 2) ^ my_bit(key)
        at[key[0]] = at[key[0]] + (bit << key[1])
    source = ((at["x"] * 2 + at["core"]) * lax.axis_size("z") + at["z"]) * lax.axis_size("y")
    source = (source + at["y"]) * sub + place % sub
    return (place[:, None] == source[None, :]).astype(bf16)


def local(
    tokens,
    cotangent,
    segments,
    joint_projection_matrix,
    output_weight_rows,
    gate_up_weight,
    down_weight_rows,
    attn_gain,
    ffn_gain,
):
    n = lax.axis_size("z") * lax.axis_size("y")
    me = lax.axis_index("z") * lax.axis_size("y") + lax.axis_index("y")
    me = me.astype(jnp.int32)
    core = lax.axis_index("core").astype(jnp.int32)
    core_arg = core.reshape(1)
    seqs, rows, width = tokens.shape
    full_len = segments.shape[1]
    heads = H // n
    qw = heads * HD
    sub = joint_projection_matrix.shape[0]
    part = FF // 4
    xs, ys, zs = axis_bits("x"), axis_bits("y"), axis_bits("z")[:-1]
    chunk_bits = (2,) * len(xs + ys + zs)
    flow = Flow()

    column = jnp.arange(full_len, dtype=jnp.int32)
    starts_here = jnp.concatenate(
        [jnp.ones((seqs, 1), dtype=bool), segments[:, 1:] != segments[:, :-1]], axis=1
    )
    doc_start = lax.cummax(jnp.where(starts_here, column, 0), axis=1)
    position = lax.dynamic_slice_in_dim(column - doc_start, me * rows, rows, 1)
    doc_start = doc_start.reshape(seqs, n, rows)
    first_block = doc_start[:, :, 0] // rows
    plain_from = jnp.minimum((doc_start[:, :, -1] + rows - 1) // rows, jnp.arange(n))
    plain_from = jnp.maximum(plain_from, first_block)
    doc_start = doc_start[:, :, None, :]
    frequency = ROTARY_BASE ** (-(jnp.arange(HD // 2, dtype=f32) * 2.0) / HD)
    angles = position.astype(f32).reshape(seqs * rows, 1) * frequency
    cosine = jnp.concatenate([jnp.cos(angles)] * 4, axis=1)
    sine = jnp.concatenate([-jnp.sin(angles), jnp.sin(angles)] * 2, axis=1)

    def core_columns(weight, widths):
        mine, other, at = [], [], 0
        for w in widths:
            block = weight[:, at : at + 2 * w].reshape(sub, 2, w)
            a, b = choose(block, CORE, 1)
            mine.append(a)
            other.append(b)
            at += 2 * w
        mine = jnp.concatenate(mine, axis=1)
        arrived = swap(jnp.concatenate(other, axis=1), CORE)
        low = core == 0
        pair = [jnp.where(low, mine, arrived), jnp.where(low, arrived, mine)]
        return jnp.concatenate(pair, axis=0)

    def flat(chunks):
        return chunks.reshape(-1, chunks.shape[-1])

    def halves(chunks):
        return jnp.split(chunks, 2, axis=-1)

    qkv_widths = (H * HD // 2, KV * HD // 2, KV * HD // 2)
    qkv = flow.close(pair_rows(core_columns(joint_projection_matrix, qkv_widths), NEAR))

    qkv = flow.open(qkv)
    ffn = jnp.concatenate([gate_up_weight, down_weight_rows], axis=1).reshape(sub, 3, 2, 2, part)
    mine, other = choose(ffn, NEAR, 2)
    other = flow.open(other)
    out = pair_rows(core_columns(output_weight_rows, (H * HD // 2,)), NEAR)
    ffn = by_bit(mine, swap(other, NEAR), NEAR, 0)
    qkv, have = gather_steps(qkv, [], zs)
    order = feature_order(width, sub)
    hidden_all = dot(tokens.reshape(seqs * rows, width), order)
    gain_one = dot(attn_gain.reshape(1, width), order)
    gain_two = dot(ffn_gain.reshape(1, width), order)
    inverse_one = rms_scale(hidden_all)
    scaled_one = hidden_all * inverse_one
    normed_one = (scaled_one * gain_one).astype(bf16)
    qkv, ffn, normed_one = flow.close(qkv, ffn, normed_one)

    qkv, ffn = flow.open(qkv, ffn)
    left, right = halves(qkv)
    left, have_left = gather_steps(left, have, ys)
    right, have_right = gather_steps(right, have, xs)
    mine, other = choose(ffn, CORE, 3)
    ffn = by_bit(mine, swap(other, CORE), CORE, 1).reshape(4 * sub, 3, part)
    gate, up, down = ffn[:, 0], ffn[:, 1], ffn[:, 2]
    grad_out_all = dot(cotangent.reshape(seqs * rows, width), order)
    grad_out_low = grad_out_all.astype(bf16)
    left, right, gate, up, down, out, grad_out_low = flow.close(
        left, right, gate, up, down, out, grad_out_low
    )
    left, right, gate = flow.open(left, right, gate)
    left, _ = gather_steps(left, have_left, xs)
    right, _ = gather_steps(right, have_right, ys)
    gate, _ = gather_steps(gate, [], zs)
    w_qkv_own = jnp.concatenate([flat(left), flat(right)], axis=1)
    w_qkv_own, gate = flow.close(w_qkv_own, gate)

    w_qkv_own, gate, up, out = flow.open(w_qkv_own, gate, up, out)
    w_qkv_other = swap(w_qkv_own, CORE)
    up, _ = gather_steps(up, [], zs)
    out, _ = gather_steps(out, [], zs)
    gate, have_gate = gather_steps(gate, have, ys)
    projected = [dot(normed_one, w_qkv_own), dot(normed_one, w_qkv_other)]
    packed = pack_heads(core_arg, projected, cosine, sine, seqs, n)
    packed_0, packed_1, up, out, gate = flow.close(*packed, up, out, gate)

    def attend_one(b, qkv_b):
        return attend(first_block[b], plain_from[b], doc_start[b], qkv_b, heads)

    packed_0, up, out = flow.open(packed_0, up, out)
    out_left, out_right = halves(out)
    out_left, have_out_left = gather_steps(out_left, have, ys)
    out_right, have_out_right = gather_steps(out_right, have, xs)
    up, have_up = gather_steps(up, have, xs)
    qkv_0 = exchange(packed_0)
    qkv_0, out_left, out_right, up = flow.close(qkv_0, out_left, out_right, up)

    qkv_0, packed_1, out_left, out_right, gate, down = flow.open(
        qkv_0, packed_1, out_left, out_right, gate, down
    )
    qkv_1 = exchange(packed_1)
    out_left, _ = gather_steps(out_left, have_out_left, xs)
    out_right, _ = gather_steps(out_right, have_out_right, ys)
    gate, _ = gather_steps(gate, have_gate, xs)
    attended_0, raw_0, lse_0 = attend_one(0, qkv_0)
    w_out_own = jnp.concatenate([flat(out_left), flat(out_right)], axis=1)
    attended_0, qkv_1, w_out_own = flow.close(attended_0, qkv_1, w_out_own)

    attended_0, qkv_1, w_out_own, up = flow.open(attended_0, qkv_1, w_out_own, up)
    back_0 = exchange(attended_0)
    w_out = jnp.concatenate([w_out_own, swap(w_out_own, CORE)], axis=1)
    up, _ = gather_steps(up, have_up, ys)
    down, _ = gather_steps(down, [], zs)
    attended_1, raw_1, lse_1 = attend_one(1, qkv_1)
    attended_1, back_0, w_out, down = flow.close(attended_1, back_0, w_out, down)

    own_half = core * (n // 2)

    def after_attention(b, back):
        attended = jnp.concatenate([pick(back, s ^ own_half) for s in range(n)], axis=1)
        middle = hidden_all[b * rows : (b + 1) * rows] + dot(attended, w_out, ((1,), (1,)))
        inverse = rms_scale(middle)
        scaled = middle * inverse
        return attended, middle, inverse, scaled, (scaled * gain_two).astype(bf16)

    def tensor_group(values):
        near = swap(values, NEAR)
        return jnp.concatenate([values, swap(values, CORE), near, swap(near, CORE)], axis=0)

    def tensor_sum(partial):
        p = [partial[k * rows : (k + 1) * rows] for k in range(4)]
        near = p[2] + swap(p[3].astype(bf16), CORE).astype(f32)
        near = swap(near.astype(bf16), NEAR)
        return p[0] + swap(p[1].astype(bf16), CORE).astype(f32) + near.astype(f32)

    attended_1, back_0, down = flow.open(attended_1, back_0, down)
    back_1 = exchange(attended_1)
    attended_0, middle_0, inverse_0, scaled_0, normed_0 = after_attention(0, back_0)
    back_1, normed_0 = flow.close(back_1, normed_0)

    back_1, normed_0, down = flow.open(back_1, normed_0, down)
    group_0 = tensor_group(normed_0)
    attended_1, middle_1, inverse_1, scaled_1, normed_1 = after_attention(1, back_1)
    w_gate = flat(gate)
    group_0, normed_1, w_gate, w_up = flow.close(group_0, normed_1, w_gate, flat(up))

    def forward(group):
        gate = dot(group, w_gate)
        up = dot(group, w_up)
        sigmoid_gate = jax.nn.sigmoid(gate)
        return gate, up, (gate * sigmoid_gate * up).astype(bf16)

    def backward(grad_group, gate, up):
        sigmoid_gate = jax.nn.sigmoid(gate)
        grad_active = dot(grad_group, w_down)
        grad_gate = grad_active * up * sigmoid_gate * (1.0 + gate * (1.0 - sigmoid_gate))
        return grad_gate.astype(bf16), (grad_active * gate * sigmoid_gate).astype(bf16)

    def normed_terms(grad_gate, grad_up):
        return dot(grad_gate, w_gate, ((1,), (1,))) + dot(grad_up, w_up, ((1,), (1,)))

    group_0, normed_1, down = flow.open(group_0, normed_1, down)
    group_1 = tensor_group(normed_1)
    down, have_down = gather_steps(down, have, ys)
    gate_0, up_0, active_0 = forward(group_0)
    group_1, active_0, down = flow.close(group_1, active_0, down)

    group_1, down = flow.open(group_1, down)
    grad_low_0, grad_low_1 = flow.open(grad_out_low[:rows], grad_out_low[rows:])
    down, _ = gather_steps(down, have_down, xs)
    grad_group_0 = tensor_group(grad_low_0)
    gate_1, up_1, active_1 = forward(group_1)
    w_down = flat(down)
    w_down, active_1, grad_group_0 = flow.close(w_down, active_1, grad_group_0)

    grad_group_0 = flow.open(grad_group_0)
    grad_group_1 = tensor_group(flow.open(grad_low_1))
    grad_gate_0, grad_up_0 = backward(grad_group_0, gate_0, up_0)
    terms_0 = normed_terms(grad_gate_0, grad_up_0)
    terms_0, grad_group_1 = flow.close(terms_0, grad_group_1)

    terms_0, grad_group_1 = flow.open(terms_0, grad_group_1)
    grad_normed_0 = tensor_sum(terms_0)
    grad_gate_1, grad_up_1 = backward(grad_group_1, gate_1, up_1)
    terms_1 = normed_terms(grad_gate_1, grad_up_1)
    terms_1, grad_normed_0 = flow.close(terms_1, grad_normed_0)

    outer = lambda a, b: dot(a, b, ((0,), (0,)))

    def weight_terms(left, right):
        return outer(left, right).astype(bf16).reshape(chunk_bits + (4 * sub, part))

    def before_attention(b, g, scaled, inverse):
        grad_middle = grad_out_all[b * rows : (b + 1) * rows] + rms_back(
            g * gain_two, scaled, inverse
        )
        grad_branch = grad_middle.astype(bf16)
        grad_attended = dot(grad_branch, w_out).astype(bf16)
        grad_heads = [pick(jnp.moveaxis(grad_attended.reshape(rows, n, qw), 1, 0), s ^ own_half)
                      for s in range(n)]
        return grad_middle, grad_branch, jnp.stack(grad_heads)

    terms_1, grad_normed_0 = flow.open(terms_1, grad_normed_0)
    grad_normed_1 = tensor_sum(terms_1)
    grad_middle_0, grad_branch_0, grad_heads_0 = before_attention(
        0, grad_normed_0, scaled_0, inverse_0
    )
    grad_heads_0, grad_normed_1 = flow.close(grad_heads_0, grad_normed_1)

    grad_heads_0, grad_normed_1 = flow.open(grad_heads_0, grad_normed_1)
    grad_heads_0 = exchange(grad_heads_0)
    grad_middle_1, grad_branch_1, grad_heads_1 = before_attention(
        1, grad_normed_1, scaled_1, inverse_1
    )
    active = flow.open(jnp.concatenate([active_0, active_1], axis=0))
    grad_group = jnp.concatenate([grad_group_0, grad_group_1], axis=0)
    d_down = weight_terms(grad_group, active)
    normed_group = jnp.concatenate([group_0, group_1], axis=0)
    grad_heads_0, grad_heads_1, d_down = flow.close(grad_heads_0, grad_heads_1, d_down)

    def attend_back_one(b, qkv_b, grad_b, raw_b, lse_b):
        dq, dkv = attend_back(
            first_block[b], plain_from[b], doc_start[b], qkv_b, grad_b, raw_b, lse_b, heads
        )
        return jnp.concatenate([dq, dkv], axis=2)

    grad_heads_1, d_down = flow.open(grad_heads_1, d_down)
    grad_heads_1 = exchange(grad_heads_1)
    normed_group, grad_gate = flow.open(
        normed_group, jnp.concatenate([grad_gate_0, grad_gate_1], axis=0)
    )
    d_gate = weight_terms(normed_group, grad_gate)
    d_up = weight_terms(normed_group, jnp.concatenate([grad_up_0, grad_up_1], axis=0))
    d_down, have_d_down = scatter_steps(d_down, xs + ys + zs, ys)
    d_gate, d_up, grad_heads_1, d_down = flow.close(d_gate, d_up, grad_heads_1, d_down)

    grad_heads_0, d_gate, d_down = flow.open(grad_heads_0, d_gate, d_down)
    d_gate, have_d_gate = scatter_steps(d_gate, xs + ys + zs, xs)
    back_0 = attend_back_one(0, qkv_0, grad_heads_0, raw_0, lse_0)
    back_0, d_gate = flow.close(back_0, d_gate)

    grad_heads_1, back_0, d_up, d_down, d_gate = flow.open(grad_heads_1, back_0, d_up, d_down, d_gate)
    back_0 = exchange(back_0)
    d_up, have_d_up = scatter_steps(d_up, xs + ys + zs, ys)
    d_down, have_d_down = scatter_steps(d_down, have_d_down, xs)
    back_1 = attend_back_one(1, qkv_1, grad_heads_1, raw_1, lse_1)
    back_0, back_1, d_up, d_down = flow.close(back_0, back_1, d_up, d_down)

    back_0, back_1, d_up, d_down, d_gate, active = flow.open(
        back_0, back_1, d_up, d_down, d_gate, active
    )
    back_1 = exchange(back_1)
    d_gate, have_d_gate = scatter_steps(d_gate, have_d_gate, ys)
    d_up, have_d_up = scatter_steps(d_up, have_d_up, xs)
    d_down, _ = scatter_steps(d_down, have_d_down, zs)
    grad_proj_0 = unpack_heads(core_arg, back_0, cosine[:rows], sine[:rows])
    partial_0 = dot(active[: 4 * rows], w_down, ((1,), (1,)))
    partial_1 = dot(active[4 * rows :], w_down, ((1,), (1,)))
    back_1, grad_proj_0, d_gate, d_up, d_down, partial_0, partial_1 = flow.close(
        back_1, grad_proj_0, d_gate, d_up, d_down, partial_0, partial_1
    )

    def attention_terms(left, right):
        half = right.shape[1] // 2
        own, other = right[:, :half], right[:, half:]
        arrived = swap(outer(left, other).astype(bf16), CORE)
        total = (outer(left, own) + arrived.astype(f32)).astype(bf16)
        return total.reshape(chunk_bits + (4 * sub, half))

    def rows_back(chunk, widths):
        chunk = chunk.reshape(2, 2, sub, -1)
        mine, send = choose(chunk, NEAR, 0)
        mine = mine + swap(send.astype(bf16), NEAR).astype(f32)
        mine, send = choose(mine, CORE, 0)
        both = by_bit(mine, swap(send, CORE), CORE, 1)
        columns, at = [], 0
        for w in widths:
            columns.append(both[:, :, at : at + w].reshape(sub, 2 * w))
            at += w
        return jnp.concatenate(columns, axis=1)

    back_1, d_gate, d_up = flow.open(back_1, d_gate, d_up)
    grad_proj_1 = unpack_heads(core_arg, back_1, cosine[rows:], sine[rows:])
    grad_proj = jnp.concatenate([grad_proj_0, grad_proj_1], axis=0)
    d_qkv = attention_terms(normed_one, grad_proj)
    d_gate, _ = scatter_steps(d_gate, have_d_gate, zs)
    d_qkv, d_gate = flow.close(d_qkv, d_gate)

    d_qkv, d_up = flow.open(d_qkv, d_up)
    left, right = halves(d_qkv)
    left, have_left = scatter_steps(left, xs + ys + zs, xs)
    right, have_right = scatter_steps(right, xs + ys + zs, ys)
    d_up, _ = scatter_steps(d_up, have_d_up, zs)
    w_qkv = jnp.concatenate([w_qkv_own, w_qkv_other], axis=1)
    grad_normed_one = dot(grad_proj, w_qkv, ((1,), (1,)))
    attn_gain_grad = jnp.sum(grad_normed_one * scaled_one, axis=0)
    grad_input = jnp.concatenate([grad_middle_0, grad_middle_1], axis=0) + rms_back(
        grad_normed_one * gain_one, scaled_one, inverse_one
    )
    high = grad_input.astype(bf16)
    low = (grad_input - high.astype(f32)).astype(bf16)
    grad_input = dot(high, order, ((1,), (1,))) + dot(low, order, ((1,), (1,)))
    grad_branch = jnp.concatenate([grad_branch_0, grad_branch_1], axis=0)
    attended = jnp.concatenate([attended_0, attended_1], axis=0)
    d_out = attention_terms(grad_branch, attended)
    left, right, d_up, d_out = flow.close(left, right, d_up, d_out)

    left, right, d_out = flow.open(left, right, d_out)
    left, have_left = scatter_steps(left, have_left, ys)
    right, have_right = scatter_steps(right, have_right, xs)
    out_left, out_right = halves(d_out)
    out_left, have_out_left = scatter_steps(out_left, xs + ys + zs, xs)
    out_right, have_out_right = scatter_steps(out_right, xs + ys + zs, ys)
    middle = jnp.concatenate([tensor_sum(partial_0), tensor_sum(partial_1)], axis=0)
    result = (middle + jnp.concatenate([middle_0, middle_1], axis=0)).astype(bf16)
    result = dot(result, order, ((1,), (1,))).astype(bf16)
    left, right, out_left, out_right, result = flow.close(left, right, out_left, out_right, result)

    left, right, out_left, out_right = flow.open(left, right, out_left, out_right)
    d_qkv, _ = scatter_steps(jnp.concatenate([left, right], axis=-1), have_left, zs)
    out_left, have_out_left = scatter_steps(out_left, have_out_left, ys)
    out_right, have_out_right = scatter_steps(out_right, have_out_right, xs)
    d_qkv = rows_back(d_qkv, qkv_widths)
    d_out, _ = scatter_steps(jnp.concatenate([out_left, out_right], axis=-1), have_out_left, zs)
    d_out = rows_back(d_out, (H * HD // 2,))

    ffn = jnp.stack([d_gate, d_up, d_down], axis=1).reshape(2, 2, sub, 3, part)
    mine, send = choose(ffn, NEAR, 0)
    ffn = by_bit(mine, swap(send.astype(bf16), NEAR).astype(f32), NEAR, 3)
    mine, send = choose(ffn, CORE, 0)
    ffn = by_bit(mine, swap(send.astype(bf16), CORE).astype(f32), CORE, 3)
    ffn = ffn.reshape(sub, 3 * FF)
    ffn_gain_grad = jnp.sum(grad_normed_0 * scaled_0, axis=0) + jnp.sum(
        grad_normed_1 * scaled_1, axis=0
    )
    gains = lax.dot_general(
        jnp.stack([attn_gain_grad, ffn_gain_grad]),
        order.astype(f32),
        (((1,), (1,)), ((), ())),
        precision=lax.Precision.HIGHEST,
        preferred_element_type=f32,
    )
    gains = sum_all(gains)
    return (
        result.reshape(tokens.shape),
        grad_input.reshape(tokens.shape),
        d_qkv,
        d_out,
        ffn[:, : 2 * FF],
        ffn[:, 2 * FF :],
        gains[0],
        gains[1],
    )


def solution(mesh):
    dp, seq = mesh.devices.shape
    fine = Mesh(mesh.devices.reshape(dp // 2, 2, seq // 2, 2), ("x", "core", "z", "y"))
    by_token = P(("x", "core"), ("z", "y"), None)
    by_row = P(("x", "core", "z", "y"), None)
    return jax.shard_map(
        local,
        mesh=fine,
        in_specs=(
            by_token,
            by_token,
            P(("x", "core"), None),
            by_row,
            by_row,
            by_row,
            by_row,
            P(),
            P(),
        ),
        out_specs=(by_token, by_token, by_row, by_row, by_row, by_row, P(), P()),
        check_vma=False,
    )
```

time: 1920 us -> 1420 us (0.74)
  waiting for transfers between devices: 1070 us -> 590 us
  starting transfers between devices: 202 us -> 119 us
  matrix products: 211 us -> 293 us
    ppermute x56 -> x0, waiting for transfers between devices: 262 us -> none  [to_owners(): lax.ppermute(piece, ('z', 'y'), [(i, i ^ r) for i in range(n)])]
    ppermute x54 -> x83, waiting for transfers between devices: 807 us -> 562 us  [swap(): lax.ppermute(values, axis, [(i, i ^ 1 << b) for i in range(lax.axis_size(...]
    ppermute x56 -> x0, starting transfers between devices: 143 us -> none  [to_owners(): lax.ppermute(piece, ('z', 'y'), [(i, i ^ r) for i in range(n)])]
    dot_general x12 -> x33, matrix products: 211 us -> 286 us  [dot(): return lax.dot_general(a, b, (dims, ((), ())), preferred_element_type=f32)]
    another operation x43 -> x38, other arithmetic: 100 us -> 42.8 us  [the longest x19 25.6 us: gather_step(): return (jnp.stack([chunks, swap(chunks, key)], axis=at), have + [key])]
    concatenate x2 -> x19, other arithmetic: 2.69 us -> 54.3 us  [the longest x4 9.84 us: tensor_group(): jnp.concatenate([values, swap(values, CORE), near, swap(near, CORE)], axi...]
    all_to_all x0 -> x8, starting transfers between devices: none -> 42.9 us  [exchange(): lax.all_to_all(pieces, ('z', 'y'), split_axis=0, concat_axis=0, tiled=True)]
    dynamic_slice x7 -> x4, local copies, waits for them, and re-layouts: 37.7 us -> 5.04 us  [choose(): lax.dynamic_index_in_dim(values, bit, axis, keepdims=False)]
  transfers between devices with their start and end apart: 110 -> 91, of which waited for: 57 -> 35; matrix products, arithmetic and copies ran while one was open for 22% -> 35% of each run, Pallas kernels for 7% -> 8%
where the time goes in v2:
time: 1420 us; the launch traced here: 1410 us
  waiting for transfers between devices  590 us (42%)
  matrix products  293 us (21%)
  other arithmetic  153 us (11%)
  Pallas kernels  130 us (9%)
  local copies, waits for them, and re-layouts  123 us (9%)
  starting transfers between devices  119 us (8%)
    ppermute x83, waiting for transfers between devices, swap(): lax.ppermute(values, axis, [(i, i ^ 1 << b) for i in range(lax.axis_size(...  562 us
    dot_general x33, matrix products, dot(): return lax.dot_general(a, b, (dims, ((), ())), preferred_element_type=f32)  286 us
    ppermute x83, starting transfers between devices, swap(): lax.ppermute(values, axis, [(i, i ^ 1 << b) for i in range(lax.axis_size(...  75.9 us
    pallas_call x2, Pallas kernels, attend_back(): pl.pallas_call(functools.partial(attend_back_kernel, heads), grid=(n,), o...  66.2 us
    pallas_call x2, Pallas kernels, attend(): pl.pallas_call(functools.partial(attend_kernel, heads), grid=(n,), out_sh...  46.4 us
    all_to_all x8, starting transfers between devices, exchange(): lax.all_to_all(pieces, ('z', 'y'), split_axis=0, concat_axis=0, tiled=True)  42.9 us
    unnamed x332, local copies, waits for them, and re-layouts  33.8 us
  transfers between devices with their start and end apart: 91, of which 35 were waited for; matrix products, arithmetic and copies ran while one was open for 35% of the time, Pallas kernels for 8%

profile of v2, /device:TPU:0, one launch (start us, length us, event | category | flops | bytes accessed | tf_op | source)
XLA Modules:
  0.0 1411.8 jit_solution(15218109567798762830)
XLA Ops:
  51.3 22.8 %collective-permute-done.2 = bf16[256,1280]{1,0:T(8,128)(2,1)S(1)} collective-permute-done((bf16[256,1280]{1,0:T(8,128)(2,1)S(1)}, bf16[256,1280]{1,0:T(8,128)(2,1)S(1)}, u32[]{:S(2)}, u32[]{:S(2)}) %collective-permute-start.2) | collective-permute-done | bytes 655392 | tf_op jit(solution)/shard_map/ppermute | solution.py:46
  74.2 11.3 collective-permute-done.3
  115.5 32.6 %collective-permute-done.11 = bf16[256,1408]{1,0:T(8,128)(2,1)S(1)} collective-permute-done((bf16[256,1408]{1,0:T(8,128)(2,1)S(1)}, bf16[256,1408]{1,0:T(8,128)(2,1)S(1)}, u32[]{:S(2)}, u32[]{:S(2)}) %collective-permute-start.11) | collective-permute-done | bytes 720928 | tf_op jit(solution)/shard_map/ppermute | solution.py:46
  166.5 30.4 %collective-permute-done.14 = bf16[256,1024]{1,0:T(8,128)(2,1)S(1)} collective-permute-done((bf16[256,1024]{1,0:T(8,128)(2,1)S(1)}, bf16[256,1024]{1,0:T(8,128)(2,1)S(1)}, u32[]{:S(2)}, u32[]{:S(2)}) %collective-permute-start.14) | collective-permute-done | bytes 524320 | tf_op jit(solution)/shard_map/ppermute | solution.py:46
  198.0 14.3 %collective-permute-done.13 = bf16[256,1408]{1,0:T(8,128)(2,1)S(1)} collective-permute-done((bf16[256,1408]{1,0:T(8,128)(2,1)S(1)}, bf16[256,1408]{1,0:T(8,128)(2,1)S(1)}, u32[]{:S(2)}, u32[]{:S(2)}) %collective-permute-start.13) | collective-permute-done | bytes 720928 | tf_op jit(solution)/shard_map/ppermute | solution.py:46
  246.8 39.0 %collective-permute-done.17 = bf16[2,256,512]{2,1,0:T(8,128)(2,1)S(1)} collective-permute-done((bf16[2,256,512]{2,1,0:T(8,128)(2,1)S(1)}, bf16[2,256,512]{2,1,0:T(8,128)(2,1)S(1)}, u32[]{:S(2)}, u32[]{:S(2)}) %collective-permute-start.17) | collective-permute-done | bytes 524320 | tf_op jit(solution)/shard_map/ppermute | solution.py:46
  298.6 27.9 %attend.2 = (bf16[8,256,256]{2,1,0:T(8,128)(2,1)S(1)}, f32[8,256,256]{2,1,0:T(8,128)S(1)}, f32[8,8,1024]{2,1,0:T(8,128)S(1)}) custom-call(s32[8]{0:T(128)S(1)} %get-tuple-element.505.lo_ref, s32[8]{0:T(128)S(1)} %get-tuple-element.485.hi_ref, s32[8,1,256]{2,1,0:T(1,128)S(1)} %bitcast.489, bf16[8,256,384]{2,1,0:T(8,128)(2,1)S(1)} %all-to-all-done.qkv_ref), custom_call_target="tpu_custom_call" | custom-call | flops 8589934592 | bytes 8388608 | tf_op jit(solution)/shard_map/attend/pallas_call | solution.py:189
  326.6 9.3 collective-permute-done.20
  347.3 28.4 %collective-permute-done.22 = bf16[256,1408]{1,0:T(8,128)(2,1)S(1)} collective-permute-done((bf16[256,1408]{1,0:T(8,128)(2,1)}, bf16[256,1408]{1,0:T(8,128)(2,1)S(1)}, u32[]{:S(2)}, u32[]{:S(2)}) %collective-permute-start.22) | collective-permute-done | bytes 720928 | tf_op jit(solution)/shard_map/ppermute | solution.py:46
  383.5 18.5 %attend.3 = (bf16[8,256,256]{2,1,0:T(8,128)(2,1)S(1)}, f32[8,256,256]{2,1,0:T(8,128)S(1)}, f32[8,8,1024]{2,1,0:T(8,128)S(1)}) custom-call(s32[8]{0:T(128)S(1)} %get-tuple-element.504.lo_ref, s32[8]{0:T(128)S(1)} %get-tuple-element.486.hi_ref, s32[8,1,256]{2,1,0:T(1,128)S(1)} %bitcast.487, bf16[8,256,384]{2,1,0:T(8,128)(2,1)S(1)} %all-to-all-done.1.qkv_ref), custom_call_target="tpu_custom_call" | custom-call | flops 8589934592 | bytes 8388608 | tf_op jit(solution)/shard_map/attend/pallas_call | solution.py:189
  440.2 28.2 %all-to-all-done.3 = bf16[8,256,256]{2,1,0:T(8,128)(2,1)} async-done(((bf16[8,256,256]{2,1,0:T(8,128)(2,1)}), bf16[8,256,256]{2,1,0:T(8,128)(2,1)}, u32[]{:S(2)}, u32[]{:S(2)}) %all-to-all-start.3) | async-done | bytes 1048608 | tf_op jit(solution)/shard_map/all_to_all | solution.py:440
  511.9 14.4 %collective-permute-done.29 = bf16[256,2048]{0,1:T(8,128)(2,1)S(1)} collective-permute-done((bf16[256,2048]{0,1:T(8,128)(2,1)S(1)}, bf16[256,2048]{0,1:T(8,128)(2,1)S(1)}, u32[]{:S(2)}, u32[]{:S(2)}) %collective-permute-start.29) | collective-permute-done | bytes 1048608 | tf_op jit(solution)/shard_map/ppermute | solution.py:46
  526.3 12.2 multiply_convert_fusion.5
  551.0 15.9 %collective-permute-done.34 = bf16[256,2048]{0,1:T(8,128)(2,1)} collective-permute-done((bf16[256,2048]{0,1:T(8,128)(2,1)}, bf16[256,2048]{0,1:T(8,128)(2,1)}, u32[]{:S(2)}, u32[]{:S(2)}) %collective-permute-start.34) | collective-permute-done | bytes 1048608 | tf_op jit(solution)/shard_map/ppermute | solution.py:46
  566.9 10.2 multiply_convert_fusion.4
  587.8 19.9 %collective-permute-done.32 = bf16[2,2,256,1408]{3,2,1,0:T(8,128)(2,1)} collective-permute-done((bf16[2,2,256,1408]{3,2,1,0:T(8,128)(2,1)}, bf16[2,2,256,1408]{3,2,1,0:T(8,128)(2,1)}, u32[]{:S(2)}, u32[]{:S(2)}) %collective-permute-start.32) | collective-permute-done | bytes 2883616 | tf_op jit(solution)/shard_map/ppermute | solution.py:46
  611.8 15.2 %multiply_convert_fusion.3 = (bf16[1024,1408]{1,0:T(8,128)(2,1)}, bf16[1024,1408]{1,0:T(8,128)(2,1)}) fusion(f32[1024,1408]{1,0:T(8,128)} %fusion.182, f32[1024,1408]{1,0:T(8,128)} %get-tuple-element.498, bf16[1024,2048]{0,1:T(8,128)(2,1)S(1)} %pad_maximum_fusion.13, bf16[2048,1408]{1,0:T(8,128)(2,1)S(1)} %bitcast.512), kind=kOutput, calls=%fused_computation.51 | convolution fusion | flops 5924323328 | bytes 27262976 | tf_op jit(solution)/shard_map/dot_general | solution.py:28
  627.0 9.1 fusion.184
  636.2 8.8 convolution_add_fusion.1
  659.5 14.9 %multiply_convert_fusion = (bf16[1024,1408]{1,0:T(8,128)(2,1)}, bf16[1024,1408]{1,0:T(8,128)(2,1)}) fusion(f32[1024,1408]{1,0:T(8,128)} %copy-done.109, f32[1024,1408]{1,0:T(8,128)} %get-tuple-element.500, bf16[1024,2048]{0,1:T(8,128)(2,1)} %pad_maximum_fusion.14, bf16[2048,1408]{1,0:T(8,128)(2,1)S(1)} %bitcast.516), kind=kOutput, calls=%fused_computation.48 | convolution fusion | flops 5924323328 | bytes 27262976 | tf_op jit(solution)/shard_map/dot_general | solution.py:28
  674.3 11.6 fusion.185
  688.2 10.6 convolution_add_fusion
  703.5 9.7 collective-permute-done.41
  731.5 24.4 %collective-permute-done.44 = bf16[256,2048]{0,1:T(8,128)(2,1)S(1)} collective-permute-done((bf16[256,2048]{0,1:T(8,128)(2,1)S(1)}, bf16[256,2048]{0,1:T(8,128)(2,1)S(1)}, u32[]{:S(2)}, u32[]{:S(2)}) %collective-permute-start.44) | collective-permute-done | bytes 1048608 | tf_op jit(solution)/shard_map/ppermute | solution.py:46
  784.1 14.9 %fusion.27 = bf16[2048,1408]{1,0:T(8,128)(2,1)} fusion(bf16[2048,1408]{1,0:T(8,128)(2,1)S(1)} %bitcast.521, bf16[1024,2048]{0,1:T(8,128)(2,1)S(1)} %copy-done.65, bf16[1024,2048]{0,1:T(8,128)(2,1)S(1)} %copy-done.64), kind=kOutput, calls=%fused_computation.31 | convolution fusion | flops 11830820864 | bytes 19922944 | tf_op jit(solution)/shard_map/dot_general | solution.py:28
  809.7 19.2 %convolution_convert_fusion.2 = bf16[2048,1408]{1,0:T(8,128)(2,1)} fusion(bf16[2048,2048]{0,1:T(8,128)(2,1)} %pad_maximum_fusion.1, bf16[2048,1408]{1,0:T(8,128)(2,1)} %pad_maximum_fusion.5), kind=kOutput, calls=%fused_computation.33 | convolution fusion | flops 11814043648 | bytes 19922944 | tf_op jit(solution)/shard_map/dot_general | solution.py:28
  828.9 17.2 %convolution_convert_fusion.1 = bf16[2048,1408]{1,0:T(8,128)(2,1)} fusion(bf16[2048,2048]{0,1:T(8,128)(2,1)S(1)} %bitcast.507, bf16[1024,1408]{1,0:T(8,128)(2,1)} %get-tuple-element.397, bf16[1024,1408]{1,0:T(8,128)(2,1)S(1)} %copy-done.110), kind=kOutput, calls=%fused_computation.32 | convolution fusion | flops 11825577984 | bytes 19922944 | tf_op jit(solution)/shard_map/dot_general | solution.py:28
  846.1 33.9 %collective-permute-done.45 = bf16[2,2,256,1408]{3,2,1,0:T(8,128)(2,1)S(1)} collective-permute-done((bf16[2,2,256,1408]{3,2,1,0:T(8,128)(2,1)S(1)}, bf16[2,2,256,1408]{3,2,1,0:T(8,128)(2,1)S(1)}, u32[]{:S(2)}, u32[]{:S(2)}) %collective-permute-start.45) | collective-permute-done | bytes 2883616 | tf_op jit(solution)/shard_map/ppermute | solution.py:46
  893.4 38.6 %attend_back.2 = (bf16[8,256,256]{2,1,0:T(8,128)(2,1)S(1)}, bf16[8,256,128]{2,1,0:T(8,128)(2,1)S(1)}) custom-call(s32[8]{0:T(128)S(1)} %copy-done.20, s32[8]{0:T(128)S(1)} %copy-done.18, s32[8,1,256]{2,1,0:T(1,128)S(1)} %bitcast.490, bf16[8,256,384]{2,1,0:T(8,128)(2,1)S(1)} %all-to-all-done.qkv_ref, bf16[8,256,256]{2,1,0:T(8,128)(2,1)} %all-to-all-done.4.g_ref, ...), custom_call_target="tpu_custom_call" | custom-call | flops 15032385536 | bytes 8388608 | tf_op jit(solution)/shard_map/attend_back/pallas_call | solution.py:299
  933.3 16.3 %collective-permute-done.46 = bf16[2,2,256,1408]{3,2,1,0:T(8,128)(2,1)} collective-permute-done((bf16[2,2,256,1408]{3,2,1,0:T(8,128)(2,1)}, bf16[2,2,256,1408]{3,2,1,0:T(8,128)(2,1)}, u32[]{:S(2)}, u32[]{:S(2)}) %collective-permute-start.46) | collective-permute-done | bytes 2883616 | tf_op jit(solution)/shard_map/ppermute | solution.py:46
  973.5 27.6 %attend_back.3 = (bf16[8,256,256]{2,1,0:T(8,128)(2,1)S(1)}, bf16[8,256,128]{2,1,0:T(8,128)(2,1)S(1)}) custom-call(s32[8]{0:T(128)S(1)} %copy-done.16, s32[8]{0:T(128)S(1)} %copy-done.14, s32[8,1,256]{2,1,0:T(1,128)S(1)} %bitcast.488, bf16[8,256,384]{2,1,0:T(8,128)(2,1)S(1)} %all-to-all-done.1.qkv_ref, bf16[8,256,256]{2,1,0:T(8,128)(2,1)} %all-to-all-done.5.g_ref, ...), custom_call_target="tpu_custom_call" | custom-call | flops 15032385536 | bytes 8388608 | tf_op jit(solution)/shard_map/attend_back/pallas_call | solution.py:299
  1006.5 27.1 %collective-permute-done.47 = bf16[2,2,256,1408]{3,2,1,0:T(8,128)(2,1)} collective-permute-done((bf16[2,2,256,1408]{3,2,1,0:T(8,128)(2,1)}, bf16[2,2,256,1408]{3,2,1,0:T(8,128)(2,1)}, u32[]{:S(2)}, u32[]{:S(2)}) %collective-permute-start.47) | collective-permute-done | bytes 2883616 | tf_op jit(solution)/shard_map/ppermute | solution.py:46
  1053.2 11.8 fusion.48
  1065.0 9.0 fusion.50
  1075.2 33.4 %collective-permute-done.51 = bf16[256,1408]{1,0:T(8,128)(2,1)S(1)} collective-permute-done((bf16[256,1408]{1,0:T(8,128)(2,1)S(1)}, bf16[256,1408]{1,0:T(8,128)(2,1)S(1)}, u32[]{:S(2)}, u32[]{:S(2)}) %collective-permute-start.51) | collective-permute-done | bytes 720928 | tf_op jit(solution)/shard_map/ppermute | solution.py:46
  1114.9 11.3 multiply_reduce_fusion
  1149.5 9.3 copy.188
  1165.6 9.6 copy.191
  1186.1 8.7 fusion.43
  1201.5 22.3 %collective-permute-done.64 = bf16[256,2048]{0,1:T(8,128)(2,1)S(1)} collective-permute-done((bf16[256,2048]{0,1:T(8,128)(2,1)S(1)}, bf16[256,2048]{0,1:T(8,128)(2,1)S(1)}, u32[]{:S(2)}, u32[]{:S(2)}) %collective-permute-start.64) | collective-permute-done | bytes 1048608 | tf_op jit(solution)/shard_map/ppermute | solution.py:46
  1224.2 21.1 %collective-permute-done.67 = bf16[256,2048]{0,1:T(8,128)(2,1)S(1)} collective-permute-done((bf16[256,2048]{0,1:T(8,128)(2,1)S(1)}, bf16[256,2048]{0,1:T(8,128)(2,1)S(1)}, u32[]{:S(2)}, u32[]{:S(2)}) %collective-permute-start.67) | collective-permute-done | bytes 1048608 | tf_op jit(solution)/shard_map/ppermute | solution.py:46
  1260.9 24.9 %collective-permute-done.56 = bf16[256,1408]{1,0:T(8,128)(2,1)S(1)} collective-permute-done((bf16[256,1408]{1,0:T(8,128)(2,1)S(1)}, bf16[256,1408]{1,0:T(8,128)(2,1)S(1)}, u32[]{:S(2)}, u32[]{:S(2)}) %collective-permute-start.56) | collective-permute-done | bytes 720928 | tf_op jit(solution)/shard_map/ppermute | solution.py:46
  1293.2 12.9 collective-permute-done.59
  1307.0 20.6 %collective-permute-done.60 = bf16[2,2,256,512]{3,2,1,0:T(8,128)(2,1)S(1)} collective-permute-done((bf16[2,2,256,512]{3,2,1,0:T(8,128)(2,1)S(1)}, bf16[2,2,256,512]{3,2,1,0:T(8,128)(2,1)S(1)}, u32[]{:S(2)}, u32[]{:S(2)}) %collective-permute-start.60) | collective-permute-done | bytes 1048608 | tf_op jit(solution)/shard_map/ppermute | solution.py:46
  1332.2 9.3 collective-permute-done.72
  1341.6 19.0 %collective-permute-done.68 = bf16[256,1280]{1,0:T(8,128)(2,1)S(1)} collective-permute-done((bf16[256,1280]{1,0:T(8,128)(2,1)S(1)}, bf16[256,1280]{1,0:T(8,128)(2,1)S(1)}, u32[]{:S(2)}, u32[]{:S(2)}) %collective-permute-start.68) | collective-permute-done | bytes 655392 | tf_op jit(solution)/shard_map/ppermute | solution.py:46
  1363.6 12.9 collective-permute-done.69
  1376.7 10.5 collective-permute-done.73
  (717 shorter events, 527.3 us)
Async XLA Ops:
  9.2 39.9 %collective-permute-start.7 = (bf16[64,1024]{1,0:T(8,128)(2,1)}, bf16[64,1024]{1,0:T(8,128)(2,1)}, u32[]{:S(2)}, u32[]{:S(2)}) collective-permute-start(bf16[64,1024]{1,0:T(8,128)(2,1)} %bitcast.474), channel_id=1, source_target_pairs={{0,8},{8,0},{1,9},{9,1},{2,10},{10,2},{3,11},{11,3},{4,12},{12,4},... | collective-permute-start | bytes 393224 | tf_op jit(solution)/shard_map/ppermute | solution.py:46
  45.7 39.9 %collective-permute-start.3 = (bf16[64,3,2,1408]{3,0,2,1:T(8,128)(2,1)S(1)}, bf16[64,3,2,1408]{3,0,2,1:T(8,128)(2,1)S(1)}, u32[]{:S(2)}, u32[]{:S(2)}) collective-permute-start(bf16[64,3,2,1408]{3,0,2,1:T(8,128)(2,1)S(1)} %bitcast.587), channel_id=1, source_target_pairs={{0,2},{2,0},{4,6},{6,4},{1,3},{3,1},{5,7},{7,5},{8,10},{10,8},{12,... | collective-permute-start | bytes 3244040 | tf_op jit(solution)/shard_map/ppermute | solution.py:46
  50.8 47.6 %collective-permute-start.8 = (bf16[128,1024]{1,0:T(8,128)(2,1)}, bf16[128,1024]{1,0:T(8,128)(2,1)}, u32[]{:S(2)}, u32[]{:S(2)}) collective-permute-start(bf16[128,1024]{1,0:T(8,128)(2,1)} %pad_maximum_fusion.51), channel_id=1, source_target_pairs={{0,2},{2,0},{4,6},{6,4},{1,3},{3,1},{5,7},{7,5},{8,10},{10,8},{12,... | collective-permute-start | bytes 786440 | tf_op jit(solution)/shard_map/ppermute | solution.py:46
  111.6 36.6 %collective-permute-start.10 = (bf16[2,2,256,640]{3,2,1,0:T(8,128)(2,1)S(1)}, bf16[2,2,256,640]{3,2,1,0:T(8,128)(2,1)S(1)}, u32[]{:S(2)}, u32[]{:S(2)}) collective-permute-start(bf16[2,2,256,640]{3,2,1,0:T(8,128)(2,1)S(1)} %pad_maximum_fusion.39), channel_id=1, source_target_pairs={{0,1},{1,0},{2,3},{3,2},{4,5},{5,4},{6,7},{7,6},{8,9},{9,8},{10,11... | collective-permute-start | bytes 3932168 | tf_op jit(solution)/shard_map/ppermute | solution.py:46
  113.0 35.7 %collective-permute-start.9 = (bf16[2,2,256,640]{3,2,1,0:T(8,128)(2,1)S(1)}, bf16[2,2,256,640]{3,2,1,0:T(8,128)(2,1)S(1)}, u32[]{:S(2)}, u32[]{:S(2)}) collective-permute-start(bf16[2,2,256,640]{3,2,1,0:T(8,128)(2,1)S(1)} %pad_maximum_fusion.38), channel_id=1, source_target_pairs={{0,16},{16,0},{1,17},{17,1},{2,18},{18,2},{3,19},{19,3},{4,20},{20... | collective-permute-start | bytes 3932168 | tf_op jit(solution)/shard_map/ppermute | solution.py:46
  114.5 33.6 %collective-permute-start.11 = (bf16[256,1408]{1,0:T(8,128)(2,1)S(1)}, bf16[256,1408]{1,0:T(8,128)(2,1)S(1)}, u32[]{:S(2)}, u32[]{:S(2)}) collective-permute-start(bf16[256,1408]{1,0:T(8,128)(2,1)S(1)} %get-tuple-element.215), channel_id=1, source_target_pairs={{0,4},{2,6},{4,0},{6,2},{1,5},{3,7},{5,1},{7,3},{8,12},{10,14},{12... | collective-permute-start | bytes 2162696 | tf_op jit(solution)/shard_map/ppermute | solution.py:46
  151.8 62.5 %collective-permute-start.12 = (bf16[2048,1280]{1,0:T(8,128)(2,1)}, bf16[2048,1280]{1,0:T(8,128)(2,1)}, u32[]{:S(2)}, u32[]{:S(2)}) collective-permute-start(bf16[2048,1280]{1,0:T(8,128)(2,1)} %pad_maximum_fusion.7), channel_id=1, source_target_pairs={{0,8},{8,0},{1,9},{9,1},{2,10},{10,2},{3,11},{11,3},{4,12},{12,4},... | collective-permute-start | bytes 15728648 | tf_op jit(solution)/shard_map/ppermute | solution.py:46
  153.1 59.3 %collective-permute-start.15 = (bf16[2,256,1408]{2,1,0:T(8,128)(2,1)S(1)}, bf16[2,256,1408]{2,1,0:T(8,128)(2,1)S(1)}, u32[]{:S(2)}, u32[]{:S(2)}) collective-permute-start(bf16[2,256,1408]{2,1,0:T(8,128)(2,1)S(1)} %pad_maximum_fusion.30), channel_id=1, source_target_pairs={{0,1},{1,0},{2,3},{3,2},{4,5},{5,4},{6,7},{7,6},{8,9},{9,8},{10,11... | collective-permute-start | bytes 4325384 | tf_op jit(solution)/shard_map/ppermute | solution.py:46
  155.9 41.0 %collective-permute-start.14 = (bf16[256,1024]{1,0:T(8,128)(2,1)S(1)}, bf16[256,1024]{1,0:T(8,128)(2,1)S(1)}, u32[]{:S(2)}, u32[]{:S(2)}) collective-permute-start(bf16[256,1024]{1,0:T(8,128)(2,1)S(1)} %copy-done.82), channel_id=1, source_target_pairs={{0,4},{2,6},{4,0},{6,2},{1,5},{3,7},{5,1},{7,3},{8,12},{10,14},{12... | collective-permute-start | bytes 1572872 | tf_op jit(solution)/shard_map/ppermute | solution.py:46
  155.9 56.3 %collective-permute-start.13 = (bf16[256,1408]{1,0:T(8,128)(2,1)S(1)}, bf16[256,1408]{1,0:T(8,128)(2,1)S(1)}, u32[]{:S(2)}, u32[]{:S(2)}) collective-permute-start(bf16[256,1408]{1,0:T(8,128)(2,1)S(1)} %get-tuple-element.222), channel_id=1, source_target_pairs={{0,4},{2,6},{4,0},{6,2},{1,5},{3,7},{5,1},{7,3},{8,12},{10,14},{12... | collective-permute-start | bytes 2162696 | tf_op jit(solution)/shard_map/ppermute | solution.py:46
  236.9 52.9 %all-to-all-start = ((bf16[8,256,384]{2,1,0:T(8,128)(2,1)}), bf16[8,256,384]{2,1,0:T(8,128)(2,1)S(1)}, u32[]{:S(2)}, u32[]{:S(2)}) async-start(bf16[8,256,384]{2,1,0:T(8,128)(2,1)} %bitcast.511), calls=%async_computation | async-start | bytes 3145728 | tf_op jit(solution)/shard_map/all_to_all | solution.py:440
  241.2 46.7 %collective-permute-start.18 = (bf16[2,256,1408]{2,1,0:T(8,128)(2,1)S(1)}, bf16[2,256,1408]{2,1,0:T(8,128)(2,1)S(1)}, u32[]{:S(2)}, u32[]{:S(2)}) collective-permute-start(bf16[2,256,1408]{2,1,0:T(8,128)(2,1)S(1)} %pad_maximum_fusion.31), channel_id=1, source_target_pairs={{0,16},{16,0},{1,17},{17,1},{2,18},{18,2},{3,19},{19,3},{4,20},{20... | collective-permute-start | bytes 4325384 | tf_op jit(solution)/shard_map/ppermute | solution.py:46
  243.2 42.6 %collective-permute-start.17 = (bf16[2,256,512]{2,1,0:T(8,128)(2,1)S(1)}, bf16[2,256,512]{2,1,0:T(8,128)(2,1)S(1)}, u32[]{:S(2)}, u32[]{:S(2)}) collective-permute-start(bf16[2,256,512]{2,1,0:T(8,128)(2,1)S(1)} %get-tuple-element.446), channel_id=1, source_target_pairs={{0,16},{16,0},{1,17},{17,1},{2,18},{18,2},{3,19},{19,3},{4,20},{20... | collective-permute-start | bytes 1572872 | tf_op jit(solution)/shard_map/ppermute | solution.py:46
  244.8 42.1 %collective-permute-start.16 = (bf16[2,256,512]{2,1,0:T(8,128)(2,1)S(1)}, bf16[2,256,512]{2,1,0:T(8,128)(2,1)S(1)}, u32[]{:S(2)}, u32[]{:S(2)}) collective-permute-start(bf16[2,256,512]{2,1,0:T(8,128)(2,1)S(1)} %get-tuple-element.447), channel_id=1, source_target_pairs={{0,1},{1,0},{2,3},{3,2},{4,5},{5,4},{6,7},{7,6},{8,9},{9,8},{10,11... | collective-permute-start | bytes 1572872 | tf_op jit(solution)/shard_map/ppermute | solution.py:46
  289.8 50.4 %all-to-all-start.1 = ((bf16[8,256,384]{2,1,0:T(8,128)(2,1)}), bf16[8,256,384]{2,1,0:T(8,128)(2,1)S(1)}, u32[]{:S(2)}, u32[]{:S(2)}) async-start(bf16[8,256,384]{2,1,0:T(8,128)(2,1)} %bitcast.510), calls=%async_computation.1 | async-start | bytes 3145728 | tf_op jit(solution)/shard_map/all_to_all | solution.py:440
  295.8 40.1 %collective-permute-start.20 = (bf16[2,2,256,512]{3,2,1,0:T(8,128)(2,1)}, bf16[2,2,256,512]{3,2,1,0:T(8,128)(2,1)S(1)}, u32[]{:S(2)}, u32[]{:S(2)}) collective-permute-start(bf16[2,2,256,512]{3,2,1,0:T(8,128)(2,1)} %pad_maximum_fusion.44), channel_id=1, source_target_pairs={{0,1},{1,0},{2,3},{3,2},{4,5},{5,4},{6,7},{7,6},{8,9},{9,8},{10,11... | collective-permute-start | bytes 3145736 | tf_op jit(solution)/shard_map/ppermute | solution.py:46
  297.9 38.3 %collective-permute-start.19 = (bf16[2,2,256,512]{3,2,1,0:T(8,128)(2,1)}, bf16[2,2,256,512]{3,2,1,0:T(8,128)(2,1)S(1)}, u32[]{:S(2)}, u32[]{:S(2)}) collective-permute-start(bf16[2,2,256,512]{3,2,1,0:T(8,128)(2,1)} %pad_maximum_fusion.43), channel_id=1, source_target_pairs={{0,16},{16,0},{1,17},{17,1},{2,18},{18,2},{3,19},{19,3},{4,20},{20... | collective-permute-start | bytes 3145736 | tf_op jit(solution)/shard_map/ppermute | solution.py:46
  340.2 70.2 %collective-permute-start.21 = (bf16[2048,1024]{1,0:T(8,128)(2,1)}, bf16[2048,1024]{1,0:T(8,128)(2,1)}, u32[]{:S(2)}, u32[]{:S(2)}) collective-permute-start(bf16[2048,1024]{1,0:T(8,128)(2,1)} %pad_maximum_fusion.10), channel_id=1, source_target_pairs={{0,8},{8,0},{1,9},{9,1},{2,10},{10,2},{3,11},{11,3},{4,12},{12,4},... | collective-permute-start | bytes 12582920 | tf_op jit(solution)/shard_map/ppermute | solution.py:46
  340.2 65.2 %collective-permute-start.26 = (bf16[2,2,256,1408]{3,2,1,0:T(8,128)(2,1)}, bf16[2,2,256,1408]{3,2,1,0:T(8,128)(2,1)}, u32[]{:S(2)}, u32[]{:S(2)}) collective-permute-start(bf16[2,2,256,1408]{3,2,1,0:T(8,128)(2,1)} %pad_maximum_fusion.16), channel_id=1, source_target_pairs={{0,16},{16,0},{1,17},{17,1},{2,18},{18,2},{3,19},{19,3},{4,20},{20... | collective-permute-start | bytes 8650760 | tf_op jit(solution)/shard_map/ppermute | solution.py:46
  340.8 34.9 %collective-permute-start.22 = (bf16[256,1408]{1,0:T(8,128)(2,1)}, bf16[256,1408]{1,0:T(8,128)(2,1)S(1)}, u32[]{:S(2)}, u32[]{:S(2)}) collective-permute-start(bf16[256,1408]{1,0:T(8,128)(2,1)} %get-tuple-element.253), channel_id=1, source_target_pairs={{0,4},{2,6},{4,0},{6,2},{1,5},{3,7},{5,1},{7,3},{8,12},{10,14},{12... | collective-permute-start | bytes 2162696 | tf_op jit(solution)/shard_map/ppermute | solution.py:46
  376.9 41.6 %all-to-all-start.2 = ((bf16[8,256,256]{2,1,0:T(8,128)(2,1)}), bf16[8,256,256]{2,1,0:T(8,128)(2,1)}, u32[]{:S(2)}, u32[]{:S(2)}) async-start(bf16[8,256,256]{2,1,0:T(8,128)(2,1)} %copy-done.6), calls=%async_computation.2 | async-start | bytes 2097152 | tf_op jit(solution)/shard_map/all_to_all | solution.py:440
  381.5 88.4 %collective-permute-start.27 = (bf16[2,2,256,1408]{3,2,1,0:T(8,128)(2,1)}, bf16[2,2,256,1408]{3,2,1,0:T(8,128)(2,1)}, u32[]{:S(2)}, u32[]{:S(2)}) collective-permute-start(bf16[2,2,256,1408]{3,2,1,0:T(8,128)(2,1)} %pad_maximum_fusion.17), channel_id=1, source_target_pairs={{0,1},{1,0},{2,3},{3,2},{4,5},{5,4},{6,7},{7,6},{8,9},{9,8},{10,11... | collective-permute-start | bytes 8650760 | tf_op jit(solution)/shard_map/ppermute | solution.py:46
  418.5 49.9 %all-to-all-start.3 = ((bf16[8,256,256]{2,1,0:T(8,128)(2,1)}), bf16[8,256,256]{2,1,0:T(8,128)(2,1)}, u32[]{:S(2)}, u32[]{:S(2)}) async-start(bf16[8,256,256]{2,1,0:T(8,128)(2,1)} %copy-done.7), calls=%async_computation.3 | async-start | bytes 2097152 | tf_op jit(solution)/shard_map/all_to_all | solution.py:440
  502.2 38.2 %collective-permute-start.28 = (bf16[256,2048]{0,1:T(8,128)(2,1)S(1)}, bf16[256,2048]{0,1:T(8,128)(2,1)S(1)}, u32[]{:S(2)}, u32[]{:S(2)}) collective-permute-start(bf16[256,2048]{0,1:T(8,128)(2,1)S(1)} %multiply_convert_fusion.7), channel_id=1, source_target_pairs={{0,8},{8,0},{1,9},{9,1},{2,10},{10,2},{3,11},{11,3},{4,12},{12,4},... | collective-permute-start | bytes 3145736 | tf_op jit(solution)/shard_map/ppermute | solution.py:46
  502.4 36.1 %collective-permute-start.31 = (bf16[2,256,1408]{2,1,0:T(8,128)(2,1)S(1)}, bf16[2,256,1408]{2,1,0:T(8,128)(2,1)S(1)}, u32[]{:S(2)}, u32[]{:S(2)}) collective-permute-start(bf16[2,256,1408]{2,1,0:T(8,128)(2,1)S(1)} %copy-done.58), channel_id=1, source_target_pairs={{0,1},{1,0},{2,3},{3,2},{4,5},{5,4},{6,7},{7,6},{8,9},{9,8},{10,11... | collective-permute-start | bytes 4325384 | tf_op jit(solution)/shard_map/ppermute | solution.py:46
  542.5 42.8 %collective-permute-start.33 = (bf16[256,2048]{0,1:T(8,128)(2,1)}, bf16[256,2048]{0,1:T(8,128)(2,1)}, u32[]{:S(2)}, u32[]{:S(2)}) collective-permute-start(bf16[256,2048]{0,1:T(8,128)(2,1)} %get-tuple-element.284), channel_id=1, source_target_pairs={{0,8},{8,0},{1,9},{9,1},{2,10},{10,2},{3,11},{11,3},{4,12},{12,4},... | collective-permute-start | bytes 3145736 | tf_op jit(solution)/shard_map/ppermute | solution.py:46
  542.7 65.0 %collective-permute-start.32 = (bf16[2,2,256,1408]{3,2,1,0:T(8,128)(2,1)}, bf16[2,2,256,1408]{3,2,1,0:T(8,128)(2,1)}, u32[]{:S(2)}, u32[]{:S(2)}) collective-permute-start(bf16[2,2,256,1408]{3,2,1,0:T(8,128)(2,1)} %pad_maximum_fusion.18), channel_id=1, source_target_pairs={{0,16},{16,0},{1,17},{17,1},{2,18},{18,2},{3,19},{19,3},{4,20},{20... | collective-permute-start | bytes 8650760 | tf_op jit(solution)/shard_map/ppermute | solution.py:46
  611.8 41.8 %collective-permute-start.36 = (bf16[256,2048]{0,1:T(8,128)(2,1)S(1)}, bf16[256,2048]{0,1:T(8,128)(2,1)S(1)}, u32[]{:S(2)}, u32[]{:S(2)}) collective-permute-start(bf16[256,2048]{0,1:T(8,128)(2,1)S(1)} %copy-done.71), channel_id=1, source_target_pairs={{0,8},{8,0},{1,9},{9,1},{2,10},{10,2},{3,11},{11,3},{4,12},{12,4},... | collective-permute-start | bytes 3145736 | tf_op jit(solution)/shard_map/ppermute | solution.py:46
  658.9 44.6 %collective-permute-start.39 = (bf16[256,2048]{0,1:T(8,128)(2,1)}, bf16[256,2048]{0,1:T(8,128)(2,1)S(1)}, u32[]{:S(2)}, u32[]{:S(2)}) collective-permute-start(bf16[256,2048]{0,1:T(8,128)(2,1)} %get-tuple-element.411), channel_id=1, source_target_pairs={{0,8},{8,0},{1,9},{9,1},{2,10},{10,2},{3,11},{11,3},{4,12},{12,4},... | collective-permute-start | bytes 3145736 | tf_op jit(solution)/shard_map/ppermute | solution.py:46
  757.7 41.4 %all-to-all-start.4 = ((bf16[8,256,256]{2,1,0:T(8,128)(2,1)}), bf16[8,256,256]{2,1,0:T(8,128)(2,1)}, u32[]{:S(2)}, u32[]{:S(2)}) async-start(bf16[8,256,256]{2,1,0:T(8,128)(2,1)} %copy-done.83), calls=%async_computation.4 | async-start | bytes 2097152 | tf_op jit(solution)/shard_map/all_to_all | solution.py:440
  799.1 83.2 %all-to-all-start.5 = ((bf16[8,256,256]{2,1,0:T(8,128)(2,1)}), bf16[8,256,256]{2,1,0:T(8,128)(2,1)}, u32[]{:S(2)}, u32[]{:S(2)}) async-start(bf16[8,256,256]{2,1,0:T(8,128)(2,1)} %fusion.98), calls=%async_computation.5 | async-start | bytes 2097152 | tf_op jit(solution)/shard_map/all_to_all | solution.py:440
  807.6 72.4 %collective-permute-start.45 = (bf16[2,2,256,1408]{3,2,1,0:T(8,128)(2,1)S(1)}, bf16[2,2,256,1408]{3,2,1,0:T(8,128)(2,1)S(1)}, u32[]{:S(2)}, u32[]{:S(2)}) collective-permute-start(bf16[2,2,256,1408]{3,2,1,0:T(8,128)(2,1)S(1)} %slice_bitcast_fusion.4), channel_id=1, source_target_pairs={{0,1},{1,0},{2,3},{3,2},{4,5},{5,4},{6,7},{7,6},{8,9},{9,8},{10,11... | collective-permute-start | bytes 8650760 | tf_op jit(solution)/shard_map/ppermute | solution.py:46
  886.2 63.4 %collective-permute-start.46 = (bf16[2,2,256,1408]{3,2,1,0:T(8,128)(2,1)}, bf16[2,2,256,1408]{3,2,1,0:T(8,128)(2,1)}, u32[]{:S(2)}, u32[]{:S(2)}) collective-permute-start(bf16[2,2,256,1408]{3,2,1,0:T(8,128)(2,1)} %slice_bitcast_fusion.3), channel_id=1, source_target_pairs={{0,16},{16,0},{1,17},{17,1},{2,18},{18,2},{3,19},{19,3},{4,20},{20... | collective-permute-start | bytes 8650760 | tf_op jit(solution)/shard_map/ppermute | solution.py:46
  892.1 65.0 %collective-permute-start.57 = (bf16[2048,1024]{1,0:T(8,128)(2,1)}, bf16[2048,1024]{1,0:T(8,128)(2,1)}, u32[]{:S(2)}, u32[]{:S(2)}) collective-permute-start(bf16[2048,1024]{1,0:T(8,128)(2,1)} %convolution_convert_fusion.3), channel_id=1, source_target_pairs={{0,8},{8,0},{1,9},{9,1},{2,10},{10,2},{3,11},{11,3},{4,12},{12,4},... | collective-permute-start | bytes 12582920 | tf_op jit(solution)/shard_map/ppermute | solution.py:46
  956.4 77.2 %collective-permute-start.47 = (bf16[2,2,256,1408]{3,2,1,0:T(8,128)(2,1)}, bf16[2,2,256,1408]{3,2,1,0:T(8,128)(2,1)}, u32[]{:S(2)}, u32[]{:S(2)}) collective-permute-start(bf16[2,2,256,1408]{3,2,1,0:T(8,128)(2,1)} %slice_bitcast_fusion.2), channel_id=1, source_target_pairs={{0,1},{1,0},{2,3},{3,2},{4,5},{5,4},{6,7},{7,6},{8,9},{9,8},{10,11... | collective-permute-start | bytes 8650760 | tf_op jit(solution)/shard_map/ppermute | solution.py:46
  963.6 74.1 %all-to-all-start.6 = ((bf16[8,256,384]{2,1,0:T(8,128)(2,1)}), bf16[8,256,384]{2,1,0:T(8,128)(2,1)S(1)}, u32[]{:S(2)}, u32[]{:S(2)}) async-start(bf16[8,256,384]{2,1,0:T(8,128)(2,1)} %pad_maximum_fusion.28), calls=%async_computation.6 | async-start | bytes 3145728 | tf_op jit(solution)/shard_map/all_to_all | solution.py:440
  1037.7 76.0 %all-to-all-start.7 = ((bf16[8,256,384]{2,1,0:T(8,128)(2,1)}), bf16[8,256,384]{2,1,0:T(8,128)(2,1)S(1)}, u32[]{:S(2)}, u32[]{:S(2)}) async-start(bf16[8,256,384]{2,1,0:T(8,128)(2,1)} %pad_maximum_fusion.29), calls=%async_computation.7 | async-start | bytes 3145728 | tf_op jit(solution)/shard_map/all_to_all | solution.py:440
  1045.5 63.0 %collective-permute-start.51 = (bf16[256,1408]{1,0:T(8,128)(2,1)S(1)}, bf16[256,1408]{1,0:T(8,128)(2,1)S(1)}, u32[]{:S(2)}, u32[]{:S(2)}) collective-permute-start(bf16[256,1408]{1,0:T(8,128)(2,1)S(1)} %slice_bitcast_fusion.19), channel_id=1, source_target_pairs={{0,4},{2,6},{4,0},{6,2},{1,5},{3,7},{5,1},{7,3},{8,12},{10,14},{12... | collective-permute-start | bytes 2162696 | tf_op jit(solution)/shard_map/ppermute | solution.py:46
  1050.1 59.6 %collective-permute-start.50 = (bf16[2,256,1408]{2,1,0:T(8,128)(2,1)S(1)}, bf16[2,256,1408]{2,1,0:T(8,128)(2,1)S(1)}, u32[]{:S(2)}, u32[]{:S(2)}) collective-permute-start(bf16[2,256,1408]{2,1,0:T(8,128)(2,1)S(1)} %slice_bitcast_fusion.5), channel_id=1, source_target_pairs={{0,16},{16,0},{1,17},{17,1},{2,18},{18,2},{3,19},{19,3},{4,20},{20... | collective-permute-start | bytes 4325384 | tf_op jit(solution)/shard_map/ppermute | solution.py:46
  1051.7 59.5 %collective-permute-start.49 = (bf16[2,256,1408]{2,1,0:T(8,128)(2,1)S(1)}, bf16[2,256,1408]{2,1,0:T(8,128)(2,1)S(1)}, u32[]{:S(2)}, u32[]{:S(2)}) collective-permute-start(bf16[2,256,1408]{2,1,0:T(8,128)(2,1)S(1)} %slice_bitcast_fusion.6), channel_id=1, source_target_pairs={{0,1},{1,0},{2,3},{3,2},{4,5},{5,4},{6,7},{7,6},{8,9},{9,8},{10,11... | collective-permute-start | bytes 4325384 | tf_op jit(solution)/shard_map/ppermute | solution.py:46
  1133.8 64.4 %collective-permute-start.53 = (bf16[256,1408]{1,0:T(8,128)(2,1)S(1)}, bf16[256,1408]{1,0:T(8,128)(2,1)}, u32[]{:S(2)}, u32[]{:S(2)}) collective-permute-start(bf16[256,1408]{1,0:T(8,128)(2,1)S(1)} %slice_bitcast_fusion.18), channel_id=1, source_target_pairs={{0,4},{2,6},{4,0},{6,2},{1,5},{3,7},{5,1},{7,3},{8,12},{10,14},{12... | collective-permute-start | bytes 2162696 | tf_op jit(solution)/shard_map/ppermute | solution.py:46
  1149.2 96.5 %collective-permute-start.52 = (bf16[2048,1280]{1,0:T(8,128)(2,1)}, bf16[2048,1280]{1,0:T(8,128)(2,1)}, u32[]{:S(2)}, u32[]{:S(2)}) collective-permute-start(bf16[2048,1280]{1,0:T(8,128)(2,1)} %convolution_convert_fusion), channel_id=1, source_target_pairs={{0,8},{8,0},{1,9},{9,1},{2,10},{10,2},{3,11},{11,3},{4,12},{12,4},... | collective-permute-start | bytes 15728648 | tf_op jit(solution)/shard_map/ppermute | solution.py:46
  1198.2 47.1 %collective-permute-start.67 = (bf16[256,2048]{0,1:T(8,128)(2,1)S(1)}, bf16[256,2048]{0,1:T(8,128)(2,1)S(1)}, u32[]{:S(2)}, u32[]{:S(2)}) collective-permute-start(bf16[256,2048]{0,1:T(8,128)(2,1)S(1)} %fusion.63), channel_id=1, source_target_pairs={{0,2},{2,0},{4,6},{6,4},{1,3},{3,1},{5,7},{7,5},{8,10},{10,8},{12,... | collective-permute-start | bytes 3145736 | tf_op jit(solution)/shard_map/ppermute | solution.py:46
  1252.1 33.6 %collective-permute-start.56 = (bf16[256,1408]{1,0:T(8,128)(2,1)S(1)}, bf16[256,1408]{1,0:T(8,128)(2,1)S(1)}, u32[]{:S(2)}, u32[]{:S(2)}) collective-permute-start(bf16[256,1408]{1,0:T(8,128)(2,1)S(1)} %slice_bitcast_fusion.17), channel_id=1, source_target_pairs={{0,4},{2,6},{4,0},{6,2},{1,5},{3,7},{5,1},{7,3},{8,12},{10,14},{12... | collective-permute-start | bytes 2162696 | tf_op jit(solution)/shard_map/ppermute | solution.py:46
  1290.3 37.3 %collective-permute-start.60 = (bf16[2,2,256,512]{3,2,1,0:T(8,128)(2,1)S(1)}, bf16[2,2,256,512]{3,2,1,0:T(8,128)(2,1)S(1)}, u32[]{:S(2)}, u32[]{:S(2)}) collective-permute-start(bf16[2,2,256,512]{3,2,1,0:T(8,128)(2,1)S(1)} %slice_bitcast_fusion.13), channel_id=1, source_target_pairs={{0,16},{16,0},{1,17},{17,1},{2,18},{18,2},{3,19},{19,3},{4,20},{20... | collective-permute-start | bytes 3145736 | tf_op jit(solution)/shard_map/ppermute | solution.py:46
  1291.8 36.2 %collective-permute-start.61 = (bf16[2,2,256,512]{3,2,1,0:T(8,128)(2,1)S(1)}, bf16[2,2,256,512]{3,2,1,0:T(8,128)(2,1)S(1)}, u32[]{:S(2)}, u32[]{:S(2)}) collective-permute-start(bf16[2,2,256,512]{3,2,1,0:T(8,128)(2,1)S(1)} %slice_bitcast_fusion.12), channel_id=1, source_target_pairs={{0,1},{1,0},{2,3},{3,2},{4,5},{5,4},{6,7},{7,6},{8,9},{9,8},{10,11... | collective-permute-start | bytes 3145736 | tf_op jit(solution)/shard_map/ppermute | solution.py:46
  1293.2 38.3 %collective-permute-start.76 = (bf16[2,64,3,1408]{3,1,2,0:T(8,128)(2,1)S(1)}, bf16[2,64,3,1408]{3,1,2,0:T(8,128)(2,1)S(1)}, u32[]{:S(2)}, u32[]{:S(2)}) collective-permute-start(bf16[2,64,3,1408]{3,1,2,0:T(8,128)(2,1)S(1)} %fusion.79), channel_id=1, source_target_pairs={{0,2},{2,0},{4,6},{6,4},{1,3},{3,1},{5,7},{7,5},{8,10},{10,8},{12,... | collective-permute-start | bytes 3244040 | tf_op jit(solution)/shard_map/ppermute | solution.py:46
  1332.1 55.4 %collective-permute-start.77 = (bf16[64,3,2,1408]{3,0,2,1:T(8,128)(2,1)S(1)}, bf16[64,3,2,1408]{3,0,2,1:T(8,128)(2,1)S(1)}, u32[]{:S(2)}, u32[]{:S(2)}) collective-permute-start(bf16[64,3,2,1408]{3,0,2,1:T(8,128)(2,1)S(1)} %fusion.80), channel_id=1, source_target_pairs={{0,8},{8,0},{1,9},{9,1},{2,10},{10,2},{3,11},{11,3},{4,12},{12,4},... | collective-permute-start | bytes 3244040 | tf_op jit(solution)/shard_map/ppermute | solution.py:46
  (184 other events, 3193.6 us)

commit v3 on v1

v3 whole, which is shorter than its diff:
```python
import functools
import math

import jax
import jax.numpy as jnp
from jax import lax
from jax.experimental import pallas as pl
from jax.experimental.pallas import tpu as pltpu
from jax.sharding import Mesh
from jax.sharding import PartitionSpec as P

H = 32
HD = 64
KV = 4
FF = 5632

EPSILON = 1e-05
NEG = -1e30
ROTARY_BASE = 10000.0
LOG2E = math.log2(math.e)
LANES = 128

bf16 = jnp.bfloat16
f32 = jnp.float32


def dot(a, b, dims=((1,), (0,))):
    return lax.dot_general(a, b, (dims, ((), ())), preferred_element_type=f32)


CORE = ("core", 0)
NEAR = ("near", 0)
SEQ = ("far", "near", "y")


def axis_bits(axis):
    return [(axis, b) for b in reversed(range((lax.axis_size(axis) - 1).bit_length()))]


def my_bit(key):
    axis, b = key
    return (lax.axis_index(axis) >> b) & 1


def swap(values, key):
    axis, b = key
    return lax.ppermute(values, axis, [(i, i ^ (1 << b)) for i in range(lax.axis_size(axis))])


class Flow:
    def __init__(self):
        self.token = jnp.zeros((), f32)

    def open(self, *values):
        opened = lax.optimization_barrier(values + (self.token,))[:-1]
        return opened if len(values) > 1 else opened[0]

    def close(self, *values, wait=()):
        arrived = tuple(transfer.arrived for transfer in wait)
        closed = lax.optimization_barrier(values + arrived + (self.token,))
        for transfer, value in zip(wait, closed[len(values) :]):
            transfer.arrived = value
        self.token = closed[-1]
        return closed[: len(values)] if len(values) > 1 else closed[0]


def choose(values, key, axis):
    bit = my_bit(key)
    return (
        lax.dynamic_index_in_dim(values, bit, axis, keepdims=False),
        lax.dynamic_index_in_dim(values, 1 - bit, axis, keepdims=False),
    )


def by_bit(mine, other, key, axis):
    low = my_bit(key) == 0
    return jnp.stack([jnp.where(low, mine, other), jnp.where(low, other, mine)], axis=axis)


class Swap:
    def __init__(self, values, key):
        self.arrived = swap(values, key)


class Gather:
    def __init__(self, values, axis, at):
        self.values, self.axis, self.at = values, axis, at
        self.arrived = swap(values, axis_bits(axis)[0])

    def done(self):
        values, other, shape = self.values, self.arrived, self.values.shape
        for step, key in enumerate(axis_bits(self.axis)):
            if step:
                other = swap(values, key)
            values = by_bit(values, other, key, self.at + step)
        return values.reshape(shape[: self.at] + (lax.axis_size(self.axis),) + shape[self.at :])


class Scatter:
    def __init__(self, values, axis, at):
        self.keys, self.at = axis_bits(axis), at
        shape = values.shape
        values = values.reshape(shape[:at] + (2,) * len(self.keys) + shape[at + 1 :])
        self.start(values)

    def start(self, values):
        self.mine, send = choose(values, self.keys[0], self.at)
        self.arrived = swap(send.astype(bf16), self.keys[0])

    def done(self, last=False):
        while True:
            values = self.mine.astype(f32) + self.arrived.astype(f32)
            if not last:
                values = values.astype(bf16)
            self.keys = self.keys[1:]
            if not self.keys:
                return values
            self.start(values)


def sum_axes(values, *axes):
    for axis in axes:
        for key in axis_bits(axis):
            values = values + swap(values, key)
    return values


def stack_heads(x, heads):
    return jnp.concatenate([x[:, h * HD : (h + 1) * HD] for h in range(heads)], axis=0)


def unstack_heads(x, heads):
    rows = x.shape[0] // heads
    return jnp.concatenate([x[h * rows : (h + 1) * rows] for h in range(heads)], axis=1)


def block_allowed(i, j, rows, start):
    key_pos = j * rows + lax.broadcasted_iota(jnp.int32, (rows, rows), 0)
    query_pos = i * rows + lax.broadcasted_iota(jnp.int32, (rows, rows), 1)
    return (key_pos <= query_pos) & (key_pos >= start)


def attend_kernel(
    heads, lo_ref, hi_ref, start_ref, qkv_ref, out_ref, raw_ref, lse_ref, m_s, l_s, acc_s
):
    rows = qkv_ref.shape[1]
    qw = heads * HD
    scale = LOG2E * HD**-0.5
    i = pl.program_id(0)
    q = stack_heads(qkv_ref[i, :, :qw], heads)
    m_s[...] = jnp.full_like(m_s, NEG)
    l_s[...] = jnp.zeros_like(l_s)
    acc_s[...] = jnp.zeros_like(acc_s)

    def block(j, masked):
        k = qkv_ref[j, :, qw : qw + HD]
        v = qkv_ref[j, :, qw + HD : qw + 2 * HD]
        s = dot(k, q, ((1,), (1,)))
        if masked:
            ok = block_allowed(i, j, rows, start_ref[0])
            s = jnp.where(jnp.concatenate([ok] * heads, axis=1), s, NEG)
        m_old = m_s[...]
        m_new = jnp.maximum(m_old, jnp.max(s, axis=0, keepdims=True) * scale)
        p = jnp.exp2(s * scale - m_new)
        keep = jnp.exp2(m_old - m_new)
        l_s[...] = l_s[...] * keep + jnp.sum(p, axis=0, keepdims=True)
        acc_s[...] = acc_s[...] * keep + dot(v, p.astype(bf16), ((0,), (0,)))
        m_s[...] = m_new

    def masked_step(j, carry):
        block(j, True)
        return carry

    def plain_step(j, carry):
        block(j, False)
        return carry

    block(i, True)
    lax.fori_loop(lo_ref[i], hi_ref[i], masked_step, 0)
    lax.fori_loop(hi_ref[i], i, plain_step, 0)
    total = l_s[...]
    result = unstack_heads(jnp.transpose(acc_s[...] / total), heads)
    raw_ref[0] = result
    out_ref[0] = result.astype(bf16)
    lse_ref[0] = jnp.broadcast_to(m_s[...] + jnp.log2(total), (8, heads * rows))


def attend(lo, hi, start, qkv, heads):
    n, rows, w = qkv.shape
    qw = heads * HD
    smem = pl.BlockSpec(memory_space=pltpu.SMEM)
    pairs = heads * (n * rows) ** 2 // 2
    per_block = lambda shape: pl.BlockSpec((1,) + shape, lambda i: (i, 0, 0))
    return pl.pallas_call(
        functools.partial(attend_kernel, heads),
        grid=(n,),
        out_shape=(
            jax.ShapeDtypeStruct((n, rows, qw), bf16),
            jax.ShapeDtypeStruct((n, rows, qw), f32),
            jax.ShapeDtypeStruct((n, 8, heads * rows), f32),
        ),
        in_specs=[
            smem,
            smem,
            per_block((1, rows)),
            pl.BlockSpec((n, rows, w), lambda i: (0, 0, 0)),
        ],
        out_specs=(per_block((rows, qw)), per_block((rows, qw)), per_block((8, heads * rows))),
        scratch_shapes=[
            pltpu.VMEM((1, heads * rows), f32),
            pltpu.VMEM((1, heads * rows), f32),
            pltpu.VMEM((HD, heads * rows), f32),
        ],
        compiler_params=pltpu.CompilerParams(vmem_limit_bytes=48 << 20),
        cost_estimate=pl.CostEstimate(flops=0, bytes_accessed=1 << 20, transcendentals=0),
        name="attend",
    )(lo, hi, start, qkv)


def attend_back_kernel(
    heads,
    lo_ref,
    hi_ref,
    start_ref,
    qkv_ref,
    g_ref,
    raw_ref,
    lse_ref,
    dq_ref,
    dkv_ref,
    dkv_s,
    dq_s,
):
    n, rows, _ = qkv_ref.shape
    qw = heads * HD
    scale = LOG2E * HD**-0.5
    i = pl.program_id(0)

    @pl.when(i == 0)
    def _():
        dkv_s[...] = jnp.zeros_like(dkv_s)

    dq_s[...] = jnp.zeros_like(dq_s)
    q = stack_heads(qkv_ref[i, :, :qw], heads)
    g_flat = g_ref[i]
    g = stack_heads(g_flat, heads)
    product = g_flat.astype(f32) * raw_ref[0]
    inner = jnp.concatenate(
        [
            jnp.sum(product[:, h * HD : (h + 1) * HD], axis=1, keepdims=True)
            for h in range(heads)
        ],
        axis=0,
    )
    inner = jnp.transpose(jnp.broadcast_to(inner, (heads * rows, LANES)))[:1]
    lse = lse_ref[0, :1]

    def block(j, masked):
        k = qkv_ref[j, :, qw : qw + HD]
        v = qkv_ref[j, :, qw + HD : qw + 2 * HD]
        s = dot(k, q, ((1,), (1,)))
        grad_probs = dot(v, g, ((1,), (1,)))
        p = jnp.exp2(s * scale - lse)
        if masked:
            ok = block_allowed(i, j, rows, start_ref[0])
            p = jnp.where(jnp.concatenate([ok] * heads, axis=1), p, 0.0)
        grad_scores = (p * (grad_probs - inner)).astype(bf16)
        dkv_s[j, :, :HD] += dot(grad_scores, q)
        dkv_s[j, :, HD:] += dot(p.astype(bf16), g)
        dq_s[...] += dot(k, grad_scores, ((0,), (0,)))

    def masked_step(j, carry):
        block(j, True)
        return carry

    def plain_step(j, carry):
        block(j, False)
        return carry

    lax.fori_loop(lo_ref[i], hi_ref[i], masked_step, 0)
    lax.fori_loop(hi_ref[i], i, plain_step, 0)
    block(i, True)
    dq = unstack_heads(jnp.transpose(dq_s[...] * HD**-0.5), heads)
    dq_ref[0] = dq.astype(bf16)

    @pl.when(i == n - 1)
    def _():
        for r in range(n):
            done = dkv_s[r]
            dkv_ref[r] = jnp.concatenate([done[:, :HD] * HD**-0.5, done[:, HD:]], axis=1).astype(
                bf16
            )


def attend_back(lo, hi, start, qkv, grad, raw, lse, heads):
    n, rows, w = qkv.shape
    qw = heads * HD
    smem = pl.BlockSpec(memory_space=pltpu.SMEM)
    pairs = heads * (n * rows) ** 2 // 2
    per_block = lambda shape: pl.BlockSpec((1,) + shape, lambda i: (i, 0, 0))
    whole = lambda shape: pl.BlockSpec(shape, lambda i: (0, 0, 0))
    return pl.pallas_call(
        functools.partial(attend_back_kernel, heads),
        grid=(n,),
        out_shape=(
            jax.ShapeDtypeStruct((n, rows, qw), bf16),
            jax.ShapeDtypeStruct((n, rows, 2 * HD), bf16),
        ),
        in_specs=[
            smem,
            smem,
            per_block((1, rows)),
            whole((n, rows, w)),
            whole((n, rows, qw)),
            per_block((rows, qw)),
            per_block((8, heads * rows)),
        ],
        out_specs=(per_block((rows, qw)), whole((n, rows, 2 * HD))),
        scratch_shapes=[
            pltpu.VMEM((n, rows, 2 * HD), f32),
            pltpu.VMEM((HD, heads * rows), f32),
        ],
        compiler_params=pltpu.CompilerParams(vmem_limit_bytes=48 << 20),
        cost_estimate=pl.CostEstimate(flops=0, bytes_accessed=1 << 20, transcendentals=0),
        name="attend_back",
    )(lo, hi, start, qkv, grad, raw, lse)


def rotate_lanes(v, cosine, signed_sine):
    parts = []
    for c in range(v.shape[1] // LANES):
        part = v[:, c * LANES : (c + 1) * LANES]
        lane = lax.broadcasted_iota(jnp.int32, part.shape, 1)
        other = jnp.where(
            lane % HD < HD // 2,
            pltpu.roll(part, LANES - HD // 2, 1),
            pltpu.roll(part, HD // 2, 1),
        )
        parts.append(part * cosine + other * signed_sine)
    return jnp.concatenate(parts, axis=1) if len(parts) > 1 else parts[0]


def pack_kernel(copies, q_ref, k_ref, v_ref, cos_ref, sin_ref, out_ref):
    qw = q_ref.shape[1]
    cosine = cos_ref[...]
    sine = sin_ref[...]
    out_ref[0, :, :qw] = rotate_lanes(q_ref[...], cosine, sine).astype(bf16)
    k = rotate_lanes(k_ref[...], cosine, sine)
    v = v_ref[...]
    first = (pl.program_id(0) // copies) % 2 == 0
    lane = lax.broadcasted_iota(jnp.int32, k.shape, 1)
    k = jnp.where(first, k, pltpu.roll(k, HD, 1))
    v = jnp.where(first, pltpu.roll(v, HD, 1), v)
    out_ref[0, :, qw:] = jnp.where(lane < HD, k, v).astype(bf16)


def pack_heads(projected, cosine, sine, seq, rows, n):
    qw = H * HD // n
    copies = n // KV
    k_at = H * HD // LANES
    v_at = k_at + KV * HD // LANES
    table = pl.BlockSpec((rows, LANES), lambda d: (seq, 0))
    return pl.pallas_call(
        functools.partial(pack_kernel, copies),
        grid=(n,),
        in_specs=[
            pl.BlockSpec((rows, qw), lambda d: (seq, d)),
            pl.BlockSpec((rows, LANES), lambda d: (seq, k_at + d // copies // 2)),
            pl.BlockSpec((rows, LANES), lambda d: (seq, v_at + d // copies // 2)),
            table,
            table,
        ],
        out_specs=pl.BlockSpec((1, rows, qw + 2 * HD), lambda d: (d, 0, 0)),
        out_shape=jax.ShapeDtypeStruct((n, rows, qw + 2 * HD), bf16),
        cost_estimate=pl.CostEstimate(flops=0, bytes_accessed=6 << 20, transcendentals=0),
        name="pack_heads",
    )(projected, projected, projected, cosine, sine)


def unpack_kernel(n, in_ref, cos_ref, sin_ref, out_ref):
    qw = in_ref.shape[2] - 2 * HD
    copies = n // KV
    cosine = cos_ref[...]
    sine = -sin_ref[...]
    lane = lax.broadcasted_iota(jnp.int32, cosine.shape, 1)
    for d in range(n):
        part = in_ref[d, :, :qw].astype(f32)
        out_ref[:, d * qw : (d + 1) * qw] = rotate_lanes(part, cosine, sine).astype(bf16)
    for pair in range(KV // 2):
        sums = []
        for head in (2 * pair, 2 * pair + 1):
            slots = [in_ref[head * copies + c, :, qw:].astype(f32) for c in range(copies)]
            sums.append(sum(slots[1:], slots[0]))
        k = jnp.where(lane < HD, sums[0], pltpu.roll(sums[1], HD, 1))
        v = jnp.where(lane < HD, pltpu.roll(sums[0], HD, 1), sums[1])
        k_at = H * HD + pair * LANES
        v_at = k_at + KV * HD
        out_ref[:, k_at : k_at + LANES] = rotate_lanes(k, cosine, sine).astype(bf16)
        out_ref[:, v_at : v_at + LANES] = v.astype(bf16)


def unpack_heads(pieces, cosine, sine):
    n, rows, w = pieces.shape
    cols = H * HD + 2 * KV * HD
    return pl.pallas_call(
        functools.partial(unpack_kernel, n),
        out_shape=jax.ShapeDtypeStruct((rows, cols), bf16),
        in_specs=[pl.BlockSpec(memory_space=pltpu.VMEM)] * 3,
        out_specs=pl.BlockSpec(memory_space=pltpu.VMEM),
        compiler_params=pltpu.CompilerParams(vmem_limit_bytes=32 << 20),
        cost_estimate=pl.CostEstimate(flops=0, bytes_accessed=4 << 20, transcendentals=0),
        name="unpack_heads",
    )(pieces, cosine, sine)


def interleave_kernel(core_ref, own_ref, other_ref, out_ref):
    del core_ref
    for i, ref in enumerate((own_ref, other_ref)):

        @pl.when(pl.program_id(2) == i)
        def _():
            out_ref[0, 0, 0] = ref[0, :, 0]


def interleave(core, own, other):
    nx, ny, inner, sub, cols = own.shape
    spec = pl.BlockSpec((1, ny, 1, sub, cols), lambda x, k, i, core_ref: (x, 0, k, 0, 0))
    return pl.pallas_call(
        interleave_kernel,
        grid_spec=pltpu.PrefetchScalarGridSpec(
            num_scalar_prefetch=1,
            grid=(nx, inner, 2),
            in_specs=[spec, spec],
            out_specs=pl.BlockSpec(
                (1, 1, 1, ny, sub, cols), lambda x, k, i, core_ref: (x, core_ref[0] ^ i, k, 0, 0, 0)
            ),
        ),
        out_shape=jax.ShapeDtypeStruct((nx, 2, inner, ny, sub, cols), own.dtype),
        compiler_params=pltpu.CompilerParams(vmem_limit_bytes=48 << 20),
        cost_estimate=pl.CostEstimate(flops=0, bytes_accessed=1 << 16, transcendentals=0),
        name="interleave",
    )(core, own, other)


ROW_TILE = 256


def small_cost(size):
    return pl.CostEstimate(flops=0, bytes_accessed=size, transcendentals=0)


def resident(shape, index):
    return pl.BlockSpec(shape, lambda i: index, pipeline_mode=pl.Buffered(1))


def by_rows(tile, cols, at=0):
    return pl.BlockSpec((tile, cols), lambda i: (i, at))


def load_rows(w_ref, w_s, sems):
    xy, _, nfar, _, sub, _ = w_ref.shape
    ny = 2
    copies = []
    for g in range(xy):
        for core in range(2):
            for far in range(nfar):
                for near in range(2):
                    block = (((g // ny * 2 + core) * nfar + far) * 2 + near) * ny + g % ny
                    copies.append(
                        pltpu.make_async_copy(
                            w_ref.at[g, core, far, near],
                            w_s.at[pl.ds(block * sub, sub)],
                            sems.at[block],
                        )
                    )
    for copy in copies:
        copy.start()
    for copy in copies:
        copy.wait()


def with_weights(kernel):
    def run(x_ref, w_ref, *refs):
        *refs, w_s, sems = refs

        @pl.when(pl.program_id(0) == 0)
        def _():
            load_rows(w_ref, w_s, sems)

        kernel(x_ref, w_s, *refs)

    return run


def over_rows(kernel, x, w, others, outs, name):
    m = x.shape[0]
    blocks = w.shape[0] * w.shape[1] * w.shape[2] * w.shape[3]
    tile = min(ROW_TILE, m)
    return pl.pallas_call(
        with_weights(kernel),
        grid=(m // tile,),
        in_specs=[by_rows(tile, x.shape[1]), pl.BlockSpec(memory_space=pl.ANY)]
        + [by_rows(tile, other.shape[1]) for other in others],
        out_specs=[by_rows(tile, cols) for cols, _ in outs],
        out_shape=[jax.ShapeDtypeStruct((m, cols), t) for cols, t in outs],
        scratch_shapes=[
            pltpu.VMEM((blocks * w.shape[4], w.shape[5]), bf16),
            pltpu.SemaphoreType.DMA((blocks,)),
        ],
        compiler_params=pltpu.CompilerParams(vmem_limit_bytes=48 << 20),
        cost_estimate=small_cost(1 << 16),
        name=name,
    )(x, w, *others)


def ffn_forward_kernel(x_ref, w_ref, gate_ref, up_ref, active_ref):
    units = gate_ref.shape[1]
    x = x_ref[...]
    gate = dot(x, w_ref[:, :units])
    gate_ref[...] = gate
    up = dot(x, w_ref[:, units:])
    up_ref[...] = up
    active_ref[...] = (gate * jax.nn.sigmoid(gate) * up).astype(bf16)


def ffn_forward(x, w_gate_up):
    units = w_gate_up.shape[-1] // 2
    outs = [(units, f32), (units, f32), (units, bf16)]
    return over_rows(ffn_forward_kernel, x, w_gate_up, [], outs, "ffn_forward")


def ffn_backward_kernel(g_ref, w_ref, gate_ref, up_ref, both_ref):
    units = gate_ref.shape[1]
    grad_active = dot(g_ref[...], w_ref[...])
    gate = gate_ref[...]
    s = jax.nn.sigmoid(gate)
    grad_gate = grad_active * up_ref[...] * s * (1.0 + gate * (1.0 - s))
    both_ref[:, :units] = grad_gate.astype(bf16)
    both_ref[:, units:] = (grad_active * gate * s).astype(bf16)


def ffn_backward(grad, w_down, gate, up):
    outs = [(2 * gate.shape[1], bf16)]
    return over_rows(ffn_backward_kernel, grad, w_down, [gate, up], outs, "ffn_backward")[0]


def project_rows_kernel(x_ref, w_ref, out_ref):
    out_ref[...] = dot(x_ref[...], w_ref[...], ((1,), (1,))).astype(bf16)


def project_rows(x, w):
    rows = w.shape[0] * w.shape[1] * w.shape[2] * w.shape[3] * w.shape[4]
    return over_rows(project_rows_kernel, x, w, [], [(rows, bf16)], "project_rows")[0]


def outer_sum_kernel(pairs, *refs):
    out_ref = refs[-1]
    _, ny, _, nfar, _, sub, _ = out_ref.shape
    total = None
    for p in range(pairs):
        term = dot(refs[2 * p][...], refs[2 * p + 1][...], ((0,), (0,)))
        total = term if total is None else total + term
    for far in range(nfar):
        for near in range(2):
            for y in range(ny):
                at = ((far * 2 + near) * ny + y) * sub
                out_ref[0, y, 0, far, near] = total[at : at + sub].astype(bf16)


def outer_sum(pairs, cols, at, owners):
    nx, nfar, ny = owners
    width = pairs[0][0].shape[1]
    tile = width // (2 * nx)
    sub = tile // (2 * nfar * ny)
    in_specs, operands = [], []
    for a, b in pairs:
        in_specs.append(pl.BlockSpec((a.shape[0], tile), lambda i: (0, i)))
        in_specs.append(resident((b.shape[0], cols), (0, at)))
        operands += [a, b]
    return pl.pallas_call(
        functools.partial(outer_sum_kernel, len(pairs)),
        grid=(2 * nx,),
        in_specs=in_specs,
        out_specs=pl.BlockSpec(
            (1, ny, 1, nfar, 2, sub, cols), lambda i: (i // 2, 0, i % 2, 0, 0, 0, 0)
        ),
        out_shape=jax.ShapeDtypeStruct((nx, ny, 2, nfar, 2, sub, cols), bf16),
        compiler_params=pltpu.CompilerParams(vmem_limit_bytes=48 << 20),
        cost_estimate=small_cost(1 << 16),
        name="outer_sum",
    )(*operands)


def rms_scale(hidden):
    return lax.rsqrt(jnp.mean(hidden * hidden, axis=-1, keepdims=True) + EPSILON)


def rms_back(grad_scaled, scaled, inverse):
    return inverse * (grad_scaled - scaled * jnp.mean(grad_scaled * scaled, axis=-1, keepdims=True))


def exchange(pieces):
    return lax.all_to_all(pieces, SEQ, split_axis=0, concat_axis=0, tiled=True)


def local(
    tokens,
    cotangent,
    segments,
    joint_projection_matrix,
    output_weight_rows,
    gate_up_weight,
    down_weight_rows,
    attn_gain,
    ffn_gain,
):
    n = lax.axis_size(SEQ)
    me = lax.axis_index(SEQ)
    seqs, rows, width = tokens.shape
    full_len = segments.shape[1]
    heads = H // n
    qw = heads * HD
    sub = joint_projection_matrix.shape[0]
    part = FF // 4
    nx, nfar, ny = (lax.axis_size(axis) for axis in ("x", "far", "y"))
    flow = Flow()

    column = jnp.arange(full_len, dtype=jnp.int32)
    starts_here = jnp.concatenate(
        [jnp.ones((seqs, 1), dtype=bool), segments[:, 1:] != segments[:, :-1]], axis=1
    )
    doc_start = lax.cummax(jnp.where(starts_here, column, 0), axis=1)
    position = lax.dynamic_slice_in_dim(column - doc_start, me * rows, rows, 1)
    doc_start = doc_start.reshape(seqs, n, rows)
    first_block = doc_start[:, :, 0] // rows
    plain_from = jnp.minimum((doc_start[:, :, -1] + rows - 1) // rows, jnp.arange(n))
    plain_from = jnp.maximum(plain_from, first_block)
    doc_start = doc_start[:, :, None, :]
    frequency = ROTARY_BASE ** (-(jnp.arange(HD // 2, dtype=f32) * 2.0) / HD)
    angles = position.astype(f32).reshape(seqs * rows, 1) * frequency
    cosine = jnp.concatenate([jnp.cos(angles)] * 4, axis=1)
    sine = jnp.concatenate([-jnp.sin(angles), jnp.sin(angles)] * 2, axis=1)

    hidden_all = tokens.reshape(seqs * rows, width).astype(f32)
    grad_out_all = cotangent.reshape(seqs * rows, width)
    gain_one = attn_gain.astype(f32)
    gain_two = ffn_gain.astype(f32)

    def own_rows(weight):
        gathered = lax.all_gather(weight, ("x",) + SEQ, axis=0, tiled=True)
        return gathered.reshape(nx, -1, weight.shape[1])

    def core_features(values):
        w = width // (2 * nx)
        bit = my_bit(CORE)
        return tuple(
            jnp.concatenate(
                [lax.dynamic_slice_in_dim(values, (2 * i + c) * w, w, 1) for i in range(nx)], axis=1
            )
            for c in (bit, 1 - bit)
        )

    def flat(values):
        return values.reshape(-1, values.shape[-1])

    def lane_halves(values, key):
        w = values.shape[-1] // 2
        bit = my_bit(key)
        return (
            lax.dynamic_slice_in_dim(values, bit * w, w, values.ndim - 1),
            lax.dynamic_slice_in_dim(values, (1 - bit) * w, w, values.ndim - 1),
        )

    def lanes_by_bit(mine, other, key):
        low = my_bit(key) == 0
        return [jnp.where(low, mine, other), jnp.where(low, other, mine)]

    class Group:
        def __init__(self, values):
            self.values, self.core = values, swap(values, CORE)
            self.arrived = swap(values, NEAR)

        def done(self):
            near = self.arrived
            return jnp.concatenate([self.values, self.core, near, swap(near, CORE)], axis=0)

    class GroupSum:
        def __init__(self, partial):
            self.mine = partial.reshape(2, 2, rows, -1)
            self.arrived = swap(self.mine[:, 1], CORE)

        def next(self):
            both = self.mine[:, 0].astype(f32) + self.arrived.astype(f32)
            self.mine = both[0]
            self.arrived = swap(both[1].astype(bf16), NEAR)

        def done(self):
            return self.mine + self.arrived.astype(f32)

    qkv = Gather(joint_projection_matrix, "near", 0)
    out = Gather(output_weight_rows, "far", 0)
    flow.close(flow.token, wait=[qkv])

    qkv = Gather(qkv.done(), "far", 0)
    near_parts, near_swaps = [], []
    for weight in (gate_up_weight[:, :FF], gate_up_weight[:, FF:], down_weight_rows):
        mine, other = lane_halves(weight, NEAR)
        near_parts.append(mine)
        near_swaps.append(other)
    near_swap = Swap(flow.open(jnp.stack(near_swaps)), NEAR)
    inverse_one = rms_scale(hidden_all)
    scaled_one = hidden_all * inverse_one
    normed_one = (scaled_one * gain_one).astype(bf16)
    normed_one_own, normed_one_other = core_features(normed_one)
    normed_one_own, normed_one_other, cosine, sine = flow.close(
        normed_one_own, normed_one_other, cosine, sine, wait=[qkv, near_swap, out]
    )

    left, right = jnp.split(qkv.done(), 2, axis=-1)
    left = Gather(left, "y", 2)
    right = Gather(right, "x", 0)
    core_parts, core_swaps = [], []
    for mine, arrived in zip(near_parts, near_swap.arrived):
        mine, other = lane_halves(by_bit(mine, arrived, NEAR, 0), CORE)
        core_parts.append(mine)
        core_swaps.append(other)
    core_swap = Swap(jnp.stack(core_swaps), CORE)
    out = Gather(out.done(), "near", 1)
    flow.close(flow.token, wait=[left, right, core_swap, out])

    def over_xy(values):
        gathered = lax.all_gather(flat(values), ("x", "y"), axis=0, tiled=True)
        return gathered.reshape((nx * ny,) + values.shape)

    left = Gather(left.done(), "x", 0)
    right = Gather(right.done(), "y", 3)
    gate, up, down = (
        by_bit(mine, arrived, CORE, 0) for mine, arrived in zip(core_parts, core_swap.arrived)
    )
    gate = Gather(gate, "far", 1)
    w_out_own = over_xy(out.done())
    up, down = flow.close(up, down, wait=[left, right, gate])

    w_own = jnp.concatenate([flat(left.done()), flat(right.done())], axis=1)
    w_swap = Swap(w_own, CORE)
    up = Gather(up, "far", 1)
    projected = dot(normed_one_own, w_own)
    w_other = w_swap.arrived
    projected = projected + dot(normed_one_other, w_other)
    packed_0 = pack_heads(projected, cosine, sine, 0, rows, n)
    packed_0 = flow.close(packed_0, wait=[up])

    def attend_one(b, qkv_b):
        return attend(first_block[b], plain_from[b], doc_start[b], qkv_b, heads)

    packed_0, projected, w_other = flow.open(packed_0, projected, w_other)
    qkv_0 = exchange(packed_0)
    w_gate_up = over_xy(jnp.concatenate([gate.done(), up.done()], axis=-1))
    packed_1 = pack_heads(projected, cosine, sine, 1, rows, n)
    core_arg = lax.axis_index("core").astype(jnp.int32).reshape(1)
    w_shape = (nx, 1, nfar * 2, -1, w_own.shape[1])
    w_qkv = flat(interleave(core_arg, w_own.reshape(w_shape), w_other.reshape(w_shape)))
    qkv_0, packed_1, w_qkv = flow.close(qkv_0, packed_1, w_qkv)

    qkv_0, packed_1 = flow.open(qkv_0, packed_1)
    qkv_1 = exchange(packed_1)
    attended_0, raw_0, lse_0 = attend_one(0, qkv_0)
    attended_0, qkv_1, w_out_own = flow.close(attended_0, qkv_1, w_out_own)

    attended_0, qkv_1 = flow.open(attended_0, qkv_1)
    back_0 = exchange(attended_0)
    out_swap = Swap(w_out_own, CORE)
    attended_1, raw_1, lse_1 = attend_one(1, qkv_1)
    attended_1, back_0 = flow.close(attended_1, back_0, wait=[out_swap])

    def after_attention(b, back):
        attended = jnp.concatenate([back[s] for s in range(n)], axis=1)
        middle = hidden_all[b * rows : (b + 1) * rows] + dot(attended, w_out, ((1,), (1,)))
        inverse = rms_scale(middle)
        scaled = middle * inverse
        return attended, middle, inverse, scaled, (scaled * gain_two).astype(bf16)

    attended_1, back_0 = flow.open(attended_1, back_0)
    back_1 = exchange(attended_1)
    w_shape = (nx, ny, nfar * 2, sub, width)
    w_out = interleave(core_arg, w_out_own.reshape(w_shape), out_swap.arrived.reshape(w_shape))
    w_out = flat(w_out)
    down = Gather(flow.open(down), "far", 1)
    attended_0, middle_0, inverse_0, scaled_0, normed_0 = after_attention(0, back_0)
    back_1, normed_0 = flow.close(back_1, normed_0)

    back_1, normed_0 = flow.open(back_1, normed_0)
    group_0 = Group(normed_0)
    attended_1, middle_1, inverse_1, scaled_1, normed_1 = after_attention(1, back_1)
    normed_1, w_gate_up = flow.close(normed_1, w_gate_up, wait=[group_0, down])
    w_down = over_xy(down.done())
    group_1 = Group(normed_1)
    group_0 = group_0.done()

    gate_0, up_0, active_0 = ffn_forward(group_0, w_gate_up)
    grad_group_0 = Group(flow.open(grad_out_all[:rows]))
    grad_group_1 = Group(flow.open(grad_out_all[rows:]))
    active_0 = flow.close(active_0, wait=[group_1])

    group_1 = group_1.done()
    gate_1, up_1, active_1 = ffn_forward(flow.open(group_1), w_gate_up)
    active_1 = flow.close(active_1, wait=[grad_group_0, grad_group_1])
    grad_group_0 = grad_group_0.done()
    grad_group_1 = grad_group_1.done()

    outer = lambda a, b: dot(a, b, ((0,), (0,)))
    owners = (nx, nfar, ny)

    def sum_to_owners(terms):
        rest = terms.shape[2:]
        terms = terms.reshape(-1, terms.shape[-1])
        total = lax.psum_scatter(terms, ("x", "y"), scatter_dimension=0, tiled=True)
        return total.reshape(rest)

    d_down = outer_sum(
        [(grad_group_0, active_0), (grad_group_1, flow.open(active_1))], part, 0, owners
    )
    d_down = flow.close(d_down)

    d_down = sum_to_owners(flow.open(d_down))
    both_0 = ffn_backward(flow.open(grad_group_0), w_down, gate_0, up_0)
    terms_0 = flow.close(project_rows(both_0, w_gate_up))

    grad_normed_0 = GroupSum(terms_0)
    partial_0 = project_rows(flow.open(active_0), w_down)
    partial_0 = flow.close(partial_0, wait=[grad_normed_0])
    grad_normed_0.next()
    result_0 = GroupSum(partial_0)
    both_1 = ffn_backward(flow.open(grad_group_1), w_down, gate_1, up_1)
    terms_1 = project_rows(both_1, w_gate_up)
    terms_1 = flow.close(terms_1, wait=[grad_normed_0, result_0])

    def before_attention(b, g, scaled, inverse):
        grad_middle = grad_out_all[b * rows : (b + 1) * rows].astype(f32) + rms_back(
            g * gain_two, scaled, inverse
        )
        grad_branch = grad_middle.astype(bf16)
        grad_attended = dot(grad_branch, w_out).astype(bf16)
        grad_heads = [grad_attended[:, d * qw : (d + 1) * qw] for d in range(n)]
        return grad_middle, grad_branch, jnp.stack(grad_heads)

    grad_normed_1 = GroupSum(terms_1)
    result_0.next()
    grad_normed_0 = grad_normed_0.done()
    grad_middle_0, grad_branch_0, grad_heads_0 = before_attention(
        0, grad_normed_0, scaled_0, inverse_0
    )
    grad_heads_0 = flow.close(grad_heads_0, wait=[grad_normed_1])

    grad_normed_1.next()
    grad_heads_0 = exchange(grad_heads_0)
    d_down = Scatter(flow.open(d_down), "far", 1)
    d_up = outer_sum([(flow.open(group_0), both_0), (group_1, both_1)], part, 1, owners)
    d_up = flow.close(d_up, wait=[grad_normed_1])

    d_up = sum_to_owners(flow.open(d_up))
    d_gate = outer_sum([(flow.open(group_0), both_0), (group_1, both_1)], part, 0, owners)
    d_gate, grad_heads_0 = flow.close(d_gate, grad_heads_0, wait=[d_down])

    d_gate = sum_to_owners(flow.open(d_gate))
    grad_normed_1 = grad_normed_1.done()
    grad_middle_1, grad_branch_1, grad_heads_1 = before_attention(
        1, grad_normed_1, scaled_1, inverse_1
    )
    grad_heads_1 = flow.close(grad_heads_1)

    grad_heads_1 = exchange(grad_heads_1)
    grad_branch = jnp.concatenate([grad_branch_0, grad_branch_1], axis=0)
    attended = jnp.concatenate([attended_0, attended_1], axis=0)
    d_out = outer(flow.open(grad_branch), attended).astype(bf16)
    d_out = flow.close(d_out.reshape((nx, 2, -1, attended.shape[1])))

    def core_sum(mine, send):
        total = mine.astype(f32) + swap(send.astype(bf16), CORE).astype(f32)
        total = total.astype(bf16).reshape((nx, nfar, 2, ny, sub, total.shape[-1]))
        return total.transpose((0, 3, 1, 2, 4, 5))

    def attend_back_one(b, qkv_b, grad_b, raw_b, lse_b):
        dq, dkv = attend_back(
            first_block[b], plain_from[b], doc_start[b], qkv_b, grad_b, raw_b, lse_b, heads
        )
        return jnp.concatenate([dq, dkv], axis=2)

    d_out = sum_to_owners(core_sum(*choose(d_out, CORE, 1)))
    back_0 = attend_back_one(0, qkv_0, flow.open(grad_heads_0), raw_0, lse_0)
    d_up = Scatter(flow.open(d_up), "far", 1)
    back_0, grad_heads_1 = flow.close(back_0, grad_heads_1)

    back_0 = exchange(back_0)
    back_1 = attend_back_one(1, qkv_1, flow.open(grad_heads_1), raw_1, lse_1)
    back_1, back_0, d_gate = flow.close(back_1, back_0, d_gate, wait=[d_up])

    back_1 = exchange(back_1)
    partial_1 = project_rows(flow.open(active_1), w_down)
    grad_proj_0 = unpack_heads(flow.open(back_0), cosine[:rows], sine[:rows])
    back_1, grad_proj_0, partial_1 = flow.close(
        back_1, grad_proj_0, partial_1, wait=[result_0]
    )

    d_gate = Scatter(d_gate, "far", 1)
    result_1 = GroupSum(partial_1)
    grad_proj_1 = unpack_heads(back_1, cosine[rows:], sine[rows:])
    grad_proj = jnp.concatenate([grad_proj_0, grad_proj_1], axis=0)
    core_back = Swap(outer(normed_one_other, grad_proj).astype(bf16), CORE)
    grad_normed_one = dot(grad_proj, w_qkv, ((1,), (1,)))
    grad_proj, grad_normed_one = flow.close(
        grad_proj, grad_normed_one, wait=[core_back, result_1, d_gate]
    )
    d_qkv = outer(normed_one_own, grad_proj) + core_back.arrived.astype(f32)
    d_qkv = d_qkv.astype(bf16).reshape((nx, nfar, 2, ny, sub, -1))
    left, right = flow.close(*jnp.split(d_qkv, 2, axis=-1))

    left = Scatter(left, "x", 0)
    right = Scatter(right, "y", 3)
    result_1.next()
    d_out = Scatter(flow.open(d_out), "far", 0)
    ffn = jnp.stack([t.done(last=True) for t in (d_gate, d_up, d_down)])
    mine, send = choose(ffn, NEAR, 2)
    near_back = Swap(send.astype(bf16), NEAR)
    flow.close(flow.token, wait=[left, right])

    left = Scatter(left.done(), "y", 2)
    right = Scatter(right.done(), "x", 0)
    attn_gain_grad = jnp.sum(grad_normed_one * scaled_one, axis=0)
    ffn_gain_grad = jnp.sum(grad_normed_0 * scaled_0, axis=0) + jnp.sum(
        grad_normed_1 * scaled_1, axis=0
    )
    gains = jnp.stack([attn_gain_grad, ffn_gain_grad])
    gains, grad_normed_one = flow.close(gains, grad_normed_one, wait=[left, right, near_back])

    d_qkv = Scatter(jnp.concatenate([left.done(), right.done()], axis=-1), "far", 0)
    gains = sum_axes(gains, "x", "y", "core")
    quarters = []
    for part_of in lanes_by_bit(mine, near_back.arrived.astype(f32), NEAR):
        part_mine, part_send = choose(part_of, CORE, 1)
        quarters += lanes_by_bit(part_mine, swap(part_send.astype(bf16), CORE).astype(f32), CORE)
    d_gate_up = jnp.concatenate([q[k] for k in (0, 1) for q in quarters], axis=1)
    d_down = jnp.concatenate([q[2] for q in quarters], axis=1)
    grad_input = jnp.concatenate([grad_middle_0, grad_middle_1], axis=0) + rms_back(
        grad_normed_one * gain_one, scaled_one, inverse_one
    )
    grad_input, gains, d_gate_up, d_down = flow.close(
        grad_input, gains, d_gate_up, d_down, wait=[d_qkv, d_out]
    )

    d_qkv = Scatter(d_qkv.done(), "near", 0)
    d_out = Scatter(d_out.done(), "near", 0)
    gains = sum_axes(gains, "near", "far")
    result = jnp.concatenate([middle_0 + result_0.done(), middle_1 + result_1.done()], axis=0)
    return (
        result.astype(bf16).reshape(tokens.shape),
        grad_input.reshape(tokens.shape),
        d_qkv.done(last=True),
        d_out.done(last=True),
        d_gate_up,
        d_down,
        gains[0],
        gains[1],
    )


def solution(mesh):
    dp, seq = mesh.devices.shape
    shape = (dp // 2, 2, seq // 4, 2, 2)
    fine = Mesh(mesh.devices.reshape(shape), ("x", "core") + SEQ)
    by_token = P(("x", "core"), SEQ, None)
    by_row = P(("x", "core") + SEQ, None)
    return jax.shard_map(
        local,
        mesh=fine,
        in_specs=(
            by_token,
            by_token,
            P(("x", "core"), None),
            by_row,
            by_row,
            by_row,
            by_row,
            P(),
            P(),
        ),
        out_specs=(by_token, by_token, by_row, by_row, by_row, by_row, P(), P()),
        check_vma=False,
    )
```

time: 1920 us -> 1060 us (0.55)
  waiting for transfers between devices: 1070 us -> 294 us
  Pallas kernels: 134 us -> 347 us
  matrix products: 211 us -> 62.1 us
  starting transfers between devices: 202 us -> 115 us
  other arithmetic: 171 us -> 103 us
    ppermute x54 -> x56, waiting for transfers between devices: 807 us -> 265 us  [swap(): lax.ppermute(values, axis, [(i, i ^ 1 << b) for i in range(lax.axis_size(...]
    ppermute x56 -> x0, waiting for transfers between devices: 262 us -> none  [to_owners(): lax.ppermute(piece, ('z', 'y'), [(i, i ^ r) for i in range(n)])]
    pallas_call x2 -> x17, Pallas kernels: 18.2 us -> 232 us  [the longest x8 132 us: over_rows(): pl.pallas_call(with_weights(kernel), grid=(m // tile,), in_specs=[by_rows...]
    dot_general x12 -> x10, matrix products: 211 us -> 62.1 us  [dot(): return lax.dot_general(a, b, (dims, ((), ())), preferred_element_type=f32)]
    ppermute x56 -> x0, starting transfers between devices: 143 us -> none  [to_owners(): lax.ppermute(piece, ('z', 'y'), [(i, i ^ r) for i in range(n)])]
    another operation x43 -> x39, other arithmetic: 100 us -> 33.8 us  [the longest x25 21.8 us: by_bit(): jnp.stack([jnp.where(low, mine, other), jnp.where(low, other, mine)], axi...]
    unnamed x201 -> x263, local copies, waits for them, and re-layouts: 20.2 us -> 74.5 us
    all_to_all x0 -> x8, starting transfers between devices: none -> 39.3 us  [exchange(): return lax.all_to_all(pieces, SEQ, split_axis=0, concat_axis=0, tiled=True)]
  transfers between devices with their start and end apart: 110 -> 71, of which waited for: 57 -> 27; matrix products, arithmetic and copies ran while one was open for 22% -> 21% of each run, Pallas kernels for 7% -> 33%
where the time goes in v3:
time: 1060 us; the launch traced here: 1040 us
  Pallas kernels  347 us (33%)
  waiting for transfers between devices  294 us (28%)
  starting transfers between devices  115 us (11%)
  local copies, waits for them, and re-layouts  106 us (10%)
  other arithmetic  103 us (10%)
  matrix products  62.1 us (6%)
  between operations  16.7 us (2%)
    ppermute x56, waiting for transfers between devices, swap(): lax.ppermute(values, axis, [(i, i ^ 1 << b) for i in range(lax.axis_size(...  265 us
    pallas_call x8, Pallas kernels, over_rows(): pl.pallas_call(with_weights(kernel), grid=(m // tile,), in_specs=[by_rows...  132 us
    unnamed x263, local copies, waits for them, and re-layouts  74.5 us
    ppermute x56, starting transfers between devices, swap(): lax.ppermute(values, axis, [(i, i ^ 1 << b) for i in range(lax.axis_size(...  74.2 us
    pallas_call x2, Pallas kernels, attend_back(): pl.pallas_call(functools.partial(attend_back_kernel, heads), grid=(n,), o...  67.4 us
    dot_general x10, matrix products, dot(): return lax.dot_general(a, b, (dims, ((), ())), preferred_element_type=f32)  62.1 us
    pallas_call x3, Pallas kernels, outer_sum(): pl.pallas_call(functools.partial(outer_sum_kernel, len(pairs)), grid=(2 *...  53.5 us
    pallas_call x2, Pallas kernels, attend(): pl.pallas_call(functools.partial(attend_kernel, heads), grid=(n,), out_sh...  47.7 us
  transfers between devices with their start and end apart: 71, of which 27 were waited for; matrix products, arithmetic and copies ran while one was open for 21% of the time, Pallas kernels for 33%

profile of v3, /device:TPU:0, one launch (start us, length us, event | category | flops | bytes accessed | tf_op | source)
XLA Modules:
  0.0 1042.9 jit_solution(11033177457062767617)
XLA Ops:
  34.9 29.0 %collective-permute-done.1 = bf16[2,64,2560]{2,1,0:T(8,128)(2,1)} collective-permute-done((bf16[2,64,2560]{2,1,0:T(8,128)(2,1)}, bf16[2,64,2560]{2,1,0:T(8,128)(2,1)}, u32[]{:S(2)}, u32[]{:S(2)}) %collective-permute-start.1) | collective-permute-done | bytes 655392 | tf_op jit(solution)/shard_map/ppermute | solution.py:47
  76.1 13.7 %collective-permute-done.7 = bf16[2,64,2048]{2,1,0:T(8,128)(2,1)} collective-permute-done((bf16[2,64,2048]{2,1,0:T(8,128)(2,1)}, bf16[2,64,2048]{2,1,0:T(8,128)(2,1)}, u32[]{:S(2)}, u32[]{:S(2)}) %collective-permute-start.7) | collective-permute-done | bytes 524320 | tf_op jit(solution)/shard_map/ppermute | solution.py:47
  99.5 28.5 %collective-permute-done.10 = bf16[2,2,64,1408]{3,2,1,0:T(8,128)(2,1)S(1)} collective-permute-done((bf16[2,2,64,1408]{3,2,1,0:T(8,128)(2,1)S(1)}, bf16[2,2,64,1408]{3,2,1,0:T(8,128)(2,1)S(1)}, u32[]{:S(2)}, u32[]{:S(2)}) %collective-permute-start.10) | collective-permute-done | bytes 720928 | tf_op jit(solution)/shard_map/ppermute | solution.py:47
  152.8 7.2 pack_heads.2
  160.0 10.3 collective-permute-done.12
  182.9 7.1 pack_heads.3
  192.5 13.7 %interleave.2 = bf16[2,2,4,1,128,2560]{5,4,3,2,1,0:T(8,128)(2,1)} custom-call(s32[1]{0:T(128)} %bitcast.51.core_ref, bf16[2,1,4,128,2560]{4,3,2,1,0:T(8,128)(2,1)S(1)} %copy-done.7, bf16[2,1,4,128,2560]{4,3,2,1,0:T(8,128)(2,1)} %bitcast.55.other_ref), custom_call_target="tpu_custom_call" | custom-call | bytes 65536 | tf_op jit(solution)/shard_map/interleave/pallas_call | solution.py:428
  206.2 9.2 all-to-all-done.qkv_ref
  222.0 19.8 %attend.2 = (bf16[8,256,256]{2,1,0:T(8,128)(2,1)S(1)}, f32[8,256,256]{2,1,0:T(8,128)S(1)}, f32[8,8,1024]{2,1,0:T(8,128)S(1)}) custom-call(s32[8]{0:T(128)S(1)} %get-tuple-element.419.lo_ref, s32[8]{0:T(128)S(1)} %get-tuple-element.410.hi_ref, s32[8,1,256]{2,1,0:T(1,128)S(1)} %bitcast.573, bf16[8,256,384]{2,1,0:T(8,128)(2,1)S(1)} %copy-done.9), custom_call_target="tpu_custom_call" | custom-call | bytes 1048576 | tf_op jit(solution)/shard_map/attend/pallas_call | solution.py:194
  244.2 13.3 %all-to-all-done.1.qkv_ref = bf16[8,256,384]{2,1,0:T(8,128)(2,1)S(1)} async-done(((bf16[8,256,384]{2,1,0:T(8,128)(2,1)}), bf16[8,256,384]{2,1,0:T(8,128)(2,1)S(1)}, u32[]{:S(2)}, u32[]{:S(2)}) %all-to-all-start.1) | async-done | bytes 1572896 | tf_op jit(solution)/shard_map/all_to_all | solution.py:603
  265.9 27.9 %attend.3 = (bf16[8,256,256]{2,1,0:T(8,128)(2,1)S(1)}, f32[8,256,256]{2,1,0:T(8,128)S(1)}, f32[8,8,1024]{2,1,0:T(8,128)S(1)}) custom-call(s32[8]{0:T(128)S(1)} %get-tuple-element.418.lo_ref, s32[8]{0:T(128)S(1)} %get-tuple-element.411.hi_ref, s32[8,1,256]{2,1,0:T(1,128)S(1)} %bitcast.571, bf16[8,256,384]{2,1,0:T(8,128)(2,1)S(1)} %all-to-all-done.1.qkv_ref), custom_call_target="tpu_custom_call" | custom-call | bytes 1048576 | tf_op jit(solution)/shard_map/attend/pallas_call | solution.py:194
  296.1 6.0 all-to-all-start.3
  314.0 12.7 %interleave.3 = bf16[2,2,4,2,64,2048]{5,4,3,2,1,0:T(8,128)(2,1)} custom-call(s32[1]{0:T(128)} %bitcast.51.core_ref, bf16[2,2,4,64,2048]{4,3,2,1,0:T(8,128)(2,1)S(1)} %bitcast.570, bf16[2,2,4,64,2048]{4,3,2,1,0:T(8,128)(2,1)} %bitcast.71.other_ref), custom_call_target="tpu_custom_call" | custom-call | bytes 65536 | tf_op jit(solution)/shard_map/interleave/pallas_call | solution.py:428
  327.7 6.3 multiply_reduce_fusion.8
  345.7 6.8 multiply_reduce_fusion.7
  355.0 17.2 %collective-permute-done.15 = bf16[256,2048]{1,0:T(8,128)(2,1)} collective-permute-done((bf16[256,2048]{1,0:T(8,128)(2,1)}, bf16[256,2048]{1,0:T(8,128)(2,1)}, u32[]{:S(2)}, u32[]{:S(2)}) %collective-permute-start.15) | collective-permute-done | bytes 1048608 | tf_op jit(solution)/shard_map/ppermute | solution.py:47
  382.1 20.9 %ffn_forward.2 = (f32[1024,1408]{1,0:T(8,128)}, f32[1024,1408]{1,0:T(8,128)}, bf16[1024,1408]{1,0:T(8,128)(2,1)S(1)}) custom-call(bf16[1024,2048]{1,0:T(8,128)(2,1)} %copy-done, bf16[4,2,2,2,64,2816]{5,4,3,2,1,0:T(8,128)(2,1)} %bitcast.575), custom_call_target="tpu_custom_call" | custom-call | bytes 65536 | tf_op jit(solution)/shard_map/ffn_forward/pallas_call | solution.py:499
  412.6 21.6 %ffn_forward.3 = (f32[1024,1408]{1,0:T(8,128)}, f32[1024,1408]{1,0:T(8,128)}, bf16[1024,1408]{1,0:T(8,128)(2,1)S(1)}) custom-call(bf16[1024,2048]{1,0:T(8,128)(2,1)} %copy-done.23, bf16[4,2,2,2,64,2816]{5,4,3,2,1,0:T(8,128)(2,1)} %bitcast.576), custom_call_target="tpu_custom_call" | custom-call | bytes 65536 | tf_op jit(solution)/shard_map/ffn_forward/pallas_call | solution.py:499
  434.3 17.2 %collective-permute-done.23 = bf16[256,2048]{1,0:T(8,128)(2,1)} collective-permute-done((bf16[256,2048]{1,0:T(8,128)(2,1)S(1)}, bf16[256,2048]{1,0:T(8,128)(2,1)}, u32[]{:S(2)}, u32[]{:S(2)}) %collective-permute-start.23) | collective-permute-done | bytes 1048608 | tf_op jit(solution)/shard_map/ppermute | solution.py:47
  461.9 16.5 %outer_sum.3 = bf16[2,2,2,2,2,64,1408]{6,5,4,3,2,1,0:T(8,128)(2,1)} custom-call(bf16[1024,2048]{1,0:T(8,128)(2,1)} %copy-done.3, bf16[1024,1408]{1,0:T(8,128)(2,1)S(1)} %copy-done.14, bf16[1024,2048]{1,0:T(8,128)(2,1)} %copy-done.5, bf16[1024,1408]{1,0:T(8,128)(2,1)S(1)} %get-tuple-element.295.refs_3_.x_ref), custom_call_target="tpu_custom_call" | custom-call | bytes 65536 | tf_op jit(solution)/shard_map/outer_sum/pallas_call | solution.py:580
  480.9 14.3 %ffn_backward.2.x_ref.refs_1_ = bf16[1024,2816]{1,0:T(8,128)(2,1)} custom-call(bf16[1024,2048]{1,0:T(8,128)(2,1)S(1)} %copy-done.4, bf16[4,2,2,2,64,1408]{5,4,3,2,1,0:T(8,128)(2,1)} %bitcast.579, f32[1024,1408]{1,0:T(8,128)} %get-tuple-element.243.refs_0_, f32[1024,1408]{1,0:T(8,128)} %get-tuple-element.244.refs_1_), custom_call_target="tpu_custom_call" | custom-call | bytes 65536 | tf_op jit(solution)/shard_map/ffn_backward/pallas_call | solution.py:499
  495.2 18.8 %project_rows.4 = bf16[1024,2048]{1,0:T(8,128)(2,1)S(1)} custom-call(bf16[1024,2816]{1,0:T(8,128)(2,1)} %ffn_backward.2.x_ref.refs_1_, bf16[4,2,2,2,64,2816]{5,4,3,2,1,0:T(8,128)(2,1)} %bitcast.577), custom_call_target="tpu_custom_call" | custom-call | bytes 65536 | tf_op jit(solution)/shard_map/project_rows/pallas_call | solution.py:499
  516.0 11.4 %project_rows.5 = bf16[1024,2048]{1,0:T(8,128)(2,1)} custom-call(bf16[1024,1408]{1,0:T(8,128)(2,1)S(1)} %copy-done.15, bf16[4,2,2,2,64,1408]{5,4,3,2,1,0:T(8,128)(2,1)} %bitcast.580), custom_call_target="tpu_custom_call" | custom-call | bytes 65536 | tf_op jit(solution)/shard_map/project_rows/pallas_call | solution.py:499
  536.5 14.6 %ffn_backward.3.x_ref.refs_3_ = bf16[1024,2816]{1,0:T(8,128)(2,1)} custom-call(bf16[1024,2048]{1,0:T(8,128)(2,1)S(1)} %copy-done.6, bf16[4,2,2,2,64,1408]{5,4,3,2,1,0:T(8,128)(2,1)} %bitcast.581, f32[1024,1408]{1,0:T(8,128)} %get-tuple-element.251.refs_0_, f32[1024,1408]{1,0:T(8,128)} %get-tuple-element.252.refs_1_), custom_call_target="tpu_custom_call" | custom-call | bytes 65536 | tf_op jit(solution)/shard_map/ffn_backward/pallas_call | solution.py:499
  551.2 19.1 %project_rows.6 = bf16[1024,2048]{1,0:T(8,128)(2,1)S(1)} custom-call(bf16[1024,2816]{1,0:T(8,128)(2,1)} %ffn_backward.3.x_ref.refs_3_, bf16[4,2,2,2,64,2816]{5,4,3,2,1,0:T(8,128)(2,1)} %bitcast.578), custom_call_target="tpu_custom_call" | custom-call | bytes 65536 | tf_op jit(solution)/shard_map/project_rows/pallas_call | solution.py:499
  577.1 6.1 convolution_convert_fusion.3
  587.8 18.3 %outer_sum.4 = bf16[2,2,2,2,2,64,1408]{6,5,4,3,2,1,0:T(8,128)(2,1)} custom-call(bf16[1024,2048]{1,0:T(8,128)(2,1)S(1)} %copy-done.1, bf16[1024,2816]{1,0:T(8,128)(2,1)} %ffn_backward.2.x_ref.refs_1_, bf16[1024,2048]{1,0:T(8,128)(2,1)} %copy-done.23, bf16[1024,2816]{1,0:T(8,128)(2,1)} %ffn_backward.3.x_ref.refs_3_), custom_call_target="tpu_custom_call" | custom-call | bytes 65536 | tf_op jit(solution)/shard_map/outer_sum/pallas_call | solution.py:580
  622.3 18.7 %outer_sum.5 = bf16[2,2,2,2,2,64,1408]{6,5,4,3,2,1,0:T(8,128)(2,1)} custom-call(bf16[1024,2048]{1,0:T(8,128)(2,1)S(1)} %copy-done.2, bf16[1024,2816]{1,0:T(8,128)(2,1)} %ffn_backward.2.x_ref.refs_1_, bf16[1024,2048]{1,0:T(8,128)(2,1)} %copy-done.23, bf16[1024,2816]{1,0:T(8,128)(2,1)} %ffn_backward.3.x_ref.refs_3_), custom_call_target="tpu_custom_call" | custom-call | bytes 65536 | tf_op jit(solution)/shard_map/outer_sum/pallas_call | solution.py:580
  640.9 31.7 %collective-permute-done.32 = bf16[2,2,64,1408]{3,2,1,0:T(8,128)(2,1)} collective-permute-done((bf16[2,2,64,1408]{3,2,1,0:T(8,128)(2,1)S(1)}, bf16[2,2,64,1408]{3,2,1,0:T(8,128)(2,1)}, u32[]{:S(2)}, u32[]{:S(2)}) %collective-permute-start.32) | collective-permute-done | bytes 720928 | tf_op jit(solution)/shard_map/ppermute | solution.py:47
  681.0 6.1 convolution_convert_fusion.2
  709.2 29.2 %attend_back.2 = (bf16[8,256,256]{2,1,0:T(8,128)(2,1)S(1)}, bf16[8,256,128]{2,1,0:T(8,128)(2,1)S(1)}) custom-call(s32[8]{0:T(128)S(1)} %get-tuple-element.419.lo_ref, s32[8]{0:T(128)S(1)} %get-tuple-element.410.hi_ref, s32[8,1,256]{2,1,0:T(1,128)S(1)} %bitcast.574, bf16[8,256,384]{2,1,0:T(8,128)(2,1)S(1)} %copy-done.10, ...), custom_call_target="tpu_custom_call" | custom-call | bytes 1048576 | tf_op jit(solution)/shard_map/attend_back/pallas_call | solution.py:302
  739.8 6.1 all-to-all-start.6
  750.8 38.2 %attend_back.3 = (bf16[8,256,256]{2,1,0:T(8,128)(2,1)S(1)}, bf16[8,256,128]{2,1,0:T(8,128)(2,1)S(1)}) custom-call(s32[8]{0:T(128)S(1)} %get-tuple-element.418.lo_ref, s32[8]{0:T(128)S(1)} %get-tuple-element.411.hi_ref, s32[8,1,256]{2,1,0:T(1,128)S(1)} %bitcast.572, bf16[8,256,384]{2,1,0:T(8,128)(2,1)S(1)} %all-to-all-done.1.qkv_ref, ...), custom_call_target="tpu_custom_call" | custom-call | bytes 1048576 | tf_op jit(solution)/shard_map/attend_back/pallas_call | solution.py:302
  795.2 15.3 %collective-permute-done.33 = bf16[2,2,64,1408]{3,2,1,0:T(8,128)(2,1)S(1)} collective-permute-done((bf16[2,2,64,1408]{3,2,1,0:T(8,128)(2,1)}, bf16[2,2,64,1408]{3,2,1,0:T(8,128)(2,1)S(1)}, u32[]{:S(2)}, u32[]{:S(2)}) %collective-permute-start.33) | collective-permute-done | bytes 720928 | tf_op jit(solution)/shard_map/ppermute | solution.py:47
  810.5 6.0 all-to-all-start.7
  822.8 5.4 fusion
  832.5 11.5 %project_rows.7 = bf16[1024,2048]{1,0:T(8,128)(2,1)} custom-call(bf16[1024,1408]{1,0:T(8,128)(2,1)S(1)} %copy-done.12, bf16[4,2,2,2,64,1408]{5,4,3,2,1,0:T(8,128)(2,1)} %bitcast.582), custom_call_target="tpu_custom_call" | custom-call | bytes 65536 | tf_op jit(solution)/shard_map/project_rows/pallas_call | solution.py:499
  846.6 19.2 %collective-permute-done.34 = bf16[256,2048]{1,0:T(8,128)(2,1)} collective-permute-done((bf16[256,2048]{1,0:T(8,128)(2,1)}, bf16[256,2048]{1,0:T(8,128)(2,1)}, u32[]{:S(2)}, u32[]{:S(2)}) %collective-permute-start.34) | collective-permute-done | bytes 1048608 | tf_op jit(solution)/shard_map/ppermute | solution.py:47
  868.4 6.1 convolution_convert_fusion.1
  884.2 9.9 fusion.84
  898.4 15.2 %collective-permute-done.37 = bf16[2,2,64,1408]{3,2,1,0:T(8,128)(2,1)S(1)} collective-permute-done((bf16[2,2,64,1408]{3,2,1,0:T(8,128)(2,1)S(1)}, bf16[2,2,64,1408]{3,2,1,0:T(8,128)(2,1)S(1)}, u32[]{:S(2)}, u32[]{:S(2)}) %collective-permute-start.37) | collective-permute-done | bytes 720928 | tf_op jit(solution)/shard_map/ppermute | solution.py:47
  913.7 6.2 add_convert_fusion
  931.5 10.3 collective-permute-start.39
  945.5 13.4 %collective-permute-done.40 = bf16[2,2,2,64,1280]{4,3,2,1,0:T(8,128)(2,1)S(1)} collective-permute-done((bf16[2,2,2,64,1280]{4,3,2,1,0:T(8,128)(2,1)S(1)}, bf16[2,2,2,64,1280]{4,3,2,1,0:T(8,128)(2,1)S(1)}, u32[]{:S(2)}, u32[]{:S(2)}) %collective-permute-start.40) | collective-permute-done | bytes 1310752 | tf_op jit(solution)/shard_map/ppermute | solution.py:47
  958.9 10.6 %collective-permute-done.39 = bf16[2,2,2,64,1280]{4,3,1,0,2:T(8,128)(2,1)S(1)} collective-permute-done((bf16[2,2,2,64,1280]{4,3,1,0,2:T(8,128)(2,1)S(1)}, bf16[2,2,2,64,1280]{4,3,1,0,2:T(8,128)(2,1)S(1)}, u32[]{:S(2)}, u32[]{:S(2)}) %collective-permute-start.39) | collective-permute-done | bytes 1310752 | tf_op jit(solution)/shard_map/ppermute | solution.py:47
  972.5 13.3 %collective-permute-done.38 = bf16[256,2048]{1,0:T(8,128)(2,1)S(1)} collective-permute-done((bf16[256,2048]{1,0:T(8,128)(2,1)S(1)}, bf16[256,2048]{1,0:T(8,128)(2,1)S(1)}, u32[]{:S(2)}, u32[]{:S(2)}) %collective-permute-start.38) | collective-permute-done | bytes 1048608 | tf_op jit(solution)/shard_map/ppermute | solution.py:47
  990.4 10.7 %collective-permute-start.44 = (f32[2,2048]{1,0:T(2,128)S(1)}, f32[2,2048]{1,0:T(2,128)S(1)}, u32[]{:S(2)}, u32[]{:S(2)}) collective-permute-start(f32[2,2048]{1,0:T(2,128)S(1)} %pad_maximum_fusion.28), channel_id=1, source_target_pairs={{0,16},{16,0},{1,17},{17,1},{2,18},{18,2},{3,19},{19,3},{4,20},{20... | collective-permute-start | bytes 49160 | tf_op jit(solution)/shard_map/ppermute | solution.py:47
  1011.9 6.4 collective-permute-done.49
  (552 shorter events, 329.2 us)
Async XLA Ops:
  7.2 237.0 %all-gather.4.cloned.1.call-start = ((), (), s32[]{:S(2)}) async-start(), calls=%async_computation.12 | async-start | bytes 5242880 | tf_op jit(solution)/shard_map/all_gather | solution.py:732
  10.3 24.6 %collective-permute-start.3 = (bf16[64,2048]{1,0:T(8,128)(2,1)}, bf16[64,2048]{1,0:T(8,128)(2,1)}, u32[]{:S(2)}, u32[]{:S(2)}) collective-permute-start(bf16[64,2048]{1,0:T(8,128)(2,1)} %param.13), channel_id=1, source_target_pairs={{0,4},{4,0},{1,5},{5,1},{2,6},{6,2},{3,7},{7,3},{8,12},{12,8},{9,1... | collective-permute-start | bytes 786440 | tf_op jit(solution)/shard_map/ppermute | solution.py:47
  26.5 39.5 %collective-permute-start.2 = (bf16[3,64,2816]{2,1,0:T(8,128)(2,1)}, bf16[3,64,2816]{2,1,0:T(8,128)(2,1)}, u32[]{:S(2)}, u32[]{:S(2)}) collective-permute-start(bf16[3,64,2816]{2,1,0:T(8,128)(2,1)} %pad_maximum_fusion.15), channel_id=1, source_target_pairs={{0,2},{2,0},{1,3},{3,1},{4,6},{6,4},{5,7},{7,5},{8,10},{10,8},{9,1... | collective-permute-start | bytes 3244040 | tf_op jit(solution)/shard_map/ppermute | solution.py:47
  29.0 34.9 %collective-permute-start.1 = (bf16[2,64,2560]{2,1,0:T(8,128)(2,1)}, bf16[2,64,2560]{2,1,0:T(8,128)(2,1)}, u32[]{:S(2)}, u32[]{:S(2)}) collective-permute-start(bf16[2,64,2560]{2,1,0:T(8,128)(2,1)} %pad_maximum_fusion.24), channel_id=1, source_target_pairs={{0,4},{4,0},{1,5},{5,1},{2,6},{6,2},{3,7},{7,3},{8,12},{12,8},{9,1... | collective-permute-start | bytes 1966088 | tf_op jit(solution)/shard_map/ppermute | solution.py:47
  68.8 21.0 %collective-permute-start.6 = (bf16[3,2,64,1408]{3,2,1,0:T(8,128)(2,1)}, bf16[3,2,64,1408]{3,2,1,0:T(8,128)(2,1)}, u32[]{:S(2)}, u32[]{:S(2)}) collective-permute-start(bf16[3,2,64,1408]{3,2,1,0:T(8,128)(2,1)} %pad_maximum_fusion.16), channel_id=1, source_target_pairs={{0,8},{8,0},{1,9},{9,1},{2,10},{10,2},{3,11},{11,3},{4,12},{12,4},... | collective-permute-start | bytes 3244040 | tf_op jit(solution)/shard_map/ppermute | solution.py:47
  91.1 36.8 %collective-permute-start.9 = (bf16[2,2,2,64,1280]{4,3,2,1,0:T(8,128)(2,1)S(1)}, bf16[2,2,2,64,1280]{4,3,2,1,0:T(8,128)(2,1)S(1)}, u32[]{:S(2)}, u32[]{:S(2)}) collective-permute-start(bf16[2,2,2,64,1280]{4,3,2,1,0:T(8,128)(2,1)S(1)} %pad_maximum_fusion.14), channel_id=1, source_target_pairs={{0,1},{1,0},{2,3},{3,2},{4,5},{5,4},{6,7},{7,6},{8,9},{9,8},{10,11... | collective-permute-start | bytes 3932168 | tf_op jit(solution)/shard_map/ppermute | solution.py:47
  93.0 35.9 %collective-permute-start.8 = (bf16[2,2,2,64,1280]{4,3,2,1,0:T(8,128)(2,1)S(1)}, bf16[2,2,2,64,1280]{4,3,2,1,0:T(8,128)(2,1)S(1)}, u32[]{:S(2)}, u32[]{:S(2)}) collective-permute-start(bf16[2,2,2,64,1280]{4,3,2,1,0:T(8,128)(2,1)S(1)} %pad_maximum_fusion.13), channel_id=1, source_target_pairs={{0,16},{16,0},{1,17},{17,1},{2,18},{18,2},{3,19},{19,3},{4,20},{20... | collective-permute-start | bytes 3932168 | tf_op jit(solution)/shard_map/ppermute | solution.py:47
  95.1 32.9 %collective-permute-start.10 = (bf16[2,2,64,1408]{3,2,1,0:T(8,128)(2,1)S(1)}, bf16[2,2,64,1408]{3,2,1,0:T(8,128)(2,1)S(1)}, u32[]{:S(2)}, u32[]{:S(2)}) collective-permute-start(bf16[2,2,64,1408]{3,2,1,0:T(8,128)(2,1)S(1)} %pad_maximum_fusion.22), channel_id=1, source_target_pairs={{0,4},{4,0},{1,5},{5,1},{2,6},{6,2},{3,7},{7,3},{8,12},{12,8},{9,1... | collective-permute-start | bytes 2162696 | tf_op jit(solution)/shard_map/ppermute | solution.py:47
  136.1 236.1 %all-gather.6.cloned.1.call-start = ((), (), s32[]{:S(2)}) async-start(), calls=%async_computation.13 | async-start | bytes 14417920 | tf_op jit(solution)/shard_map/all_gather | solution.py:732
  136.4 34.0 %collective-permute-start.12 = (bf16[2,2,64,1408]{3,2,1,0:T(8,128)(2,1)}, bf16[2,2,64,1408]{3,2,1,0:T(8,128)(2,1)}, u32[]{:S(2)}, u32[]{:S(2)}) collective-permute-start(bf16[2,2,64,1408]{3,2,1,0:T(8,128)(2,1)} %pad_maximum_fusion.20), channel_id=1, source_target_pairs={{0,4},{4,0},{1,5},{5,1},{2,6},{6,2},{3,7},{7,3},{8,12},{12,8},{9,1... | collective-permute-start | bytes 2162696 | tf_op jit(solution)/shard_map/ppermute | solution.py:47
  173.4 42.0 %all-to-all-start = ((bf16[8,256,384]{2,1,0:T(8,128)(2,1)}), bf16[8,256,384]{2,1,0:T(8,128)(2,1)S(1)}, u32[]{:S(2)}, u32[]{:S(2)}) async-start(bf16[8,256,384]{2,1,0:T(8,128)(2,1)} %pack_heads.2), calls=%async_computation | async-start | bytes 3145728 | tf_op jit(solution)/shard_map/all_to_all | solution.py:603
  216.5 40.9 %all-to-all-start.1 = ((bf16[8,256,384]{2,1,0:T(8,128)(2,1)}), bf16[8,256,384]{2,1,0:T(8,128)(2,1)S(1)}, u32[]{:S(2)}, u32[]{:S(2)}) async-start(bf16[8,256,384]{2,1,0:T(8,128)(2,1)} %pack_heads.3), calls=%async_computation.1 | async-start | bytes 3145728 | tf_op jit(solution)/shard_map/all_to_all | solution.py:603
  257.5 38.6 %collective-permute-start.13 = (bf16[4,2,2,64,2048]{4,3,2,1,0:T(8,128)(2,1)}, bf16[4,2,2,64,2048]{4,3,2,1,0:T(8,128)(2,1)}, u32[]{:S(2)}, u32[]{:S(2)}) collective-permute-start(bf16[4,2,2,64,2048]{4,3,2,1,0:T(8,128)(2,1)} %bitcast.569), channel_id=1, source_target_pairs={{0,8},{8,0},{1,9},{9,1},{2,10},{10,2},{3,11},{11,3},{4,12},{12,4},... | collective-permute-start | bytes 12582920 | tf_op jit(solution)/shard_map/ppermute | solution.py:47
  257.5 38.6 %all-to-all-start.2 = ((bf16[8,256,256]{2,1,0:T(8,128)(2,1)}), bf16[8,256,256]{2,1,0:T(8,128)(2,1)}, u32[]{:S(2)}, u32[]{:S(2)}) async-start(bf16[8,256,256]{2,1,0:T(8,128)(2,1)} %copy-done.20), calls=%async_computation.2 | async-start | bytes 2097152 | tf_op jit(solution)/shard_map/all_to_all | solution.py:603
  296.1 42.2 %all-to-all-start.3 = ((bf16[8,256,256]{2,1,0:T(8,128)(2,1)}), bf16[8,256,256]{2,1,0:T(8,128)(2,1)}, u32[]{:S(2)}, u32[]{:S(2)}) async-start(bf16[8,256,256]{2,1,0:T(8,128)(2,1)} %copy-done.19), calls=%async_computation.3 | async-start | bytes 2097152 | tf_op jit(solution)/shard_map/all_to_all | solution.py:603
  302.1 176.5 %all-gather.8.cloned.1.call-start = ((), (), s32[]{:S(2)}) async-start(), calls=%async_computation.14 | async-start | bytes 7208960 | tf_op jit(solution)/shard_map/all_gather | solution.py:732
  308.9 46.1 %collective-permute-start.16 = (bf16[2,2,64,1408]{3,2,1,0:T(8,128)(2,1)S(1)}, bf16[2,2,64,1408]{3,2,1,0:T(8,128)(2,1)}, u32[]{:S(2)}, u32[]{:S(2)}) collective-permute-start(bf16[2,2,64,1408]{3,2,1,0:T(8,128)(2,1)S(1)} %copy-done.61), channel_id=1, source_target_pairs={{0,4},{4,0},{1,5},{5,1},{2,6},{6,2},{3,7},{7,3},{8,12},{12,8},{9,1... | collective-permute-start | bytes 2162696 | tf_op jit(solution)/shard_map/ppermute | solution.py:47
  338.3 33.9 %collective-permute-start.15 = (bf16[256,2048]{1,0:T(8,128)(2,1)}, bf16[256,2048]{1,0:T(8,128)(2,1)}, u32[]{:S(2)}, u32[]{:S(2)}) collective-permute-start(bf16[256,2048]{1,0:T(8,128)(2,1)} %multiply_convert_fusion.2), channel_id=1, source_target_pairs={{0,2},{2,0},{1,3},{3,1},{4,6},{6,4},{5,7},{7,5},{8,10},{10,8},{9,1... | collective-permute-start | bytes 3145736 | tf_op jit(solution)/shard_map/ppermute | solution.py:47
  374.9 241.2 %reduce-scatter.5.cloned.1.call-start = ((), (), s32[]{:S(2)}) async-start(), calls=%async_computation.15 | async-start | bytes 7208960 | tf_op jit(solution)/shard_map/reduce_scatter | solution.py:817
  375.9 27.0 %collective-permute-start.18 = (bf16[256,2048]{1,0:T(8,128)(2,1)}, bf16[256,2048]{1,0:T(8,128)(2,1)}, u32[]{:S(2)}, u32[]{:S(2)}) collective-permute-start(bf16[256,2048]{1,0:T(8,128)(2,1)} %multiply_convert_fusion.1), channel_id=1, source_target_pairs={{0,2},{2,0},{1,3},{3,1},{4,6},{6,4},{5,7},{7,5},{8,10},{10,8},{9,1... | collective-permute-start | bytes 3145736 | tf_op jit(solution)/shard_map/ppermute | solution.py:47
  378.4 28.9 %collective-permute-start.20 = (bf16[256,2048]{1,0:T(8,128)(2,1)}, bf16[256,2048]{1,0:T(8,128)(2,1)}, u32[]{:S(2)}, u32[]{:S(2)}) collective-permute-start(bf16[256,2048]{1,0:T(8,128)(2,1)} %multiply_convert_fusion.1), channel_id=1, source_target_pairs={{0,8},{8,0},{1,9},{9,1},{2,10},{10,2},{3,11},{11,3},{4,12},{12,4},... | collective-permute-start | bytes 3145736 | tf_op jit(solution)/shard_map/ppermute | solution.py:47
  403.7 30.6 %collective-permute-start.22 = (bf16[256,2048]{1,0:T(8,128)(2,1)S(1)}, bf16[256,2048]{1,0:T(8,128)(2,1)}, u32[]{:S(2)}, u32[]{:S(2)}) collective-permute-start(bf16[256,2048]{1,0:T(8,128)(2,1)S(1)} %get-tuple-element.229), channel_id=1, source_target_pairs={{0,2},{2,0},{1,3},{3,1},{4,6},{6,4},{5,7},{7,5},{8,10},{10,8},{9,1... | collective-permute-start | bytes 3145736 | tf_op jit(solution)/shard_map/ppermute | solution.py:47
  404.8 46.8 %collective-permute-start.23 = (bf16[256,2048]{1,0:T(8,128)(2,1)S(1)}, bf16[256,2048]{1,0:T(8,128)(2,1)}, u32[]{:S(2)}, u32[]{:S(2)}) collective-permute-start(bf16[256,2048]{1,0:T(8,128)(2,1)S(1)} %get-tuple-element.234), channel_id=1, source_target_pairs={{0,2},{2,0},{1,3},{3,1},{4,6},{6,4},{5,7},{7,5},{8,10},{10,8},{9,1... | collective-permute-start | bytes 3145736 | tf_op jit(solution)/shard_map/ppermute | solution.py:47
  407.1 45.1 %collective-permute-start.19 = (bf16[256,2048]{1,0:T(8,128)(2,1)S(1)}, bf16[256,2048]{1,0:T(8,128)(2,1)}, u32[]{:S(2)}, u32[]{:S(2)}) collective-permute-start(bf16[256,2048]{1,0:T(8,128)(2,1)S(1)} %get-tuple-element.229), channel_id=1, source_target_pairs={{0,8},{8,0},{1,9},{9,1},{2,10},{10,2},{3,11},{11,3},{4,12},{12,4},... | collective-permute-start | bytes 3145736 | tf_op jit(solution)/shard_map/ppermute | solution.py:47
  407.3 46.2 %collective-permute-start.25 = (bf16[256,2048]{1,0:T(8,128)(2,1)S(1)}, bf16[256,2048]{1,0:T(8,128)(2,1)}, u32[]{:S(2)}, u32[]{:S(2)}) collective-permute-start(bf16[256,2048]{1,0:T(8,128)(2,1)S(1)} %get-tuple-element.234), channel_id=1, source_target_pairs={{0,8},{8,0},{1,9},{9,1},{2,10},{10,2},{3,11},{11,3},{4,12},{12,4},... | collective-permute-start | bytes 3145736 | tf_op jit(solution)/shard_map/ppermute | solution.py:47
  478.5 267.4 %reduce-scatter.9.cloned.1.call-start = ((), (), s32[]{:S(2)}) async-start(), calls=%async_computation.17 | async-start | bytes 7208960 | tf_op jit(solution)/shard_map/reduce_scatter | solution.py:817
  531.5 38.8 %collective-permute-start.29 = (bf16[2,256,2048]{2,1,0:T(8,128)(2,1)}, bf16[2,256,2048]{2,1,0:T(8,128)(2,1)}, u32[]{:S(2)}, u32[]{:S(2)}) collective-permute-start(bf16[2,256,2048]{2,1,0:T(8,128)(2,1)} %slice_bitcast_fusion.8), channel_id=1, source_target_pairs={{0,8},{8,0},{1,9},{9,1},{2,10},{10,2},{3,11},{11,3},{4,12},{12,4},... | collective-permute-start | bytes 6291464 | tf_op jit(solution)/shard_map/ppermute | solution.py:47
  535.4 34.9 %collective-permute-start.28 = (bf16[256,2048]{1,0:T(8,128)(2,1)}, bf16[256,2048]{1,0:T(8,128)(2,1)S(1)}, u32[]{:S(2)}, u32[]{:S(2)}) collective-permute-start(bf16[256,2048]{1,0:T(8,128)(2,1)} %fusion.21), channel_id=1, source_target_pairs={{0,2},{2,0},{1,3},{3,1},{4,6},{6,4},{5,7},{7,5},{8,10},{10,8},{9,1... | collective-permute-start | bytes 3145736 | tf_op jit(solution)/shard_map/ppermute | solution.py:47
  585.3 25.4 %collective-permute-start.31 = (bf16[256,2048]{1,0:T(8,128)(2,1)S(1)}, bf16[256,2048]{1,0:T(8,128)(2,1)S(1)}, u32[]{:S(2)}, u32[]{:S(2)}) collective-permute-start(bf16[256,2048]{1,0:T(8,128)(2,1)S(1)} %fusion.22), channel_id=1, source_target_pairs={{0,2},{2,0},{1,3},{3,1},{4,6},{6,4},{5,7},{7,5},{8,10},{10,8},{9,1... | collective-permute-start | bytes 3145736 | tf_op jit(solution)/shard_map/ppermute | solution.py:47
  611.8 60.9 %all-to-all-start.4 = ((bf16[8,256,256]{2,1,0:T(8,128)(2,1)}), bf16[8,256,256]{2,1,0:T(8,128)(2,1)}, u32[]{:S(2)}, u32[]{:S(2)}) async-start(bf16[8,256,256]{2,1,0:T(8,128)(2,1)} %copy-done.80), calls=%async_computation.4 | async-start | bytes 2097152 | tf_op jit(solution)/shard_map/all_to_all | solution.py:603
  616.0 194.5 %reduce-scatter.7.cloned.1.call-start = ((), (), s32[]{:S(2)}) async-start(), calls=%async_computation.16 | async-start | bytes 7208960 | tf_op jit(solution)/shard_map/reduce_scatter | solution.py:817
  617.3 55.4 %collective-permute-start.32 = (bf16[2,2,64,1408]{3,2,1,0:T(8,128)(2,1)S(1)}, bf16[2,2,64,1408]{3,2,1,0:T(8,128)(2,1)}, u32[]{:S(2)}, u32[]{:S(2)}) collective-permute-start(bf16[2,2,64,1408]{3,2,1,0:T(8,128)(2,1)S(1)} %dynamic-slice_bitcast_fusion.6), channel_id=1, source_target_pairs={{0,4},{4,0},{1,5},{5,1},{2,6},{6,2},{3,7},{7,3},{8,12},{12,8},{9,1... | collective-permute-start | bytes 2162696 | tf_op jit(solution)/shard_map/ppermute | solution.py:47
  692.6 47.2 %all-to-all-start.5 = ((bf16[8,256,256]{2,1,0:T(8,128)(2,1)}), bf16[8,256,256]{2,1,0:T(8,128)(2,1)}, u32[]{:S(2)}, u32[]{:S(2)}) async-start(bf16[8,256,256]{2,1,0:T(8,128)(2,1)} %fusion.62), calls=%async_computation.6 | async-start | bytes 2097152 | tf_op jit(solution)/shard_map/all_to_all | solution.py:603
  709.2 113.7 %collective-permute-start.50 = (bf16[2,512,2048]{2,1,0:T(8,128)(2,1)}, bf16[2,512,2048]{2,1,0:T(8,128)(2,1)}, u32[]{:S(2)}, u32[]{:S(2)}) collective-permute-start(bf16[2,512,2048]{2,1,0:T(8,128)(2,1)} %dynamic-slice_bitcast_fusion), channel_id=1, source_target_pairs={{0,8},{8,0},{1,9},{9,1},{2,10},{10,2},{3,11},{11,3},{4,12},{12,4},... | collective-permute-start | bytes 12582920 | tf_op jit(solution)/shard_map/ppermute | solution.py:47
  739.8 55.4 %all-to-all-start.6 = ((bf16[8,256,384]{2,1,0:T(8,128)(2,1)}), bf16[8,256,384]{2,1,0:T(8,128)(2,1)}, u32[]{:S(2)}, u32[]{:S(2)}) async-start(bf16[8,256,384]{2,1,0:T(8,128)(2,1)} %pad_maximum_fusion.8), calls=%async_computation.7 | async-start | bytes 3145728 | tf_op jit(solution)/shard_map/all_to_all | solution.py:603
  747.9 62.6 %collective-permute-start.33 = (bf16[2,2,64,1408]{3,2,1,0:T(8,128)(2,1)}, bf16[2,2,64,1408]{3,2,1,0:T(8,128)(2,1)S(1)}, u32[]{:S(2)}, u32[]{:S(2)}) collective-permute-start(bf16[2,2,64,1408]{3,2,1,0:T(8,128)(2,1)} %dynamic-slice_bitcast_fusion.5), channel_id=1, source_target_pairs={{0,4},{4,0},{1,5},{5,1},{2,6},{6,2},{3,7},{7,3},{8,12},{12,8},{9,1... | collective-permute-start | bytes 2162696 | tf_op jit(solution)/shard_map/ppermute | solution.py:47
  810.5 55.3 %all-to-all-start.7 = ((bf16[8,256,384]{2,1,0:T(8,128)(2,1)}), bf16[8,256,384]{2,1,0:T(8,128)(2,1)}, u32[]{:S(2)}, u32[]{:S(2)}) async-start(bf16[8,256,384]{2,1,0:T(8,128)(2,1)} %pad_maximum_fusion.9), calls=%async_computation.10 | async-start | bytes 3145728 | tf_op jit(solution)/shard_map/all_to_all | solution.py:603
  816.5 106.0 %reduce-scatter.11.cloned.1.call-start = ((), (), s32[]{:S(2)}) async-start(), calls=%async_computation.18 | async-start | bytes 5242880 | tf_op jit(solution)/shard_map/reduce_scatter | solution.py:817
  820.8 45.0 %collective-permute-start.34 = (bf16[256,2048]{1,0:T(8,128)(2,1)}, bf16[256,2048]{1,0:T(8,128)(2,1)}, u32[]{:S(2)}, u32[]{:S(2)}) collective-permute-start(bf16[256,2048]{1,0:T(8,128)(2,1)} %fusion.23), channel_id=1, source_target_pairs={{0,2},{2,0},{1,3},{3,1},{4,6},{6,4},{5,7},{7,5},{8,10},{10,8},{9,1... | collective-permute-start | bytes 3145736 | tf_op jit(solution)/shard_map/ppermute | solution.py:47
  874.5 39.2 %collective-permute-start.35 = (bf16[1024,2560]{1,0:T(8,128)(2,1)}, bf16[1024,2560]{1,0:T(8,128)(2,1)}, u32[]{:S(2)}, u32[]{:S(2)}) collective-permute-start(bf16[1024,2560]{1,0:T(8,128)(2,1)} %convolution_convert_fusion.1), channel_id=1, source_target_pairs={{0,8},{8,0},{1,9},{9,1},{2,10},{10,2},{3,11},{11,3},{4,12},{12,4},... | collective-permute-start | bytes 15728648 | tf_op jit(solution)/shard_map/ppermute | solution.py:47
  879.8 33.9 %collective-permute-start.37 = (bf16[2,2,64,1408]{3,2,1,0:T(8,128)(2,1)S(1)}, bf16[2,2,64,1408]{3,2,1,0:T(8,128)(2,1)S(1)}, u32[]{:S(2)}, u32[]{:S(2)}) collective-permute-start(bf16[2,2,64,1408]{3,2,1,0:T(8,128)(2,1)S(1)} %dynamic-slice_bitcast_fusion.4), channel_id=1, source_target_pairs={{0,4},{4,0},{1,5},{5,1},{2,6},{6,2},{3,7},{7,3},{8,12},{12,8},{9,1... | collective-permute-start | bytes 2162696 | tf_op jit(solution)/shard_map/ppermute | solution.py:47
  884.1 29.6 %collective-permute-start.36 = (bf16[2,256,2048]{2,1,0:T(8,128)(2,1)S(1)}, bf16[2,256,2048]{2,1,0:T(8,128)(2,1)S(1)}, u32[]{:S(2)}, u32[]{:S(2)}) collective-permute-start(bf16[2,256,2048]{2,1,0:T(8,128)(2,1)S(1)} %slice_bitcast_fusion.1), channel_id=1, source_target_pairs={{0,8},{8,0},{1,9},{9,1},{2,10},{10,2},{3,11},{11,3},{4,12},{12,4},... | collective-permute-start | bytes 6291464 | tf_op jit(solution)/shard_map/ppermute | solution.py:47
  924.5 87.4 %collective-permute-start.51 = (bf16[2,64,2048]{2,1,0:T(8,128)(2,1)}, bf16[2,64,2048]{2,1,0:T(8,128)(2,1)}, u32[]{:S(2)}, u32[]{:S(2)}) collective-permute-start(bf16[2,64,2048]{2,1,0:T(8,128)(2,1)} %dynamic-slice_bitcast_fusion.9), channel_id=1, source_target_pairs={{0,4},{4,0},{1,5},{5,1},{2,6},{6,2},{3,7},{7,3},{8,12},{12,8},{9,1... | collective-permute-start | bytes 1572872 | tf_op jit(solution)/shard_map/ppermute | solution.py:47
  926.3 61.7 %collective-permute-start.43 = (bf16[3,2,64,1408]{3,2,1,0:T(8,128)(2,1)S(1)}, bf16[3,2,64,1408]{3,2,1,0:T(8,128)(2,1)S(1)}, u32[]{:S(2)}, u32[]{:S(2)}) collective-permute-start(bf16[3,2,64,1408]{3,2,1,0:T(8,128)(2,1)S(1)} %fusion.20), channel_id=1, source_target_pairs={{0,2},{2,0},{1,3},{3,1},{4,6},{6,4},{5,7},{7,5},{8,10},{10,8},{9,1... | collective-permute-start | bytes 3244040 | tf_op jit(solution)/shard_map/ppermute | solution.py:47
  929.4 29.5 %collective-permute-start.40 = (bf16[2,2,2,64,1280]{4,3,2,1,0:T(8,128)(2,1)S(1)}, bf16[2,2,2,64,1280]{4,3,2,1,0:T(8,128)(2,1)S(1)}, u32[]{:S(2)}, u32[]{:S(2)}) collective-permute-start(bf16[2,2,2,64,1280]{4,3,2,1,0:T(8,128)(2,1)S(1)} %dynamic-slice_bitcast_fusion.2), channel_id=1, source_target_pairs={{0,1},{1,0},{2,3},{3,2},{4,5},{5,4},{6,7},{7,6},{8,9},{9,8},{10,11... | collective-permute-start | bytes 3932168 | tf_op jit(solution)/shard_map/ppermute | solution.py:47
  931.5 38.1 %collective-permute-start.39 = (bf16[2,2,2,64,1280]{4,3,1,0,2:T(8,128)(2,1)S(1)}, bf16[2,2,2,64,1280]{4,3,1,0,2:T(8,128)(2,1)S(1)}, u32[]{:S(2)}, u32[]{:S(2)}) collective-permute-start(bf16[2,2,2,64,1280]{4,3,1,0,2:T(8,128)(2,1)S(1)} %dynamic-slice_bitcast_fusion.3), channel_id=1, source_target_pairs={{0,16},{16,0},{1,17},{17,1},{2,18},{18,2},{3,19},{19,3},{4,20},{20... | collective-permute-start | bytes 3932168 | tf_op jit(solution)/shard_map/ppermute | solution.py:47
  942.8 43.1 %collective-permute-start.38 = (bf16[256,2048]{1,0:T(8,128)(2,1)S(1)}, bf16[256,2048]{1,0:T(8,128)(2,1)S(1)}, u32[]{:S(2)}, u32[]{:S(2)}) collective-permute-start(bf16[256,2048]{1,0:T(8,128)(2,1)S(1)} %fusion.24), channel_id=1, source_target_pairs={{0,2},{2,0},{1,3},{3,1},{4,6},{6,4},{5,7},{7,5},{8,10},{10,8},{9,1... | collective-permute-start | bytes 3145736 | tf_op jit(solution)/shard_map/ppermute | solution.py:47
  988.4 29.9 %collective-permute-start.49 = (bf16[2,64,2560]{2,1,0:T(8,128)(2,1)S(1)}, bf16[2,64,2560]{2,1,0:T(8,128)(2,1)S(1)}, u32[]{:S(2)}, u32[]{:S(2)}) collective-permute-start(bf16[2,64,2560]{2,1,0:T(8,128)(2,1)S(1)} %fusion.30), channel_id=1, source_target_pairs={{0,4},{4,0},{1,5},{5,1},{2,6},{6,2},{3,7},{7,3},{8,12},{12,8},{9,1... | collective-permute-start | bytes 1966088 | tf_op jit(solution)/shard_map/ppermute | solution.py:47
  (128 other events, 974.4 us)
Sparse Core Ops, SparseCore 0:
  136.2 65.5 all-gather.3
  204.3 156.2 all-gather.5
  375.0 74.4 all-gather.7
  478.6 75.7 reduce-scatter.4
  611.9 84.6 reduce-scatter.8
  699.4 86.1 reduce-scatter.6
  830.6 65.7 reduce-scatter.10

commit v4 on v3

--- a/solution.py
+++ b/solution.py
@@ -553,6 +553,54 @@
     return over_rows(project_rows_kernel, x, w, [], [(rows, bf16)], "project_rows")[0]
 
 
+def rows_by_kernel(x_ref, w_ref, out_ref):
+    out_ref[...] = dot(x_ref[...], w_ref[...], ((1,), (1,)))
+
+
+def rows_by(x, w):
+    m = x.shape[0]
+    tile = min(ROW_TILE, m)
+    return pl.pallas_call(
+        rows_by_kernel,
+        grid=(m // tile,),
+        in_specs=[by_rows(tile, x.shape[1]), resident(w.shape, (0, 0))],
+        out_specs=by_rows(tile, w.shape[0]),
+        out_shape=jax.ShapeDtypeStruct((m, w.shape[0]), f32),
+        compiler_params=pltpu.CompilerParams(vmem_limit_bytes=48 << 20),
+        cost_estimate=small_cost(1 << 16),
+        name="rows_by",
+    )(x, w)
+
+
+def outer_rows_kernel(*refs):
+    total = None
+    for p in range(len(refs) // 2):
+        term = dot(refs[2 * p][...], refs[2 * p + 1][...], ((0,), (0,)))
+        total = term if total is None else total + term
+    refs[-1][...] = total.astype(bf16)
+
+
+def outer_rows(pairs):
+    width = pairs[0][0].shape[1]
+    cols = pairs[0][1].shape[1]
+    tile = min(ROW_TILE, width)
+    in_specs, operands = [], []
+    for a, b in pairs:
+        in_specs.append(pl.BlockSpec((a.shape[0], tile), lambda i: (0, i)))
+        in_specs.append(resident(b.shape, (0, 0)))
+        operands += [a, b]
+    return pl.pallas_call(
+        outer_rows_kernel,
+        grid=(width // tile,),
+        in_specs=in_specs,
+        out_specs=by_rows(tile, cols),
+        out_shape=jax.ShapeDtypeStruct((width, cols), bf16),
+        compiler_params=pltpu.CompilerParams(vmem_limit_bytes=48 << 20),
+        cost_estimate=small_cost(1 << 16),
+        name="outer_rows",
+    )(*operands)
+
+
 def outer_sum_kernel(pairs, *refs):
     out_ref = refs[-1]
     _, ny, _, nfar, _, sub, _ = out_ref.shape
@@ -739,16 +787,18 @@
     )
     gate = Gather(gate, "far", 1)
     w_out_own = over_xy(out.done())
-    up, down = flow.close(up, down, wait=[left, right, gate])
+    grad_group_0 = Group(flow.open(grad_out_all[:rows]))
+    up, down = flow.close(up, down, wait=[left, right, gate, grad_group_0])
 
     w_own = jnp.concatenate([flat(left.done()), flat(right.done())], axis=1)
     w_swap = Swap(w_own, CORE)
     up = Gather(up, "far", 1)
+    grad_group_1 = Group(flow.open(grad_out_all[rows:]))
     projected = dot(normed_one_own, w_own)
     w_other = w_swap.arrived
     projected = projected + dot(normed_one_other, w_other)
     packed_0 = pack_heads(projected, cosine, sine, 0, rows, n)
-    packed_0 = flow.close(packed_0, wait=[up])
+    packed_0 = flow.close(packed_0, wait=[up, grad_group_1])
 
     def attend_one(b, qkv_b):
         return attend(first_block[b], plain_from[b], doc_start[b], qkv_b, heads)
@@ -775,7 +825,8 @@
 
     def after_attention(b, back):
         attended = jnp.concatenate([back[s] for s in range(n)], axis=1)
-        middle = hidden_all[b * rows : (b + 1) * rows] + dot(attended, w_out, ((1,), (1,)))
+        hidden = flow.open(tokens[b]).astype(f32)
+        middle = hidden + dot(attended, w_out, ((1,), (1,)))
         inverse = rms_scale(middle)
         scaled = middle * inverse
         return attended, middle, inverse, scaled, (scaled * gain_two).astype(bf16)
@@ -798,15 +849,13 @@
     group_0 = group_0.done()
 
     gate_0, up_0, active_0 = ffn_forward(group_0, w_gate_up)
-    grad_group_0 = Group(flow.open(grad_out_all[:rows]))
-    grad_group_1 = Group(flow.open(grad_out_all[rows:]))
+    grad_group_0 = grad_group_0.done()
+    grad_group_1 = grad_group_1.done()
     active_0 = flow.close(active_0, wait=[group_1])
 
     group_1 = group_1.done()
     gate_1, up_1, active_1 = ffn_forward(flow.open(group_1), w_gate_up)
-    active_1 = flow.close(active_1, wait=[grad_group_0, grad_group_1])
-    grad_group_0 = grad_group_0.done()
-    grad_group_1 = grad_group_1.done()
+    active_1 = flow.close(active_1)
 
     outer = lambda a, b: dot(a, b, ((0,), (0,)))
     owners = (nx, nfar, ny)
@@ -845,7 +894,6 @@
         return grad_middle, grad_branch, jnp.stack(grad_heads)
 
     grad_normed_1 = GroupSum(terms_1)
-    result_0.next()
     grad_normed_0 = grad_normed_0.done()
     grad_middle_0, grad_branch_0, grad_heads_0 = before_attention(
         0, grad_normed_0, scaled_0, inverse_0
@@ -854,13 +902,12 @@
 
     grad_normed_1.next()
     grad_heads_0 = exchange(grad_heads_0)
-    d_down = Scatter(flow.open(d_down), "far", 1)
     d_up = outer_sum([(flow.open(group_0), both_0), (group_1, both_1)], part, 1, owners)
     d_up = flow.close(d_up, wait=[grad_normed_1])
 
     d_up = sum_to_owners(flow.open(d_up))
     d_gate = outer_sum([(flow.open(group_0), both_0), (group_1, both_1)], part, 0, owners)
-    d_gate, grad_heads_0 = flow.close(d_gate, grad_heads_0, wait=[d_down])
+    d_gate, grad_heads_0 = flow.close(d_gate, grad_heads_0)
 
     d_gate = sum_to_owners(flow.open(d_gate))
     grad_normed_1 = grad_normed_1.done()
@@ -888,26 +935,29 @@
 
     d_out = sum_to_owners(core_sum(*choose(d_out, CORE, 1)))
     back_0 = attend_back_one(0, qkv_0, flow.open(grad_heads_0), raw_0, lse_0)
-    d_up = Scatter(flow.open(d_up), "far", 1)
-    back_0, grad_heads_1 = flow.close(back_0, grad_heads_1)
+    d_down = Scatter(flow.open(d_down), "far", 1)
+    result_0.next()
+    back_0, grad_heads_1 = flow.close(back_0, grad_heads_1, wait=[d_down, result_0])
 
     back_0 = exchange(back_0)
     back_1 = attend_back_one(1, qkv_1, flow.open(grad_heads_1), raw_1, lse_1)
-    back_1, back_0, d_gate = flow.close(back_1, back_0, d_gate, wait=[d_up])
+    back_1, back_0 = flow.close(back_1, back_0)
 
     back_1 = exchange(back_1)
     partial_1 = project_rows(flow.open(active_1), w_down)
     grad_proj_0 = unpack_heads(flow.open(back_0), cosine[:rows], sine[:rows])
-    back_1, grad_proj_0, partial_1 = flow.close(
-        back_1, grad_proj_0, partial_1, wait=[result_0]
-    )
-
-    d_gate = Scatter(d_gate, "far", 1)
+    d_up = Scatter(flow.open(d_up), "far", 1)
+    back_1, grad_proj_0, partial_1 = flow.close(back_1, grad_proj_0, partial_1, wait=[d_up])
+
+    d_gate = Scatter(flow.open(d_gate), "far", 1)
     result_1 = GroupSum(partial_1)
     grad_proj_1 = unpack_heads(back_1, cosine[rows:], sine[rows:])
     grad_proj = jnp.concatenate([grad_proj_0, grad_proj_1], axis=0)
-    core_back = Swap(outer(normed_one_other, grad_proj).astype(bf16), CORE)
-    grad_normed_one = dot(grad_proj, w_qkv, ((1,), (1,)))
+    core_back = outer_rows(
+        [(normed_one_other[:rows], grad_proj_0), (normed_one_other[rows:], grad_proj_1)]
+    )
+    core_back = Swap(core_back, CORE)
+    grad_normed_one = rows_by(grad_proj, w_qkv)
     grad_proj, grad_normed_one = flow.close(
         grad_proj, grad_normed_one, wait=[core_back, result_1, d_gate]
     )
@@ -927,9 +977,8 @@
     left = Scatter(left.done(), "y", 2)
     right = Scatter(right.done(), "x", 0)
     attn_gain_grad = jnp.sum(grad_normed_one * scaled_one, axis=0)
-    ffn_gain_grad = jnp.sum(grad_normed_0 * scaled_0, axis=0) + jnp.sum(
-        grad_normed_1 * scaled_1, axis=0
-    )
+    late_0, late_1 = flow.open(grad_normed_0, grad_normed_1)
+    ffn_gain_grad = jnp.sum(late_0 * scaled_0, axis=0) + jnp.sum(late_1 * scaled_1, axis=0)
     gains = jnp.stack([attn_gain_grad, ffn_gain_grad])
     gains, grad_normed_one = flow.close(gains, grad_normed_one, wait=[left, right, near_back])
 
@@ -945,7 +994,7 @@
         grad_normed_one * gain_one, scaled_one, inverse_one
     )
     grad_input, gains, d_gate_up, d_down = flow.close(
-        grad_input, gains, d_gate_up, d_down, wait=[d_qkv, d_out]
+        grad_input, gains, d_gate_up, d_down, wait=[d_qkv, d_out, result_1]
     )
 
     d_qkv = Scatter(d_qkv.done(), "near", 0)

time: 1060 us -> 1010 us (0.953)
  starting transfers between devices: 115 us -> 91.6 us
  matrix products: 62.1 us -> 38.9 us
  other arithmetic: 103 us -> 90.8 us
  Pallas kernels: 347 us -> 358 us
    all_to_all x8, waiting for transfers between devices: 29.1 us -> 72.4 us  [exchange(): return lax.all_to_all(pieces, SEQ, split_axis=0, concat_axis=0, tiled=True)]
    ppermute x56, waiting for transfers between devices: 265 us -> 229 us  [swap(): lax.ppermute(values, axis, [(i, i ^ 1 << b) for i in range(lax.axis_size(...]
    ppermute x56, starting transfers between devices: 74.2 us -> 46.2 us  [swap(): lax.ppermute(values, axis, [(i, i ^ 1 << b) for i in range(lax.axis_size(...]
    dot_general x10 -> x8, matrix products: 62.1 us -> 38.9 us  [dot(): return lax.dot_general(a, b, (dims, ((), ())), preferred_element_type=f32)]
    pallas_call x0 -> x2, Pallas kernels: none -> 16.4 us  [the longest x1 11.3 us: rows_by(): pl.pallas_call(rows_by_kernel, grid=(m // tile,), in_specs=[by_rows(tile,...]
    unnamed x263 -> x269, local copies, waits for them, and re-layouts: 74.5 us -> 65.8 us
  transfers between devices with their start and end apart: 71 -> 71, of which waited for: 27 -> 34; matrix products, arithmetic and copies ran while one was open for 21% -> 18% of each run, Pallas kernels for 33% -> 32%
where the time goes in v4:
time: 1010 us; the launch traced here: 1000 us
  Pallas kernels  358 us (35%)
  waiting for transfers between devices  302 us (30%)
  local copies, waits for them, and re-layouts  104 us (10%)
  starting transfers between devices  91.6 us (9%)
  other arithmetic  90.8 us (9%)
  matrix products  38.9 us (4%)
  between operations  16.6 us (2%)
    ppermute x56, waiting for transfers between devices, swap(): lax.ppermute(values, axis, [(i, i ^ 1 << b) for i in range(lax.axis_size(...  229 us
    pallas_call x8, Pallas kernels, over_rows(): pl.pallas_call(with_weights(kernel), grid=(m // tile,), in_specs=[by_rows...  131 us
    all_to_all x8, waiting for transfers between devices, exchange(): return lax.all_to_all(pieces, SEQ, split_axis=0, concat_axis=0, tiled=True)  72.4 us
    unnamed x269, local copies, waits for them, and re-layouts  65.8 us
    pallas_call x2, Pallas kernels, attend_back(): pl.pallas_call(functools.partial(attend_back_kernel, heads), grid=(n,), o...  65.4 us
    pallas_call x3, Pallas kernels, outer_sum(): pl.pallas_call(functools.partial(outer_sum_kernel, len(pairs)), grid=(2 *...  53.5 us
    pallas_call x2, Pallas kernels, attend(): pl.pallas_call(functools.partial(attend_kernel, heads), grid=(n,), out_sh...  47.1 us
    ppermute x56, starting transfers between devices, swap(): lax.ppermute(values, axis, [(i, i ^ 1 << b) for i in range(lax.axis_size(...  46.2 us
  transfers between devices with their start and end apart: 71, of which 34 were waited for; matrix products, arithmetic and copies ran while one was open for 18% of the time, Pallas kernels for 32%

profile of v4, /device:TPU:0, one launch (start us, length us, event | category | flops | bytes accessed | tf_op | source)
XLA Modules:
  0.0 1002.4 jit_solution(3388410575798347968)
XLA Ops:
  34.9 28.9 %collective-permute-done.1 = bf16[2,64,2560]{2,1,0:T(8,128)(2,1)} collective-permute-done((bf16[2,64,2560]{2,1,0:T(8,128)(2,1)}, bf16[2,64,2560]{2,1,0:T(8,128)(2,1)}, u32[]{:S(2)}, u32[]{:S(2)}) %collective-permute-start.1) | collective-permute-done | bytes 655392 | tf_op jit(solution)/shard_map/ppermute | solution.py:47
  75.0 12.0 %collective-permute-done.7 = bf16[2,64,2048]{2,1,0:T(8,128)(2,1)S(1)} collective-permute-done((bf16[2,64,2048]{2,1,0:T(8,128)(2,1)S(1)}, bf16[2,64,2048]{2,1,0:T(8,128)(2,1)S(1)}, u32[]{:S(2)}, u32[]{:S(2)}) %collective-permute-start.7) | collective-permute-done | bytes 524320 | tf_op jit(solution)/shard_map/ppermute | solution.py:47
  94.3 33.4 %collective-permute-done.10 = bf16[2,2,64,1408]{3,2,1,0:T(8,128)(2,1)S(1)} collective-permute-done((bf16[2,2,64,1408]{3,2,1,0:T(8,128)(2,1)S(1)}, bf16[2,2,64,1408]{3,2,1,0:T(8,128)(2,1)S(1)}, u32[]{:S(2)}, u32[]{:S(2)}) %collective-permute-start.10) | collective-permute-done | bytes 720928 | tf_op jit(solution)/shard_map/ppermute | solution.py:47
  143.9 5.0 fusion.96
  149.0 4.8 convolution_add_fusion.q_ref.k_ref.v_ref
  153.8 7.2 pack_heads.2
  161.1 16.4 %collective-permute-done.13 = bf16[2,2,64,1408]{3,2,1,0:T(8,128)(2,1)} collective-permute-done((bf16[2,2,64,1408]{3,2,1,0:T(8,128)(2,1)}, bf16[2,2,64,1408]{3,2,1,0:T(8,128)(2,1)}, u32[]{:S(2)}, u32[]{:S(2)}) %collective-permute-start.13) | collective-permute-done | bytes 720928 | tf_op jit(solution)/shard_map/ppermute | solution.py:47
  181.2 4.9 all-to-all-start
  190.9 7.1 pack_heads.3
  200.5 14.0 %interleave.2 = bf16[2,2,4,1,128,2560]{5,4,3,2,1,0:T(8,128)(2,1)} custom-call(s32[1]{0:T(128)} %bitcast.53.core_ref, bf16[2,1,4,128,2560]{4,3,2,1,0:T(8,128)(2,1)S(1)} %copy-done.7, bf16[2,1,4,128,2560]{4,3,2,1,0:T(8,128)(2,1)} %bitcast.57.other_ref), custom_call_target="tpu_custom_call" | custom-call | bytes 65536 | tf_op jit(solution)/shard_map/interleave/pallas_call | solution.py:428
  214.5 8.6 all-to-all-done.qkv_ref
  227.1 18.5 %attend.2 = (bf16[8,256,256]{2,1,0:T(8,128)(2,1)S(1)}, f32[8,256,256]{2,1,0:T(8,128)S(1)}, f32[8,8,1024]{2,1,0:T(8,128)S(1)}) custom-call(s32[8]{0:T(128)S(1)} %get-tuple-element.436.lo_ref, s32[8]{0:T(128)S(1)} %get-tuple-element.427.hi_ref, s32[8,1,256]{2,1,0:T(1,128)S(1)} %bitcast.555, bf16[8,256,384]{2,1,0:T(8,128)(2,1)S(1)} %all-to-all-done.qkv_ref), custom_call_target="tpu_custom_call" | custom-call | bytes 1048576 | tf_op jit(solution)/shard_map/attend/pallas_call | solution.py:194
  248.7 15.2 %all-to-all-done.1.qkv_ref = bf16[8,256,384]{2,1,0:T(8,128)(2,1)S(1)} async-done(((bf16[8,256,384]{2,1,0:T(8,128)(2,1)}), bf16[8,256,384]{2,1,0:T(8,128)(2,1)S(1)}, u32[]{:S(2)}, u32[]{:S(2)}) %all-to-all-start.1) | async-done | bytes 1572896 | tf_op jit(solution)/shard_map/all_to_all | solution.py:651
  270.9 28.6 %attend.3 = (bf16[8,256,256]{2,1,0:T(8,128)(2,1)}, f32[8,256,256]{2,1,0:T(8,128)S(1)}, f32[8,8,1024]{2,1,0:T(8,128)S(1)}) custom-call(s32[8]{0:T(128)S(1)} %get-tuple-element.435.lo_ref, s32[8]{0:T(128)S(1)} %get-tuple-element.428.hi_ref, s32[8,1,256]{2,1,0:T(1,128)S(1)} %bitcast.553, bf16[8,256,384]{2,1,0:T(8,128)(2,1)S(1)} %all-to-all-done.1.qkv_ref), custom_call_target="tpu_custom_call" | custom-call | bytes 1048576 | tf_op jit(solution)/shard_map/attend/pallas_call | solution.py:194
  300.8 6.0 all-to-all-start.3
  312.1 12.5 %interleave.3 = bf16[2,2,4,2,64,2048]{5,4,3,2,1,0:T(8,128)(2,1)} custom-call(s32[1]{0:T(128)} %bitcast.53.core_ref, bf16[2,2,4,64,2048]{4,3,2,1,0:T(8,128)(2,1)S(1)} %bitcast.552, bf16[2,2,4,64,2048]{4,3,2,1,0:T(8,128)(2,1)} %bitcast.73.other_ref), custom_call_target="tpu_custom_call" | custom-call | bytes 65536 | tf_op jit(solution)/shard_map/interleave/pallas_call | solution.py:428
  324.7 6.3 multiply_reduce_fusion.8
  332.6 16.8 %all-to-all-done.3 = bf16[8,256,256]{2,1,0:T(8,128)(2,1)S(1)} async-done(((bf16[8,256,256]{2,1,0:T(8,128)(2,1)}), bf16[8,256,256]{2,1,0:T(8,128)(2,1)S(1)}, u32[]{:S(2)}, u32[]{:S(2)}) %all-to-all-start.3) | async-done | bytes 1048608 | tf_op jit(solution)/shard_map/all_to_all | solution.py:651
  349.5 6.5 multiply_reduce_fusion.7
  358.6 5.3 collective-permute-done.18
  363.9 22.3 %collective-permute-done.17 = bf16[256,2048]{1,0:T(8,128)(2,1)S(1)} collective-permute-done((bf16[256,2048]{1,0:T(8,128)(2,1)S(1)}, bf16[256,2048]{1,0:T(8,128)(2,1)S(1)}, u32[]{:S(2)}, u32[]{:S(2)}) %collective-permute-start.17) | collective-permute-done | bytes 1048608 | tf_op jit(solution)/shard_map/ppermute | solution.py:47
  389.8 8.7 reduce-scatter.5.cloned.1.call-start
  409.3 20.7 %ffn_forward.2 = (f32[1024,1408]{1,0:T(8,128)}, f32[1024,1408]{1,0:T(8,128)}, bf16[1024,1408]{1,0:T(8,128)(2,1)S(1)}) custom-call(bf16[1024,2048]{1,0:T(8,128)(2,1)} %copy-done, bf16[4,2,2,2,64,2816]{5,4,3,2,1,0:T(8,128)(2,1)} %bitcast.557), custom_call_target="tpu_custom_call" | custom-call | bytes 65536 | tf_op jit(solution)/shard_map/ffn_forward/pallas_call | solution.py:499
  440.7 21.0 %ffn_forward.3 = (f32[1024,1408]{1,0:T(8,128)}, f32[1024,1408]{1,0:T(8,128)}, bf16[1024,1408]{1,0:T(8,128)(2,1)S(1)}) custom-call(bf16[1024,2048]{1,0:T(8,128)(2,1)} %copy-done.32, bf16[4,2,2,2,64,2816]{5,4,3,2,1,0:T(8,128)(2,1)} %bitcast.558), custom_call_target="tpu_custom_call" | custom-call | bytes 65536 | tf_op jit(solution)/shard_map/ffn_forward/pallas_call | solution.py:499
  461.7 16.6 %outer_sum.3 = bf16[2,2,2,2,2,64,1408]{6,5,4,3,2,1,0:T(8,128)(2,1)} custom-call(bf16[1024,2048]{1,0:T(8,128)(2,1)} %copy-done.5, bf16[1024,1408]{1,0:T(8,128)(2,1)S(1)} %copy-done.17, bf16[1024,2048]{1,0:T(8,128)(2,1)} %copy-done.3, bf16[1024,1408]{1,0:T(8,128)(2,1)S(1)} %get-tuple-element.298.refs_3_.x_ref), custom_call_target="tpu_custom_call" | custom-call | bytes 65536 | tf_op jit(solution)/shard_map/outer_sum/pallas_call | solution.py:628
  482.0 14.3 %ffn_backward.2.x_ref.refs_1_ = bf16[1024,2816]{1,0:T(8,128)(2,1)} custom-call(bf16[1024,2048]{1,0:T(8,128)(2,1)S(1)} %copy-done.6, bf16[4,2,2,2,64,1408]{5,4,3,2,1,0:T(8,128)(2,1)} %bitcast.561, f32[1024,1408]{1,0:T(8,128)} %get-tuple-element.250.refs_0_, f32[1024,1408]{1,0:T(8,128)} %get-tuple-element.251.refs_1_), custom_call_target="tpu_custom_call" | custom-call | bytes 65536 | tf_op jit(solution)/shard_map/ffn_backward/pallas_call | solution.py:499
  496.3 18.9 %project_rows.4 = bf16[1024,2048]{1,0:T(8,128)(2,1)S(1)} custom-call(bf16[1024,2816]{1,0:T(8,128)(2,1)} %ffn_backward.2.x_ref.refs_1_, bf16[4,2,2,2,64,2816]{5,4,3,2,1,0:T(8,128)(2,1)} %bitcast.559), custom_call_target="tpu_custom_call" | custom-call | bytes 65536 | tf_op jit(solution)/shard_map/project_rows/pallas_call | solution.py:499
  518.2 11.3 %project_rows.5 = bf16[1024,2048]{1,0:T(8,128)(2,1)} custom-call(bf16[1024,1408]{1,0:T(8,128)(2,1)S(1)} %copy-done.17, bf16[4,2,2,2,64,1408]{5,4,3,2,1,0:T(8,128)(2,1)} %bitcast.562), custom_call_target="tpu_custom_call" | custom-call | bytes 65536 | tf_op jit(solution)/shard_map/project_rows/pallas_call | solution.py:499
  537.3 14.6 %ffn_backward.3.x_ref.refs_3_ = bf16[1024,2816]{1,0:T(8,128)(2,1)} custom-call(bf16[1024,2048]{1,0:T(8,128)(2,1)S(1)} %copy-done.4, bf16[4,2,2,2,64,1408]{5,4,3,2,1,0:T(8,128)(2,1)} %bitcast.563, f32[1024,1408]{1,0:T(8,128)} %get-tuple-element.258.refs_0_, f32[1024,1408]{1,0:T(8,128)} %get-tuple-element.259.refs_1_), custom_call_target="tpu_custom_call" | custom-call | bytes 65536 | tf_op jit(solution)/shard_map/ffn_backward/pallas_call | solution.py:499
  551.8 19.1 %project_rows.6 = bf16[1024,2048]{1,0:T(8,128)(2,1)S(1)} custom-call(bf16[1024,2816]{1,0:T(8,128)(2,1)} %ffn_backward.3.x_ref.refs_3_, bf16[4,2,2,2,64,2816]{5,4,3,2,1,0:T(8,128)(2,1)} %bitcast.560), custom_call_target="tpu_custom_call" | custom-call | bytes 65536 | tf_op jit(solution)/shard_map/project_rows/pallas_call | solution.py:499
  589.8 18.7 %outer_sum.4 = bf16[2,2,2,2,2,64,1408]{6,5,4,3,2,1,0:T(8,128)(2,1)} custom-call(bf16[1024,2048]{1,0:T(8,128)(2,1)S(1)} %copy-done.1, bf16[1024,2816]{1,0:T(8,128)(2,1)} %ffn_backward.2.x_ref.refs_1_, bf16[1024,2048]{1,0:T(8,128)(2,1)} %copy-done.32, bf16[1024,2816]{1,0:T(8,128)(2,1)} %ffn_backward.3.x_ref.refs_3_), custom_call_target="tpu_custom_call" | custom-call | bytes 65536 | tf_op jit(solution)/shard_map/outer_sum/pallas_call | solution.py:628
  619.8 18.2 %outer_sum.5 = bf16[2,2,2,2,2,64,1408]{6,5,4,3,2,1,0:T(8,128)(2,1)} custom-call(bf16[1024,2048]{1,0:T(8,128)(2,1)S(1)} %copy-done.2, bf16[1024,2816]{1,0:T(8,128)(2,1)} %ffn_backward.2.x_ref.refs_1_, bf16[1024,2048]{1,0:T(8,128)(2,1)} %copy-done.32, bf16[1024,2816]{1,0:T(8,128)(2,1)} %ffn_backward.3.x_ref.refs_3_), custom_call_target="tpu_custom_call" | custom-call | bytes 65536 | tf_op jit(solution)/shard_map/outer_sum/pallas_call | solution.py:628
  668.1 6.4 convolution_convert_fusion
  683.5 27.1 %attend_back.2 = (bf16[8,256,256]{2,1,0:T(8,128)(2,1)S(1)}, bf16[8,256,128]{2,1,0:T(8,128)(2,1)S(1)}) custom-call(s32[8]{0:T(128)S(1)} %get-tuple-element.436.lo_ref, s32[8]{0:T(128)S(1)} %get-tuple-element.427.hi_ref, s32[8,1,256]{2,1,0:T(1,128)S(1)} %bitcast.556, bf16[8,256,384]{2,1,0:T(8,128)(2,1)S(1)} %copy-done.13, ...), custom_call_target="tpu_custom_call" | custom-call | bytes 1048576 | tf_op jit(solution)/shard_map/attend_back/pallas_call | solution.py:302
  711.9 12.6 %collective-permute-done.32 = bf16[2,2,64,1408]{3,2,1,0:T(8,128)(2,1)} collective-permute-done((bf16[2,2,64,1408]{3,2,1,0:T(8,128)(2,1)S(1)}, bf16[2,2,64,1408]{3,2,1,0:T(8,128)(2,1)}, u32[]{:S(2)}, u32[]{:S(2)}) %collective-permute-start.32) | collective-permute-done | bytes 720928 | tf_op jit(solution)/shard_map/ppermute | solution.py:47
  728.2 38.3 %attend_back.3 = (bf16[8,256,256]{2,1,0:T(8,128)(2,1)S(1)}, bf16[8,256,128]{2,1,0:T(8,128)(2,1)S(1)}) custom-call(s32[8]{0:T(128)S(1)} %get-tuple-element.435.lo_ref, s32[8]{0:T(128)S(1)} %get-tuple-element.428.hi_ref, s32[8,1,256]{2,1,0:T(1,128)S(1)} %bitcast.554, bf16[8,256,384]{2,1,0:T(8,128)(2,1)S(1)} %copy-done.11, ...), custom_call_target="tpu_custom_call" | custom-call | bytes 1048576 | tf_op jit(solution)/shard_map/attend_back/pallas_call | solution.py:302
  767.8 6.0 all-to-all-start.7
  774.1 5.4 fusion
  788.1 11.3 %project_rows.7 = bf16[1024,2048]{1,0:T(8,128)(2,1)} custom-call(bf16[1024,1408]{1,0:T(8,128)(2,1)S(1)} %copy-done.15, bf16[4,2,2,2,64,1408]{5,4,3,2,1,0:T(8,128)(2,1)} %bitcast.564), custom_call_target="tpu_custom_call" | custom-call | bytes 65536 | tf_op jit(solution)/shard_map/project_rows/pallas_call | solution.py:499
  800.5 27.3 %all-to-all-done.7.in_ref = bf16[8,256,384]{2,1,0:T(8,128)(2,1)} async-done(((bf16[8,256,384]{2,1,0:T(8,128)(2,1)}), bf16[8,256,384]{2,1,0:T(8,128)(2,1)}, u32[]{:S(2)}, u32[]{:S(2)}) %all-to-all-start.7) | async-done | bytes 1572896 | tf_op jit(solution)/shard_map/all_to_all | solution.py:651
  827.8 12.5 %collective-permute-done.34 = bf16[2,2,64,1408]{3,2,1,0:T(8,128)(2,1)} collective-permute-done((bf16[2,2,64,1408]{3,2,1,0:T(8,128)(2,1)}, bf16[2,2,64,1408]{3,2,1,0:T(8,128)(2,1)}, u32[]{:S(2)}, u32[]{:S(2)}) %collective-permute-start.34) | collective-permute-done | bytes 720928 | tf_op jit(solution)/shard_map/ppermute | solution.py:47
  842.9 5.1 outer_rows.1
  854.0 11.3 %rows_by.1 = f32[512,2048]{1,0:T(8,128)} custom-call(bf16[512,2560]{1,0:T(8,128)(2,1)S(1)} %pad_maximum_fusion.5.x_ref, bf16[2048,2560]{1,0:T(8,128)(2,1)} %bitcast.565), custom_call_target="tpu_custom_call" | custom-call | bytes 65536 | tf_op jit(solution)/shard_map/rows_by/pallas_call | solution.py:563
  867.9 18.6 %collective-permute-done.37 = bf16[2,2,64,1408]{3,2,1,0:T(8,128)(2,1)S(1)} collective-permute-done((bf16[2,2,64,1408]{3,2,1,0:T(8,128)(2,1)S(1)}, bf16[2,2,64,1408]{3,2,1,0:T(8,128)(2,1)S(1)}, u32[]{:S(2)}, u32[]{:S(2)}) %collective-permute-start.37) | collective-permute-done | bytes 720928 | tf_op jit(solution)/shard_map/ppermute | solution.py:47
  886.5 5.2 add_convert_fusion
  908.7 22.7 %collective-permute-done.39 = bf16[2,2,2,64,1280]{4,3,2,1,0:T(8,128)(2,1)S(1)} collective-permute-done((bf16[2,2,2,64,1280]{4,3,2,1,0:T(8,128)(2,1)S(1)}, bf16[2,2,2,64,1280]{4,3,2,1,0:T(8,128)(2,1)S(1)}, u32[]{:S(2)}, u32[]{:S(2)}) %collective-permute-start.39) | collective-permute-done | bytes 1310752 | tf_op jit(solution)/shard_map/ppermute | solution.py:47
  940.9 7.5 collective-permute-done.41
  966.2 13.7 %collective-permute-done.48 = bf16[2,64,2560]{2,1,0:T(8,128)(2,1)} collective-permute-done((bf16[2,64,2560]{2,1,0:T(8,128)(2,1)}, bf16[2,64,2560]{2,1,0:T(8,128)(2,1)}, u32[]{:S(2)}, u32[]{:S(2)}) %collective-permute-start.48) | collective-permute-done | bytes 655392 | tf_op jit(solution)/shard_map/ppermute | solution.py:47
  (562 shorter events, 292.4 us)
Async XLA Ops:
  7.2 241.6 %all-gather.4.cloned.1.call-start = ((), (), s32[]{:S(2)}) async-start(), calls=%async_computation.12 | async-start | bytes 5242880 | tf_op jit(solution)/shard_map/all_gather | solution.py:780
  7.2 19.1 %collective-permute-start = (bf16[64,2560]{1,0:T(8,128)(2,1)}, bf16[64,2560]{1,0:T(8,128)(2,1)}, u32[]{:S(2)}, u32[]{:S(2)}) collective-permute-start(bf16[64,2560]{1,0:T(8,128)(2,1)} %param.12), channel_id=1, source_target_pairs={{0,2},{2,0},{1,3},{3,1},{4,6},{6,4},{5,7},{7,5},{8,10},{10,8},{9,1... | collective-permute-start | bytes 983048 | tf_op jit(solution)/shard_map/ppermute | solution.py:47
  10.3 24.5 %collective-permute-start.3 = (bf16[64,2048]{1,0:T(8,128)(2,1)}, bf16[64,2048]{1,0:T(8,128)(2,1)}, u32[]{:S(2)}, u32[]{:S(2)}) collective-permute-start(bf16[64,2048]{1,0:T(8,128)(2,1)} %param.13), channel_id=1, source_target_pairs={{0,4},{4,0},{1,5},{5,1},{2,6},{6,2},{3,7},{7,3},{8,12},{12,8},{9,1... | collective-permute-start | bytes 786440 | tf_op jit(solution)/shard_map/ppermute | solution.py:47
  26.4 39.4 %collective-permute-start.2 = (bf16[3,64,2816]{2,1,0:T(8,128)(2,1)}, bf16[3,64,2816]{2,1,0:T(8,128)(2,1)}, u32[]{:S(2)}, u32[]{:S(2)}) collective-permute-start(bf16[3,64,2816]{2,1,0:T(8,128)(2,1)} %pad_maximum_fusion.15), channel_id=1, source_target_pairs={{0,2},{2,0},{1,3},{3,1},{4,6},{6,4},{5,7},{7,5},{8,10},{10,8},{9,1... | collective-permute-start | bytes 3244040 | tf_op jit(solution)/shard_map/ppermute | solution.py:47
  28.7 35.0 %collective-permute-start.1 = (bf16[2,64,2560]{2,1,0:T(8,128)(2,1)}, bf16[2,64,2560]{2,1,0:T(8,128)(2,1)}, u32[]{:S(2)}, u32[]{:S(2)}) collective-permute-start(bf16[2,64,2560]{2,1,0:T(8,128)(2,1)} %pad_maximum_fusion.24), channel_id=1, source_target_pairs={{0,4},{4,0},{1,5},{5,1},{2,6},{6,2},{3,7},{7,3},{8,12},{12,8},{9,1... | collective-permute-start | bytes 1966088 | tf_op jit(solution)/shard_map/ppermute | solution.py:47
  67.6 19.8 %collective-permute-start.6 = (bf16[3,2,64,1408]{3,2,1,0:T(8,128)(2,1)S(1)}, bf16[3,2,64,1408]{3,2,1,0:T(8,128)(2,1)S(1)}, u32[]{:S(2)}, u32[]{:S(2)}) collective-permute-start(bf16[3,2,64,1408]{3,2,1,0:T(8,128)(2,1)S(1)} %pad_maximum_fusion.16), channel_id=1, source_target_pairs={{0,8},{8,0},{1,9},{9,1},{2,10},{10,2},{3,11},{11,3},{4,12},{12,4},... | collective-permute-start | bytes 3244040 | tf_op jit(solution)/shard_map/ppermute | solution.py:47
  87.7 42.2 %collective-permute-start.9 = (bf16[2,2,2,64,1280]{4,3,2,1,0:T(8,128)(2,1)S(1)}, bf16[2,2,2,64,1280]{4,3,2,1,0:T(8,128)(2,1)S(1)}, u32[]{:S(2)}, u32[]{:S(2)}) collective-permute-start(bf16[2,2,2,64,1280]{4,3,2,1,0:T(8,128)(2,1)S(1)} %pad_maximum_fusion.14), channel_id=1, source_target_pairs={{0,1},{1,0},{2,3},{3,2},{4,5},{5,4},{6,7},{7,6},{8,9},{9,8},{10,11... | collective-permute-start | bytes 3932168 | tf_op jit(solution)/shard_map/ppermute | solution.py:47
  88.6 41.3 %collective-permute-start.8 = (bf16[2,2,2,64,1280]{4,3,2,1,0:T(8,128)(2,1)S(1)}, bf16[2,2,2,64,1280]{4,3,2,1,0:T(8,128)(2,1)S(1)}, u32[]{:S(2)}, u32[]{:S(2)}) collective-permute-start(bf16[2,2,2,64,1280]{4,3,2,1,0:T(8,128)(2,1)S(1)} %pad_maximum_fusion.13), channel_id=1, source_target_pairs={{0,16},{16,0},{1,17},{17,1},{2,18},{18,2},{3,19},{19,3},{4,20},{20... | collective-permute-start | bytes 3932168 | tf_op jit(solution)/shard_map/ppermute | solution.py:47
  90.2 39.8 %collective-permute-start.11 = (bf16[256,2048]{1,0:T(8,128)(2,1)}, bf16[256,2048]{1,0:T(8,128)(2,1)}, u32[]{:S(2)}, u32[]{:S(2)}) collective-permute-start(bf16[256,2048]{1,0:T(8,128)(2,1)} %get-tuple-element.188), channel_id=1, source_target_pairs={{0,2},{2,0},{1,3},{3,1},{4,6},{6,4},{5,7},{7,5},{8,10},{10,8},{9,1... | collective-permute-start | bytes 3145736 | tf_op jit(solution)/shard_map/ppermute | solution.py:47
  90.9 36.8 %collective-permute-start.10 = (bf16[2,2,64,1408]{3,2,1,0:T(8,128)(2,1)S(1)}, bf16[2,2,64,1408]{3,2,1,0:T(8,128)(2,1)S(1)}, u32[]{:S(2)}, u32[]{:S(2)}) collective-permute-start(bf16[2,2,64,1408]{3,2,1,0:T(8,128)(2,1)S(1)} %pad_maximum_fusion.22), channel_id=1, source_target_pairs={{0,4},{4,0},{1,5},{5,1},{2,6},{6,2},{3,7},{7,3},{8,12},{12,8},{9,1... | collective-permute-start | bytes 2162696 | tf_op jit(solution)/shard_map/ppermute | solution.py:47
  136.1 250.0 %all-gather.6.cloned.1.call-start = ((), (), s32[]{:S(2)}) async-start(), calls=%async_computation.13 | async-start | bytes 14417920 | tf_op jit(solution)/shard_map/all_gather | solution.py:780
  136.4 41.8 %collective-permute-start.14 = (bf16[256,2048]{1,0:T(8,128)(2,1)}, bf16[256,2048]{1,0:T(8,128)(2,1)}, u32[]{:S(2)}, u32[]{:S(2)}) collective-permute-start(bf16[256,2048]{1,0:T(8,128)(2,1)} %get-tuple-element.196), channel_id=1, source_target_pairs={{0,2},{2,0},{1,3},{3,1},{4,6},{6,4},{5,7},{7,5},{8,10},{10,8},{9,1... | collective-permute-start | bytes 3145736 | tf_op jit(solution)/shard_map/ppermute | solution.py:47
  138.6 38.9 %collective-permute-start.13 = (bf16[2,2,64,1408]{3,2,1,0:T(8,128)(2,1)}, bf16[2,2,64,1408]{3,2,1,0:T(8,128)(2,1)}, u32[]{:S(2)}, u32[]{:S(2)}) collective-permute-start(bf16[2,2,64,1408]{3,2,1,0:T(8,128)(2,1)} %pad_maximum_fusion.20), channel_id=1, source_target_pairs={{0,4},{4,0},{1,5},{5,1},{2,6},{6,2},{3,7},{7,3},{8,12},{12,8},{9,1... | collective-permute-start | bytes 2162696 | tf_op jit(solution)/shard_map/ppermute | solution.py:47
  181.2 41.9 %all-to-all-start = ((bf16[8,256,384]{2,1,0:T(8,128)(2,1)}), bf16[8,256,384]{2,1,0:T(8,128)(2,1)S(1)}, u32[]{:S(2)}, u32[]{:S(2)}) async-start(bf16[8,256,384]{2,1,0:T(8,128)(2,1)} %pack_heads.2), calls=%async_computation | async-start | bytes 3145728 | tf_op jit(solution)/shard_map/all_to_all | solution.py:651
  223.1 40.9 %all-to-all-start.1 = ((bf16[8,256,384]{2,1,0:T(8,128)(2,1)}), bf16[8,256,384]{2,1,0:T(8,128)(2,1)S(1)}, u32[]{:S(2)}, u32[]{:S(2)}) async-start(bf16[8,256,384]{2,1,0:T(8,128)(2,1)} %pack_heads.3), calls=%async_computation.1 | async-start | bytes 3145728 | tf_op jit(solution)/shard_map/all_to_all | solution.py:651
  263.9 36.8 %collective-permute-start.15 = (bf16[4,2,2,64,2048]{4,3,2,1,0:T(8,128)(2,1)}, bf16[4,2,2,64,2048]{4,3,2,1,0:T(8,128)(2,1)}, u32[]{:S(2)}, u32[]{:S(2)}) collective-permute-start(bf16[4,2,2,64,2048]{4,3,2,1,0:T(8,128)(2,1)} %bitcast.551), channel_id=1, source_target_pairs={{0,8},{8,0},{1,9},{9,1},{2,10},{10,2},{3,11},{11,3},{4,12},{12,4},... | collective-permute-start | bytes 12582920 | tf_op jit(solution)/shard_map/ppermute | solution.py:47
  263.9 36.8 %all-to-all-start.2 = ((bf16[8,256,256]{2,1,0:T(8,128)(2,1)}), bf16[8,256,256]{2,1,0:T(8,128)(2,1)S(1)}, u32[]{:S(2)}, u32[]{:S(2)}) async-start(bf16[8,256,256]{2,1,0:T(8,128)(2,1)} %copy-done.23), calls=%async_computation.2 | async-start | bytes 2097152 | tf_op jit(solution)/shard_map/all_to_all | solution.py:651
  300.8 48.6 %all-to-all-start.3 = ((bf16[8,256,256]{2,1,0:T(8,128)(2,1)}), bf16[8,256,256]{2,1,0:T(8,128)(2,1)S(1)}, u32[]{:S(2)}, u32[]{:S(2)}) async-start(bf16[8,256,256]{2,1,0:T(8,128)(2,1)} %get-tuple-element.222), calls=%async_computation.3 | async-start | bytes 2097152 | tf_op jit(solution)/shard_map/all_to_all | solution.py:651
  306.8 173.1 %all-gather.8.cloned.1.call-start = ((), (), s32[]{:S(2)}) async-start(), calls=%async_computation.14 | async-start | bytes 7208960 | tf_op jit(solution)/shard_map/all_gather | solution.py:780
  307.0 56.9 %collective-permute-start.18 = (bf16[2,2,64,1408]{3,2,1,0:T(8,128)(2,1)}, bf16[2,2,64,1408]{3,2,1,0:T(8,128)(2,1)}, u32[]{:S(2)}, u32[]{:S(2)}) collective-permute-start(bf16[2,2,64,1408]{3,2,1,0:T(8,128)(2,1)} %pad_maximum_fusion.21), channel_id=1, source_target_pairs={{0,4},{4,0},{1,5},{5,1},{2,6},{6,2},{3,7},{7,3},{8,12},{12,8},{9,1... | collective-permute-start | bytes 2162696 | tf_op jit(solution)/shard_map/ppermute | solution.py:47
  349.4 36.7 %collective-permute-start.17 = (bf16[256,2048]{1,0:T(8,128)(2,1)S(1)}, bf16[256,2048]{1,0:T(8,128)(2,1)S(1)}, u32[]{:S(2)}, u32[]{:S(2)}) collective-permute-start(bf16[256,2048]{1,0:T(8,128)(2,1)S(1)} %multiply_convert_fusion.2), channel_id=1, source_target_pairs={{0,2},{2,0},{1,3},{3,1},{4,6},{6,4},{5,7},{7,5},{8,10},{10,8},{9,1... | collective-permute-start | bytes 3145736 | tf_op jit(solution)/shard_map/ppermute | solution.py:47
  389.8 289.5 %reduce-scatter.5.cloned.1.call-start = ((), (), s32[]{:S(2)}) async-start(), calls=%async_computation.15 | async-start | bytes 7208960 | tf_op jit(solution)/shard_map/reduce_scatter | solution.py:866
  404.9 25.7 %collective-permute-start.20 = (bf16[256,2048]{1,0:T(8,128)(2,1)}, bf16[256,2048]{1,0:T(8,128)(2,1)}, u32[]{:S(2)}, u32[]{:S(2)}) collective-permute-start(bf16[256,2048]{1,0:T(8,128)(2,1)} %multiply_convert_fusion.1), channel_id=1, source_target_pairs={{0,2},{2,0},{1,3},{3,1},{4,6},{6,4},{5,7},{7,5},{8,10},{10,8},{9,1... | collective-permute-start | bytes 3145736 | tf_op jit(solution)/shard_map/ppermute | solution.py:47
  405.1 27.3 %collective-permute-start.24 = (bf16[256,2048]{1,0:T(8,128)(2,1)}, bf16[256,2048]{1,0:T(8,128)(2,1)}, u32[]{:S(2)}, u32[]{:S(2)}) collective-permute-start(bf16[256,2048]{1,0:T(8,128)(2,1)} %collective-permute-done.14), channel_id=1, source_target_pairs={{0,8},{8,0},{1,9},{9,1},{2,10},{10,2},{3,11},{11,3},{4,12},{12,4},... | collective-permute-start | bytes 3145736 | tf_op jit(solution)/shard_map/ppermute | solution.py:47
  405.8 30.0 %collective-permute-start.25 = (bf16[256,2048]{1,0:T(8,128)(2,1)}, bf16[256,2048]{1,0:T(8,128)(2,1)}, u32[]{:S(2)}, u32[]{:S(2)}) collective-permute-start(bf16[256,2048]{1,0:T(8,128)(2,1)} %multiply_convert_fusion.1), channel_id=1, source_target_pairs={{0,8},{8,0},{1,9},{9,1},{2,10},{10,2},{3,11},{11,3},{4,12},{12,4},... | collective-permute-start | bytes 3145736 | tf_op jit(solution)/shard_map/ppermute | solution.py:47
  518.2 263.7 %reduce-scatter.7.cloned.1.call-start = ((), (), s32[]{:S(2)}) async-start(), calls=%async_computation.16 | async-start | bytes 7208960 | tf_op jit(solution)/shard_map/reduce_scatter | solution.py:866
  531.8 39.2 %collective-permute-start.29 = (bf16[2,256,2048]{2,1,0:T(8,128)(2,1)S(1)}, bf16[2,256,2048]{2,1,0:T(8,128)(2,1)S(1)}, u32[]{:S(2)}, u32[]{:S(2)}) collective-permute-start(bf16[2,256,2048]{2,1,0:T(8,128)(2,1)S(1)} %slice_bitcast_fusion.8), channel_id=1, source_target_pairs={{0,8},{8,0},{1,9},{9,1},{2,10},{10,2},{3,11},{11,3},{4,12},{12,4},... | collective-permute-start | bytes 6291464 | tf_op jit(solution)/shard_map/ppermute | solution.py:47
  535.4 35.6 %collective-permute-start.28 = (bf16[256,2048]{1,0:T(8,128)(2,1)S(1)}, bf16[256,2048]{1,0:T(8,128)(2,1)S(1)}, u32[]{:S(2)}, u32[]{:S(2)}) collective-permute-start(bf16[256,2048]{1,0:T(8,128)(2,1)S(1)} %fusion.21), channel_id=1, source_target_pairs={{0,2},{2,0},{1,3},{3,1},{4,6},{6,4},{5,7},{7,5},{8,10},{10,8},{9,1... | collective-permute-start | bytes 3145736 | tf_op jit(solution)/shard_map/ppermute | solution.py:47
  587.4 25.7 %collective-permute-start.31 = (bf16[256,2048]{1,0:T(8,128)(2,1)S(1)}, bf16[256,2048]{1,0:T(8,128)(2,1)S(1)}, u32[]{:S(2)}, u32[]{:S(2)}) collective-permute-start(bf16[256,2048]{1,0:T(8,128)(2,1)S(1)} %fusion.22), channel_id=1, source_target_pairs={{0,2},{2,0},{1,3},{3,1},{4,6},{6,4},{5,7},{7,5},{8,10},{10,8},{9,1... | collective-permute-start | bytes 3145736 | tf_op jit(solution)/shard_map/ppermute | solution.py:47
  613.1 29.5 %all-to-all-start.4 = ((bf16[8,256,256]{2,1,0:T(8,128)(2,1)}), bf16[8,256,256]{2,1,0:T(8,128)(2,1)S(1)}, u32[]{:S(2)}, u32[]{:S(2)}) async-start(bf16[8,256,256]{2,1,0:T(8,128)(2,1)} %fusion.70), calls=%async_computation.4 | async-start | bytes 2097152 | tf_op jit(solution)/shard_map/all_to_all | solution.py:651
  616.7 235.9 %reduce-scatter.9.cloned.1.call-start = ((), (), s32[]{:S(2)}) async-start(), calls=%async_computation.17 | async-start | bytes 7208960 | tf_op jit(solution)/shard_map/reduce_scatter | solution.py:866
  648.7 63.3 %collective-permute-start.33 = (bf16[256,2048]{1,0:T(8,128)(2,1)}, bf16[256,2048]{1,0:T(8,128)(2,1)}, u32[]{:S(2)}, u32[]{:S(2)}) collective-permute-start(bf16[256,2048]{1,0:T(8,128)(2,1)} %fusion.23), channel_id=1, source_target_pairs={{0,2},{2,0},{1,3},{3,1},{4,6},{6,4},{5,7},{7,5},{8,10},{10,8},{9,1... | collective-permute-start | bytes 3145736 | tf_op jit(solution)/shard_map/ppermute | solution.py:47
  663.6 61.0 %all-to-all-start.5 = ((bf16[8,256,256]{2,1,0:T(8,128)(2,1)}), bf16[8,256,256]{2,1,0:T(8,128)(2,1)}, u32[]{:S(2)}, u32[]{:S(2)}) async-start(bf16[8,256,256]{2,1,0:T(8,128)(2,1)} %fusion.62), calls=%async_computation.5 | async-start | bytes 2097152 | tf_op jit(solution)/shard_map/all_to_all | solution.py:651
  679.3 94.8 %collective-permute-start.49 = (bf16[2,512,2048]{2,1,0:T(8,128)(2,1)}, bf16[2,512,2048]{2,1,0:T(8,128)(2,1)}, u32[]{:S(2)}, u32[]{:S(2)}) collective-permute-start(bf16[2,512,2048]{2,1,0:T(8,128)(2,1)} %dynamic-slice_bitcast_fusion), channel_id=1, source_target_pairs={{0,8},{8,0},{1,9},{9,1},{2,10},{10,2},{3,11},{11,3},{4,12},{12,4},... | collective-permute-start | bytes 12582920 | tf_op jit(solution)/shard_map/ppermute | solution.py:47
  680.4 44.1 %collective-permute-start.32 = (bf16[2,2,64,1408]{3,2,1,0:T(8,128)(2,1)S(1)}, bf16[2,2,64,1408]{3,2,1,0:T(8,128)(2,1)}, u32[]{:S(2)}, u32[]{:S(2)}) collective-permute-start(bf16[2,2,64,1408]{3,2,1,0:T(8,128)(2,1)S(1)} %dynamic-slice_bitcast_fusion.6), channel_id=1, source_target_pairs={{0,4},{4,0},{1,5},{5,1},{2,6},{6,2},{3,7},{7,3},{8,12},{12,8},{9,1... | collective-permute-start | bytes 2162696 | tf_op jit(solution)/shard_map/ppermute | solution.py:47
  724.5 43.3 %all-to-all-start.6 = ((bf16[8,256,384]{2,1,0:T(8,128)(2,1)}), bf16[8,256,384]{2,1,0:T(8,128)(2,1)S(1)}, u32[]{:S(2)}, u32[]{:S(2)}) async-start(bf16[8,256,384]{2,1,0:T(8,128)(2,1)} %pad_maximum_fusion.8), calls=%async_computation.7 | async-start | bytes 3145728 | tf_op jit(solution)/shard_map/all_to_all | solution.py:651
  767.8 60.0 %all-to-all-start.7 = ((bf16[8,256,384]{2,1,0:T(8,128)(2,1)}), bf16[8,256,384]{2,1,0:T(8,128)(2,1)}, u32[]{:S(2)}, u32[]{:S(2)}) async-start(bf16[8,256,384]{2,1,0:T(8,128)(2,1)} %pad_maximum_fusion.9), calls=%async_computation.8 | async-start | bytes 3145728 | tf_op jit(solution)/shard_map/all_to_all | solution.py:651
  773.8 120.5 %reduce-scatter.11.cloned.1.call-start = ((), (), s32[]{:S(2)}) async-start(), calls=%async_computation.18 | async-start | bytes 5242880 | tf_op jit(solution)/shard_map/reduce_scatter | solution.py:866
  784.1 56.2 %collective-permute-start.34 = (bf16[2,2,64,1408]{3,2,1,0:T(8,128)(2,1)}, bf16[2,2,64,1408]{3,2,1,0:T(8,128)(2,1)}, u32[]{:S(2)}, u32[]{:S(2)}) collective-permute-start(bf16[2,2,64,1408]{3,2,1,0:T(8,128)(2,1)} %dynamic-slice_bitcast_fusion.5), channel_id=1, source_target_pairs={{0,4},{4,0},{1,5},{5,1},{2,6},{6,2},{3,7},{7,3},{8,12},{12,8},{9,1... | collective-permute-start | bytes 2162696 | tf_op jit(solution)/shard_map/ppermute | solution.py:47
  847.9 38.6 %collective-permute-start.35 = (bf16[1024,2560]{1,0:T(8,128)(2,1)}, bf16[1024,2560]{1,0:T(8,128)(2,1)}, u32[]{:S(2)}, u32[]{:S(2)}) collective-permute-start(bf16[1024,2560]{1,0:T(8,128)(2,1)} %outer_rows.1), channel_id=1, source_target_pairs={{0,8},{8,0},{1,9},{9,1},{2,10},{10,2},{3,11},{11,3},{4,12},{12,4},... | collective-permute-start | bytes 15728648 | tf_op jit(solution)/shard_map/ppermute | solution.py:47
  849.5 37.0 %collective-permute-start.36 = (bf16[2,256,2048]{2,1,0:T(8,128)(2,1)}, bf16[2,256,2048]{2,1,0:T(8,128)(2,1)}, u32[]{:S(2)}, u32[]{:S(2)}) collective-permute-start(bf16[2,256,2048]{2,1,0:T(8,128)(2,1)} %slice_bitcast_fusion.1), channel_id=1, source_target_pairs={{0,8},{8,0},{1,9},{9,1},{2,10},{10,2},{3,11},{11,3},{4,12},{12,4},... | collective-permute-start | bytes 6291464 | tf_op jit(solution)/shard_map/ppermute | solution.py:47
  853.7 32.8 %collective-permute-start.37 = (bf16[2,2,64,1408]{3,2,1,0:T(8,128)(2,1)S(1)}, bf16[2,2,64,1408]{3,2,1,0:T(8,128)(2,1)S(1)}, u32[]{:S(2)}, u32[]{:S(2)}) collective-permute-start(bf16[2,2,64,1408]{3,2,1,0:T(8,128)(2,1)S(1)} %dynamic-slice_bitcast_fusion.4), channel_id=1, source_target_pairs={{0,4},{4,0},{1,5},{5,1},{2,6},{6,2},{3,7},{7,3},{8,12},{12,8},{9,1... | collective-permute-start | bytes 2162696 | tf_op jit(solution)/shard_map/ppermute | solution.py:47
  896.3 69.9 %collective-permute-start.50 = (bf16[2,64,2048]{2,1,0:T(8,128)(2,1)}, bf16[2,64,2048]{2,1,0:T(8,128)(2,1)}, u32[]{:S(2)}, u32[]{:S(2)}) collective-permute-start(bf16[2,64,2048]{2,1,0:T(8,128)(2,1)} %dynamic-slice_bitcast_fusion.9), channel_id=1, source_target_pairs={{0,4},{4,0},{1,5},{5,1},{2,6},{6,2},{3,7},{7,3},{8,12},{12,8},{9,1... | collective-permute-start | bytes 1572872 | tf_op jit(solution)/shard_map/ppermute | solution.py:47
  898.1 42.8 %collective-permute-start.42 = (bf16[3,2,64,1408]{3,2,1,0:T(8,128)(2,1)S(1)}, bf16[3,2,64,1408]{3,2,1,0:T(8,128)(2,1)S(1)}, u32[]{:S(2)}, u32[]{:S(2)}) collective-permute-start(bf16[3,2,64,1408]{3,2,1,0:T(8,128)(2,1)S(1)} %fusion.20), channel_id=1, source_target_pairs={{0,2},{2,0},{1,3},{3,1},{4,6},{6,4},{5,7},{7,5},{8,10},{10,8},{9,1... | collective-permute-start | bytes 3244040 | tf_op jit(solution)/shard_map/ppermute | solution.py:47
  901.5 30.0 %collective-permute-start.39 = (bf16[2,2,2,64,1280]{4,3,2,1,0:T(8,128)(2,1)S(1)}, bf16[2,2,2,64,1280]{4,3,2,1,0:T(8,128)(2,1)S(1)}, u32[]{:S(2)}, u32[]{:S(2)}) collective-permute-start(bf16[2,2,2,64,1280]{4,3,2,1,0:T(8,128)(2,1)S(1)} %dynamic-slice_bitcast_fusion.2), channel_id=1, source_target_pairs={{0,1},{1,0},{2,3},{3,2},{4,5},{5,4},{6,7},{7,6},{8,9},{9,8},{10,11... | collective-permute-start | bytes 3932168 | tf_op jit(solution)/shard_map/ppermute | solution.py:47
  903.2 29.9 %collective-permute-start.38 = (bf16[2,2,2,64,1280]{4,3,1,0,2:T(8,128)(2,1)S(1)}, bf16[2,2,2,64,1280]{4,3,1,0,2:T(8,128)(2,1)S(1)}, u32[]{:S(2)}, u32[]{:S(2)}) collective-permute-start(bf16[2,2,2,64,1280]{4,3,1,0,2:T(8,128)(2,1)S(1)} %dynamic-slice_bitcast_fusion.3), channel_id=1, source_target_pairs={{0,16},{16,0},{1,17},{17,1},{2,18},{18,2},{3,19},{19,3},{4,20},{20... | collective-permute-start | bytes 3932168 | tf_op jit(solution)/shard_map/ppermute | solution.py:47
  906.9 59.3 %collective-permute-start.51 = (bf16[256,2048]{1,0:T(8,128)(2,1)}, bf16[256,2048]{1,0:T(8,128)(2,1)}, u32[]{:S(2)}, u32[]{:S(2)}) collective-permute-start(bf16[256,2048]{1,0:T(8,128)(2,1)} %fusion.24), channel_id=1, source_target_pairs={{0,2},{2,0},{1,3},{3,1},{4,6},{6,4},{5,7},{7,5},{8,10},{10,8},{9,1... | collective-permute-start | bytes 3145736 | tf_op jit(solution)/shard_map/ppermute | solution.py:47
  950.5 29.5 %collective-permute-start.48 = (bf16[2,64,2560]{2,1,0:T(8,128)(2,1)}, bf16[2,64,2560]{2,1,0:T(8,128)(2,1)}, u32[]{:S(2)}, u32[]{:S(2)}) collective-permute-start(bf16[2,64,2560]{2,1,0:T(8,128)(2,1)} %fusion.30), channel_id=1, source_target_pairs={{0,4},{4,0},{1,5},{5,1},{2,6},{6,2},{3,7},{7,3},{8,12},{12,8},{9,1... | collective-permute-start | bytes 1966088 | tf_op jit(solution)/shard_map/ppermute | solution.py:47
  (131 other events, 1029.8 us)
Sparse Core Ops, SparseCore 0:
  136.2 51.5 all-gather.3
  190.3 165.0 all-gather.5
  389.9 64.0 all-gather.7
  518.3 64.0 reduce-scatter.4
  613.2 84.4 reduce-scatter.6
  700.5 96.2 reduce-scatter.8
  799.8 58.1 reduce-scatter.10

commit v5 on v4

--- a/solution.py
+++ b/solution.py
@@ -810,48 +810,51 @@
     core_arg = lax.axis_index("core").astype(jnp.int32).reshape(1)
     w_shape = (nx, 1, nfar * 2, -1, w_own.shape[1])
     w_qkv = flat(interleave(core_arg, w_own.reshape(w_shape), w_other.reshape(w_shape)))
-    qkv_0, packed_1, w_qkv = flow.close(qkv_0, packed_1, w_qkv)
+    qkv_0, packed_1, w_qkv, w_out_own = flow.close(qkv_0, packed_1, w_qkv, w_out_own)
 
     qkv_0, packed_1 = flow.open(qkv_0, packed_1)
     qkv_1 = exchange(packed_1)
+    out_swap = Swap(flow.open(w_out_own), CORE)
     attended_0, raw_0, lse_0 = attend_one(0, qkv_0)
-    attended_0, qkv_1, w_out_own = flow.close(attended_0, qkv_1, w_out_own)
+    attended_0, qkv_1 = flow.close(attended_0, qkv_1, wait=[out_swap])
 
     attended_0, qkv_1 = flow.open(attended_0, qkv_1)
     back_0 = exchange(attended_0)
-    out_swap = Swap(w_out_own, CORE)
+    w_shape = (nx, ny, nfar * 2, sub, width)
+    w_out = interleave(core_arg, w_out_own.reshape(w_shape), out_swap.arrived.reshape(w_shape))
+    down = Gather(flow.open(down), "far", 1)
     attended_1, raw_1, lse_1 = attend_one(1, qkv_1)
-    attended_1, back_0 = flow.close(attended_1, back_0, wait=[out_swap])
+    attended_1, back_0, w_out = flow.close(attended_1, back_0, flat(w_out), wait=[down])
 
     def after_attention(b, back):
         attended = jnp.concatenate([back[s] for s in range(n)], axis=1)
         hidden = flow.open(tokens[b]).astype(f32)
-        middle = hidden + dot(attended, w_out, ((1,), (1,)))
+        middle = hidden + rows_by(attended, w_out)
         inverse = rms_scale(middle)
         scaled = middle * inverse
         return attended, middle, inverse, scaled, (scaled * gain_two).astype(bf16)
 
-    attended_1, back_0 = flow.open(attended_1, back_0)
+    attended_1, back_0, w_out = flow.open(attended_1, back_0, w_out)
     back_1 = exchange(attended_1)
-    w_shape = (nx, ny, nfar * 2, sub, width)
-    w_out = interleave(core_arg, w_out_own.reshape(w_shape), out_swap.arrived.reshape(w_shape))
-    w_out = flat(w_out)
-    down = Gather(flow.open(down), "far", 1)
     attended_0, middle_0, inverse_0, scaled_0, normed_0 = after_attention(0, back_0)
-    back_1, normed_0 = flow.close(back_1, normed_0)
-
-    back_1, normed_0 = flow.open(back_1, normed_0)
+    normed_0 = flow.close(normed_0)
+
     group_0 = Group(normed_0)
+    back_1 = flow.close(back_1)
     attended_1, middle_1, inverse_1, scaled_1, normed_1 = after_attention(1, back_1)
-    normed_1, w_gate_up = flow.close(normed_1, w_gate_up, wait=[group_0, down])
+    normed_1, w_gate_up = flow.close(normed_1, w_gate_up, wait=[group_0])
+    down.arrived = flow.open(down.arrived)
     w_down = over_xy(down.done())
     group_1 = Group(normed_1)
     group_0 = group_0.done()
 
     gate_0, up_0, active_0 = ffn_forward(group_0, w_gate_up)
+    active_0 = flow.close(active_0, wait=[group_1])
+    grad_group_0.arrived, grad_group_1.arrived = flow.open(
+        grad_group_0.arrived, grad_group_1.arrived
+    )
     grad_group_0 = grad_group_0.done()
     grad_group_1 = grad_group_1.done()
-    active_0 = flow.close(active_0, wait=[group_1])
 
     group_1 = group_1.done()
     gate_1, up_1, active_1 = ffn_forward(flow.open(group_1), w_gate_up)

time: 1010 us -> 1000 us (0.990)
  waiting for transfers between devices: 302 us -> 286 us
  matrix products: 38.9 us -> 26.2 us
  Pallas kernels: 358 us -> 370 us
    dot_general x8 -> x6, matrix products: 38.9 us -> 26.2 us  [dot(): return lax.dot_general(a, b, (dims, ((), ())), preferred_element_type=f32)]
    pallas_call x1 -> x3, Pallas kernels: 11.3 us -> 23.6 us  [rows_by(): pl.pallas_call(rows_by_kernel, grid=(m // tile,), in_specs=[by_rows(tile,...]
    ppermute x56, waiting for transfers between devices: 229 us -> 219 us  [swap(): lax.ppermute(values, axis, [(i, i ^ 1 << b) for i in range(lax.axis_size(...]
    unnamed x269 -> x267, local copies, waits for them, and re-layouts: 65.8 us -> 63.6 us
  transfers between devices with their start and end apart: 71 -> 71, of which waited for: 34 -> 34; matrix products, arithmetic and copies ran while one was open for 18% -> 17% of each run, Pallas kernels for 32% -> 34%
where the time goes in v5:
time: 1000 us; the launch traced here: 995 us
  Pallas kernels  370 us (37%)
  waiting for transfers between devices  286 us (29%)
  local copies, waits for them, and re-layouts  107 us (11%)
  starting transfers between devices  96.1 us (10%)
  other arithmetic  92.8 us (9%)
  matrix products  26.2 us (3%)
  between operations  16.6 us (2%)
    ppermute x56, waiting for transfers between devices, swap(): lax.ppermute(values, axis, [(i, i ^ 1 << b) for i in range(lax.axis_size(...  219 us
    pallas_call x8, Pallas kernels, over_rows(): pl.pallas_call(with_weights(kernel), grid=(m // tile,), in_specs=[by_rows...  131 us
    all_to_all x8, waiting for transfers between devices, exchange(): return lax.all_to_all(pieces, SEQ, split_axis=0, concat_axis=0, tiled=True)  66.9 us
    pallas_call x2, Pallas kernels, attend_back(): pl.pallas_call(functools.partial(attend_back_kernel, heads), grid=(n,), o...  65.3 us
    unnamed x267, local copies, waits for them, and re-layouts  63.6 us
    pallas_call x3, Pallas kernels, outer_sum(): pl.pallas_call(functools.partial(outer_sum_kernel, len(pairs)), grid=(2 *...  53.5 us
    ppermute x56, starting transfers between devices, swap(): lax.ppermute(values, axis, [(i, i ^ 1 << b) for i in range(lax.axis_size(...  53.3 us
    pallas_call x2, Pallas kernels, attend(): pl.pallas_call(functools.partial(attend_kernel, heads), grid=(n,), out_sh...  47.1 us
  transfers between devices with their start and end apart: 71, of which 34 were waited for; matrix products, arithmetic and copies ran while one was open for 17% of the time, Pallas kernels for 34%

profile of v5, /device:TPU:0, one launch (start us, length us, event | category | flops | bytes accessed | tf_op | source)
XLA Modules:
  0.0 994.9 jit_solution(695643070212329376)
XLA Ops:
  34.8 28.9 %collective-permute-done.1 = bf16[2,64,2560]{2,1,0:T(8,128)(2,1)} collective-permute-done((bf16[2,64,2560]{2,1,0:T(8,128)(2,1)}, bf16[2,64,2560]{2,1,0:T(8,128)(2,1)}, u32[]{:S(2)}, u32[]{:S(2)}) %collective-permute-start.1) | collective-permute-done | bytes 655392 | tf_op jit(solution)/shard_map/ppermute | solution.py:47
  75.0 12.0 %collective-permute-done.7 = bf16[2,64,2048]{2,1,0:T(8,128)(2,1)S(1)} collective-permute-done((bf16[2,64,2048]{2,1,0:T(8,128)(2,1)S(1)}, bf16[2,64,2048]{2,1,0:T(8,128)(2,1)S(1)}, u32[]{:S(2)}, u32[]{:S(2)}) %collective-permute-start.7) | collective-permute-done | bytes 524320 | tf_op jit(solution)/shard_map/ppermute | solution.py:47
  94.3 33.4 %collective-permute-done.10 = bf16[2,2,64,1408]{3,2,1,0:T(8,128)(2,1)S(1)} collective-permute-done((bf16[2,2,64,1408]{3,2,1,0:T(8,128)(2,1)S(1)}, bf16[2,2,64,1408]{3,2,1,0:T(8,128)(2,1)S(1)}, u32[]{:S(2)}, u32[]{:S(2)}) %collective-permute-start.10) | collective-permute-done | bytes 720928 | tf_op jit(solution)/shard_map/ppermute | solution.py:47
  143.9 5.0 fusion.96
  149.0 4.9 convolution_add_fusion.q_ref.k_ref.v_ref
  153.9 7.2 pack_heads.2
  161.2 16.3 %collective-permute-done.13 = bf16[2,2,64,1408]{3,2,1,0:T(8,128)(2,1)} collective-permute-done((bf16[2,2,64,1408]{3,2,1,0:T(8,128)(2,1)}, bf16[2,2,64,1408]{3,2,1,0:T(8,128)(2,1)}, u32[]{:S(2)}, u32[]{:S(2)}) %collective-permute-start.13) | collective-permute-done | bytes 720928 | tf_op jit(solution)/shard_map/ppermute | solution.py:47
  181.2 4.9 all-to-all-start
  186.2 4.8 pad_maximum_fusion.1.own_ref
  190.9 7.1 pack_heads.3
  200.5 14.0 %interleave.2 = bf16[2,2,4,1,128,2560]{5,4,3,2,1,0:T(8,128)(2,1)} custom-call(s32[1]{0:T(128)} %bitcast.53.core_ref, bf16[2,1,4,128,2560]{4,3,2,1,0:T(8,128)(2,1)S(1)} %copy-done.7, bf16[2,1,4,128,2560]{4,3,2,1,0:T(8,128)(2,1)} %bitcast.57.other_ref), custom_call_target="tpu_custom_call" | custom-call | bytes 65536 | tf_op jit(solution)/shard_map/interleave/pallas_call | solution.py:428
  214.5 8.6 all-to-all-done.qkv_ref
  227.2 27.9 %attend.2 = (bf16[8,256,256]{2,1,0:T(8,128)(2,1)S(1)}, f32[8,256,256]{2,1,0:T(8,128)S(1)}, f32[8,8,1024]{2,1,0:T(8,128)S(1)}) custom-call(s32[8]{0:T(128)S(1)} %get-tuple-element.444.lo_ref, s32[8]{0:T(128)S(1)} %get-tuple-element.439.hi_ref, s32[8,1,256]{2,1,0:T(1,128)S(1)} %bitcast.551, bf16[8,256,384]{2,1,0:T(8,128)(2,1)S(1)} %all-to-all-done.qkv_ref), custom_call_target="tpu_custom_call" | custom-call | bytes 1048576 | tf_op jit(solution)/shard_map/attend/pallas_call | solution.py:194
  258.2 6.5 all-to-all-done.1.qkv_ref
  275.4 12.5 %interleave.3 = bf16[2,2,4,2,64,2048]{5,4,3,2,1,0:T(8,128)(2,1)} custom-call(s32[1]{0:T(128)} %bitcast.53.core_ref, bf16[2,2,4,64,2048]{4,3,2,1,0:T(8,128)(2,1)S(1)} %bitcast.548, bf16[2,2,4,64,2048]{4,3,2,1,0:T(8,128)(2,1)} %bitcast.65.other_ref), custom_call_target="tpu_custom_call" | custom-call | bytes 65536 | tf_op jit(solution)/shard_map/interleave/pallas_call | solution.py:428
  287.9 19.2 %attend.3 = (bf16[8,256,256]{2,1,0:T(8,128)(2,1)}, f32[8,256,256]{2,1,0:T(8,128)S(1)}, f32[8,8,1024]{2,1,0:T(8,128)S(1)}) custom-call(s32[8]{0:T(128)S(1)} %get-tuple-element.443.lo_ref, s32[8]{0:T(128)S(1)} %get-tuple-element.440.hi_ref, s32[8,1,256]{2,1,0:T(1,128)S(1)} %bitcast.549, bf16[8,256,384]{2,1,0:T(8,128)(2,1)S(1)} %all-to-all-done.1.qkv_ref), custom_call_target="tpu_custom_call" | custom-call | bytes 1048576 | tf_op jit(solution)/shard_map/attend/pallas_call | solution.py:194
  308.4 16.9 %collective-permute-done.16 = bf16[2,2,64,1408]{3,2,1,0:T(8,128)(2,1)} collective-permute-done((bf16[2,2,64,1408]{3,2,1,0:T(8,128)(2,1)}, bf16[2,2,64,1408]{3,2,1,0:T(8,128)(2,1)}, u32[]{:S(2)}, u32[]{:S(2)}) %collective-permute-start.16) | collective-permute-done | bytes 720928 | tf_op jit(solution)/shard_map/ppermute | solution.py:47
  329.2 6.1 rows_by.3
  340.3 14.7 %all-to-all-done.3 = bf16[8,256,256]{2,1,0:T(8,128)(2,1)S(1)} async-done(((bf16[8,256,256]{2,1,0:T(8,128)(2,1)}), bf16[8,256,256]{2,1,0:T(8,128)(2,1)S(1)}, u32[]{:S(2)}, u32[]{:S(2)}) %all-to-all-start.3) | async-done | bytes 1048608 | tf_op jit(solution)/shard_map/all_to_all | solution.py:651
  355.2 6.1 rows_by.4
  364.3 6.8 collective-permute-done.18
  374.4 8.7 reduce-scatter.5.cloned.1.call-start
  392.4 20.7 %ffn_forward.2 = (f32[1024,1408]{1,0:T(8,128)}, f32[1024,1408]{1,0:T(8,128)}, bf16[1024,1408]{1,0:T(8,128)(2,1)S(1)}) custom-call(bf16[1024,2048]{1,0:T(8,128)(2,1)} %copy-done, bf16[4,2,2,2,64,2816]{5,4,3,2,1,0:T(8,128)(2,1)} %bitcast.553), custom_call_target="tpu_custom_call" | custom-call | bytes 65536 | tf_op jit(solution)/shard_map/ffn_forward/pallas_call | solution.py:499
  423.5 20.7 %ffn_forward.3 = (f32[1024,1408]{1,0:T(8,128)}, f32[1024,1408]{1,0:T(8,128)}, bf16[1024,1408]{1,0:T(8,128)(2,1)S(1)}) custom-call(bf16[1024,2048]{1,0:T(8,128)(2,1)} %copy-done.39, bf16[4,2,2,2,64,2816]{5,4,3,2,1,0:T(8,128)(2,1)} %bitcast.554), custom_call_target="tpu_custom_call" | custom-call | bytes 65536 | tf_op jit(solution)/shard_map/ffn_forward/pallas_call | solution.py:499
  450.8 16.5 %outer_sum.3 = bf16[2,2,2,2,2,64,1408]{6,5,4,3,2,1,0:T(8,128)(2,1)} custom-call(bf16[1024,2048]{1,0:T(8,128)(2,1)} %copy-done.5, bf16[1024,1408]{1,0:T(8,128)(2,1)S(1)} %copy-done.17, bf16[1024,2048]{1,0:T(8,128)(2,1)} %copy-done.3, bf16[1024,1408]{1,0:T(8,128)(2,1)S(1)} %get-tuple-element.306.refs_3_.x_ref), custom_call_target="tpu_custom_call" | custom-call | bytes 65536 | tf_op jit(solution)/shard_map/outer_sum/pallas_call | solution.py:628
  469.5 14.3 %ffn_backward.2.x_ref.refs_1_ = bf16[1024,2816]{1,0:T(8,128)(2,1)} custom-call(bf16[1024,2048]{1,0:T(8,128)(2,1)S(1)} %copy-done.6, bf16[4,2,2,2,64,1408]{5,4,3,2,1,0:T(8,128)(2,1)} %bitcast.557, f32[1024,1408]{1,0:T(8,128)} %get-tuple-element.258.refs_0_, f32[1024,1408]{1,0:T(8,128)} %get-tuple-element.259.refs_1_), custom_call_target="tpu_custom_call" | custom-call | bytes 65536 | tf_op jit(solution)/shard_map/ffn_backward/pallas_call | solution.py:499
  483.8 18.9 %project_rows.4 = bf16[1024,2048]{1,0:T(8,128)(2,1)S(1)} custom-call(bf16[1024,2816]{1,0:T(8,128)(2,1)} %ffn_backward.2.x_ref.refs_1_, bf16[4,2,2,2,64,2816]{5,4,3,2,1,0:T(8,128)(2,1)} %bitcast.555), custom_call_target="tpu_custom_call" | custom-call | bytes 65536 | tf_op jit(solution)/shard_map/project_rows/pallas_call | solution.py:499
  507.3 11.3 %project_rows.5 = bf16[1024,2048]{1,0:T(8,128)(2,1)} custom-call(bf16[1024,1408]{1,0:T(8,128)(2,1)S(1)} %copy-done.18, bf16[4,2,2,2,64,1408]{5,4,3,2,1,0:T(8,128)(2,1)} %bitcast.558), custom_call_target="tpu_custom_call" | custom-call | bytes 65536 | tf_op jit(solution)/shard_map/project_rows/pallas_call | solution.py:499
  526.3 14.7 %ffn_backward.3.x_ref.refs_3_ = bf16[1024,2816]{1,0:T(8,128)(2,1)} custom-call(bf16[1024,2048]{1,0:T(8,128)(2,1)S(1)} %copy-done.4, bf16[4,2,2,2,64,1408]{5,4,3,2,1,0:T(8,128)(2,1)} %bitcast.559, f32[1024,1408]{1,0:T(8,128)} %get-tuple-element.266.refs_0_, f32[1024,1408]{1,0:T(8,128)} %get-tuple-element.267.refs_1_), custom_call_target="tpu_custom_call" | custom-call | bytes 65536 | tf_op jit(solution)/shard_map/ffn_backward/pallas_call | solution.py:499
  541.0 19.2 %project_rows.6 = bf16[1024,2048]{1,0:T(8,128)(2,1)S(1)} custom-call(bf16[1024,2816]{1,0:T(8,128)(2,1)} %ffn_backward.3.x_ref.refs_3_, bf16[4,2,2,2,64,2816]{5,4,3,2,1,0:T(8,128)(2,1)} %bitcast.556), custom_call_target="tpu_custom_call" | custom-call | bytes 65536 | tf_op jit(solution)/shard_map/project_rows/pallas_call | solution.py:499
  579.2 18.7 %outer_sum.4 = bf16[2,2,2,2,2,64,1408]{6,5,4,3,2,1,0:T(8,128)(2,1)} custom-call(bf16[1024,2048]{1,0:T(8,128)(2,1)S(1)} %copy-done.1, bf16[1024,2816]{1,0:T(8,128)(2,1)} %ffn_backward.2.x_ref.refs_1_, bf16[1024,2048]{1,0:T(8,128)(2,1)} %copy-done.39, bf16[1024,2816]{1,0:T(8,128)(2,1)} %ffn_backward.3.x_ref.refs_3_), custom_call_target="tpu_custom_call" | custom-call | bytes 65536 | tf_op jit(solution)/shard_map/outer_sum/pallas_call | solution.py:628
  602.2 5.0 all-to-all-start.4
  610.4 18.3 %outer_sum.5 = bf16[2,2,2,2,2,64,1408]{6,5,4,3,2,1,0:T(8,128)(2,1)} custom-call(bf16[1024,2048]{1,0:T(8,128)(2,1)S(1)} %copy-done.2, bf16[1024,2816]{1,0:T(8,128)(2,1)} %ffn_backward.2.x_ref.refs_1_, bf16[1024,2048]{1,0:T(8,128)(2,1)} %copy-done.39, bf16[1024,2816]{1,0:T(8,128)(2,1)} %ffn_backward.3.x_ref.refs_3_), custom_call_target="tpu_custom_call" | custom-call | bytes 65536 | tf_op jit(solution)/shard_map/outer_sum/pallas_call | solution.py:628
  658.4 6.4 convolution_convert_fusion
  673.7 37.8 %attend_back.2 = (bf16[8,256,256]{2,1,0:T(8,128)(2,1)S(1)}, bf16[8,256,128]{2,1,0:T(8,128)(2,1)S(1)}) custom-call(s32[8]{0:T(128)S(1)} %get-tuple-element.444.lo_ref, s32[8]{0:T(128)S(1)} %get-tuple-element.439.hi_ref, s32[8,1,256]{2,1,0:T(1,128)S(1)} %bitcast.552, bf16[8,256,384]{2,1,0:T(8,128)(2,1)S(1)} %copy-done.13, ...), custom_call_target="tpu_custom_call" | custom-call | bytes 1048576 | tf_op jit(solution)/shard_map/attend_back/pallas_call | solution.py:302
  718.2 27.5 %attend_back.3 = (bf16[8,256,256]{2,1,0:T(8,128)(2,1)S(1)}, bf16[8,256,128]{2,1,0:T(8,128)(2,1)S(1)}) custom-call(s32[8]{0:T(128)S(1)} %get-tuple-element.443.lo_ref, s32[8]{0:T(128)S(1)} %get-tuple-element.440.hi_ref, s32[8,1,256]{2,1,0:T(1,128)S(1)} %bitcast.550, bf16[8,256,384]{2,1,0:T(8,128)(2,1)S(1)} %copy-done.11, ...), custom_call_target="tpu_custom_call" | custom-call | bytes 1048576 | tf_op jit(solution)/shard_map/attend_back/pallas_call | solution.py:302
  747.0 7.3 all-to-all-done.6.in_ref
  758.9 5.5 fusion
  772.9 11.3 %project_rows.7 = bf16[1024,2048]{1,0:T(8,128)(2,1)} custom-call(bf16[1024,1408]{1,0:T(8,128)(2,1)S(1)} %copy-done.15, bf16[4,2,2,2,64,1408]{5,4,3,2,1,0:T(8,128)(2,1)} %bitcast.560), custom_call_target="tpu_custom_call" | custom-call | bytes 65536 | tf_op jit(solution)/shard_map/project_rows/pallas_call | solution.py:499
  785.3 25.7 %all-to-all-done.7.in_ref = bf16[8,256,384]{2,1,0:T(8,128)(2,1)} async-done(((bf16[8,256,384]{2,1,0:T(8,128)(2,1)}), bf16[8,256,384]{2,1,0:T(8,128)(2,1)}, u32[]{:S(2)}, u32[]{:S(2)}) %all-to-all-start.7) | async-done | bytes 1572896 | tf_op jit(solution)/shard_map/all_to_all | solution.py:651
  811.1 15.4 %collective-permute-done.34 = bf16[2,2,64,1408]{3,2,1,0:T(8,128)(2,1)} collective-permute-done((bf16[2,2,64,1408]{3,2,1,0:T(8,128)(2,1)}, bf16[2,2,64,1408]{3,2,1,0:T(8,128)(2,1)}, u32[]{:S(2)}, u32[]{:S(2)}) %collective-permute-start.34) | collective-permute-done | bytes 720928 | tf_op jit(solution)/shard_map/ppermute | solution.py:47
  829.1 5.1 outer_rows.1
  841.6 11.4 %rows_by.5 = f32[512,2048]{1,0:T(8,128)} custom-call(bf16[512,2560]{1,0:T(8,128)(2,1)S(1)} %pad_maximum_fusion.5.x_ref, bf16[2048,2560]{1,0:T(8,128)(2,1)} %bitcast.569), custom_call_target="tpu_custom_call" | custom-call | bytes 65536 | tf_op jit(solution)/shard_map/rows_by/pallas_call | solution.py:563
  855.4 18.6 %collective-permute-done.37 = bf16[2,2,64,1408]{3,2,1,0:T(8,128)(2,1)S(1)} collective-permute-done((bf16[2,2,64,1408]{3,2,1,0:T(8,128)(2,1)S(1)}, bf16[2,2,64,1408]{3,2,1,0:T(8,128)(2,1)S(1)}, u32[]{:S(2)}, u32[]{:S(2)}) %collective-permute-start.37) | collective-permute-done | bytes 720928 | tf_op jit(solution)/shard_map/ppermute | solution.py:47
  874.0 5.2 add_convert_fusion
  900.0 20.1 %collective-permute-done.39 = bf16[2,2,2,64,1280]{4,3,2,1,0:T(8,128)(2,1)S(1)} collective-permute-done((bf16[2,2,2,64,1280]{4,3,2,1,0:T(8,128)(2,1)S(1)}, bf16[2,2,2,64,1280]{4,3,2,1,0:T(8,128)(2,1)S(1)}, u32[]{:S(2)}, u32[]{:S(2)}) %collective-permute-start.39) | collective-permute-done | bytes 1310752 | tf_op jit(solution)/shard_map/ppermute | solution.py:47
  931.1 7.5 collective-permute-done.41
  956.7 13.9 %collective-permute-done.48 = bf16[2,64,2560]{2,1,0:T(8,128)(2,1)} collective-permute-done((bf16[2,64,2560]{2,1,0:T(8,128)(2,1)}, bf16[2,64,2560]{2,1,0:T(8,128)(2,1)}, u32[]{:S(2)}, u32[]{:S(2)}) %collective-permute-start.48) | collective-permute-done | bytes 655392 | tf_op jit(solution)/shard_map/ppermute | solution.py:47
  (562 shorter events, 308.8 us)
Async XLA Ops:
  7.2 207.4 %all-gather.4.cloned.1.call-start = ((), (), s32[]{:S(2)}) async-start(), calls=%async_computation.12 | async-start | bytes 5242880 | tf_op jit(solution)/shard_map/all_gather | solution.py:780
  10.3 24.5 %collective-permute-start.3 = (bf16[64,2048]{1,0:T(8,128)(2,1)}, bf16[64,2048]{1,0:T(8,128)(2,1)}, u32[]{:S(2)}, u32[]{:S(2)}) collective-permute-start(bf16[64,2048]{1,0:T(8,128)(2,1)} %param.13), channel_id=1, source_target_pairs={{0,4},{4,0},{1,5},{5,1},{2,6},{6,2},{3,7},{7,3},{8,12},{12,8},{9,1... | collective-permute-start | bytes 786440 | tf_op jit(solution)/shard_map/ppermute | solution.py:47
  26.4 39.4 %collective-permute-start.2 = (bf16[3,64,2816]{2,1,0:T(8,128)(2,1)}, bf16[3,64,2816]{2,1,0:T(8,128)(2,1)}, u32[]{:S(2)}, u32[]{:S(2)}) collective-permute-start(bf16[3,64,2816]{2,1,0:T(8,128)(2,1)} %pad_maximum_fusion.15), channel_id=1, source_target_pairs={{0,2},{2,0},{1,3},{3,1},{4,6},{6,4},{5,7},{7,5},{8,10},{10,8},{9,1... | collective-permute-start | bytes 3244040 | tf_op jit(solution)/shard_map/ppermute | solution.py:47
  28.7 35.0 %collective-permute-start.1 = (bf16[2,64,2560]{2,1,0:T(8,128)(2,1)}, bf16[2,64,2560]{2,1,0:T(8,128)(2,1)}, u32[]{:S(2)}, u32[]{:S(2)}) collective-permute-start(bf16[2,64,2560]{2,1,0:T(8,128)(2,1)} %pad_maximum_fusion.24), channel_id=1, source_target_pairs={{0,4},{4,0},{1,5},{5,1},{2,6},{6,2},{3,7},{7,3},{8,12},{12,8},{9,1... | collective-permute-start | bytes 1966088 | tf_op jit(solution)/shard_map/ppermute | solution.py:47
  67.6 19.8 %collective-permute-start.6 = (bf16[3,2,64,1408]{3,2,1,0:T(8,128)(2,1)S(1)}, bf16[3,2,64,1408]{3,2,1,0:T(8,128)(2,1)S(1)}, u32[]{:S(2)}, u32[]{:S(2)}) collective-permute-start(bf16[3,2,64,1408]{3,2,1,0:T(8,128)(2,1)S(1)} %pad_maximum_fusion.16), channel_id=1, source_target_pairs={{0,8},{8,0},{1,9},{9,1},{2,10},{10,2},{3,11},{11,3},{4,12},{12,4},... | collective-permute-start | bytes 3244040 | tf_op jit(solution)/shard_map/ppermute | solution.py:47
  87.7 42.2 %collective-permute-start.9 = (bf16[2,2,2,64,1280]{4,3,2,1,0:T(8,128)(2,1)S(1)}, bf16[2,2,2,64,1280]{4,3,2,1,0:T(8,128)(2,1)S(1)}, u32[]{:S(2)}, u32[]{:S(2)}) collective-permute-start(bf16[2,2,2,64,1280]{4,3,2,1,0:T(8,128)(2,1)S(1)} %pad_maximum_fusion.14), channel_id=1, source_target_pairs={{0,1},{1,0},{2,3},{3,2},{4,5},{5,4},{6,7},{7,6},{8,9},{9,8},{10,11... | collective-permute-start | bytes 3932168 | tf_op jit(solution)/shard_map/ppermute | solution.py:47
  88.6 41.3 %collective-permute-start.8 = (bf16[2,2,2,64,1280]{4,3,2,1,0:T(8,128)(2,1)S(1)}, bf16[2,2,2,64,1280]{4,3,2,1,0:T(8,128)(2,1)S(1)}, u32[]{:S(2)}, u32[]{:S(2)}) collective-permute-start(bf16[2,2,2,64,1280]{4,3,2,1,0:T(8,128)(2,1)S(1)} %pad_maximum_fusion.13), channel_id=1, source_target_pairs={{0,16},{16,0},{1,17},{17,1},{2,18},{18,2},{3,19},{19,3},{4,20},{20... | collective-permute-start | bytes 3932168 | tf_op jit(solution)/shard_map/ppermute | solution.py:47
  90.2 39.8 %collective-permute-start.11 = (bf16[256,2048]{1,0:T(8,128)(2,1)}, bf16[256,2048]{1,0:T(8,128)(2,1)}, u32[]{:S(2)}, u32[]{:S(2)}) collective-permute-start(bf16[256,2048]{1,0:T(8,128)(2,1)} %get-tuple-element.191), channel_id=1, source_target_pairs={{0,2},{2,0},{1,3},{3,1},{4,6},{6,4},{5,7},{7,5},{8,10},{10,8},{9,1... | collective-permute-start | bytes 3145736 | tf_op jit(solution)/shard_map/ppermute | solution.py:47
  90.9 36.8 %collective-permute-start.10 = (bf16[2,2,64,1408]{3,2,1,0:T(8,128)(2,1)S(1)}, bf16[2,2,64,1408]{3,2,1,0:T(8,128)(2,1)S(1)}, u32[]{:S(2)}, u32[]{:S(2)}) collective-permute-start(bf16[2,2,64,1408]{3,2,1,0:T(8,128)(2,1)S(1)} %pad_maximum_fusion.22), channel_id=1, source_target_pairs={{0,4},{4,0},{1,5},{5,1},{2,6},{6,2},{3,7},{7,3},{8,12},{12,8},{9,1... | collective-permute-start | bytes 2162696 | tf_op jit(solution)/shard_map/ppermute | solution.py:47
  136.1 235.0 %all-gather.6.cloned.1.call-start = ((), (), s32[]{:S(2)}) async-start(), calls=%async_computation.13 | async-start | bytes 14417920 | tf_op jit(solution)/shard_map/all_gather | solution.py:780
  136.5 41.8 %collective-permute-start.14 = (bf16[256,2048]{1,0:T(8,128)(2,1)}, bf16[256,2048]{1,0:T(8,128)(2,1)}, u32[]{:S(2)}, u32[]{:S(2)}) collective-permute-start(bf16[256,2048]{1,0:T(8,128)(2,1)} %get-tuple-element.199), channel_id=1, source_target_pairs={{0,2},{2,0},{1,3},{3,1},{4,6},{6,4},{5,7},{7,5},{8,10},{10,8},{9,1... | collective-permute-start | bytes 3145736 | tf_op jit(solution)/shard_map/ppermute | solution.py:47
  138.6 38.9 %collective-permute-start.13 = (bf16[2,2,64,1408]{3,2,1,0:T(8,128)(2,1)}, bf16[2,2,64,1408]{3,2,1,0:T(8,128)(2,1)}, u32[]{:S(2)}, u32[]{:S(2)}) collective-permute-start(bf16[2,2,64,1408]{3,2,1,0:T(8,128)(2,1)} %pad_maximum_fusion.20), channel_id=1, source_target_pairs={{0,4},{4,0},{1,5},{5,1},{2,6},{6,2},{3,7},{7,3},{8,12},{12,8},{9,1... | collective-permute-start | bytes 2162696 | tf_op jit(solution)/shard_map/ppermute | solution.py:47
  181.2 41.9 %all-to-all-start = ((bf16[8,256,384]{2,1,0:T(8,128)(2,1)}), bf16[8,256,384]{2,1,0:T(8,128)(2,1)S(1)}, u32[]{:S(2)}, u32[]{:S(2)}) async-start(bf16[8,256,384]{2,1,0:T(8,128)(2,1)} %pack_heads.2), calls=%async_computation | async-start | bytes 3145728 | tf_op jit(solution)/shard_map/all_to_all | solution.py:651
  223.1 41.5 %collective-permute-start.15 = (bf16[4,2,2,64,2048]{4,3,2,1,0:T(8,128)(2,1)}, bf16[4,2,2,64,2048]{4,3,2,1,0:T(8,128)(2,1)}, u32[]{:S(2)}, u32[]{:S(2)}) collective-permute-start(bf16[4,2,2,64,2048]{4,3,2,1,0:T(8,128)(2,1)} %bitcast.547), channel_id=1, source_target_pairs={{0,8},{8,0},{1,9},{9,1},{2,10},{10,2},{3,11},{11,3},{4,12},{12,4},... | collective-permute-start | bytes 12582920 | tf_op jit(solution)/shard_map/ppermute | solution.py:47
  223.1 41.5 %all-to-all-start.1 = ((bf16[8,256,384]{2,1,0:T(8,128)(2,1)}), bf16[8,256,384]{2,1,0:T(8,128)(2,1)S(1)}, u32[]{:S(2)}, u32[]{:S(2)}) async-start(bf16[8,256,384]{2,1,0:T(8,128)(2,1)} %pack_heads.3), calls=%async_computation.1 | async-start | bytes 3145728 | tf_op jit(solution)/shard_map/all_to_all | solution.py:651
  264.6 60.7 %all-to-all-start.2 = ((bf16[8,256,256]{2,1,0:T(8,128)(2,1)}), bf16[8,256,256]{2,1,0:T(8,128)(2,1)S(1)}, u32[]{:S(2)}, u32[]{:S(2)}) async-start(bf16[8,256,256]{2,1,0:T(8,128)(2,1)} %copy-done.27), calls=%async_computation.2 | async-start | bytes 2097152 | tf_op jit(solution)/shard_map/all_to_all | solution.py:651
  268.3 57.0 %collective-permute-start.16 = (bf16[2,2,64,1408]{3,2,1,0:T(8,128)(2,1)}, bf16[2,2,64,1408]{3,2,1,0:T(8,128)(2,1)}, u32[]{:S(2)}, u32[]{:S(2)}) collective-permute-start(bf16[2,2,64,1408]{3,2,1,0:T(8,128)(2,1)} %pad_maximum_fusion.21), channel_id=1, source_target_pairs={{0,4},{4,0},{1,5},{5,1},{2,6},{6,2},{3,7},{7,3},{8,12},{12,8},{9,1... | collective-permute-start | bytes 2162696 | tf_op jit(solution)/shard_map/ppermute | solution.py:47
  325.3 29.8 %all-to-all-start.3 = ((bf16[8,256,256]{2,1,0:T(8,128)(2,1)}), bf16[8,256,256]{2,1,0:T(8,128)(2,1)S(1)}, u32[]{:S(2)}, u32[]{:S(2)}) async-start(bf16[8,256,256]{2,1,0:T(8,128)(2,1)} %get-tuple-element.231), calls=%async_computation.3 | async-start | bytes 2097152 | tf_op jit(solution)/shard_map/all_to_all | solution.py:651
  329.0 138.3 %all-gather.8.cloned.1.call-start = ((), (), s32[]{:S(2)}) async-start(), calls=%async_computation.14 | async-start | bytes 7208960 | tf_op jit(solution)/shard_map/all_gather | solution.py:780
  338.4 32.8 %collective-permute-start.18 = (bf16[256,2048]{1,0:T(8,128)(2,1)}, bf16[256,2048]{1,0:T(8,128)(2,1)S(1)}, u32[]{:S(2)}, u32[]{:S(2)}) collective-permute-start(bf16[256,2048]{1,0:T(8,128)(2,1)} %multiply_convert_fusion.2), channel_id=1, source_target_pairs={{0,2},{2,0},{1,3},{3,1},{4,6},{6,4},{5,7},{7,5},{8,10},{10,8},{9,1... | collective-permute-start | bytes 3145736 | tf_op jit(solution)/shard_map/ppermute | solution.py:47
  374.4 295.2 %reduce-scatter.5.cloned.1.call-start = ((), (), s32[]{:S(2)}) async-start(), calls=%async_computation.15 | async-start | bytes 7208960 | tf_op jit(solution)/shard_map/reduce_scatter | solution.py:869
  387.7 25.8 %collective-permute-start.20 = (bf16[256,2048]{1,0:T(8,128)(2,1)}, bf16[256,2048]{1,0:T(8,128)(2,1)}, u32[]{:S(2)}, u32[]{:S(2)}) collective-permute-start(bf16[256,2048]{1,0:T(8,128)(2,1)} %multiply_convert_fusion.1), channel_id=1, source_target_pairs={{0,2},{2,0},{1,3},{3,1},{4,6},{6,4},{5,7},{7,5},{8,10},{10,8},{9,1... | collective-permute-start | bytes 3145736 | tf_op jit(solution)/shard_map/ppermute | solution.py:47
  388.3 27.7 %collective-permute-start.25 = (bf16[256,2048]{1,0:T(8,128)(2,1)}, bf16[256,2048]{1,0:T(8,128)(2,1)}, u32[]{:S(2)}, u32[]{:S(2)}) collective-permute-start(bf16[256,2048]{1,0:T(8,128)(2,1)} %multiply_convert_fusion.1), channel_id=1, source_target_pairs={{0,8},{8,0},{1,9},{9,1},{2,10},{10,2},{3,11},{11,3},{4,12},{12,4},... | collective-permute-start | bytes 3145736 | tf_op jit(solution)/shard_map/ppermute | solution.py:47
  415.5 28.8 %collective-permute-start.22 = (bf16[256,2048]{1,0:T(8,128)(2,1)}, bf16[256,2048]{1,0:T(8,128)(2,1)}, u32[]{:S(2)}, u32[]{:S(2)}) collective-permute-start(bf16[256,2048]{1,0:T(8,128)(2,1)} %collective-permute-done.11), channel_id=1, source_target_pairs={{0,8},{8,0},{1,9},{9,1},{2,10},{10,2},{3,11},{11,3},{4,12},{12,4},... | collective-permute-start | bytes 3145736 | tf_op jit(solution)/shard_map/ppermute | solution.py:47
  415.7 30.9 %collective-permute-start.24 = (bf16[256,2048]{1,0:T(8,128)(2,1)}, bf16[256,2048]{1,0:T(8,128)(2,1)}, u32[]{:S(2)}, u32[]{:S(2)}) collective-permute-start(bf16[256,2048]{1,0:T(8,128)(2,1)} %collective-permute-done.14), channel_id=1, source_target_pairs={{0,8},{8,0},{1,9},{9,1},{2,10},{10,2},{3,11},{11,3},{4,12},{12,4},... | collective-permute-start | bytes 3145736 | tf_op jit(solution)/shard_map/ppermute | solution.py:47
  505.5 261.2 %reduce-scatter.7.cloned.1.call-start = ((), (), s32[]{:S(2)}) async-start(), calls=%async_computation.16 | async-start | bytes 7208960 | tf_op jit(solution)/shard_map/reduce_scatter | solution.py:869
  520.9 39.3 %collective-permute-start.29 = (bf16[2,256,2048]{2,1,0:T(8,128)(2,1)S(1)}, bf16[2,256,2048]{2,1,0:T(8,128)(2,1)S(1)}, u32[]{:S(2)}, u32[]{:S(2)}) collective-permute-start(bf16[2,256,2048]{2,1,0:T(8,128)(2,1)S(1)} %slice_bitcast_fusion.8), channel_id=1, source_target_pairs={{0,8},{8,0},{1,9},{9,1},{2,10},{10,2},{3,11},{11,3},{4,12},{12,4},... | collective-permute-start | bytes 6291464 | tf_op jit(solution)/shard_map/ppermute | solution.py:47
  524.5 35.7 %collective-permute-start.28 = (bf16[256,2048]{1,0:T(8,128)(2,1)S(1)}, bf16[256,2048]{1,0:T(8,128)(2,1)S(1)}, u32[]{:S(2)}, u32[]{:S(2)}) collective-permute-start(bf16[256,2048]{1,0:T(8,128)(2,1)S(1)} %fusion.21), channel_id=1, source_target_pairs={{0,2},{2,0},{1,3},{3,1},{4,6},{6,4},{5,7},{7,5},{8,10},{10,8},{9,1... | collective-permute-start | bytes 3145736 | tf_op jit(solution)/shard_map/ppermute | solution.py:47
  576.7 25.5 %collective-permute-start.31 = (bf16[256,2048]{1,0:T(8,128)(2,1)S(1)}, bf16[256,2048]{1,0:T(8,128)(2,1)S(1)}, u32[]{:S(2)}, u32[]{:S(2)}) collective-permute-start(bf16[256,2048]{1,0:T(8,128)(2,1)S(1)} %fusion.22), channel_id=1, source_target_pairs={{0,2},{2,0},{1,3},{3,1},{4,6},{6,4},{5,7},{7,5},{8,10},{10,8},{9,1... | collective-permute-start | bytes 3145736 | tf_op jit(solution)/shard_map/ppermute | solution.py:47
  602.2 30.6 %all-to-all-start.4 = ((bf16[8,256,256]{2,1,0:T(8,128)(2,1)}), bf16[8,256,256]{2,1,0:T(8,128)(2,1)S(1)}, u32[]{:S(2)}, u32[]{:S(2)}) async-start(bf16[8,256,256]{2,1,0:T(8,128)(2,1)} %fusion.70), calls=%async_computation.4 | async-start | bytes 2097152 | tf_op jit(solution)/shard_map/all_to_all | solution.py:651
  607.2 232.9 %reduce-scatter.9.cloned.1.call-start = ((), (), s32[]{:S(2)}) async-start(), calls=%async_computation.17 | async-start | bytes 7208960 | tf_op jit(solution)/shard_map/reduce_scatter | solution.py:869
  638.9 73.9 %collective-permute-start.33 = (bf16[256,2048]{1,0:T(8,128)(2,1)}, bf16[256,2048]{1,0:T(8,128)(2,1)}, u32[]{:S(2)}, u32[]{:S(2)}) collective-permute-start(bf16[256,2048]{1,0:T(8,128)(2,1)} %fusion.23), channel_id=1, source_target_pairs={{0,2},{2,0},{1,3},{3,1},{4,6},{6,4},{5,7},{7,5},{8,10},{10,8},{9,1... | collective-permute-start | bytes 3145736 | tf_op jit(solution)/shard_map/ppermute | solution.py:47
  653.8 60.8 %all-to-all-start.5 = ((bf16[8,256,256]{2,1,0:T(8,128)(2,1)}), bf16[8,256,256]{2,1,0:T(8,128)(2,1)}, u32[]{:S(2)}, u32[]{:S(2)}) async-start(bf16[8,256,256]{2,1,0:T(8,128)(2,1)} %fusion.62), calls=%async_computation.5 | async-start | bytes 2097152 | tf_op jit(solution)/shard_map/all_to_all | solution.py:651
  669.5 89.4 %collective-permute-start.49 = (bf16[2,512,2048]{2,1,0:T(8,128)(2,1)}, bf16[2,512,2048]{2,1,0:T(8,128)(2,1)}, u32[]{:S(2)}, u32[]{:S(2)}) collective-permute-start(bf16[2,512,2048]{2,1,0:T(8,128)(2,1)} %dynamic-slice_bitcast_fusion), channel_id=1, source_target_pairs={{0,8},{8,0},{1,9},{9,1},{2,10},{10,2},{3,11},{11,3},{4,12},{12,4},... | collective-permute-start | bytes 12582920 | tf_op jit(solution)/shard_map/ppermute | solution.py:47
  670.7 43.9 %collective-permute-start.32 = (bf16[2,2,64,1408]{3,2,1,0:T(8,128)(2,1)S(1)}, bf16[2,2,64,1408]{3,2,1,0:T(8,128)(2,1)}, u32[]{:S(2)}, u32[]{:S(2)}) collective-permute-start(bf16[2,2,64,1408]{3,2,1,0:T(8,128)(2,1)S(1)} %dynamic-slice_bitcast_fusion.6), channel_id=1, source_target_pairs={{0,4},{4,0},{1,5},{5,1},{2,6},{6,2},{3,7},{7,3},{8,12},{12,8},{9,1... | collective-permute-start | bytes 2162696 | tf_op jit(solution)/shard_map/ppermute | solution.py:47
  714.6 39.7 %all-to-all-start.6 = ((bf16[8,256,384]{2,1,0:T(8,128)(2,1)}), bf16[8,256,384]{2,1,0:T(8,128)(2,1)S(1)}, u32[]{:S(2)}, u32[]{:S(2)}) async-start(bf16[8,256,384]{2,1,0:T(8,128)(2,1)} %pad_maximum_fusion.8), calls=%async_computation.7 | async-start | bytes 3145728 | tf_op jit(solution)/shard_map/all_to_all | solution.py:651
  754.3 56.7 %all-to-all-start.7 = ((bf16[8,256,384]{2,1,0:T(8,128)(2,1)}), bf16[8,256,384]{2,1,0:T(8,128)(2,1)}, u32[]{:S(2)}, u32[]{:S(2)}) async-start(bf16[8,256,384]{2,1,0:T(8,128)(2,1)} %pad_maximum_fusion.9), calls=%async_computation.8 | async-start | bytes 3145728 | tf_op jit(solution)/shard_map/all_to_all | solution.py:651
  758.6 123.2 %reduce-scatter.11.cloned.1.call-start = ((), (), s32[]{:S(2)}) async-start(), calls=%async_computation.18 | async-start | bytes 5242880 | tf_op jit(solution)/shard_map/reduce_scatter | solution.py:869
  769.0 57.5 %collective-permute-start.34 = (bf16[2,2,64,1408]{3,2,1,0:T(8,128)(2,1)}, bf16[2,2,64,1408]{3,2,1,0:T(8,128)(2,1)}, u32[]{:S(2)}, u32[]{:S(2)}) collective-permute-start(bf16[2,2,64,1408]{3,2,1,0:T(8,128)(2,1)} %dynamic-slice_bitcast_fusion.5), channel_id=1, source_target_pairs={{0,4},{4,0},{1,5},{5,1},{2,6},{6,2},{3,7},{7,3},{8,12},{12,8},{9,1... | collective-permute-start | bytes 2162696 | tf_op jit(solution)/shard_map/ppermute | solution.py:47
  834.2 39.9 %collective-permute-start.35 = (bf16[1024,2560]{1,0:T(8,128)(2,1)}, bf16[1024,2560]{1,0:T(8,128)(2,1)}, u32[]{:S(2)}, u32[]{:S(2)}) collective-permute-start(bf16[1024,2560]{1,0:T(8,128)(2,1)} %outer_rows.1), channel_id=1, source_target_pairs={{0,8},{8,0},{1,9},{9,1},{2,10},{10,2},{3,11},{11,3},{4,12},{12,4},... | collective-permute-start | bytes 15728648 | tf_op jit(solution)/shard_map/ppermute | solution.py:47
  837.5 36.5 %collective-permute-start.36 = (bf16[2,256,2048]{2,1,0:T(8,128)(2,1)}, bf16[2,256,2048]{2,1,0:T(8,128)(2,1)}, u32[]{:S(2)}, u32[]{:S(2)}) collective-permute-start(bf16[2,256,2048]{2,1,0:T(8,128)(2,1)} %slice_bitcast_fusion.1), channel_id=1, source_target_pairs={{0,8},{8,0},{1,9},{9,1},{2,10},{10,2},{3,11},{11,3},{4,12},{12,4},... | collective-permute-start | bytes 6291464 | tf_op jit(solution)/shard_map/ppermute | solution.py:47
  841.3 32.7 %collective-permute-start.37 = (bf16[2,2,64,1408]{3,2,1,0:T(8,128)(2,1)S(1)}, bf16[2,2,64,1408]{3,2,1,0:T(8,128)(2,1)S(1)}, u32[]{:S(2)}, u32[]{:S(2)}) collective-permute-start(bf16[2,2,64,1408]{3,2,1,0:T(8,128)(2,1)S(1)} %dynamic-slice_bitcast_fusion.4), channel_id=1, source_target_pairs={{0,4},{4,0},{1,5},{5,1},{2,6},{6,2},{3,7},{7,3},{8,12},{12,8},{9,1... | collective-permute-start | bytes 2162696 | tf_op jit(solution)/shard_map/ppermute | solution.py:47
  883.8 72.9 %collective-permute-start.50 = (bf16[2,64,2048]{2,1,0:T(8,128)(2,1)}, bf16[2,64,2048]{2,1,0:T(8,128)(2,1)}, u32[]{:S(2)}, u32[]{:S(2)}) collective-permute-start(bf16[2,64,2048]{2,1,0:T(8,128)(2,1)} %dynamic-slice_bitcast_fusion.9), channel_id=1, source_target_pairs={{0,4},{4,0},{1,5},{5,1},{2,6},{6,2},{3,7},{7,3},{8,12},{12,8},{9,1... | collective-permute-start | bytes 1572872 | tf_op jit(solution)/shard_map/ppermute | solution.py:47
  886.6 44.5 %collective-permute-start.42 = (bf16[3,2,64,1408]{3,2,1,0:T(8,128)(2,1)}, bf16[3,2,64,1408]{3,2,1,0:T(8,128)(2,1)S(1)}, u32[]{:S(2)}, u32[]{:S(2)}) collective-permute-start(bf16[3,2,64,1408]{3,2,1,0:T(8,128)(2,1)} %fusion.20), channel_id=1, source_target_pairs={{0,2},{2,0},{1,3},{3,1},{4,6},{6,4},{5,7},{7,5},{8,10},{10,8},{9,1... | collective-permute-start | bytes 3244040 | tf_op jit(solution)/shard_map/ppermute | solution.py:47
  889.9 30.2 %collective-permute-start.39 = (bf16[2,2,2,64,1280]{4,3,2,1,0:T(8,128)(2,1)S(1)}, bf16[2,2,2,64,1280]{4,3,2,1,0:T(8,128)(2,1)S(1)}, u32[]{:S(2)}, u32[]{:S(2)}) collective-permute-start(bf16[2,2,2,64,1280]{4,3,2,1,0:T(8,128)(2,1)S(1)} %dynamic-slice_bitcast_fusion.2), channel_id=1, source_target_pairs={{0,1},{1,0},{2,3},{3,2},{4,5},{5,4},{6,7},{7,6},{8,9},{9,8},{10,11... | collective-permute-start | bytes 3932168 | tf_op jit(solution)/shard_map/ppermute | solution.py:47
  891.8 31.2 %collective-permute-start.38 = (bf16[2,2,2,64,1280]{4,3,1,0,2:T(8,128)(2,1)S(1)}, bf16[2,2,2,64,1280]{4,3,1,0,2:T(8,128)(2,1)S(1)}, u32[]{:S(2)}, u32[]{:S(2)}) collective-permute-start(bf16[2,2,2,64,1280]{4,3,1,0,2:T(8,128)(2,1)S(1)} %dynamic-slice_bitcast_fusion.3), channel_id=1, source_target_pairs={{0,16},{16,0},{1,17},{17,1},{2,18},{18,2},{3,19},{19,3},{4,20},{20... | collective-permute-start | bytes 3932168 | tf_op jit(solution)/shard_map/ppermute | solution.py:47
  898.5 58.2 %collective-permute-start.51 = (bf16[256,2048]{1,0:T(8,128)(2,1)}, bf16[256,2048]{1,0:T(8,128)(2,1)}, u32[]{:S(2)}, u32[]{:S(2)}) collective-permute-start(bf16[256,2048]{1,0:T(8,128)(2,1)} %fusion.24), channel_id=1, source_target_pairs={{0,2},{2,0},{1,3},{3,1},{4,6},{6,4},{5,7},{7,5},{8,10},{10,8},{9,1... | collective-permute-start | bytes 3145736 | tf_op jit(solution)/shard_map/ppermute | solution.py:47
  941.5 29.1 %collective-permute-start.48 = (bf16[2,64,2560]{2,1,0:T(8,128)(2,1)}, bf16[2,64,2560]{2,1,0:T(8,128)(2,1)}, u32[]{:S(2)}, u32[]{:S(2)}) collective-permute-start(bf16[2,64,2560]{2,1,0:T(8,128)(2,1)} %fusion.30), channel_id=1, source_target_pairs={{0,4},{4,0},{1,5},{5,1},{2,6},{6,2},{3,7},{7,3},{8,12},{12,8},{9,1... | collective-permute-start | bytes 1966088 | tf_op jit(solution)/shard_map/ppermute | solution.py:47
  (130 other events, 964.9 us)
Sparse Core Ops, SparseCore 0:
  136.3 51.5 all-gather.3
  190.3 165.1 all-gather.5
  374.5 64.6 all-gather.7
  505.7 65.4 reduce-scatter.4
  602.3 85.5 reduce-scatter.6
  690.7 98.8 reduce-scatter.8
  792.6 56.3 reduce-scatter.10

commit v6 on v5

--- a/solution.py
+++ b/solution.py
@@ -457,22 +457,28 @@
     return pl.BlockSpec((tile, cols), lambda i: (i, at))
 
 
-def load_rows(w_ref, w_s, sems):
+def row_copies(w_ref, w_s, sems):
     xy, _, nfar, _, sub, _ = w_ref.shape
     ny = 2
     copies = []
-    for g in range(xy):
+    for x in range(xy // ny):
         for core in range(2):
             for far in range(nfar):
                 for near in range(2):
-                    block = (((g // ny * 2 + core) * nfar + far) * 2 + near) * ny + g % ny
-                    copies.append(
-                        pltpu.make_async_copy(
-                            w_ref.at[g, core, far, near],
-                            w_s.at[pl.ds(block * sub, sub)],
-                            sems.at[block],
+                    for y in range(ny):
+                        block = len(copies)
+                        copies.append(
+                            pltpu.make_async_copy(
+                                w_ref.at[x * ny + y, core, far, near],
+                                w_s.at[pl.ds(block * sub, sub)],
+                                sems.at[block],
+                            )
                         )
-                    )
+    return copies
+
+
+def load_rows(w_ref, w_s, sems):
+    copies = row_copies(w_ref, w_s, sems)
     for copy in copies:
         copy.start()
     for copy in copies:
@@ -544,13 +550,44 @@
     return over_rows(ffn_backward_kernel, grad, w_down, [gate, up], outs, "ffn_backward")[0]
 
 
-def project_rows_kernel(x_ref, w_ref, out_ref):
-    out_ref[...] = dot(x_ref[...], w_ref[...], ((1,), (1,))).astype(bf16)
+def project_rows_kernel(x_ref, w_ref, out_ref, w_s, sems):
+    first = pl.program_id(0) == 0
+    x = x_ref[...]
+
+    @pl.when(first)
+    def _():
+        copies = row_copies(w_ref, w_s, sems)
+        for copy in copies:
+            copy.start()
+        rows = w_s.shape[0] // 8
+        count = len(copies) // 8
+        for group in range(8):
+            for copy in copies[group * count : (group + 1) * count]:
+                copy.wait()
+            part = slice(group * rows, (group + 1) * rows)
+            out_ref[:, part] = dot(x, w_s[part, :], ((1,), (1,))).astype(bf16)
+
+    @pl.when(jnp.logical_not(first))
+    def _():
+        out_ref[...] = dot(x, w_s[...], ((1,), (1,))).astype(bf16)
 
 
 def project_rows(x, w):
-    rows = w.shape[0] * w.shape[1] * w.shape[2] * w.shape[3] * w.shape[4]
-    return over_rows(project_rows_kernel, x, w, [], [(rows, bf16)], "project_rows")[0]
+    m = x.shape[0]
+    blocks = w.shape[0] * w.shape[1] * w.shape[2] * w.shape[3]
+    rows = blocks * w.shape[4]
+    tile = min(ROW_TILE, m)
+    return pl.pallas_call(
+        project_rows_kernel,
+        grid=(m // tile,),
+        in_specs=[by_rows(tile, x.shape[1]), pl.BlockSpec(memory_space=pl.ANY)],
+        out_specs=by_rows(tile, rows),
+        out_shape=jax.ShapeDtypeStruct((m, rows), bf16),
+        scratch_shapes=[pltpu.VMEM((rows, w.shape[5]), bf16), pltpu.SemaphoreType.DMA((blocks,))],
+        compiler_params=pltpu.CompilerParams(vmem_limit_bytes=48 << 20),
+        cost_estimate=small_cost(1 << 16),
+        name="project_rows",
+    )(x, w)
 
 
 def rows_by_kernel(x_ref, w_ref, out_ref):
@@ -793,12 +830,11 @@
     w_own = jnp.concatenate([flat(left.done()), flat(right.done())], axis=1)
     w_swap = Swap(w_own, CORE)
     up = Gather(up, "far", 1)
-    grad_group_1 = Group(flow.open(grad_out_all[rows:]))
     projected = dot(normed_one_own, w_own)
     w_other = w_swap.arrived
     projected = projected + dot(normed_one_other, w_other)
     packed_0 = pack_heads(projected, cosine, sine, 0, rows, n)
-    packed_0 = flow.close(packed_0, wait=[up, grad_group_1])
+    packed_0 = flow.close(packed_0, wait=[up])
 
     def attend_one(b, qkv_b):
         return attend(first_block[b], plain_from[b], doc_start[b], qkv_b, heads)
@@ -850,15 +886,14 @@
 
     gate_0, up_0, active_0 = ffn_forward(group_0, w_gate_up)
     active_0 = flow.close(active_0, wait=[group_1])
-    grad_group_0.arrived, grad_group_1.arrived = flow.open(
-        grad_group_0.arrived, grad_group_1.arrived
-    )
+    grad_group_0.arrived = flow.open(grad_group_0.arrived)
     grad_group_0 = grad_group_0.done()
-    grad_group_1 = grad_group_1.done()
+    grad_group_1 = Group(flow.open(grad_out_all[rows:]))
 
     group_1 = group_1.done()
     gate_1, up_1, active_1 = ffn_forward(flow.open(group_1), w_gate_up)
-    active_1 = flow.close(active_1)
+    active_1 = flow.close(active_1, wait=[grad_group_1])
+    grad_group_1 = grad_group_1.done()
 
     outer = lambda a, b: dot(a, b, ((0,), (0,)))
     owners = (nx, nfar, ny)

time: 1000 us -> 1000 us (level)
  waiting for transfers between devices: 286 us -> 258 us
  local copies, waits for them, and re-layouts: 107 us -> 126 us
  Pallas kernels: 370 us -> 383 us
    pallas_call x0 -> x4, Pallas kernels: none -> 67.5 us  [project_rows(): pl.pallas_call(project_rows_kernel, grid=(m // tile,), in_specs=[by_rows(...]
    pallas_call x8 -> x4, Pallas kernels: 131 us -> 71.1 us  [over_rows(): pl.pallas_call(with_weights(kernel), grid=(m // tile,), in_specs=[by_rows...]
    unnamed x267 -> x275, local copies, waits for them, and re-layouts: 63.6 us -> 83.8 us
    ppermute x56, waiting for transfers between devices: 219 us -> 203 us  [swap(): lax.ppermute(values, axis, [(i, i ^ 1 << b) for i in range(lax.axis_size(...]
    all_to_all x8, waiting for transfers between devices: 66.9 us -> 55.3 us  [exchange(): return lax.all_to_all(pieces, SEQ, split_axis=0, concat_axis=0, tiled=True)]
    all_gather x3, starting transfers between devices: 0.37 us -> 11.2 us  [over_xy(): gathered = lax.all_gather(flat(values), ('x', 'y'), axis=0, tiled=True)]
  transfers between devices with their start and end apart: 71 -> 71, of which waited for: 34 -> 29; matrix products, arithmetic and copies ran while one was open for 17% -> 18% of each run, Pallas kernels for 34% -> 35%
where the time goes in v6:
time: 1000 us; the launch traced here: 997 us
  Pallas kernels  383 us (38%)
  waiting for transfers between devices  258 us (26%)
  local copies, waits for them, and re-layouts  126 us (13%)
  starting transfers between devices  95.6 us (10%)
  other arithmetic  92.2 us (9%)
  matrix products  26.3 us (3%)
  between operations  16.3 us (2%)
    ppermute x56, waiting for transfers between devices, swap(): lax.ppermute(values, axis, [(i, i ^ 1 << b) for i in range(lax.axis_size(...  203 us
    unnamed x275, local copies, waits for them, and re-layouts  83.8 us
    pallas_call x4, Pallas kernels, over_rows(): pl.pallas_call(with_weights(kernel), grid=(m // tile,), in_specs=[by_rows...  71.1 us
    pallas_call x2, Pallas kernels, attend_back(): pl.pallas_call(functools.partial(attend_back_kernel, heads), grid=(n,), o...  68.8 us
    pallas_call x4, Pallas kernels, project_rows(): pl.pallas_call(project_rows_kernel, grid=(m // tile,), in_specs=[by_rows(...  67.5 us
    all_to_all x8, waiting for transfers between devices, exchange(): return lax.all_to_all(pieces, SEQ, split_axis=0, concat_axis=0, tiled=True)  55.3 us
    pallas_call x3, Pallas kernels, outer_sum(): pl.pallas_call(functools.partial(outer_sum_kernel, len(pairs)), grid=(2 *...  53.1 us
    ppermute x56, starting transfers between devices, swap(): lax.ppermute(values, axis, [(i, i ^ 1 << b) for i in range(lax.axis_size(...  50.3 us
  transfers between devices with their start and end apart: 71, of which 29 were waited for; matrix products, arithmetic and copies ran while one was open for 18% of the time, Pallas kernels for 35%

profile of v6, /device:TPU:0, one launch (start us, length us, event | category | flops | bytes accessed | tf_op | source)
XLA Modules:
  0.0 997.4 jit_solution(15462283660518532251)
XLA Ops:
  34.9 28.8 %collective-permute-done.1 = bf16[2,64,2560]{2,1,0:T(8,128)(2,1)} collective-permute-done((bf16[2,64,2560]{2,1,0:T(8,128)(2,1)}, bf16[2,64,2560]{2,1,0:T(8,128)(2,1)}, u32[]{:S(2)}, u32[]{:S(2)}) %collective-permute-start.1) | collective-permute-done | bytes 655392 | tf_op jit(solution)/shard_map/ppermute | solution.py:47
  74.8 12.2 %collective-permute-done.7 = bf16[2,64,2048]{2,1,0:T(8,128)(2,1)S(1)} collective-permute-done((bf16[2,64,2048]{2,1,0:T(8,128)(2,1)S(1)}, bf16[2,64,2048]{2,1,0:T(8,128)(2,1)S(1)}, u32[]{:S(2)}, u32[]{:S(2)}) %collective-permute-start.7) | collective-permute-done | bytes 524320 | tf_op jit(solution)/shard_map/ppermute | solution.py:47
  94.3 33.2 %collective-permute-done.10 = bf16[2,2,64,1408]{3,2,1,0:T(8,128)(2,1)S(1)} collective-permute-done((bf16[2,2,64,1408]{3,2,1,0:T(8,128)(2,1)S(1)}, bf16[2,2,64,1408]{3,2,1,0:T(8,128)(2,1)S(1)}, u32[]{:S(2)}, u32[]{:S(2)}) %collective-permute-start.10) | collective-permute-done | bytes 720928 | tf_op jit(solution)/shard_map/ppermute | solution.py:47
  135.9 11.1 %all-gather.6.cloned.1.call-start = ((), (), s32[]{:S(2)}) async-start(), calls=%async_computation.13 | async-start | bytes 14417920 | tf_op jit(solution)/shard_map/all_gather | solution.py:817
  151.4 5.0 fusion.96
  156.4 4.8 convolution_add_fusion.q_ref.k_ref.v_ref
  161.2 7.3 pack_heads.2
  168.5 13.8 %collective-permute-done.13 = bf16[2,2,64,1408]{3,2,1,0:T(8,128)(2,1)} collective-permute-done((bf16[2,2,64,1408]{3,2,1,0:T(8,128)(2,1)}, bf16[2,2,64,1408]{3,2,1,0:T(8,128)(2,1)}, u32[]{:S(2)}, u32[]{:S(2)}) %collective-permute-start.13) | collective-permute-done | bytes 720928 | tf_op jit(solution)/shard_map/ppermute | solution.py:47
  189.3 4.8 pad_maximum_fusion.1.own_ref
  194.0 7.4 pack_heads.3
  204.6 13.7 %interleave.2 = bf16[2,2,4,1,128,2560]{5,4,3,2,1,0:T(8,128)(2,1)} custom-call(s32[1]{0:T(128)} %bitcast.52.core_ref, bf16[2,1,4,128,2560]{4,3,2,1,0:T(8,128)(2,1)S(1)} %copy-done.7, bf16[2,1,4,128,2560]{4,3,2,1,0:T(8,128)(2,1)} %bitcast.56.other_ref), custom_call_target="tpu_custom_call" | custom-call | bytes 65536 | tf_op jit(solution)/shard_map/interleave/pallas_call | solution.py:428
  218.3 8.1 all-to-all-done.qkv_ref
  233.2 27.9 %attend.2 = (bf16[8,256,256]{2,1,0:T(8,128)(2,1)S(1)}, f32[8,256,256]{2,1,0:T(8,128)S(1)}, f32[8,8,1024]{2,1,0:T(8,128)S(1)}) custom-call(s32[8]{0:T(128)S(1)} %get-tuple-element.443.lo_ref, s32[8]{0:T(128)S(1)} %get-tuple-element.438.hi_ref, s32[8,1,256]{2,1,0:T(1,128)S(1)} %bitcast.551, bf16[8,256,384]{2,1,0:T(8,128)(2,1)S(1)} %copy-done.11), custom_call_target="tpu_custom_call" | custom-call | bytes 1048576 | tf_op jit(solution)/shard_map/attend/pallas_call | solution.py:194
  263.4 5.8 all-to-all-done.1.qkv_ref
  279.5 12.5 %interleave.3 = bf16[2,2,4,2,64,2048]{5,4,3,2,1,0:T(8,128)(2,1)} custom-call(s32[1]{0:T(128)} %bitcast.52.core_ref, bf16[2,2,4,64,2048]{4,3,2,1,0:T(8,128)(2,1)S(1)} %bitcast.548, bf16[2,2,4,64,2048]{4,3,2,1,0:T(8,128)(2,1)} %bitcast.64.other_ref), custom_call_target="tpu_custom_call" | custom-call | bytes 65536 | tf_op jit(solution)/shard_map/interleave/pallas_call | solution.py:428
  292.0 21.2 %attend.3 = (bf16[8,256,256]{2,1,0:T(8,128)(2,1)S(1)}, f32[8,256,256]{2,1,0:T(8,128)S(1)}, f32[8,8,1024]{2,1,0:T(8,128)S(1)}) custom-call(s32[8]{0:T(128)S(1)} %get-tuple-element.442.lo_ref, s32[8]{0:T(128)S(1)} %get-tuple-element.439.hi_ref, s32[8,1,256]{2,1,0:T(1,128)S(1)} %bitcast.549, bf16[8,256,384]{2,1,0:T(8,128)(2,1)S(1)} %all-to-all-done.1.qkv_ref), custom_call_target="tpu_custom_call" | custom-call | bytes 1048576 | tf_op jit(solution)/shard_map/attend/pallas_call | solution.py:194
  315.5 14.6 %collective-permute-done.15 = bf16[2,2,64,1408]{3,2,1,0:T(8,128)(2,1)} collective-permute-done((bf16[2,2,64,1408]{3,2,1,0:T(8,128)(2,1)S(1)}, bf16[2,2,64,1408]{3,2,1,0:T(8,128)(2,1)}, u32[]{:S(2)}, u32[]{:S(2)}) %collective-permute-start.15) | collective-permute-done | bytes 720928 | tf_op jit(solution)/shard_map/ppermute | solution.py:47
  341.8 6.1 rows_by.3
  352.7 7.3 all-to-all-done.3
  367.5 6.1 rows_by.4
  389.6 21.4 %ffn_forward.2 = (f32[1024,1408]{1,0:T(8,128)}, f32[1024,1408]{1,0:T(8,128)}, bf16[1024,1408]{1,0:T(8,128)(2,1)S(1)}) custom-call(bf16[1024,2048]{1,0:T(8,128)(2,1)} %copy-done, bf16[4,2,2,2,64,2816]{5,4,3,2,1,0:T(8,128)(2,1)} %bitcast.553), custom_call_target="tpu_custom_call" | custom-call | bytes 65536 | tf_op jit(solution)/shard_map/ffn_forward/pallas_call | solution.py:505
  421.5 20.7 %ffn_forward.3 = (f32[1024,1408]{1,0:T(8,128)}, f32[1024,1408]{1,0:T(8,128)}, bf16[1024,1408]{1,0:T(8,128)(2,1)S(1)}) custom-call(bf16[1024,2048]{1,0:T(8,128)(2,1)} %copy-done.38, bf16[4,2,2,2,64,2816]{5,4,3,2,1,0:T(8,128)(2,1)} %bitcast.554), custom_call_target="tpu_custom_call" | custom-call | bytes 65536 | tf_op jit(solution)/shard_map/ffn_forward/pallas_call | solution.py:505
  451.7 16.6 %outer_sum.3 = bf16[2,2,2,2,2,64,1408]{6,5,4,3,2,1,0:T(8,128)(2,1)} custom-call(bf16[1024,2048]{1,0:T(8,128)(2,1)} %copy-done.3, bf16[1024,1408]{1,0:T(8,128)(2,1)S(1)} %copy-done.16, bf16[1024,2048]{1,0:T(8,128)(2,1)} %copy-done.5, bf16[1024,1408]{1,0:T(8,128)(2,1)S(1)} %get-tuple-element.305.refs_3_.x_ref), custom_call_target="tpu_custom_call" | custom-call | bytes 65536 | tf_op jit(solution)/shard_map/outer_sum/pallas_call | solution.py:665
  470.5 14.3 %ffn_backward.2.x_ref.refs_1_ = bf16[1024,2816]{1,0:T(8,128)(2,1)} custom-call(bf16[1024,2048]{1,0:T(8,128)(2,1)S(1)} %copy-done.4, bf16[4,2,2,2,64,1408]{5,4,3,2,1,0:T(8,128)(2,1)} %bitcast.557, f32[1024,1408]{1,0:T(8,128)} %get-tuple-element.257.refs_0_, f32[1024,1408]{1,0:T(8,128)} %get-tuple-element.258.refs_1_), custom_call_target="tpu_custom_call" | custom-call | bytes 65536 | tf_op jit(solution)/shard_map/ffn_backward/pallas_call | solution.py:505
  484.8 20.6 %project_rows.4 = bf16[1024,2048]{1,0:T(8,128)(2,1)S(1)} custom-call(bf16[1024,2816]{1,0:T(8,128)(2,1)} %ffn_backward.2.x_ref.refs_1_, bf16[4,2,2,2,64,2816]{5,4,3,2,1,0:T(8,128)(2,1)} %bitcast.555), custom_call_target="tpu_custom_call" | custom-call | bytes 65536 | tf_op jit(solution)/shard_map/project_rows/pallas_call | solution.py:580
  510.0 12.9 %project_rows.5 = bf16[1024,2048]{1,0:T(8,128)(2,1)} custom-call(bf16[1024,1408]{1,0:T(8,128)(2,1)S(1)} %copy-done.17, bf16[4,2,2,2,64,1408]{5,4,3,2,1,0:T(8,128)(2,1)} %bitcast.558), custom_call_target="tpu_custom_call" | custom-call | bytes 65536 | tf_op jit(solution)/shard_map/project_rows/pallas_call | solution.py:580
  530.6 14.8 %ffn_backward.3.x_ref.refs_3_ = bf16[1024,2816]{1,0:T(8,128)(2,1)} custom-call(bf16[1024,2048]{1,0:T(8,128)(2,1)S(1)} %copy-done.6, bf16[4,2,2,2,64,1408]{5,4,3,2,1,0:T(8,128)(2,1)} %bitcast.559, f32[1024,1408]{1,0:T(8,128)} %get-tuple-element.265.refs_0_, f32[1024,1408]{1,0:T(8,128)} %get-tuple-element.266.refs_1_), custom_call_target="tpu_custom_call" | custom-call | bytes 65536 | tf_op jit(solution)/shard_map/ffn_backward/pallas_call | solution.py:505
  545.4 21.1 %project_rows.6 = bf16[1024,2048]{1,0:T(8,128)(2,1)S(1)} custom-call(bf16[1024,2816]{1,0:T(8,128)(2,1)} %ffn_backward.3.x_ref.refs_3_, bf16[4,2,2,2,64,2816]{5,4,3,2,1,0:T(8,128)(2,1)} %bitcast.556), custom_call_target="tpu_custom_call" | custom-call | bytes 65536 | tf_op jit(solution)/shard_map/project_rows/pallas_call | solution.py:580
  581.3 18.3 %outer_sum.4 = bf16[2,2,2,2,2,64,1408]{6,5,4,3,2,1,0:T(8,128)(2,1)} custom-call(bf16[1024,2048]{1,0:T(8,128)(2,1)S(1)} %copy-done.1, bf16[1024,2816]{1,0:T(8,128)(2,1)} %ffn_backward.2.x_ref.refs_1_, bf16[1024,2048]{1,0:T(8,128)(2,1)} %copy-done.38, bf16[1024,2816]{1,0:T(8,128)(2,1)} %ffn_backward.3.x_ref.refs_3_), custom_call_target="tpu_custom_call" | custom-call | bytes 65536 | tf_op jit(solution)/shard_map/outer_sum/pallas_call | solution.py:665
  599.6 4.9 collective-permute-done.31
  605.4 4.5 all-to-all-start.4
  613.0 18.3 %outer_sum.5 = bf16[2,2,2,2,2,64,1408]{6,5,4,3,2,1,0:T(8,128)(2,1)} custom-call(bf16[1024,2048]{1,0:T(8,128)(2,1)S(1)} %copy-done.2, bf16[1024,2816]{1,0:T(8,128)(2,1)} %ffn_backward.2.x_ref.refs_1_, bf16[1024,2048]{1,0:T(8,128)(2,1)} %copy-done.38, bf16[1024,2816]{1,0:T(8,128)(2,1)} %ffn_backward.3.x_ref.refs_3_), custom_call_target="tpu_custom_call" | custom-call | bytes 65536 | tf_op jit(solution)/shard_map/outer_sum/pallas_call | solution.py:665
  631.3 5.1 all-to-all-done.4.g_ref
  661.5 6.7 convolution_convert_fusion
  678.4 38.2 %attend_back.2 = (bf16[8,256,256]{2,1,0:T(8,128)(2,1)S(1)}, bf16[8,256,128]{2,1,0:T(8,128)(2,1)S(1)}) custom-call(s32[8]{0:T(128)S(1)} %get-tuple-element.443.lo_ref, s32[8]{0:T(128)S(1)} %get-tuple-element.438.hi_ref, s32[8,1,256]{2,1,0:T(1,128)S(1)} %bitcast.552, bf16[8,256,384]{2,1,0:T(8,128)(2,1)S(1)} %copy-done.12, ...), custom_call_target="tpu_custom_call" | custom-call | bytes 1048576 | tf_op jit(solution)/shard_map/attend_back/pallas_call | solution.py:302
  722.3 30.6 %attend_back.3 = (bf16[8,256,256]{2,1,0:T(8,128)(2,1)S(1)}, bf16[8,256,128]{2,1,0:T(8,128)(2,1)S(1)}) custom-call(s32[8]{0:T(128)S(1)} %get-tuple-element.442.lo_ref, s32[8]{0:T(128)S(1)} %get-tuple-element.439.hi_ref, s32[8,1,256]{2,1,0:T(1,128)S(1)} %bitcast.550, bf16[8,256,384]{2,1,0:T(8,128)(2,1)S(1)} %all-to-all-done.1.qkv_ref, ...), custom_call_target="tpu_custom_call" | custom-call | bytes 1048576 | tf_op jit(solution)/shard_map/attend_back/pallas_call | solution.py:302
  754.3 5.6 all-to-all-done.6.in_ref
  764.0 5.4 fusion
  778.5 12.9 %project_rows.7 = bf16[1024,2048]{1,0:T(8,128)(2,1)} custom-call(bf16[1024,1408]{1,0:T(8,128)(2,1)S(1)} %copy-done.14, bf16[4,2,2,2,64,1408]{5,4,3,2,1,0:T(8,128)(2,1)} %bitcast.560), custom_call_target="tpu_custom_call" | custom-call | bytes 65536 | tf_op jit(solution)/shard_map/project_rows/pallas_call | solution.py:580
  794.0 23.4 %all-to-all-done.7.in_ref = bf16[8,256,384]{2,1,0:T(8,128)(2,1)S(1)} async-done(((bf16[8,256,384]{2,1,0:T(8,128)(2,1)}), bf16[8,256,384]{2,1,0:T(8,128)(2,1)S(1)}, u32[]{:S(2)}, u32[]{:S(2)}) %all-to-all-start.7) | async-done | bytes 1572896 | tf_op jit(solution)/shard_map/all_to_all | solution.py:688
  818.6 13.2 %collective-permute-done.34 = bf16[2,2,64,1408]{3,2,1,0:T(8,128)(2,1)} collective-permute-done((bf16[2,2,64,1408]{3,2,1,0:T(8,128)(2,1)}, bf16[2,2,64,1408]{3,2,1,0:T(8,128)(2,1)}, u32[]{:S(2)}, u32[]{:S(2)}) %collective-permute-start.34) | collective-permute-done | bytes 720928 | tf_op jit(solution)/shard_map/ppermute | solution.py:47
  835.3 5.0 outer_rows.1
  846.5 11.4 %rows_by.5 = f32[512,2048]{1,0:T(8,128)} custom-call(bf16[512,2560]{1,0:T(8,128)(2,1)S(1)} %pad_maximum_fusion.5.x_ref, bf16[2048,2560]{1,0:T(8,128)(2,1)} %bitcast.569), custom_call_target="tpu_custom_call" | custom-call | bytes 65536 | tf_op jit(solution)/shard_map/rows_by/pallas_call | solution.py:600
  860.3 19.9 %collective-permute-done.37 = bf16[2,2,64,1408]{3,2,1,0:T(8,128)(2,1)S(1)} collective-permute-done((bf16[2,2,64,1408]{3,2,1,0:T(8,128)(2,1)S(1)}, bf16[2,2,64,1408]{3,2,1,0:T(8,128)(2,1)S(1)}, u32[]{:S(2)}, u32[]{:S(2)}) %collective-permute-start.37) | collective-permute-done | bytes 720928 | tf_op jit(solution)/shard_map/ppermute | solution.py:47
  880.3 5.1 add_convert_fusion
  904.2 21.1 %collective-permute-done.39 = bf16[2,2,2,64,1280]{4,3,2,1,0:T(8,128)(2,1)S(1)} collective-permute-done((bf16[2,2,2,64,1280]{4,3,2,1,0:T(8,128)(2,1)S(1)}, bf16[2,2,2,64,1280]{4,3,2,1,0:T(8,128)(2,1)S(1)}, u32[]{:S(2)}, u32[]{:S(2)}) %collective-permute-start.39) | collective-permute-done | bytes 1310752 | tf_op jit(solution)/shard_map/ppermute | solution.py:47
  935.3 7.5 collective-permute-done.41
  961.0 13.9 %collective-permute-done.48 = bf16[2,64,2560]{2,1,0:T(8,128)(2,1)} collective-permute-done((bf16[2,64,2560]{2,1,0:T(8,128)(2,1)}, bf16[2,64,2560]{2,1,0:T(8,128)(2,1)}, u32[]{:S(2)}, u32[]{:S(2)}) %collective-permute-start.48) | collective-permute-done | bytes 655392 | tf_op jit(solution)/shard_map/ppermute | solution.py:47
  (570 shorter events, 316.2 us)
Async XLA Ops:
  7.2 211.1 %all-gather.4.cloned.1.call-start = ((), (), s32[]{:S(2)}) async-start(), calls=%async_computation.12 | async-start | bytes 5242880 | tf_op jit(solution)/shard_map/all_gather | solution.py:817
  10.3 24.6 %collective-permute-start.3 = (bf16[64,2048]{1,0:T(8,128)(2,1)}, bf16[64,2048]{1,0:T(8,128)(2,1)}, u32[]{:S(2)}, u32[]{:S(2)}) collective-permute-start(bf16[64,2048]{1,0:T(8,128)(2,1)} %param.13), channel_id=1, source_target_pairs={{0,4},{4,0},{1,5},{5,1},{2,6},{6,2},{3,7},{7,3},{8,12},{12,8},{9,1... | collective-permute-start | bytes 786440 | tf_op jit(solution)/shard_map/ppermute | solution.py:47
  26.4 39.4 %collective-permute-start.2 = (bf16[3,64,2816]{2,1,0:T(8,128)(2,1)}, bf16[3,64,2816]{2,1,0:T(8,128)(2,1)}, u32[]{:S(2)}, u32[]{:S(2)}) collective-permute-start(bf16[3,64,2816]{2,1,0:T(8,128)(2,1)} %pad_maximum_fusion.15), channel_id=1, source_target_pairs={{0,2},{2,0},{1,3},{3,1},{4,6},{6,4},{5,7},{7,5},{8,10},{10,8},{9,1... | collective-permute-start | bytes 3244040 | tf_op jit(solution)/shard_map/ppermute | solution.py:47
  28.7 35.0 %collective-permute-start.1 = (bf16[2,64,2560]{2,1,0:T(8,128)(2,1)}, bf16[2,64,2560]{2,1,0:T(8,128)(2,1)}, u32[]{:S(2)}, u32[]{:S(2)}) collective-permute-start(bf16[2,64,2560]{2,1,0:T(8,128)(2,1)} %pad_maximum_fusion.24), channel_id=1, source_target_pairs={{0,4},{4,0},{1,5},{5,1},{2,6},{6,2},{3,7},{7,3},{8,12},{12,8},{9,1... | collective-permute-start | bytes 1966088 | tf_op jit(solution)/shard_map/ppermute | solution.py:47
  87.8 42.0 %collective-permute-start.9 = (bf16[2,2,2,64,1280]{4,3,2,1,0:T(8,128)(2,1)S(1)}, bf16[2,2,2,64,1280]{4,3,2,1,0:T(8,128)(2,1)S(1)}, u32[]{:S(2)}, u32[]{:S(2)}) collective-permute-start(bf16[2,2,2,64,1280]{4,3,2,1,0:T(8,128)(2,1)S(1)} %pad_maximum_fusion.14), channel_id=1, source_target_pairs={{0,1},{1,0},{2,3},{3,2},{4,5},{5,4},{6,7},{7,6},{8,9},{9,8},{10,11... | collective-permute-start | bytes 3932168 | tf_op jit(solution)/shard_map/ppermute | solution.py:47
  88.6 41.1 %collective-permute-start.8 = (bf16[2,2,2,64,1280]{4,3,2,1,0:T(8,128)(2,1)S(1)}, bf16[2,2,2,64,1280]{4,3,2,1,0:T(8,128)(2,1)S(1)}, u32[]{:S(2)}, u32[]{:S(2)}) collective-permute-start(bf16[2,2,2,64,1280]{4,3,2,1,0:T(8,128)(2,1)S(1)} %pad_maximum_fusion.13), channel_id=1, source_target_pairs={{0,16},{16,0},{1,17},{17,1},{2,18},{18,2},{3,19},{19,3},{4,20},{20... | collective-permute-start | bytes 3932168 | tf_op jit(solution)/shard_map/ppermute | solution.py:47
  90.2 39.5 %collective-permute-start.11 = (bf16[256,2048]{1,0:T(8,128)(2,1)S(1)}, bf16[256,2048]{1,0:T(8,128)(2,1)}, u32[]{:S(2)}, u32[]{:S(2)}) collective-permute-start(bf16[256,2048]{1,0:T(8,128)(2,1)S(1)} %get-tuple-element.190), channel_id=1, source_target_pairs={{0,2},{2,0},{1,3},{3,1},{4,6},{6,4},{5,7},{7,5},{8,10},{10,8},{9,1... | collective-permute-start | bytes 3145736 | tf_op jit(solution)/shard_map/ppermute | solution.py:47
  90.9 36.6 %collective-permute-start.10 = (bf16[2,2,64,1408]{3,2,1,0:T(8,128)(2,1)S(1)}, bf16[2,2,64,1408]{3,2,1,0:T(8,128)(2,1)S(1)}, u32[]{:S(2)}, u32[]{:S(2)}) collective-permute-start(bf16[2,2,64,1408]{3,2,1,0:T(8,128)(2,1)S(1)} %pad_maximum_fusion.22), channel_id=1, source_target_pairs={{0,4},{4,0},{1,5},{5,1},{2,6},{6,2},{3,7},{7,3},{8,12},{12,8},{9,1... | collective-permute-start | bytes 2162696 | tf_op jit(solution)/shard_map/ppermute | solution.py:47
  135.9 243.8 %all-gather.6.cloned.1.call-start = ((), (), s32[]{:S(2)}) async-start(), calls=%async_computation.13 | async-start | bytes 14417920 | tf_op jit(solution)/shard_map/all_gather | solution.py:817
  147.0 35.3 %collective-permute-start.13 = (bf16[2,2,64,1408]{3,2,1,0:T(8,128)(2,1)}, bf16[2,2,64,1408]{3,2,1,0:T(8,128)(2,1)}, u32[]{:S(2)}, u32[]{:S(2)}) collective-permute-start(bf16[2,2,64,1408]{3,2,1,0:T(8,128)(2,1)} %pad_maximum_fusion.20), channel_id=1, source_target_pairs={{0,4},{4,0},{1,5},{5,1},{2,6},{6,2},{3,7},{7,3},{8,12},{12,8},{9,1... | collective-permute-start | bytes 2162696 | tf_op jit(solution)/shard_map/ppermute | solution.py:47
  185.3 41.1 %all-to-all-start = ((bf16[8,256,384]{2,1,0:T(8,128)(2,1)}), bf16[8,256,384]{2,1,0:T(8,128)(2,1)S(1)}, u32[]{:S(2)}, u32[]{:S(2)}) async-start(bf16[8,256,384]{2,1,0:T(8,128)(2,1)} %pack_heads.2), calls=%async_computation | async-start | bytes 3145728 | tf_op jit(solution)/shard_map/all_to_all | solution.py:688
  227.6 41.6 %collective-permute-start.14 = (bf16[4,2,2,64,2048]{4,3,2,1,0:T(8,128)(2,1)}, bf16[4,2,2,64,2048]{4,3,2,1,0:T(8,128)(2,1)}, u32[]{:S(2)}, u32[]{:S(2)}) collective-permute-start(bf16[4,2,2,64,2048]{4,3,2,1,0:T(8,128)(2,1)} %bitcast.547), channel_id=1, source_target_pairs={{0,8},{8,0},{1,9},{9,1},{2,10},{10,2},{3,11},{11,3},{4,12},{12,4},... | collective-permute-start | bytes 12582920 | tf_op jit(solution)/shard_map/ppermute | solution.py:47
  227.6 41.6 %all-to-all-start.1 = ((bf16[8,256,384]{2,1,0:T(8,128)(2,1)}), bf16[8,256,384]{2,1,0:T(8,128)(2,1)S(1)}, u32[]{:S(2)}, u32[]{:S(2)}) async-start(bf16[8,256,384]{2,1,0:T(8,128)(2,1)} %pack_heads.3), calls=%async_computation.1 | async-start | bytes 3145728 | tf_op jit(solution)/shard_map/all_to_all | solution.py:688
  269.2 60.9 %all-to-all-start.2 = ((bf16[8,256,256]{2,1,0:T(8,128)(2,1)}), bf16[8,256,256]{2,1,0:T(8,128)(2,1)}, u32[]{:S(2)}, u32[]{:S(2)}) async-start(bf16[8,256,256]{2,1,0:T(8,128)(2,1)} %copy-done.27), calls=%async_computation.2 | async-start | bytes 2097152 | tf_op jit(solution)/shard_map/all_to_all | solution.py:688
  273.4 56.6 %collective-permute-start.15 = (bf16[2,2,64,1408]{3,2,1,0:T(8,128)(2,1)S(1)}, bf16[2,2,64,1408]{3,2,1,0:T(8,128)(2,1)}, u32[]{:S(2)}, u32[]{:S(2)}) collective-permute-start(bf16[2,2,64,1408]{3,2,1,0:T(8,128)(2,1)S(1)} %copy-done.79), channel_id=1, source_target_pairs={{0,4},{4,0},{1,5},{5,1},{2,6},{6,2},{3,7},{7,3},{8,12},{12,8},{9,1... | collective-permute-start | bytes 2162696 | tf_op jit(solution)/shard_map/ppermute | solution.py:47
  330.1 30.0 %all-to-all-start.3 = ((bf16[8,256,256]{2,1,0:T(8,128)(2,1)}), bf16[8,256,256]{2,1,0:T(8,128)(2,1)}, u32[]{:S(2)}, u32[]{:S(2)}) async-start(bf16[8,256,256]{2,1,0:T(8,128)(2,1)} %copy-done.26), calls=%async_computation.3 | async-start | bytes 2097152 | tf_op jit(solution)/shard_map/all_to_all | solution.py:688
  334.4 133.9 %all-gather.8.cloned.1.call-start = ((), (), s32[]{:S(2)}) async-start(), calls=%async_computation.14 | async-start | bytes 7208960 | tf_op jit(solution)/shard_map/all_gather | solution.py:817
  350.9 28.9 %collective-permute-start.17 = (bf16[256,2048]{1,0:T(8,128)(2,1)}, bf16[256,2048]{1,0:T(8,128)(2,1)}, u32[]{:S(2)}, u32[]{:S(2)}) collective-permute-start(bf16[256,2048]{1,0:T(8,128)(2,1)} %multiply_convert_fusion.2), channel_id=1, source_target_pairs={{0,2},{2,0},{1,3},{3,1},{4,6},{6,4},{5,7},{7,5},{8,10},{10,8},{9,1... | collective-permute-start | bytes 3145736 | tf_op jit(solution)/shard_map/ppermute | solution.py:47
  382.4 290.5 %reduce-scatter.5.cloned.1.call-start = ((), (), s32[]{:S(2)}) async-start(), calls=%async_computation.15 | async-start | bytes 7208960 | tf_op jit(solution)/shard_map/reduce_scatter | solution.py:904
  383.4 27.6 %collective-permute-start.19 = (bf16[256,2048]{1,0:T(8,128)(2,1)}, bf16[256,2048]{1,0:T(8,128)(2,1)}, u32[]{:S(2)}, u32[]{:S(2)}) collective-permute-start(bf16[256,2048]{1,0:T(8,128)(2,1)} %multiply_convert_fusion.1), channel_id=1, source_target_pairs={{0,2},{2,0},{1,3},{3,1},{4,6},{6,4},{5,7},{7,5},{8,10},{10,8},{9,1... | collective-permute-start | bytes 3145736 | tf_op jit(solution)/shard_map/ppermute | solution.py:47
  383.4 31.0 %collective-permute-start.20 = (bf16[256,2048]{1,0:T(8,128)(2,1)}, bf16[256,2048]{1,0:T(8,128)(2,1)S(1)}, u32[]{:S(2)}, u32[]{:S(2)}) collective-permute-start(bf16[256,2048]{1,0:T(8,128)(2,1)} %copy-done.73), channel_id=1, source_target_pairs={{0,8},{8,0},{1,9},{9,1},{2,10},{10,2},{3,11},{11,3},{4,12},{12,4},... | collective-permute-start | bytes 3145736 | tf_op jit(solution)/shard_map/ppermute | solution.py:47
  385.9 30.9 %collective-permute-start.23 = (bf16[256,2048]{1,0:T(8,128)(2,1)}, bf16[256,2048]{1,0:T(8,128)(2,1)}, u32[]{:S(2)}, u32[]{:S(2)}) collective-permute-start(bf16[256,2048]{1,0:T(8,128)(2,1)} %multiply_convert_fusion.1), channel_id=1, source_target_pairs={{0,8},{8,0},{1,9},{9,1},{2,10},{10,2},{3,11},{11,3},{4,12},{12,4},... | collective-permute-start | bytes 3145736 | tf_op jit(solution)/shard_map/ppermute | solution.py:47
  413.0 29.2 %collective-permute-start.25 = (bf16[256,2048]{1,0:T(8,128)(2,1)S(1)}, bf16[256,2048]{1,0:T(8,128)(2,1)}, u32[]{:S(2)}, u32[]{:S(2)}) collective-permute-start(bf16[256,2048]{1,0:T(8,128)(2,1)S(1)} %copy-done.72), channel_id=1, source_target_pairs={{0,2},{2,0},{1,3},{3,1},{4,6},{6,4},{5,7},{7,5},{8,10},{10,8},{9,1... | collective-permute-start | bytes 3145736 | tf_op jit(solution)/shard_map/ppermute | solution.py:47
  416.2 28.4 %collective-permute-start.22 = (bf16[256,2048]{1,0:T(8,128)(2,1)S(1)}, bf16[256,2048]{1,0:T(8,128)(2,1)S(1)}, u32[]{:S(2)}, u32[]{:S(2)}) collective-permute-start(bf16[256,2048]{1,0:T(8,128)(2,1)S(1)} %copy-done.72), channel_id=1, source_target_pairs={{0,8},{8,0},{1,9},{9,1},{2,10},{10,2},{3,11},{11,3},{4,12},{12,4},... | collective-permute-start | bytes 3145736 | tf_op jit(solution)/shard_map/ppermute | solution.py:47
  416.3 29.8 %collective-permute-start.21 = (bf16[256,2048]{1,0:T(8,128)(2,1)}, bf16[256,2048]{1,0:T(8,128)(2,1)}, u32[]{:S(2)}, u32[]{:S(2)}) collective-permute-start(bf16[256,2048]{1,0:T(8,128)(2,1)} %collective-permute-done.11), channel_id=1, source_target_pairs={{0,8},{8,0},{1,9},{9,1},{2,10},{10,2},{3,11},{11,3},{4,12},{12,4},... | collective-permute-start | bytes 3145736 | tf_op jit(solution)/shard_map/ppermute | solution.py:47
  508.1 263.7 %reduce-scatter.7.cloned.1.call-start = ((), (), s32[]{:S(2)}) async-start(), calls=%async_computation.16 | async-start | bytes 7208960 | tf_op jit(solution)/shard_map/reduce_scatter | solution.py:904
  524.9 41.6 %collective-permute-start.29 = (bf16[2,256,2048]{2,1,0:T(8,128)(2,1)S(1)}, bf16[2,256,2048]{2,1,0:T(8,128)(2,1)S(1)}, u32[]{:S(2)}, u32[]{:S(2)}) collective-permute-start(bf16[2,256,2048]{2,1,0:T(8,128)(2,1)S(1)} %slice_bitcast_fusion.8), channel_id=1, source_target_pairs={{0,8},{8,0},{1,9},{9,1},{2,10},{10,2},{3,11},{11,3},{4,12},{12,4},... | collective-permute-start | bytes 6291464 | tf_op jit(solution)/shard_map/ppermute | solution.py:47
  529.5 37.0 %collective-permute-start.28 = (bf16[256,2048]{1,0:T(8,128)(2,1)}, bf16[256,2048]{1,0:T(8,128)(2,1)S(1)}, u32[]{:S(2)}, u32[]{:S(2)}) collective-permute-start(bf16[256,2048]{1,0:T(8,128)(2,1)} %fusion.21), channel_id=1, source_target_pairs={{0,2},{2,0},{1,3},{3,1},{4,6},{6,4},{5,7},{7,5},{8,10},{10,8},{9,1... | collective-permute-start | bytes 3145736 | tf_op jit(solution)/shard_map/ppermute | solution.py:47
  578.8 25.6 %collective-permute-start.31 = (bf16[256,2048]{1,0:T(8,128)(2,1)S(1)}, bf16[256,2048]{1,0:T(8,128)(2,1)S(1)}, u32[]{:S(2)}, u32[]{:S(2)}) collective-permute-start(bf16[256,2048]{1,0:T(8,128)(2,1)S(1)} %fusion.22), channel_id=1, source_target_pairs={{0,2},{2,0},{1,3},{3,1},{4,6},{6,4},{5,7},{7,5},{8,10},{10,8},{9,1... | collective-permute-start | bytes 3145736 | tf_op jit(solution)/shard_map/ppermute | solution.py:47
  605.4 30.9 %all-to-all-start.4 = ((bf16[8,256,256]{2,1,0:T(8,128)(2,1)}), bf16[8,256,256]{2,1,0:T(8,128)(2,1)}, u32[]{:S(2)}, u32[]{:S(2)}) async-start(bf16[8,256,256]{2,1,0:T(8,128)(2,1)} %copy-done.89), calls=%async_computation.4 | async-start | bytes 2097152 | tf_op jit(solution)/shard_map/all_to_all | solution.py:688
  609.9 235.1 %reduce-scatter.9.cloned.1.call-start = ((), (), s32[]{:S(2)}) async-start(), calls=%async_computation.17 | async-start | bytes 7208960 | tf_op jit(solution)/shard_map/reduce_scatter | solution.py:904
  642.2 75.8 %collective-permute-start.33 = (bf16[256,2048]{1,0:T(8,128)(2,1)}, bf16[256,2048]{1,0:T(8,128)(2,1)}, u32[]{:S(2)}, u32[]{:S(2)}) collective-permute-start(bf16[256,2048]{1,0:T(8,128)(2,1)} %fusion.23), channel_id=1, source_target_pairs={{0,2},{2,0},{1,3},{3,1},{4,6},{6,4},{5,7},{7,5},{8,10},{10,8},{9,1... | collective-permute-start | bytes 3145736 | tf_op jit(solution)/shard_map/ppermute | solution.py:47
  657.1 60.9 %all-to-all-start.5 = ((bf16[8,256,256]{2,1,0:T(8,128)(2,1)}), bf16[8,256,256]{2,1,0:T(8,128)(2,1)}, u32[]{:S(2)}, u32[]{:S(2)}) async-start(bf16[8,256,256]{2,1,0:T(8,128)(2,1)} %fusion.62), calls=%async_computation.5 | async-start | bytes 2097152 | tf_op jit(solution)/shard_map/all_to_all | solution.py:688
  672.9 91.1 %collective-permute-start.49 = (bf16[2,512,2048]{2,1,0:T(8,128)(2,1)}, bf16[2,512,2048]{2,1,0:T(8,128)(2,1)}, u32[]{:S(2)}, u32[]{:S(2)}) collective-permute-start(bf16[2,512,2048]{2,1,0:T(8,128)(2,1)} %dynamic-slice_bitcast_fusion), channel_id=1, source_target_pairs={{0,8},{8,0},{1,9},{9,1},{2,10},{10,2},{3,11},{11,3},{4,12},{12,4},... | collective-permute-start | bytes 12582920 | tf_op jit(solution)/shard_map/ppermute | solution.py:47
  674.1 43.9 %collective-permute-start.32 = (bf16[2,2,64,1408]{3,2,1,0:T(8,128)(2,1)S(1)}, bf16[2,2,64,1408]{3,2,1,0:T(8,128)(2,1)}, u32[]{:S(2)}, u32[]{:S(2)}) collective-permute-start(bf16[2,2,64,1408]{3,2,1,0:T(8,128)(2,1)S(1)} %dynamic-slice_bitcast_fusion.6), channel_id=1, source_target_pairs={{0,4},{4,0},{1,5},{5,1},{2,6},{6,2},{3,7},{7,3},{8,12},{12,8},{9,1... | collective-permute-start | bytes 2162696 | tf_op jit(solution)/shard_map/ppermute | solution.py:47
  718.0 41.9 %all-to-all-start.6 = ((bf16[8,256,384]{2,1,0:T(8,128)(2,1)}), bf16[8,256,384]{2,1,0:T(8,128)(2,1)}, u32[]{:S(2)}, u32[]{:S(2)}) async-start(bf16[8,256,384]{2,1,0:T(8,128)(2,1)} %pad_maximum_fusion.8), calls=%async_computation.7 | async-start | bytes 3145728 | tf_op jit(solution)/shard_map/all_to_all | solution.py:688
  759.9 57.6 %all-to-all-start.7 = ((bf16[8,256,384]{2,1,0:T(8,128)(2,1)}), bf16[8,256,384]{2,1,0:T(8,128)(2,1)S(1)}, u32[]{:S(2)}, u32[]{:S(2)}) async-start(bf16[8,256,384]{2,1,0:T(8,128)(2,1)} %pad_maximum_fusion.9), calls=%async_computation.8 | async-start | bytes 3145728 | tf_op jit(solution)/shard_map/all_to_all | solution.py:688
  763.6 124.4 %reduce-scatter.11.cloned.1.call-start = ((), (), s32[]{:S(2)}) async-start(), calls=%async_computation.18 | async-start | bytes 5242880 | tf_op jit(solution)/shard_map/reduce_scatter | solution.py:904
  774.0 57.8 %collective-permute-start.34 = (bf16[2,2,64,1408]{3,2,1,0:T(8,128)(2,1)}, bf16[2,2,64,1408]{3,2,1,0:T(8,128)(2,1)}, u32[]{:S(2)}, u32[]{:S(2)}) collective-permute-start(bf16[2,2,64,1408]{3,2,1,0:T(8,128)(2,1)} %dynamic-slice_bitcast_fusion.5), channel_id=1, source_target_pairs={{0,4},{4,0},{1,5},{5,1},{2,6},{6,2},{3,7},{7,3},{8,12},{12,8},{9,1... | collective-permute-start | bytes 2162696 | tf_op jit(solution)/shard_map/ppermute | solution.py:47
  840.4 39.9 %collective-permute-start.35 = (bf16[1024,2560]{1,0:T(8,128)(2,1)}, bf16[1024,2560]{1,0:T(8,128)(2,1)}, u32[]{:S(2)}, u32[]{:S(2)}) collective-permute-start(bf16[1024,2560]{1,0:T(8,128)(2,1)} %outer_rows.1), channel_id=1, source_target_pairs={{0,8},{8,0},{1,9},{9,1},{2,10},{10,2},{3,11},{11,3},{4,12},{12,4},... | collective-permute-start | bytes 15728648 | tf_op jit(solution)/shard_map/ppermute | solution.py:47
  841.9 38.3 %collective-permute-start.36 = (bf16[2,256,2048]{2,1,0:T(8,128)(2,1)}, bf16[2,256,2048]{2,1,0:T(8,128)(2,1)}, u32[]{:S(2)}, u32[]{:S(2)}) collective-permute-start(bf16[2,256,2048]{2,1,0:T(8,128)(2,1)} %slice_bitcast_fusion.1), channel_id=1, source_target_pairs={{0,8},{8,0},{1,9},{9,1},{2,10},{10,2},{3,11},{11,3},{4,12},{12,4},... | collective-permute-start | bytes 6291464 | tf_op jit(solution)/shard_map/ppermute | solution.py:47
  846.2 34.1 %collective-permute-start.37 = (bf16[2,2,64,1408]{3,2,1,0:T(8,128)(2,1)S(1)}, bf16[2,2,64,1408]{3,2,1,0:T(8,128)(2,1)S(1)}, u32[]{:S(2)}, u32[]{:S(2)}) collective-permute-start(bf16[2,2,64,1408]{3,2,1,0:T(8,128)(2,1)S(1)} %dynamic-slice_bitcast_fusion.4), channel_id=1, source_target_pairs={{0,4},{4,0},{1,5},{5,1},{2,6},{6,2},{3,7},{7,3},{8,12},{12,8},{9,1... | collective-permute-start | bytes 2162696 | tf_op jit(solution)/shard_map/ppermute | solution.py:47
  890.0 71.0 %collective-permute-start.50 = (bf16[2,64,2048]{2,1,0:T(8,128)(2,1)}, bf16[2,64,2048]{2,1,0:T(8,128)(2,1)}, u32[]{:S(2)}, u32[]{:S(2)}) collective-permute-start(bf16[2,64,2048]{2,1,0:T(8,128)(2,1)} %dynamic-slice_bitcast_fusion.9), channel_id=1, source_target_pairs={{0,4},{4,0},{1,5},{5,1},{2,6},{6,2},{3,7},{7,3},{8,12},{12,8},{9,1... | collective-permute-start | bytes 1572872 | tf_op jit(solution)/shard_map/ppermute | solution.py:47
  892.8 42.5 %collective-permute-start.42 = (bf16[3,2,64,1408]{3,2,1,0:T(8,128)(2,1)}, bf16[3,2,64,1408]{3,2,1,0:T(8,128)(2,1)S(1)}, u32[]{:S(2)}, u32[]{:S(2)}) collective-permute-start(bf16[3,2,64,1408]{3,2,1,0:T(8,128)(2,1)} %fusion.20), channel_id=1, source_target_pairs={{0,2},{2,0},{1,3},{3,1},{4,6},{6,4},{5,7},{7,5},{8,10},{10,8},{9,1... | collective-permute-start | bytes 3244040 | tf_op jit(solution)/shard_map/ppermute | solution.py:47
  895.1 30.2 %collective-permute-start.39 = (bf16[2,2,2,64,1280]{4,3,2,1,0:T(8,128)(2,1)S(1)}, bf16[2,2,2,64,1280]{4,3,2,1,0:T(8,128)(2,1)S(1)}, u32[]{:S(2)}, u32[]{:S(2)}) collective-permute-start(bf16[2,2,2,64,1280]{4,3,2,1,0:T(8,128)(2,1)S(1)} %dynamic-slice_bitcast_fusion.2), channel_id=1, source_target_pairs={{0,1},{1,0},{2,3},{3,2},{4,5},{5,4},{6,7},{7,6},{8,9},{9,8},{10,11... | collective-permute-start | bytes 3932168 | tf_op jit(solution)/shard_map/ppermute | solution.py:47
  896.7 30.5 %collective-permute-start.38 = (bf16[2,2,2,64,1280]{4,3,1,0,2:T(8,128)(2,1)S(1)}, bf16[2,2,2,64,1280]{4,3,1,0,2:T(8,128)(2,1)S(1)}, u32[]{:S(2)}, u32[]{:S(2)}) collective-permute-start(bf16[2,2,2,64,1280]{4,3,1,0,2:T(8,128)(2,1)S(1)} %dynamic-slice_bitcast_fusion.3), channel_id=1, source_target_pairs={{0,16},{16,0},{1,17},{17,1},{2,18},{18,2},{3,19},{19,3},{4,20},{20... | collective-permute-start | bytes 3932168 | tf_op jit(solution)/shard_map/ppermute | solution.py:47
  902.7 58.3 %collective-permute-start.51 = (bf16[256,2048]{1,0:T(8,128)(2,1)}, bf16[256,2048]{1,0:T(8,128)(2,1)}, u32[]{:S(2)}, u32[]{:S(2)}) collective-permute-start(bf16[256,2048]{1,0:T(8,128)(2,1)} %fusion.24), channel_id=1, source_target_pairs={{0,2},{2,0},{1,3},{3,1},{4,6},{6,4},{5,7},{7,5},{8,10},{10,8},{9,1... | collective-permute-start | bytes 3145736 | tf_op jit(solution)/shard_map/ppermute | solution.py:47
  945.7 29.1 %collective-permute-start.48 = (bf16[2,64,2560]{2,1,0:T(8,128)(2,1)}, bf16[2,64,2560]{2,1,0:T(8,128)(2,1)}, u32[]{:S(2)}, u32[]{:S(2)}) collective-permute-start(bf16[2,64,2560]{2,1,0:T(8,128)(2,1)} %fusion.30), channel_id=1, source_target_pairs={{0,4},{4,0},{1,5},{5,1},{2,6},{6,2},{3,7},{7,3},{8,12},{12,8},{9,1... | collective-permute-start | bytes 1966088 | tf_op jit(solution)/shard_map/ppermute | solution.py:47
  (134 other events, 921.3 us)
Sparse Core Ops, SparseCore 0:
  136.0 51.4 all-gather.3
  189.9 158.3 all-gather.5
  382.5 65.1 all-gather.7
  508.2 65.2 reduce-scatter.4
  605.6 85.2 reduce-scatter.6
  693.7 98.7 reduce-scatter.8
  795.5 56.2 reduce-scatter.10

commit v7 on v5

--- a/solution.py
+++ b/solution.py
@@ -793,12 +793,11 @@
     w_own = jnp.concatenate([flat(left.done()), flat(right.done())], axis=1)
     w_swap = Swap(w_own, CORE)
     up = Gather(up, "far", 1)
-    grad_group_1 = Group(flow.open(grad_out_all[rows:]))
     projected = dot(normed_one_own, w_own)
     w_other = w_swap.arrived
     projected = projected + dot(normed_one_other, w_other)
     packed_0 = pack_heads(projected, cosine, sine, 0, rows, n)
-    packed_0 = flow.close(packed_0, wait=[up, grad_group_1])
+    packed_0 = flow.close(packed_0, wait=[up])
 
     def attend_one(b, qkv_b):
         return attend(first_block[b], plain_from[b], doc_start[b], qkv_b, heads)
@@ -850,15 +849,14 @@
 
     gate_0, up_0, active_0 = ffn_forward(group_0, w_gate_up)
     active_0 = flow.close(active_0, wait=[group_1])
-    grad_group_0.arrived, grad_group_1.arrived = flow.open(
-        grad_group_0.arrived, grad_group_1.arrived
-    )
+    grad_group_0.arrived = flow.open(grad_group_0.arrived)
     grad_group_0 = grad_group_0.done()
-    grad_group_1 = grad_group_1.done()
+    grad_group_1 = Group(flow.open(grad_out_all[rows:]))
 
     group_1 = group_1.done()
     gate_1, up_1, active_1 = ffn_forward(flow.open(group_1), w_gate_up)
-    active_1 = flow.close(active_1)
+    active_1 = flow.close(active_1, wait=[grad_group_1])
+    grad_group_1 = grad_group_1.done()
 
     outer = lambda a, b: dot(a, b, ((0,), (0,)))
     owners = (nx, nfar, ny)

time: 1000 us -> 997 us (level)
  waiting for transfers between devices: 286 us -> 253 us
  local copies, waits for them, and re-layouts: 107 us -> 127 us
  Pallas kernels: 370 us -> 381 us
    unnamed x267 -> x275, local copies, waits for them, and re-layouts: 63.6 us -> 84.4 us
    ppermute x56, waiting for transfers between devices: 219 us -> 198 us  [swap(): lax.ppermute(values, axis, [(i, i ^ 1 << b) for i in range(lax.axis_size(...]
    all_to_all x8, waiting for transfers between devices: 66.9 us -> 54.1 us  [exchange(): return lax.all_to_all(pieces, SEQ, split_axis=0, concat_axis=0, tiled=True)]
  transfers between devices with their start and end apart: 71 -> 71, of which waited for: 34 -> 29; matrix products, arithmetic and copies ran while one was open for 17% -> 18% of each run, Pallas kernels for 34% -> 35%
where the time goes in v7:
time: 997 us; the launch traced here: 987 us
  Pallas kernels  381 us (38%)
  waiting for transfers between devices  253 us (25%)
  local copies, waits for them, and re-layouts  127 us (13%)
  other arithmetic  92.5 us (9%)
  starting transfers between devices  90.7 us (9%)
  matrix products  26.4 us (3%)
  between operations  16.6 us (2%)
    ppermute x56, waiting for transfers between devices, swap(): lax.ppermute(values, axis, [(i, i ^ 1 << b) for i in range(lax.axis_size(...  198 us
    pallas_call x8, Pallas kernels, over_rows(): pl.pallas_call(with_weights(kernel), grid=(m // tile,), in_specs=[by_rows...  131 us
    unnamed x275, local copies, waits for them, and re-layouts  84.4 us
    pallas_call x2, Pallas kernels, attend_back(): pl.pallas_call(functools.partial(attend_back_kernel, heads), grid=(n,), o...  72 us
    all_to_all x8, waiting for transfers between devices, exchange(): return lax.all_to_all(pieces, SEQ, split_axis=0, concat_axis=0, tiled=True)  54.1 us
    pallas_call x3, Pallas kernels, outer_sum(): pl.pallas_call(functools.partial(outer_sum_kernel, len(pairs)), grid=(2 *...  53.5 us
    pallas_call x2, Pallas kernels, attend(): pl.pallas_call(functools.partial(attend_kernel, heads), grid=(n,), out_sh...  51.8 us
    ppermute x56, starting transfers between devices, swap(): lax.ppermute(values, axis, [(i, i ^ 1 << b) for i in range(lax.axis_size(...  47.7 us
  transfers between devices with their start and end apart: 71, of which 29 were waited for; matrix products, arithmetic and copies ran while one was open for 18% of the time, Pallas kernels for 35%

profile of v7, /device:TPU:0, one launch (start us, length us, event | category | flops | bytes accessed | tf_op | source)
XLA Modules:
  0.0 987.3 jit_solution(16098180788070039038)
XLA Ops:
  34.9 28.8 %collective-permute-done.1 = bf16[2,64,2560]{2,1,0:T(8,128)(2,1)} collective-permute-done((bf16[2,64,2560]{2,1,0:T(8,128)(2,1)}, bf16[2,64,2560]{2,1,0:T(8,128)(2,1)}, u32[]{:S(2)}, u32[]{:S(2)}) %collective-permute-start.1) | collective-permute-done | bytes 655392 | tf_op jit(solution)/shard_map/ppermute | solution.py:47
  74.8 12.2 %collective-permute-done.7 = bf16[2,64,2048]{2,1,0:T(8,128)(2,1)S(1)} collective-permute-done((bf16[2,64,2048]{2,1,0:T(8,128)(2,1)S(1)}, bf16[2,64,2048]{2,1,0:T(8,128)(2,1)S(1)}, u32[]{:S(2)}, u32[]{:S(2)}) %collective-permute-start.7) | collective-permute-done | bytes 524320 | tf_op jit(solution)/shard_map/ppermute | solution.py:47
  94.3 33.2 %collective-permute-done.10 = bf16[2,2,64,1408]{3,2,1,0:T(8,128)(2,1)S(1)} collective-permute-done((bf16[2,2,64,1408]{3,2,1,0:T(8,128)(2,1)S(1)}, bf16[2,2,64,1408]{3,2,1,0:T(8,128)(2,1)S(1)}, u32[]{:S(2)}, u32[]{:S(2)}) %collective-permute-start.10) | collective-permute-done | bytes 720928 | tf_op jit(solution)/shard_map/ppermute | solution.py:47
  143.7 5.0 fusion.96
  148.7 4.8 convolution_add_fusion.q_ref.k_ref.v_ref
  153.6 7.2 pack_heads.2
  160.8 10.7 %collective-permute-done.13 = bf16[2,2,64,1408]{3,2,1,0:T(8,128)(2,1)} collective-permute-done((bf16[2,2,64,1408]{3,2,1,0:T(8,128)(2,1)}, bf16[2,2,64,1408]{3,2,1,0:T(8,128)(2,1)}, u32[]{:S(2)}, u32[]{:S(2)}) %collective-permute-start.13) | collective-permute-done | bytes 720928 | tf_op jit(solution)/shard_map/ppermute | solution.py:47
  178.5 4.8 pad_maximum_fusion.1.own_ref
  183.2 7.1 pack_heads.3
  192.9 13.7 %interleave.2 = bf16[2,2,4,1,128,2560]{5,4,3,2,1,0:T(8,128)(2,1)} custom-call(s32[1]{0:T(128)} %bitcast.52.core_ref, bf16[2,1,4,128,2560]{4,3,2,1,0:T(8,128)(2,1)S(1)} %copy-done.7, bf16[2,1,4,128,2560]{4,3,2,1,0:T(8,128)(2,1)} %bitcast.56.other_ref), custom_call_target="tpu_custom_call" | custom-call | bytes 65536 | tf_op jit(solution)/shard_map/interleave/pallas_call | solution.py:428
  206.6 9.0 all-to-all-done.qkv_ref
  222.4 27.9 %attend.2 = (bf16[8,256,256]{2,1,0:T(8,128)(2,1)S(1)}, f32[8,256,256]{2,1,0:T(8,128)S(1)}, f32[8,8,1024]{2,1,0:T(8,128)S(1)}) custom-call(s32[8]{0:T(128)S(1)} %get-tuple-element.443.lo_ref, s32[8]{0:T(128)S(1)} %get-tuple-element.438.hi_ref, s32[8,1,256]{2,1,0:T(1,128)S(1)} %bitcast.551, bf16[8,256,384]{2,1,0:T(8,128)(2,1)S(1)} %copy-done.11), custom_call_target="tpu_custom_call" | custom-call | bytes 1048576 | tf_op jit(solution)/shard_map/attend/pallas_call | solution.py:194
  252.6 5.8 all-to-all-done.1.qkv_ref
  268.8 12.5 %interleave.3 = bf16[2,2,4,2,64,2048]{5,4,3,2,1,0:T(8,128)(2,1)} custom-call(s32[1]{0:T(128)} %bitcast.52.core_ref, bf16[2,2,4,64,2048]{4,3,2,1,0:T(8,128)(2,1)S(1)} %bitcast.548, bf16[2,2,4,64,2048]{4,3,2,1,0:T(8,128)(2,1)} %bitcast.64.other_ref), custom_call_target="tpu_custom_call" | custom-call | bytes 65536 | tf_op jit(solution)/shard_map/interleave/pallas_call | solution.py:428
  281.3 23.9 %attend.3 = (bf16[8,256,256]{2,1,0:T(8,128)(2,1)S(1)}, f32[8,256,256]{2,1,0:T(8,128)S(1)}, f32[8,8,1024]{2,1,0:T(8,128)S(1)}) custom-call(s32[8]{0:T(128)S(1)} %get-tuple-element.442.lo_ref, s32[8]{0:T(128)S(1)} %get-tuple-element.439.hi_ref, s32[8,1,256]{2,1,0:T(1,128)S(1)} %bitcast.549, bf16[8,256,384]{2,1,0:T(8,128)(2,1)S(1)} %all-to-all-done.1.qkv_ref), custom_call_target="tpu_custom_call" | custom-call | bytes 1048576 | tf_op jit(solution)/shard_map/attend/pallas_call | solution.py:194
  307.4 11.9 %collective-permute-done.15 = bf16[2,2,64,1408]{3,2,1,0:T(8,128)(2,1)} collective-permute-done((bf16[2,2,64,1408]{3,2,1,0:T(8,128)(2,1)S(1)}, bf16[2,2,64,1408]{3,2,1,0:T(8,128)(2,1)}, u32[]{:S(2)}, u32[]{:S(2)}) %collective-permute-start.15) | collective-permute-done | bytes 720928 | tf_op jit(solution)/shard_map/ppermute | solution.py:47
  331.0 6.1 rows_by.3
  342.0 7.3 all-to-all-done.3
  356.7 6.1 rows_by.4
  371.6 8.8 reduce-scatter.5.cloned.1.call-start
  387.1 20.8 %ffn_forward.2 = (f32[1024,1408]{1,0:T(8,128)}, f32[1024,1408]{1,0:T(8,128)}, bf16[1024,1408]{1,0:T(8,128)(2,1)S(1)}) custom-call(bf16[1024,2048]{1,0:T(8,128)(2,1)} %copy-done, bf16[4,2,2,2,64,2816]{5,4,3,2,1,0:T(8,128)(2,1)} %bitcast.553), custom_call_target="tpu_custom_call" | custom-call | bytes 65536 | tf_op jit(solution)/shard_map/ffn_forward/pallas_call | solution.py:499
  418.1 20.7 %ffn_forward.3 = (f32[1024,1408]{1,0:T(8,128)}, f32[1024,1408]{1,0:T(8,128)}, bf16[1024,1408]{1,0:T(8,128)(2,1)S(1)}) custom-call(bf16[1024,2048]{1,0:T(8,128)(2,1)} %copy-done.38, bf16[4,2,2,2,64,2816]{5,4,3,2,1,0:T(8,128)(2,1)} %bitcast.554), custom_call_target="tpu_custom_call" | custom-call | bytes 65536 | tf_op jit(solution)/shard_map/ffn_forward/pallas_call | solution.py:499
  448.3 16.6 %outer_sum.3 = bf16[2,2,2,2,2,64,1408]{6,5,4,3,2,1,0:T(8,128)(2,1)} custom-call(bf16[1024,2048]{1,0:T(8,128)(2,1)} %copy-done.3, bf16[1024,1408]{1,0:T(8,128)(2,1)S(1)} %copy-done.16, bf16[1024,2048]{1,0:T(8,128)(2,1)} %copy-done.5, bf16[1024,1408]{1,0:T(8,128)(2,1)S(1)} %get-tuple-element.305.refs_3_.x_ref), custom_call_target="tpu_custom_call" | custom-call | bytes 65536 | tf_op jit(solution)/shard_map/outer_sum/pallas_call | solution.py:628
  467.1 14.3 %ffn_backward.2.x_ref.refs_1_ = bf16[1024,2816]{1,0:T(8,128)(2,1)} custom-call(bf16[1024,2048]{1,0:T(8,128)(2,1)S(1)} %copy-done.4, bf16[4,2,2,2,64,1408]{5,4,3,2,1,0:T(8,128)(2,1)} %bitcast.557, f32[1024,1408]{1,0:T(8,128)} %get-tuple-element.257.refs_0_, f32[1024,1408]{1,0:T(8,128)} %get-tuple-element.258.refs_1_), custom_call_target="tpu_custom_call" | custom-call | bytes 65536 | tf_op jit(solution)/shard_map/ffn_backward/pallas_call | solution.py:499
  481.4 18.9 %project_rows.4 = bf16[1024,2048]{1,0:T(8,128)(2,1)S(1)} custom-call(bf16[1024,2816]{1,0:T(8,128)(2,1)} %ffn_backward.2.x_ref.refs_1_, bf16[4,2,2,2,64,2816]{5,4,3,2,1,0:T(8,128)(2,1)} %bitcast.555), custom_call_target="tpu_custom_call" | custom-call | bytes 65536 | tf_op jit(solution)/shard_map/project_rows/pallas_call | solution.py:499
  504.9 11.3 %project_rows.5 = bf16[1024,2048]{1,0:T(8,128)(2,1)} custom-call(bf16[1024,1408]{1,0:T(8,128)(2,1)S(1)} %copy-done.17, bf16[4,2,2,2,64,1408]{5,4,3,2,1,0:T(8,128)(2,1)} %bitcast.558), custom_call_target="tpu_custom_call" | custom-call | bytes 65536 | tf_op jit(solution)/shard_map/project_rows/pallas_call | solution.py:499
  524.2 14.7 %ffn_backward.3.x_ref.refs_3_ = bf16[1024,2816]{1,0:T(8,128)(2,1)} custom-call(bf16[1024,2048]{1,0:T(8,128)(2,1)S(1)} %copy-done.6, bf16[4,2,2,2,64,1408]{5,4,3,2,1,0:T(8,128)(2,1)} %bitcast.559, f32[1024,1408]{1,0:T(8,128)} %get-tuple-element.265.refs_0_, f32[1024,1408]{1,0:T(8,128)} %get-tuple-element.266.refs_1_), custom_call_target="tpu_custom_call" | custom-call | bytes 65536 | tf_op jit(solution)/shard_map/ffn_backward/pallas_call | solution.py:499
  538.9 19.1 %project_rows.6 = bf16[1024,2048]{1,0:T(8,128)(2,1)S(1)} custom-call(bf16[1024,2816]{1,0:T(8,128)(2,1)} %ffn_backward.3.x_ref.refs_3_, bf16[4,2,2,2,64,2816]{5,4,3,2,1,0:T(8,128)(2,1)} %bitcast.556), custom_call_target="tpu_custom_call" | custom-call | bytes 65536 | tf_op jit(solution)/shard_map/project_rows/pallas_call | solution.py:499
  572.9 18.7 %outer_sum.4 = bf16[2,2,2,2,2,64,1408]{6,5,4,3,2,1,0:T(8,128)(2,1)} custom-call(bf16[1024,2048]{1,0:T(8,128)(2,1)S(1)} %copy-done.1, bf16[1024,2816]{1,0:T(8,128)(2,1)} %ffn_backward.2.x_ref.refs_1_, bf16[1024,2048]{1,0:T(8,128)(2,1)} %copy-done.38, bf16[1024,2816]{1,0:T(8,128)(2,1)} %ffn_backward.3.x_ref.refs_3_), custom_call_target="tpu_custom_call" | custom-call | bytes 65536 | tf_op jit(solution)/shard_map/outer_sum/pallas_call | solution.py:628
  591.5 4.3 collective-permute-done.31
  596.9 4.8 all-to-all-start.4
  604.9 18.3 %outer_sum.5 = bf16[2,2,2,2,2,64,1408]{6,5,4,3,2,1,0:T(8,128)(2,1)} custom-call(bf16[1024,2048]{1,0:T(8,128)(2,1)S(1)} %copy-done.2, bf16[1024,2816]{1,0:T(8,128)(2,1)} %ffn_backward.2.x_ref.refs_1_, bf16[1024,2048]{1,0:T(8,128)(2,1)} %copy-done.38, bf16[1024,2816]{1,0:T(8,128)(2,1)} %ffn_backward.3.x_ref.refs_3_), custom_call_target="tpu_custom_call" | custom-call | bytes 65536 | tf_op jit(solution)/shard_map/outer_sum/pallas_call | solution.py:628
  648.4 4.4 all-to-all-start.5
  652.8 6.8 convolution_convert_fusion
  669.8 38.2 %attend_back.2 = (bf16[8,256,256]{2,1,0:T(8,128)(2,1)S(1)}, bf16[8,256,128]{2,1,0:T(8,128)(2,1)S(1)}) custom-call(s32[8]{0:T(128)S(1)} %get-tuple-element.443.lo_ref, s32[8]{0:T(128)S(1)} %get-tuple-element.438.hi_ref, s32[8,1,256]{2,1,0:T(1,128)S(1)} %bitcast.552, bf16[8,256,384]{2,1,0:T(8,128)(2,1)S(1)} %copy-done.12, ...), custom_call_target="tpu_custom_call" | custom-call | bytes 1048576 | tf_op jit(solution)/shard_map/attend_back/pallas_call | solution.py:302
  709.3 4.3 all-to-all-start.6
  713.6 33.8 %attend_back.3 = (bf16[8,256,256]{2,1,0:T(8,128)(2,1)S(1)}, bf16[8,256,128]{2,1,0:T(8,128)(2,1)S(1)}) custom-call(s32[8]{0:T(128)S(1)} %get-tuple-element.442.lo_ref, s32[8]{0:T(128)S(1)} %get-tuple-element.439.hi_ref, s32[8,1,256]{2,1,0:T(1,128)S(1)} %bitcast.550, bf16[8,256,384]{2,1,0:T(8,128)(2,1)S(1)} %all-to-all-done.1.qkv_ref, ...), custom_call_target="tpu_custom_call" | custom-call | bytes 1048576 | tf_op jit(solution)/shard_map/attend_back/pallas_call | solution.py:302
  755.2 5.5 fusion
  769.7 11.3 %project_rows.7 = bf16[1024,2048]{1,0:T(8,128)(2,1)} custom-call(bf16[1024,1408]{1,0:T(8,128)(2,1)S(1)} %copy-done.14, bf16[4,2,2,2,64,1408]{5,4,3,2,1,0:T(8,128)(2,1)} %bitcast.560), custom_call_target="tpu_custom_call" | custom-call | bytes 65536 | tf_op jit(solution)/shard_map/project_rows/pallas_call | solution.py:499
  783.5 25.3 %all-to-all-done.7.in_ref = bf16[8,256,384]{2,1,0:T(8,128)(2,1)S(1)} async-done(((bf16[8,256,384]{2,1,0:T(8,128)(2,1)}), bf16[8,256,384]{2,1,0:T(8,128)(2,1)S(1)}, u32[]{:S(2)}, u32[]{:S(2)}) %all-to-all-start.7) | async-done | bytes 1572896 | tf_op jit(solution)/shard_map/all_to_all | solution.py:651
  810.0 13.2 %collective-permute-done.34 = bf16[2,2,64,1408]{3,2,1,0:T(8,128)(2,1)} collective-permute-done((bf16[2,2,64,1408]{3,2,1,0:T(8,128)(2,1)}, bf16[2,2,64,1408]{3,2,1,0:T(8,128)(2,1)}, u32[]{:S(2)}, u32[]{:S(2)}) %collective-permute-start.34) | collective-permute-done | bytes 720928 | tf_op jit(solution)/shard_map/ppermute | solution.py:47
  826.7 5.0 outer_rows.1
  837.8 11.4 %rows_by.5 = f32[512,2048]{1,0:T(8,128)} custom-call(bf16[512,2560]{1,0:T(8,128)(2,1)S(1)} %pad_maximum_fusion.5.x_ref, bf16[2048,2560]{1,0:T(8,128)(2,1)} %bitcast.569), custom_call_target="tpu_custom_call" | custom-call | bytes 65536 | tf_op jit(solution)/shard_map/rows_by/pallas_call | solution.py:563
  851.7 19.9 %collective-permute-done.37 = bf16[2,2,64,1408]{3,2,1,0:T(8,128)(2,1)S(1)} collective-permute-done((bf16[2,2,64,1408]{3,2,1,0:T(8,128)(2,1)S(1)}, bf16[2,2,64,1408]{3,2,1,0:T(8,128)(2,1)S(1)}, u32[]{:S(2)}, u32[]{:S(2)}) %collective-permute-start.37) | collective-permute-done | bytes 720928 | tf_op jit(solution)/shard_map/ppermute | solution.py:47
  871.6 5.2 add_convert_fusion
  893.3 23.3 %collective-permute-done.39 = bf16[2,2,2,64,1280]{4,3,2,1,0:T(8,128)(2,1)S(1)} collective-permute-done((bf16[2,2,2,64,1280]{4,3,2,1,0:T(8,128)(2,1)S(1)}, bf16[2,2,2,64,1280]{4,3,2,1,0:T(8,128)(2,1)S(1)}, u32[]{:S(2)}, u32[]{:S(2)}) %collective-permute-start.39) | collective-permute-done | bytes 1310752 | tf_op jit(solution)/shard_map/ppermute | solution.py:47
  925.8 7.5 collective-permute-done.41
  951.4 13.4 %collective-permute-done.48 = bf16[2,64,2560]{2,1,0:T(8,128)(2,1)} collective-permute-done((bf16[2,64,2560]{2,1,0:T(8,128)(2,1)}, bf16[2,64,2560]{2,1,0:T(8,128)(2,1)}, u32[]{:S(2)}, u32[]{:S(2)}) %collective-permute-start.48) | collective-permute-done | bytes 655392 | tf_op jit(solution)/shard_map/ppermute | solution.py:47
  (570 shorter events, 312.6 us)
Async XLA Ops:
  7.2 199.4 %all-gather.4.cloned.1.call-start = ((), (), s32[]{:S(2)}) async-start(), calls=%async_computation.12 | async-start | bytes 5242880 | tf_op jit(solution)/shard_map/all_gather | solution.py:780
  10.3 24.6 %collective-permute-start.3 = (bf16[64,2048]{1,0:T(8,128)(2,1)}, bf16[64,2048]{1,0:T(8,128)(2,1)}, u32[]{:S(2)}, u32[]{:S(2)}) collective-permute-start(bf16[64,2048]{1,0:T(8,128)(2,1)} %param.13), channel_id=1, source_target_pairs={{0,4},{4,0},{1,5},{5,1},{2,6},{6,2},{3,7},{7,3},{8,12},{12,8},{9,1... | collective-permute-start | bytes 786440 | tf_op jit(solution)/shard_map/ppermute | solution.py:47
  26.4 39.4 %collective-permute-start.2 = (bf16[3,64,2816]{2,1,0:T(8,128)(2,1)}, bf16[3,64,2816]{2,1,0:T(8,128)(2,1)}, u32[]{:S(2)}, u32[]{:S(2)}) collective-permute-start(bf16[3,64,2816]{2,1,0:T(8,128)(2,1)} %pad_maximum_fusion.15), channel_id=1, source_target_pairs={{0,2},{2,0},{1,3},{3,1},{4,6},{6,4},{5,7},{7,5},{8,10},{10,8},{9,1... | collective-permute-start | bytes 3244040 | tf_op jit(solution)/shard_map/ppermute | solution.py:47
  28.7 35.0 %collective-permute-start.1 = (bf16[2,64,2560]{2,1,0:T(8,128)(2,1)}, bf16[2,64,2560]{2,1,0:T(8,128)(2,1)}, u32[]{:S(2)}, u32[]{:S(2)}) collective-permute-start(bf16[2,64,2560]{2,1,0:T(8,128)(2,1)} %pad_maximum_fusion.24), channel_id=1, source_target_pairs={{0,4},{4,0},{1,5},{5,1},{2,6},{6,2},{3,7},{7,3},{8,12},{12,8},{9,1... | collective-permute-start | bytes 1966088 | tf_op jit(solution)/shard_map/ppermute | solution.py:47
  87.8 42.0 %collective-permute-start.9 = (bf16[2,2,2,64,1280]{4,3,2,1,0:T(8,128)(2,1)S(1)}, bf16[2,2,2,64,1280]{4,3,2,1,0:T(8,128)(2,1)S(1)}, u32[]{:S(2)}, u32[]{:S(2)}) collective-permute-start(bf16[2,2,2,64,1280]{4,3,2,1,0:T(8,128)(2,1)S(1)} %pad_maximum_fusion.14), channel_id=1, source_target_pairs={{0,1},{1,0},{2,3},{3,2},{4,5},{5,4},{6,7},{7,6},{8,9},{9,8},{10,11... | collective-permute-start | bytes 3932168 | tf_op jit(solution)/shard_map/ppermute | solution.py:47
  88.6 41.1 %collective-permute-start.8 = (bf16[2,2,2,64,1280]{4,3,2,1,0:T(8,128)(2,1)S(1)}, bf16[2,2,2,64,1280]{4,3,2,1,0:T(8,128)(2,1)S(1)}, u32[]{:S(2)}, u32[]{:S(2)}) collective-permute-start(bf16[2,2,2,64,1280]{4,3,2,1,0:T(8,128)(2,1)S(1)} %pad_maximum_fusion.13), channel_id=1, source_target_pairs={{0,16},{16,0},{1,17},{17,1},{2,18},{18,2},{3,19},{19,3},{4,20},{20... | collective-permute-start | bytes 3932168 | tf_op jit(solution)/shard_map/ppermute | solution.py:47
  90.2 39.5 %collective-permute-start.11 = (bf16[256,2048]{1,0:T(8,128)(2,1)S(1)}, bf16[256,2048]{1,0:T(8,128)(2,1)}, u32[]{:S(2)}, u32[]{:S(2)}) collective-permute-start(bf16[256,2048]{1,0:T(8,128)(2,1)S(1)} %get-tuple-element.190), channel_id=1, source_target_pairs={{0,2},{2,0},{1,3},{3,1},{4,6},{6,4},{5,7},{7,5},{8,10},{10,8},{9,1... | collective-permute-start | bytes 3145736 | tf_op jit(solution)/shard_map/ppermute | solution.py:47
  90.9 36.6 %collective-permute-start.10 = (bf16[2,2,64,1408]{3,2,1,0:T(8,128)(2,1)S(1)}, bf16[2,2,64,1408]{3,2,1,0:T(8,128)(2,1)S(1)}, u32[]{:S(2)}, u32[]{:S(2)}) collective-permute-start(bf16[2,2,64,1408]{3,2,1,0:T(8,128)(2,1)S(1)} %pad_maximum_fusion.22), channel_id=1, source_target_pairs={{0,4},{4,0},{1,5},{5,1},{2,6},{6,2},{3,7},{7,3},{8,12},{12,8},{9,1... | collective-permute-start | bytes 2162696 | tf_op jit(solution)/shard_map/ppermute | solution.py:47
  135.9 233.1 %all-gather.6.cloned.1.call-start = ((), (), s32[]{:S(2)}) async-start(), calls=%async_computation.13 | async-start | bytes 14417920 | tf_op jit(solution)/shard_map/all_gather | solution.py:780
  136.2 35.3 %collective-permute-start.13 = (bf16[2,2,64,1408]{3,2,1,0:T(8,128)(2,1)}, bf16[2,2,64,1408]{3,2,1,0:T(8,128)(2,1)}, u32[]{:S(2)}, u32[]{:S(2)}) collective-permute-start(bf16[2,2,64,1408]{3,2,1,0:T(8,128)(2,1)} %pad_maximum_fusion.20), channel_id=1, source_target_pairs={{0,4},{4,0},{1,5},{5,1},{2,6},{6,2},{3,7},{7,3},{8,12},{12,8},{9,1... | collective-permute-start | bytes 2162696 | tf_op jit(solution)/shard_map/ppermute | solution.py:47
  174.5 41.1 %all-to-all-start = ((bf16[8,256,384]{2,1,0:T(8,128)(2,1)}), bf16[8,256,384]{2,1,0:T(8,128)(2,1)S(1)}, u32[]{:S(2)}, u32[]{:S(2)}) async-start(bf16[8,256,384]{2,1,0:T(8,128)(2,1)} %pack_heads.2), calls=%async_computation | async-start | bytes 3145728 | tf_op jit(solution)/shard_map/all_to_all | solution.py:651
  216.7 41.7 %collective-permute-start.14 = (bf16[4,2,2,64,2048]{4,3,2,1,0:T(8,128)(2,1)}, bf16[4,2,2,64,2048]{4,3,2,1,0:T(8,128)(2,1)}, u32[]{:S(2)}, u32[]{:S(2)}) collective-permute-start(bf16[4,2,2,64,2048]{4,3,2,1,0:T(8,128)(2,1)} %bitcast.547), channel_id=1, source_target_pairs={{0,8},{8,0},{1,9},{9,1},{2,10},{10,2},{3,11},{11,3},{4,12},{12,4},... | collective-permute-start | bytes 12582920 | tf_op jit(solution)/shard_map/ppermute | solution.py:47
  216.7 41.7 %all-to-all-start.1 = ((bf16[8,256,384]{2,1,0:T(8,128)(2,1)}), bf16[8,256,384]{2,1,0:T(8,128)(2,1)S(1)}, u32[]{:S(2)}, u32[]{:S(2)}) async-start(bf16[8,256,384]{2,1,0:T(8,128)(2,1)} %pack_heads.3), calls=%async_computation.1 | async-start | bytes 3145728 | tf_op jit(solution)/shard_map/all_to_all | solution.py:651
  258.4 60.9 %all-to-all-start.2 = ((bf16[8,256,256]{2,1,0:T(8,128)(2,1)}), bf16[8,256,256]{2,1,0:T(8,128)(2,1)}, u32[]{:S(2)}, u32[]{:S(2)}) async-start(bf16[8,256,256]{2,1,0:T(8,128)(2,1)} %copy-done.27), calls=%async_computation.2 | async-start | bytes 2097152 | tf_op jit(solution)/shard_map/all_to_all | solution.py:651
  262.7 56.6 %collective-permute-start.15 = (bf16[2,2,64,1408]{3,2,1,0:T(8,128)(2,1)S(1)}, bf16[2,2,64,1408]{3,2,1,0:T(8,128)(2,1)}, u32[]{:S(2)}, u32[]{:S(2)}) collective-permute-start(bf16[2,2,64,1408]{3,2,1,0:T(8,128)(2,1)S(1)} %copy-done.79), channel_id=1, source_target_pairs={{0,4},{4,0},{1,5},{5,1},{2,6},{6,2},{3,7},{7,3},{8,12},{12,8},{9,1... | collective-permute-start | bytes 2162696 | tf_op jit(solution)/shard_map/ppermute | solution.py:47
  319.3 30.0 %all-to-all-start.3 = ((bf16[8,256,256]{2,1,0:T(8,128)(2,1)}), bf16[8,256,256]{2,1,0:T(8,128)(2,1)}, u32[]{:S(2)}, u32[]{:S(2)}) async-start(bf16[8,256,256]{2,1,0:T(8,128)(2,1)} %copy-done.26), calls=%async_computation.3 | async-start | bytes 2097152 | tf_op jit(solution)/shard_map/all_to_all | solution.py:651
  323.6 141.3 %all-gather.8.cloned.1.call-start = ((), (), s32[]{:S(2)}) async-start(), calls=%async_computation.14 | async-start | bytes 7208960 | tf_op jit(solution)/shard_map/all_gather | solution.py:780
  340.1 28.9 %collective-permute-start.17 = (bf16[256,2048]{1,0:T(8,128)(2,1)}, bf16[256,2048]{1,0:T(8,128)(2,1)}, u32[]{:S(2)}, u32[]{:S(2)}) collective-permute-start(bf16[256,2048]{1,0:T(8,128)(2,1)} %multiply_convert_fusion.2), channel_id=1, source_target_pairs={{0,2},{2,0},{1,3},{3,1},{4,6},{6,4},{5,7},{7,5},{8,10},{10,8},{9,1... | collective-permute-start | bytes 3145736 | tf_op jit(solution)/shard_map/ppermute | solution.py:47
  371.6 292.6 %reduce-scatter.5.cloned.1.call-start = ((), (), s32[]{:S(2)}) async-start(), calls=%async_computation.15 | async-start | bytes 7208960 | tf_op jit(solution)/shard_map/reduce_scatter | solution.py:867
  381.0 27.0 %collective-permute-start.19 = (bf16[256,2048]{1,0:T(8,128)(2,1)}, bf16[256,2048]{1,0:T(8,128)(2,1)}, u32[]{:S(2)}, u32[]{:S(2)}) collective-permute-start(bf16[256,2048]{1,0:T(8,128)(2,1)} %multiply_convert_fusion.1), channel_id=1, source_target_pairs={{0,2},{2,0},{1,3},{3,1},{4,6},{6,4},{5,7},{7,5},{8,10},{10,8},{9,1... | collective-permute-start | bytes 3145736 | tf_op jit(solution)/shard_map/ppermute | solution.py:47
  381.0 30.3 %collective-permute-start.20 = (bf16[256,2048]{1,0:T(8,128)(2,1)}, bf16[256,2048]{1,0:T(8,128)(2,1)S(1)}, u32[]{:S(2)}, u32[]{:S(2)}) collective-permute-start(bf16[256,2048]{1,0:T(8,128)(2,1)} %copy-done.73), channel_id=1, source_target_pairs={{0,8},{8,0},{1,9},{9,1},{2,10},{10,2},{3,11},{11,3},{4,12},{12,4},... | collective-permute-start | bytes 3145736 | tf_op jit(solution)/shard_map/ppermute | solution.py:47
  383.5 29.9 %collective-permute-start.23 = (bf16[256,2048]{1,0:T(8,128)(2,1)}, bf16[256,2048]{1,0:T(8,128)(2,1)}, u32[]{:S(2)}, u32[]{:S(2)}) collective-permute-start(bf16[256,2048]{1,0:T(8,128)(2,1)} %multiply_convert_fusion.1), channel_id=1, source_target_pairs={{0,8},{8,0},{1,9},{9,1},{2,10},{10,2},{3,11},{11,3},{4,12},{12,4},... | collective-permute-start | bytes 3145736 | tf_op jit(solution)/shard_map/ppermute | solution.py:47
  409.9 28.9 %collective-permute-start.25 = (bf16[256,2048]{1,0:T(8,128)(2,1)S(1)}, bf16[256,2048]{1,0:T(8,128)(2,1)}, u32[]{:S(2)}, u32[]{:S(2)}) collective-permute-start(bf16[256,2048]{1,0:T(8,128)(2,1)S(1)} %copy-done.72), channel_id=1, source_target_pairs={{0,2},{2,0},{1,3},{3,1},{4,6},{6,4},{5,7},{7,5},{8,10},{10,8},{9,1... | collective-permute-start | bytes 3145736 | tf_op jit(solution)/shard_map/ppermute | solution.py:47
  412.8 28.4 %collective-permute-start.22 = (bf16[256,2048]{1,0:T(8,128)(2,1)S(1)}, bf16[256,2048]{1,0:T(8,128)(2,1)S(1)}, u32[]{:S(2)}, u32[]{:S(2)}) collective-permute-start(bf16[256,2048]{1,0:T(8,128)(2,1)S(1)} %copy-done.72), channel_id=1, source_target_pairs={{0,8},{8,0},{1,9},{9,1},{2,10},{10,2},{3,11},{11,3},{4,12},{12,4},... | collective-permute-start | bytes 3145736 | tf_op jit(solution)/shard_map/ppermute | solution.py:47
  412.9 29.8 %collective-permute-start.21 = (bf16[256,2048]{1,0:T(8,128)(2,1)}, bf16[256,2048]{1,0:T(8,128)(2,1)}, u32[]{:S(2)}, u32[]{:S(2)}) collective-permute-start(bf16[256,2048]{1,0:T(8,128)(2,1)} %collective-permute-done.11), channel_id=1, source_target_pairs={{0,8},{8,0},{1,9},{9,1},{2,10},{10,2},{3,11},{11,3},{4,12},{12,4},... | collective-permute-start | bytes 3145736 | tf_op jit(solution)/shard_map/ppermute | solution.py:47
  503.1 260.0 %reduce-scatter.7.cloned.1.call-start = ((), (), s32[]{:S(2)}) async-start(), calls=%async_computation.16 | async-start | bytes 7208960 | tf_op jit(solution)/shard_map/reduce_scatter | solution.py:867
  518.5 39.6 %collective-permute-start.29 = (bf16[2,256,2048]{2,1,0:T(8,128)(2,1)S(1)}, bf16[2,256,2048]{2,1,0:T(8,128)(2,1)S(1)}, u32[]{:S(2)}, u32[]{:S(2)}) collective-permute-start(bf16[2,256,2048]{2,1,0:T(8,128)(2,1)S(1)} %slice_bitcast_fusion.8), channel_id=1, source_target_pairs={{0,8},{8,0},{1,9},{9,1},{2,10},{10,2},{3,11},{11,3},{4,12},{12,4},... | collective-permute-start | bytes 6291464 | tf_op jit(solution)/shard_map/ppermute | solution.py:47
  523.2 34.9 %collective-permute-start.28 = (bf16[256,2048]{1,0:T(8,128)(2,1)}, bf16[256,2048]{1,0:T(8,128)(2,1)S(1)}, u32[]{:S(2)}, u32[]{:S(2)}) collective-permute-start(bf16[256,2048]{1,0:T(8,128)(2,1)} %fusion.21), channel_id=1, source_target_pairs={{0,2},{2,0},{1,3},{3,1},{4,6},{6,4},{5,7},{7,5},{8,10},{10,8},{9,1... | collective-permute-start | bytes 3145736 | tf_op jit(solution)/shard_map/ppermute | solution.py:47
  570.4 25.5 %collective-permute-start.31 = (bf16[256,2048]{1,0:T(8,128)(2,1)S(1)}, bf16[256,2048]{1,0:T(8,128)(2,1)S(1)}, u32[]{:S(2)}, u32[]{:S(2)}) collective-permute-start(bf16[256,2048]{1,0:T(8,128)(2,1)S(1)} %fusion.22), channel_id=1, source_target_pairs={{0,2},{2,0},{1,3},{3,1},{4,6},{6,4},{5,7},{7,5},{8,10},{10,8},{9,1... | collective-permute-start | bytes 3145736 | tf_op jit(solution)/shard_map/ppermute | solution.py:47
  596.9 30.5 %all-to-all-start.4 = ((bf16[8,256,256]{2,1,0:T(8,128)(2,1)}), bf16[8,256,256]{2,1,0:T(8,128)(2,1)}, u32[]{:S(2)}, u32[]{:S(2)}) async-start(bf16[8,256,256]{2,1,0:T(8,128)(2,1)} %copy-done.89), calls=%async_computation.4 | async-start | bytes 2097152 | tf_op jit(solution)/shard_map/all_to_all | solution.py:651
  601.7 234.7 %reduce-scatter.9.cloned.1.call-start = ((), (), s32[]{:S(2)}) async-start(), calls=%async_computation.17 | async-start | bytes 7208960 | tf_op jit(solution)/shard_map/reduce_scatter | solution.py:867
  633.5 75.8 %collective-permute-start.33 = (bf16[256,2048]{1,0:T(8,128)(2,1)}, bf16[256,2048]{1,0:T(8,128)(2,1)}, u32[]{:S(2)}, u32[]{:S(2)}) collective-permute-start(bf16[256,2048]{1,0:T(8,128)(2,1)} %fusion.23), channel_id=1, source_target_pairs={{0,2},{2,0},{1,3},{3,1},{4,6},{6,4},{5,7},{7,5},{8,10},{10,8},{9,1... | collective-permute-start | bytes 3145736 | tf_op jit(solution)/shard_map/ppermute | solution.py:47
  648.4 60.9 %all-to-all-start.5 = ((bf16[8,256,256]{2,1,0:T(8,128)(2,1)}), bf16[8,256,256]{2,1,0:T(8,128)(2,1)}, u32[]{:S(2)}, u32[]{:S(2)}) async-start(bf16[8,256,256]{2,1,0:T(8,128)(2,1)} %fusion.62), calls=%async_computation.5 | async-start | bytes 2097152 | tf_op jit(solution)/shard_map/all_to_all | solution.py:651
  664.2 91.0 %collective-permute-start.49 = (bf16[2,512,2048]{2,1,0:T(8,128)(2,1)}, bf16[2,512,2048]{2,1,0:T(8,128)(2,1)}, u32[]{:S(2)}, u32[]{:S(2)}) collective-permute-start(bf16[2,512,2048]{2,1,0:T(8,128)(2,1)} %dynamic-slice_bitcast_fusion), channel_id=1, source_target_pairs={{0,8},{8,0},{1,9},{9,1},{2,10},{10,2},{3,11},{11,3},{4,12},{12,4},... | collective-permute-start | bytes 12582920 | tf_op jit(solution)/shard_map/ppermute | solution.py:47
  665.4 43.9 %collective-permute-start.32 = (bf16[2,2,64,1408]{3,2,1,0:T(8,128)(2,1)S(1)}, bf16[2,2,64,1408]{3,2,1,0:T(8,128)(2,1)}, u32[]{:S(2)}, u32[]{:S(2)}) collective-permute-start(bf16[2,2,64,1408]{3,2,1,0:T(8,128)(2,1)S(1)} %dynamic-slice_bitcast_fusion.6), channel_id=1, source_target_pairs={{0,4},{4,0},{1,5},{5,1},{2,6},{6,2},{3,7},{7,3},{8,12},{12,8},{9,1... | collective-permute-start | bytes 2162696 | tf_op jit(solution)/shard_map/ppermute | solution.py:47
  709.3 42.0 %all-to-all-start.6 = ((bf16[8,256,384]{2,1,0:T(8,128)(2,1)}), bf16[8,256,384]{2,1,0:T(8,128)(2,1)}, u32[]{:S(2)}, u32[]{:S(2)}) async-start(bf16[8,256,384]{2,1,0:T(8,128)(2,1)} %pad_maximum_fusion.8), calls=%async_computation.7 | async-start | bytes 3145728 | tf_op jit(solution)/shard_map/all_to_all | solution.py:651
  751.3 57.6 %all-to-all-start.7 = ((bf16[8,256,384]{2,1,0:T(8,128)(2,1)}), bf16[8,256,384]{2,1,0:T(8,128)(2,1)S(1)}, u32[]{:S(2)}, u32[]{:S(2)}) async-start(bf16[8,256,384]{2,1,0:T(8,128)(2,1)} %pad_maximum_fusion.9), calls=%async_computation.8 | async-start | bytes 3145728 | tf_op jit(solution)/shard_map/all_to_all | solution.py:651
  754.9 124.5 %reduce-scatter.11.cloned.1.call-start = ((), (), s32[]{:S(2)}) async-start(), calls=%async_computation.18 | async-start | bytes 5242880 | tf_op jit(solution)/shard_map/reduce_scatter | solution.py:867
  765.3 57.9 %collective-permute-start.34 = (bf16[2,2,64,1408]{3,2,1,0:T(8,128)(2,1)}, bf16[2,2,64,1408]{3,2,1,0:T(8,128)(2,1)}, u32[]{:S(2)}, u32[]{:S(2)}) collective-permute-start(bf16[2,2,64,1408]{3,2,1,0:T(8,128)(2,1)} %dynamic-slice_bitcast_fusion.5), channel_id=1, source_target_pairs={{0,4},{4,0},{1,5},{5,1},{2,6},{6,2},{3,7},{7,3},{8,12},{12,8},{9,1... | collective-permute-start | bytes 2162696 | tf_op jit(solution)/shard_map/ppermute | solution.py:47
  831.7 39.9 %collective-permute-start.35 = (bf16[1024,2560]{1,0:T(8,128)(2,1)}, bf16[1024,2560]{1,0:T(8,128)(2,1)}, u32[]{:S(2)}, u32[]{:S(2)}) collective-permute-start(bf16[1024,2560]{1,0:T(8,128)(2,1)} %outer_rows.1), channel_id=1, source_target_pairs={{0,8},{8,0},{1,9},{9,1},{2,10},{10,2},{3,11},{11,3},{4,12},{12,4},... | collective-permute-start | bytes 15728648 | tf_op jit(solution)/shard_map/ppermute | solution.py:47
  833.3 38.3 %collective-permute-start.36 = (bf16[2,256,2048]{2,1,0:T(8,128)(2,1)}, bf16[2,256,2048]{2,1,0:T(8,128)(2,1)}, u32[]{:S(2)}, u32[]{:S(2)}) collective-permute-start(bf16[2,256,2048]{2,1,0:T(8,128)(2,1)} %slice_bitcast_fusion.1), channel_id=1, source_target_pairs={{0,8},{8,0},{1,9},{9,1},{2,10},{10,2},{3,11},{11,3},{4,12},{12,4},... | collective-permute-start | bytes 6291464 | tf_op jit(solution)/shard_map/ppermute | solution.py:47
  837.5 34.1 %collective-permute-start.37 = (bf16[2,2,64,1408]{3,2,1,0:T(8,128)(2,1)S(1)}, bf16[2,2,64,1408]{3,2,1,0:T(8,128)(2,1)S(1)}, u32[]{:S(2)}, u32[]{:S(2)}) collective-permute-start(bf16[2,2,64,1408]{3,2,1,0:T(8,128)(2,1)S(1)} %dynamic-slice_bitcast_fusion.4), channel_id=1, source_target_pairs={{0,4},{4,0},{1,5},{5,1},{2,6},{6,2},{3,7},{7,3},{8,12},{12,8},{9,1... | collective-permute-start | bytes 2162696 | tf_op jit(solution)/shard_map/ppermute | solution.py:47
  881.4 69.9 %collective-permute-start.50 = (bf16[2,64,2048]{2,1,0:T(8,128)(2,1)}, bf16[2,64,2048]{2,1,0:T(8,128)(2,1)}, u32[]{:S(2)}, u32[]{:S(2)}) collective-permute-start(bf16[2,64,2048]{2,1,0:T(8,128)(2,1)} %dynamic-slice_bitcast_fusion.9), channel_id=1, source_target_pairs={{0,4},{4,0},{1,5},{5,1},{2,6},{6,2},{3,7},{7,3},{8,12},{12,8},{9,1... | collective-permute-start | bytes 1572872 | tf_op jit(solution)/shard_map/ppermute | solution.py:47
  884.2 41.6 %collective-permute-start.42 = (bf16[3,2,64,1408]{3,2,1,0:T(8,128)(2,1)}, bf16[3,2,64,1408]{3,2,1,0:T(8,128)(2,1)S(1)}, u32[]{:S(2)}, u32[]{:S(2)}) collective-permute-start(bf16[3,2,64,1408]{3,2,1,0:T(8,128)(2,1)} %fusion.20), channel_id=1, source_target_pairs={{0,2},{2,0},{1,3},{3,1},{4,6},{6,4},{5,7},{7,5},{8,10},{10,8},{9,1... | collective-permute-start | bytes 3244040 | tf_op jit(solution)/shard_map/ppermute | solution.py:47
  886.4 30.2 %collective-permute-start.39 = (bf16[2,2,2,64,1280]{4,3,2,1,0:T(8,128)(2,1)S(1)}, bf16[2,2,2,64,1280]{4,3,2,1,0:T(8,128)(2,1)S(1)}, u32[]{:S(2)}, u32[]{:S(2)}) collective-permute-start(bf16[2,2,2,64,1280]{4,3,2,1,0:T(8,128)(2,1)S(1)} %dynamic-slice_bitcast_fusion.2), channel_id=1, source_target_pairs={{0,1},{1,0},{2,3},{3,2},{4,5},{5,4},{6,7},{7,6},{8,9},{9,8},{10,11... | collective-permute-start | bytes 3932168 | tf_op jit(solution)/shard_map/ppermute | solution.py:47
  888.0 29.9 %collective-permute-start.38 = (bf16[2,2,2,64,1280]{4,3,1,0,2:T(8,128)(2,1)S(1)}, bf16[2,2,2,64,1280]{4,3,1,0,2:T(8,128)(2,1)S(1)}, u32[]{:S(2)}, u32[]{:S(2)}) collective-permute-start(bf16[2,2,2,64,1280]{4,3,1,0,2:T(8,128)(2,1)S(1)} %dynamic-slice_bitcast_fusion.3), channel_id=1, source_target_pairs={{0,16},{16,0},{1,17},{17,1},{2,18},{18,2},{3,19},{19,3},{4,20},{20... | collective-permute-start | bytes 3932168 | tf_op jit(solution)/shard_map/ppermute | solution.py:47
  891.8 59.5 %collective-permute-start.51 = (bf16[256,2048]{1,0:T(8,128)(2,1)}, bf16[256,2048]{1,0:T(8,128)(2,1)}, u32[]{:S(2)}, u32[]{:S(2)}) collective-permute-start(bf16[256,2048]{1,0:T(8,128)(2,1)} %fusion.24), channel_id=1, source_target_pairs={{0,2},{2,0},{1,3},{3,1},{4,6},{6,4},{5,7},{7,5},{8,10},{10,8},{9,1... | collective-permute-start | bytes 3145736 | tf_op jit(solution)/shard_map/ppermute | solution.py:47
  935.4 29.5 %collective-permute-start.48 = (bf16[2,64,2560]{2,1,0:T(8,128)(2,1)}, bf16[2,64,2560]{2,1,0:T(8,128)(2,1)}, u32[]{:S(2)}, u32[]{:S(2)}) collective-permute-start(bf16[2,64,2560]{2,1,0:T(8,128)(2,1)} %fusion.30), channel_id=1, source_target_pairs={{0,4},{4,0},{1,5},{5,1},{2,6},{6,2},{3,7},{7,3},{8,12},{12,8},{9,1... | collective-permute-start | bytes 1966088 | tf_op jit(solution)/shard_map/ppermute | solution.py:47
  (134 other events, 903.2 us)
Sparse Core Ops, SparseCore 0:
  136.0 64.5 all-gather.3
  203.0 156.8 all-gather.5
  371.7 65.1 all-gather.7
  503.2 65.3 reduce-scatter.4
  597.0 85.5 reduce-scatter.6
  685.4 99.0 reduce-scatter.8
  787.5 56.1 reduce-scatter.10
